TPU v7x, 1024 devices: a whole 4x8x16 slice. The times are simulated.
1024 devices in a mesh: dp: 2 (over core), expert: 64 (over x, z), etp: 8 (over y).
Axes of the slice: x: 4, y: 8, z: 16, core: 2. Of those that a mesh axis runs over, the one named last changes fastest.
Arguments:
- tokens: bfloat16 [4096, 4096], P(('dp', 'expert')), may hold values from -6 to 6
- cotangent: bfloat16 [4096, 4096], P(('dp', 'expert')), may hold values from -6 to 6
- expert_ids: int32 [4096, 8], P(('dp', 'expert')), may hold values from 0 to 63, all different within a row; in each aligned block of 32 rows (0 to 31, 32 to 63, ...) at most 5 rows name the same one
- probs: bfloat16 [4096, 8], P(('dp', 'expert')), may hold values from 0.049804688 to 1
- gate_weight: bfloat16 [64, 4096, 1024], P('expert', 'dp', 'etp'), may hold values from -0.09375 to 0.09375
- up_weight: bfloat16 [64, 4096, 1024], P('expert', 'dp', 'etp'), may hold values from -0.09375 to 0.09375
- down_weight: bfloat16 [64, 4096, 1024], P('expert', 'dp', 'etp'), may hold values from -0.1875 to 0.1875
Outputs:
- d_tokens: bfloat16 [4096, 4096], P(('dp', 'expert'), 'etp')
- grad_gate: bfloat16 [64, 4096, 1024], P('expert', 'dp', 'etp')
- grad_up: bfloat16 [64, 4096, 1024], P('expert', 'dp', 'etp')
- grad_down: bfloat16 [64, 4096, 1024], P('expert', 'dp', 'etp')
Inputs may be any that keep to these rules, and one draw needn't show every extreme that they name: `expert_ids`: each row names 8 different experts. Among the 32 rows of one index pair of dp and expert (aligned blocks), no expert is named by more than 5 rows, a bound that some block reaches.
All inputs are finite; a program needn't handle non-finite values.
Results may differ from a plain program's by a relative error of at most 0.02.
Values may be sent and summed in bfloat16 or wider, within the bound.
No kernel may reach another device: no remote copies, remote signals or barrier semaphores. Data moves between devices by JAX's collectives and lax.ppermute only.
A program may use at most 64 MiB of HBM per device.

v0:
```python
import jax
import jax.numpy as jnp
from jax import lax
from jax.sharding import PartitionSpec as P


def route_slots(ids, experts):
    onehot = (ids[..., None] == jnp.arange(experts, dtype=jnp.int32)).astype(jnp.int32)
    counts = jnp.sum(onehot, axis=1)
    before = jnp.cumsum(counts, axis=0) - counts
    return jnp.sum(onehot * before[:, None, :], axis=2)


def spread(occupied, values, owners):
    placed = jnp.einsum("ts,td->sd", occupied, values, preferred_element_type=jnp.float32)
    return placed.astype(jnp.bfloat16).reshape(owners, -1, values.shape[1])


def shards(tokens, cotangent, expert_ids, probs, gate_weight, up_weight, down_weight):
    owners = lax.axis_size("expert")
    local = gate_weight.shape[0]
    width = tokens.shape[1]
    tok_dev = tokens.shape[0]
    choose = expert_ids.shape[1]
    experts = owners * local
    capacity = min(tok_dev, (5 * tok_dev * choose + 4 * experts - 1) // (4 * experts))
    slots = route_slots(expert_ids, experts)
    dest = expert_ids * capacity + slots
    places = (dest[..., None] == jnp.arange(experts * capacity, dtype=jnp.int32)).astype(
        jnp.bfloat16
    )
    occupied = jnp.sum(places, axis=1)
    p_buf = jnp.einsum("tks,tk->s", places, probs, preferred_element_type=jnp.float32)
    p_buf = p_buf.astype(jnp.bfloat16).reshape(owners, local * capacity)
    weight_table = jnp.einsum(
        "tks,tk->ts", places, probs, preferred_element_type=jnp.float32
    ).astype(jnp.bfloat16)
    x_recv, dy_recv, p_recv = (
        lax.all_to_all(
            spread(occupied, tokens, owners), "expert", split_axis=0, concat_axis=0, tiled=True
        ),
        lax.all_to_all(
            spread(occupied, cotangent, owners), "expert", split_axis=0, concat_axis=0, tiled=True
        ),
        lax.all_to_all(p_buf, "expert", split_axis=0, concat_axis=0, tiled=True),
    )
    rows = x_recv.reshape(owners, local, capacity, width)
    dy_rows = dy_recv.reshape(owners, local, capacity, width)
    p_rows = p_recv.reshape(owners, local, capacity)
    scaled = (p_rows[..., None].astype(jnp.float32) * dy_rows.astype(jnp.float32)).astype(
        jnp.bfloat16
    )
    piece_gate = lax.all_gather(gate_weight, "dp", axis=1, tiled=True)
    piece_up = lax.all_gather(up_weight, "dp", axis=1, tiled=True)
    piece_down = lax.all_gather(down_weight, "dp", axis=1, tiled=True)
    gate_acc = jnp.einsum("sjcd,jdf->sjcf", rows, piece_gate, preferred_element_type=jnp.float32)
    up_acc = jnp.einsum("sjcd,jdf->sjcf", rows, piece_up, preferred_element_type=jnp.float32)
    back_acc = jnp.einsum("sjcd,jdf->sjcf", scaled, piece_down, preferred_element_type=jnp.float32)
    sig = jax.nn.sigmoid(gate_acc)
    act = gate_acc * sig
    hidden = (act * up_acc).astype(jnp.bfloat16)
    d_up = (back_acc * act).astype(jnp.bfloat16)
    d_gate = (back_acc * up_acc * sig * (1.0 + gate_acc * (1.0 - sig))).astype(jnp.bfloat16)
    stacked = jnp.stack((gate_weight, up_weight))
    piece = lax.all_gather(stacked, "dp", axis=2, tiled=True)
    out = jnp.einsum("sjcf,jdf->sjcd", d_gate, piece[0], preferred_element_type=jnp.float32)
    d_rows = out + jnp.einsum("sjcf,jdf->sjcd", d_up, piece[1], preferred_element_type=jnp.float32)
    shares = lax.psum_scatter(
        d_rows.reshape(owners, local * capacity, width).astype(jnp.bfloat16),
        "etp",
        scatter_dimension=2,
        tiled=True,
    )
    returned = lax.all_to_all(shares, "expert", split_axis=0, concat_axis=0, tiled=True)
    d_tokens = jnp.dot(
        weight_table, returned.reshape(experts * capacity, -1), preferred_element_type=jnp.float32
    )
    part_gate = jnp.einsum("sjcd,sjcf->jdf", rows, d_gate, preferred_element_type=jnp.float32)
    part_up = jnp.einsum("sjcd,sjcf->jdf", rows, d_up, preferred_element_type=jnp.float32)
    part_down = jnp.einsum("sjcd,sjcf->jdf", scaled, hidden, preferred_element_type=jnp.float32)
    grad_gate, grad_up, grad_down = (
        lax.psum_scatter(
            part_gate.astype(jnp.bfloat16), "dp", scatter_dimension=1, tiled=True
        ).astype(jnp.float32),
        lax.psum_scatter(
            part_up.astype(jnp.bfloat16), "dp", scatter_dimension=1, tiled=True
        ).astype(jnp.float32),
        lax.psum_scatter(
            part_down.astype(jnp.bfloat16), "dp", scatter_dimension=1, tiled=True
        ).astype(jnp.float32),
    )
    return (
        d_tokens.astype(jnp.bfloat16),
        grad_gate.astype(jnp.bfloat16),
        grad_up.astype(jnp.bfloat16),
        grad_down.astype(jnp.bfloat16),
    )


def solution(mesh):
    return jax.shard_map(
        shards,
        mesh=mesh,
        in_specs=(
            P(("dp", "expert"), None),
            P(("dp", "expert"), None),
            P(("dp", "expert"), None),
            P(("dp", "expert"), None),
            P("expert", "dp", "etp"),
            P("expert", "dp", "etp"),
            P("expert", "dp", "etp"),
        ),
        out_specs=(
            P(("dp", "expert"), "etp"),
            P("expert", "dp", "etp"),
            P("expert", "dp", "etp"),
            P("expert", "dp", "etp"),
        ),
        check_vma=False,
    )
```

profile of v0, /device:TPU:6, one launch (start us, length us, event | category | flops | bytes accessed | tf_op | source)
XLA Modules:
  0.0 579.5 jit_solution(4943946051973963628)
XLA Ops:
  7.2 0.8 copy.52
  9.8 0.9 convolution_reduce_fusion
  10.7 0.8 all_to_all.20
  11.5 22.5 %all-to-all-start = ((bf16[64,1,5]{2,1,0:T(2,128)(2,1)}), bf16[64,1,5]{2,1,0:T(2,128)(2,1)S(1)}, u32[]{:S(2)}, u32[]{:S(2)}) async-start(bf16[64,1,5]{2,1,0:T(2,128)(2,1)} %all_to_all.20), calls=%async_computation | async-start | bytes 65536 | tf_op jit(solution)/shard_map/all_to_all | solution.py:45
  34.2 0.9 convolution_convert_fusion
  35.0 2.9 reshape.105
  37.9 8.5 %all-to-all-done = bf16[64,1,5]{2,1,0:T(2,128)(2,1)S(1)} async-done(((bf16[64,1,5]{2,1,0:T(2,128)(2,1)}), bf16[64,1,5]{2,1,0:T(2,128)(2,1)S(1)}, u32[]{:S(2)}, u32[]{:S(2)}) %all-to-all-start) | async-done | bytes 672 | tf_op jit(solution)/shard_map/all_to_all | solution.py:45
  46.4 7.5 %all-to-all-start.2 = ((bf16[64,5,4096]{2,1,0:T(8,128)(2,1)}), bf16[64,5,4096]{2,1,0:T(8,128)(2,1)}, u32[]{:S(2)}, u32[]{:S(2)}) async-start(bf16[64,5,4096]{2,1,0:T(8,128)(2,1)} %reshape.105), calls=%async_computation.2 | async-start | bytes 8388608 | tf_op jit(solution)/shard_map/all_to_all | solution.py:39
  53.9 0.9 convolution_convert_fusion.1
  54.8 2.9 reshape.103
  57.7 180.8 %all-to-all-done.2 = bf16[64,5,4096]{2,1,0:T(8,128)(2,1)} async-done(((bf16[64,5,4096]{2,1,0:T(8,128)(2,1)}), bf16[64,5,4096]{2,1,0:T(8,128)(2,1)}, u32[]{:S(2)}, u32[]{:S(2)}) %all-to-all-start.2) | async-done | bytes 2621472 | tf_op jit(solution)/shard_map/all_to_all | solution.py:39
  238.5 9.9 %all-to-all-start.1 = ((bf16[64,5,4096]{2,1,0:T(8,128)(2,1)}), bf16[64,5,4096]{2,1,0:T(8,128)(2,1)}, u32[]{:S(2)}, u32[]{:S(2)}) async-start(bf16[64,5,4096]{2,1,0:T(8,128)(2,1)} %reshape.103), calls=%async_computation.1 | async-start | bytes 8388608 | tf_op jit(solution)/shard_map/all_to_all | solution.py:42
  250.7 1.1 pad_maximum_fusion
  252.1 22.7 %all-gather.11.cloned.1.call-done = bf16[1,4096,128]{2,1,0:T(8,128)(2,1)} async-done(((bf16[1,2048,128]{2,1,0:T(8,128)(2,1)}), bf16[1,4096,128]{2,1,0:T(8,128)(2,1)}) %all-gather.11.cloned.1.call-update) | async-done | bytes 1048592 | tf_op jit(solution)/shard_map/all_gather | solution.py:53
  274.8 5.3 convolution_bitcast_fusion.3
  280.2 21.4 %all-gather.9.cloned.1.call-done = bf16[1,4096,128]{2,1,0:T(8,128)(2,1)} async-done(((bf16[1,2048,128]{2,1,0:T(8,128)(2,1)}), bf16[1,4096,128]{2,1,0:T(8,128)(2,1)}) %all-gather.9.cloned.1.call-update) | async-done | bytes 1048592 | tf_op jit(solution)/shard_map/all_gather | solution.py:54
  301.5 5.3 convolution_bitcast_fusion.4
  306.9 21.4 %all-gather.7.cloned.1.call-done = bf16[1,4096,128]{2,1,0:T(8,128)(2,1)} async-done(((bf16[1,2048,128]{2,1,0:T(8,128)(2,1)}), bf16[1,4096,128]{2,1,0:T(8,128)(2,1)}) %all-gather.7.cloned.1.call-update) | async-done | bytes 1048592 | tf_op jit(solution)/shard_map/all_gather | solution.py:55
  328.3 105.9 %all-to-all-done.1 = bf16[64,5,4096]{2,1,0:T(8,128)(2,1)} async-done(((bf16[64,5,4096]{2,1,0:T(8,128)(2,1)}), bf16[64,5,4096]{2,1,0:T(8,128)(2,1)}, u32[]{:S(2)}, u32[]{:S(2)}) %all-to-all-start.1) | async-done | bytes 2621472 | tf_op jit(solution)/shard_map/all_to_all | solution.py:42
  434.1 5.6 fusion.20
  439.7 2.2 fusion.10
  442.0 2.4 fusion.1
  444.7 5.8 %fusion.5 = bf16[1,4096,128]{2,1,0:T(8,128)(2,1)} fusion(bf16[64,5,4096]{2,1,0:T(8,128)(2,1)} %all-to-all-done.1, f32[64,5]{0,1:T(8,128)S(1)} %copy.56, f32[64,1,5,128]{3,0,2,1:T(8,128)S(1)} %convolution_bitcast_fusion.4, f32[64,1,5,128]{3,0,2,1:T(8,128)S(1)} %convolution_bitcast_fusion.3), kind=kOutput, calls=%fused_computation.12 | convolution fusion | flops 340246528 | bytes 3998976 | tf_op jit(solution)/shard_map/sjcd,sjcf->jdf/dot_general | solution.py:80
  450.6 5.4 fusion.7
  456.1 5.4 fusion.6
  461.6 29.7 %reduce-scatter.5.cloned.1.call-done = bf16[64,5,512]{2,0,1:T(8,128)(2,1)} async-done(((bf16[64,5,4096]{2,0,1:T(8,128)(2,1)}), bf16[64,5,512]{2,0,1:T(8,128)(2,1)}) %reduce-scatter.5.cloned.1.call-update) | async-done | bytes 327696 | tf_op jit(solution)/shard_map/reduce_scatter | solution.py:68
  491.3 2.0 copy.60
  493.3 16.6 %all-to-all-start.3 = ((bf16[64,5,512]{2,1,0:T(8,128)(2,1)}), bf16[64,5,512]{2,1,0:T(8,128)(2,1)S(1)}, u32[]{:S(2)}, u32[]{:S(2)}) async-start(bf16[64,5,512]{2,1,0:T(8,128)(2,1)} %copy.60), calls=%async_computation.4 | async-start | bytes 1048576 | tf_op jit(solution)/shard_map/all_to_all | solution.py:74
  510.2 27.5 %all-to-all-done.3 = bf16[64,5,512]{2,1,0:T(8,128)(2,1)S(1)} async-done(((bf16[64,5,512]{2,1,0:T(8,128)(2,1)}), bf16[64,5,512]{2,1,0:T(8,128)(2,1)S(1)}, u32[]{:S(2)}, u32[]{:S(2)}) %all-to-all-start.3) | async-done | bytes 327712 | tf_op jit(solution)/shard_map/all_to_all | solution.py:74
  537.8 0.8 convolution_convert_fusion.2
  538.6 6.5 %reduce-scatter.7.cloned.1.call-done = bf16[1,2048,128]{2,1,0:T(8,128)(2,1)} async-done(((bf16[1,4096,128]{2,1,0:T(8,128)(2,1)}), bf16[1,2048,128]{2,1,0:T(8,128)(2,1)}) %reduce-scatter.7.cloned.1.call-update) | async-done | bytes 524304 | tf_op jit(solution)/shard_map/reduce_scatter | solution.py:82
  545.1 27.5 %reduce-scatter.9.cloned.1.call-done = bf16[1,2048,128]{2,1,0:T(8,128)(2,1)} async-done(((bf16[1,4096,128]{2,1,0:T(8,128)(2,1)}), bf16[1,2048,128]{2,1,0:T(8,128)(2,1)}) %reduce-scatter.9.cloned.1.call-update) | async-done | bytes 524304 | tf_op jit(solution)/shard_map/reduce_scatter | solution.py:85
  (44 shorter events, 5.6 us)
Async XLA Ops:
  7.2 27.0 %copy-start = (bf16[32,4096]{1,0:T(8,128)(2,1)S(1)}, bf16[32,4096]{1,0:T(8,128)(2,1)}, u32[]{:S(2)}) copy-start(bf16[32,4096]{1,0:T(8,128)(2,1)} %param.7) | copy-start | bytes 786436
  11.5 34.9 %all-to-all-start = ((bf16[64,1,5]{2,1,0:T(2,128)(2,1)}), bf16[64,1,5]{2,1,0:T(2,128)(2,1)S(1)}, u32[]{:S(2)}, u32[]{:S(2)}) async-start(bf16[64,1,5]{2,1,0:T(2,128)(2,1)} %all_to_all.20), calls=%async_computation | async-start | bytes 65536 | tf_op jit(solution)/shard_map/all_to_all | solution.py:45
  37.9 16.0 %copy-start.4 = (bf16[32,4096]{1,0:T(8,128)(2,1)S(1)}, bf16[32,4096]{1,0:T(8,128)(2,1)}, u32[]{:S(2)}) copy-start(bf16[32,4096]{1,0:T(8,128)(2,1)} %param.8) | copy-start | bytes 786436
  46.4 192.0 %all-to-all-start.2 = ((bf16[64,5,4096]{2,1,0:T(8,128)(2,1)}), bf16[64,5,4096]{2,1,0:T(8,128)(2,1)}, u32[]{:S(2)}, u32[]{:S(2)}) async-start(bf16[64,5,4096]{2,1,0:T(8,128)(2,1)} %reshape.105), calls=%async_computation.2 | async-start | bytes 8388608 | tf_op jit(solution)/shard_map/all_to_all | solution.py:39
  57.7 193.0 %copy-start.1 = (bf16[1,2048,128]{2,1,0:T(8,128)(2,1)S(1)}, bf16[1,2048,128]{2,1,0:T(8,128)(2,1)}, u32[]{:S(2)}) copy-start(bf16[1,2048,128]{2,1,0:T(8,128)(2,1)} %param.11) | copy-start | bytes 1572868
  57.7 193.0 %copy-start.2 = (bf16[1,2048,128]{2,1,0:T(8,128)(2,1)S(1)}, bf16[1,2048,128]{2,1,0:T(8,128)(2,1)}, u32[]{:S(2)}) copy-start(bf16[1,2048,128]{2,1,0:T(8,128)(2,1)} %param.12) | copy-start | bytes 1572868
  238.5 195.6 %all-to-all-start.1 = ((bf16[64,5,4096]{2,1,0:T(8,128)(2,1)}), bf16[64,5,4096]{2,1,0:T(8,128)(2,1)}, u32[]{:S(2)}, u32[]{:S(2)}) async-start(bf16[64,5,4096]{2,1,0:T(8,128)(2,1)} %reshape.103), calls=%async_computation.1 | async-start | bytes 8388608 | tf_op jit(solution)/shard_map/all_to_all | solution.py:42
  248.4 26.4 %all-gather.11.cloned.1.call-start = ((), (), s32[]{:S(2)}) async-start(), calls=%async_computation.11 | async-start | bytes 1572864 | tf_op jit(solution)/shard_map/all_gather | solution.py:53
  249.2 52.4 %all-gather.9.cloned.1.call-start = ((), (), s32[]{:S(2)}) async-start(), calls=%async_computation.10 | async-start | bytes 1572864 | tf_op jit(solution)/shard_map/all_gather | solution.py:54
  249.9 78.3 %all-gather.7.cloned.1.call-start = ((), (), s32[]{:S(2)}) async-start(), calls=%async_computation.9 | async-start | bytes 1572864 | tf_op jit(solution)/shard_map/all_gather | solution.py:55
  250.6 189.1 %all-gather.5.cloned.1.call-start = ((), (), s32[]{:S(2)}) async-start(), calls=%async_computation.8 | async-start | bytes 3145728 | tf_op jit(solution)/shard_map/all_gather | solution.py:65
  251.8 239.5 %reduce-scatter.5.cloned.1.call-start = ((), (), s32[]{:S(2)}) async-start(), calls=%async_computation.12 | async-start | bytes 2949120 | tf_op jit(solution)/shard_map/reduce_scatter | solution.py:68
  439.7 2.2 copy-start.3
  444.4 94.2 %reduce-scatter.11.cloned.1.call-start = ((), (), s32[]{:S(2)}) async-start(), calls=%async_computation.15 | async-start | bytes 1572864 | tf_op jit(solution)/shard_map/reduce_scatter | solution.py:88
  450.5 94.6 %reduce-scatter.7.cloned.1.call-start = ((), (), s32[]{:S(2)}) async-start(), calls=%async_computation.13 | async-start | bytes 1572864 | tf_op jit(solution)/shard_map/reduce_scatter | solution.py:82
  456.0 53.8 %copy-start.5 = (bf16[32,8]{0,1:T(8,128)(2,1)S(1)}, bf16[32,8]{0,1:T(8,128)(2,1)}, u32[]{:S(2)}) copy-start(bf16[32,8]{0,1:T(8,128)(2,1)} %param.10) | copy-start | bytes 1540
  456.0 116.6 %reduce-scatter.9.cloned.1.call-start = ((), (), s32[]{:S(2)}) async-start(), calls=%async_computation.14 | async-start | bytes 1572864 | tf_op jit(solution)/shard_map/reduce_scatter | solution.py:85
  493.3 44.4 %all-to-all-start.3 = ((bf16[64,5,512]{2,1,0:T(8,128)(2,1)}), bf16[64,5,512]{2,1,0:T(8,128)(2,1)S(1)}, u32[]{:S(2)}, u32[]{:S(2)}) async-start(bf16[64,5,512]{2,1,0:T(8,128)(2,1)} %copy.60), calls=%async_computation.4 | async-start | bytes 1048576 | tf_op jit(solution)/shard_map/all_to_all | solution.py:74
Sparse Core Ops, SparseCore 0:
  251.9 22.8 all-gather.10
  277.5 23.9 all-gather.8
  304.2 23.9 all-gather.6
  330.8 25.5 all-gather.4
  444.5 46.7 reduce-scatter.4
  495.1 22.1 reduce-scatter.10
  521.6 23.4 reduce-scatter.6
  549.1 23.4 reduce-scatter.8
where the time goes:
time: 584 us; the launch traced here: 579 us
  waiting for transfers between devices  454 us (78%)
  starting transfers between devices  57.2 us (10%)
  matrix products  41.3 us (7%)
  between operations  14.3 us (2%)
  local copies, waits for them, and re-layouts  9.82 us (2%)
    all_to_all x1, waiting for transfers between devices, shards(): lax.all_to_all(spread(occupied, tokens, owners), 'expert', split_axis=0,...  181 us
    all_to_all x1, waiting for transfers between devices, shards(): lax.all_to_all(spread(occupied, cotangent, owners), 'expert', split_axis=...  106 us
    reduce_scatter x1, waiting for transfers between devices, shards(): lax.psum_scatter(d_rows.reshape(owners, local * capacity, width).astype(j...  29.7 us
    reduce_scatter x1, waiting for transfers between devices, shards(): lax.psum_scatter(part_up.astype(jnp.bfloat16), 'dp', scatter_dimension=1,...  27.5 us
    all_to_all x1, waiting for transfers between devices, shards(): lax.all_to_all(shares, 'expert', split_axis=0, concat_axis=0, tiled=True)  27.5 us
    all_gather x1, waiting for transfers between devices, shards(): piece_gate = lax.all_gather(gate_weight, 'dp', axis=1, tiled=True)  22.7 us
    all_to_all x1, starting transfers between devices, shards(): lax.all_to_all(p_buf, 'expert', split_axis=0, concat_axis=0, tiled=True)  22.5 us
    all_gather x1, waiting for transfers between devices, shards(): piece_down = lax.all_gather(down_weight, 'dp', axis=1, tiled=True)  21.4 us
  transfers between devices with their start and end apart: 12, of which 10 were waited for; matrix products, arithmetic and copies ran while one was open for 8% of the time, Pallas kernels for 0%

commit v1 on v0

v1 whole, which is shorter than its diff:
```python
import jax
import jax.numpy as jnp
from jax import lax
from jax.experimental import pallas as pl
from jax.experimental.pallas import tpu as pltpu
from jax.sharding import Mesh
from jax.sharding import PartitionSpec as P

F32 = jnp.float32
BF16 = jnp.bfloat16
LANES = 128


def pack_kernel(capacity, ids_ref, probs_ref, x_ref, dy_ref, out_ref, table_ref, flat):
    choose, tok = ids_ref.shape
    rows = table_ref.shape[0]
    experts = rows // capacity
    width = x_ref.shape[1]
    chunks = width // LANES
    expert = lax.broadcasted_iota(jnp.int32, (experts, tok), 0)
    named = [expert == ids_ref[k : k + 1, :] for k in range(choose)]
    counts = sum(m.astype(F32) for m in named)
    earlier = lax.broadcasted_iota(jnp.int32, (tok, tok), 0) < lax.broadcasted_iota(
        jnp.int32, (tok, tok), 1
    )
    before = jnp.dot(
        counts.astype(BF16), earlier.astype(F32).astype(BF16), preferred_element_type=F32
    )
    row = lax.broadcasted_iota(jnp.int32, (rows, tok), 0)
    occupied = jnp.zeros((rows, tok), F32)
    weights = jnp.zeros((rows, tok), F32)
    for k in range(choose):
        slot = jnp.sum(jnp.where(named[k], before, 0.0), axis=0, keepdims=True)
        dest = ids_ref[k : k + 1, :] * capacity + slot.astype(jnp.int32)
        here = row == dest
        occupied = jnp.where(here, 1.0, occupied)
        weights = jnp.where(here, probs_ref[k : k + 1, :].astype(F32), weights)
    table = weights.astype(BF16)
    table_ref[...] = table
    placed = jnp.dot(occupied.astype(BF16), x_ref[...], preferred_element_type=F32)
    scaled = jnp.dot(table, dy_ref[...], preferred_element_type=F32)
    for c in range(chunks):
        cols = slice(c * LANES, (c + 1) * LANES)
        flat[pl.ds(c, rows, stride=2 * chunks), :] = placed[:, cols]
        flat[pl.ds(chunks + c, rows, stride=2 * chunks), :] = scaled[:, cols]
    out_ref[...] = flat[...].astype(BF16)


def pack(ids, probs, tokens, cotangent, column, width, rows, capacity):
    tok = tokens.shape[0]
    height = rows * 2 * (width // LANES)
    whole = pl.BlockSpec(memory_space=pltpu.VMEM)
    return pl.pallas_call(
        lambda col, *refs: pack_kernel(capacity, *refs),
        grid_spec=pltpu.PrefetchScalarGridSpec(
            num_scalar_prefetch=1,
            grid=(1,),
            in_specs=[
                whole,
                whole,
                pl.BlockSpec((tok, width), lambda i, col: (0, col[0])),
                pl.BlockSpec((tok, width), lambda i, col: (0, col[0])),
            ],
            out_specs=[whole, whole],
            scratch_shapes=[pltpu.VMEM((height, LANES), F32)],
        ),
        out_shape=[
            jax.ShapeDtypeStruct((height, LANES), BF16),
            jax.ShapeDtypeStruct((rows, tok), BF16),
        ],
        compiler_params=pltpu.CompilerParams(vmem_limit_bytes=32 << 20),
        name="pack",
    )(column, ids, probs, tokens, cotangent)


def unpack_kernel(flat_ref, x_ref, dy_ref, flat):
    rows, width = x_ref.shape
    chunks = width // LANES
    flat[...] = flat_ref[...].astype(F32)
    for c in range(chunks):
        cols = slice(c * LANES, (c + 1) * LANES)
        x_ref[:, cols] = flat[pl.ds(c, rows, stride=2 * chunks), :].astype(BF16)
        dy_ref[:, cols] = flat[pl.ds(chunks + c, rows, stride=2 * chunks), :].astype(BF16)


def unpack(flat, rows, width):
    whole = pl.BlockSpec(memory_space=pltpu.VMEM)
    return pl.pallas_call(
        unpack_kernel,
        in_specs=[whole],
        out_specs=[whole, whole],
        scratch_shapes=[pltpu.VMEM(flat.shape, F32)],
        out_shape=[jax.ShapeDtypeStruct((rows, width), BF16)] * 2,
        compiler_params=pltpu.CompilerParams(vmem_limit_bytes=32 << 20),
        name="unpack",
    )(flat)


def shift(axis, step):
    n = lax.axis_size(axis)
    return [(i, (i + step) % n) for i in range(n)]


def ring(value, axis, rightward, leftward):
    held = {0: value}
    n = lax.axis_size(axis)
    right = left = value
    for s in range(1, max(rightward, leftward) + 1):
        if s <= rightward:
            right = lax.ppermute(right, axis, shift(axis, 1))
            held[s] = right
        if s <= leftward:
            left = lax.ppermute(left, axis, shift(axis, -1))
            held[n - s] = left
    return held


def shards(tokens, cotangent, expert_ids, probs, gate_weight, up_weight, down_weight):
    peers = ("x", "z")
    owners = lax.axis_size("x") * lax.axis_size("z")
    parts = lax.axis_size("y")
    core, place = lax.axis_index("dp"), lax.axis_index("y")
    tok, model = tokens.shape
    choose = expert_ids.shape[1]
    half = model // 2
    width = model // parts
    per_half = half // width
    hid = gate_weight.shape[2]
    capacity = min(tok, (5 * tok * choose + 4 * owners - 1) // (4 * owners))
    rows = owners * capacity

    swap = shift("dp", 1)
    gate_own, up_own, down_own = gate_weight[0], up_weight[0], down_weight[0]
    gate_other = lax.ppermute(gate_own, "dp", swap)
    up_other = lax.ppermute(up_own, "dp", swap)
    down_other = lax.ppermute(down_own, "dp", swap)
    first = core == 0

    flat, table = pack(
        expert_ids.T,
        probs.T,
        tokens,
        cotangent,
        place.astype(jnp.int32)[None],
        width,
        rows,
        capacity,
    )
    flat = lax.all_to_all(
        flat.reshape(owners, -1, LANES), peers, split_axis=0, concat_axis=0, tiled=True
    )

    low = jnp.where(first, gate_own, up_other)
    high = jnp.where(first, gate_other, up_own)
    turned = jnp.concatenate((low, high)).reshape(parts, width, hid)
    turned = lax.all_to_all(turned, "y", split_axis=0, concat_axis=0)
    turned_other = lax.ppermute(turned, "dp", swap)
    columns = jnp.concatenate(
        (jnp.where(first, turned, turned_other), jnp.where(first, turned_other, turned)), axis=2
    )

    both = jnp.concatenate(
        (
            jnp.concatenate((gate_own, up_own), axis=1),
            jnp.concatenate((gate_other, up_other), axis=1),
        )
    )
    down = jnp.concatenate((down_own, down_other))

    x_own, dy_own = unpack(flat.reshape(-1, LANES), rows, width)
    x_ring = ring(x_own, "y", parts // 2, parts // 2 - 1)
    dy_ring = ring(dy_own, "y", parts // 2 - 1, parts // 2)

    def block_of(distance):
        return lax.rem(place - distance + parts, parts)

    acc = jnp.zeros((rows, 2 * hid), F32)
    back = jnp.zeros((rows, hid), F32)
    for d in sorted(x_ring, key=lambda d: min(d, parts - d)):
        block = block_of(d)
        start = jnp.where(block // per_half == core, 0, half) + lax.rem(block, per_half) * width
        piece = lax.dynamic_slice_in_dim(both, start, width, 0)
        acc = acc + jnp.dot(x_ring[d], piece, preferred_element_type=F32)
        piece = lax.dynamic_slice_in_dim(down, start, width, 0)
        back = back + jnp.dot(dy_ring[d], piece, preferred_element_type=F32)
    gate, up = acc[:, :hid], acc[:, hid:]
    sig = jax.nn.sigmoid(gate)
    act = gate * sig
    hidden = (act * up).astype(BF16)
    d_up = (back * act).astype(BF16)
    d_gate = (back * up * sig * (1.0 + gate * (1.0 - sig))).astype(BF16)
    d_both = jnp.concatenate((d_gate, d_up), axis=1)

    d_ring = ring(d_both, "y", parts // 2, parts // 2 - 1)
    d_rows = jnp.zeros((rows, width), F32)
    for d in sorted(d_ring, key=lambda d: min(d, parts - d)):
        piece = lax.dynamic_index_in_dim(columns, block_of(d), 0, keepdims=False)
        d_rows = d_rows + lax.dot_general(
            d_ring[d], piece, (((1,), (1,)), ((), ())), preferred_element_type=F32
        )
    d_rows = d_rows.astype(BF16).reshape(owners, -1, LANES)
    returned = lax.all_to_all(d_rows, peers, split_axis=0, concat_axis=0, tiled=True)
    d_tokens = lax.dot_general(
        table,
        returned.reshape(rows, width),
        (((0,), (0,)), ((), ())),
        preferred_element_type=F32,
    ).astype(BF16)

    x_all = jnp.stack([x_ring[d] for d in range(parts)])
    dy_all = jnp.stack([dy_ring[d] for d in range(parts)])
    grads_both = jnp.einsum("prc,rf->pcf", x_all, d_both, preferred_element_type=F32).astype(BF16)
    grads_down = jnp.einsum("prc,rf->pcf", dy_all, hidden, preferred_element_type=F32).astype(BF16)
    grads = jnp.concatenate((grads_both, grads_down), axis=2)

    def of_half(which):
        order = lax.rem(place - which * per_half - jnp.arange(per_half) + 2 * parts, parts)
        return jnp.take(grads, order, axis=0).reshape(half, 3 * hid)

    received = lax.ppermute(of_half(1 - core), "dp", swap)
    total = (of_half(core).astype(F32) + received.astype(F32)).astype(BF16)
    return (
        d_tokens,
        total[None, :, :hid],
        total[None, :, hid : 2 * hid],
        total[None, :, 2 * hid :],
    )


def solution(mesh):
    dp, experts, etp = mesh.devices.shape
    inner = min(16, experts)
    grid = Mesh(mesh.devices.reshape(dp, experts // inner, inner, etp), ("dp", "x", "z", "y"))
    row = P(("dp", "x", "z"), None)
    weight = P(("x", "z"), "dp", "y")
    return jax.shard_map(
        shards,
        mesh=grid,
        in_specs=(row, row, row, row, weight, weight, weight),
        out_specs=(P(("dp", "x", "z"), "y"), weight, weight, weight),
        check_vma=False,
    )
```

time: 584 us -> 256 us (0.44)
  waiting for transfers between devices: 454 us -> 82.6 us
  starting transfers between devices: 57.2 us -> 118 us
  matrix products: 41.3 us -> 14.4 us
  other arithmetic: 2.97 us -> 16.5 us
  between operations: 14.3 us -> 1.79 us
  local copies, waits for them, and re-layouts: 9.82 us -> 19.9 us
    all_to_all x4 -> x3, waiting for transfers between devices: 323 us -> 57.8 us  [the longest x1 30 us: shards(): lax.all_to_all(flat.reshape(owners, -1, LANES), peers, split_axis=0, conc...]
    ppermute x0 -> x26, starting transfers between devices: none -> 79.5 us  [the longest x10 35.5 us: ring(): left = lax.ppermute(left, axis, shift(axis, -1))]
    all_gather x4 -> x0, waiting for transfers between devices: 65.4 us -> none  [the longest x1 22.7 us: shards(): piece_gate = lax.all_gather(gate_weight, 'dp', axis=1, tiled=True)]
    reduce_scatter x4 -> x0, waiting for transfers between devices: 63.7 us -> none  [the longest x1 29.7 us: shards(): lax.psum_scatter(d_rows.reshape(owners, local * capacity, width).astype(j...]
    dot_general x13 -> x27, matrix products: 41.3 us -> 14.4 us  [the longest x8 5.37 us: shards(): back = back + jnp.dot(dy_ring[d], piece, preferred_element_type=F32)]
    ppermute x0 -> x26, waiting for transfers between devices: none -> 24.8 us  [the longest x11 20.2 us: ring(): right = lax.ppermute(right, axis, shift(axis, 1))]
    all_to_all x4 -> x3, starting transfers between devices: 56.5 us -> 38.3 us  [the longest x1 22.5 us: shards(): lax.all_to_all(flat.reshape(owners, -1, LANES), peers, split_axis=0, conc...]
    gather x0 -> x2, local copies, waits for them, and re-layouts: none -> 7.44 us  [of_half(): return jnp.take(grads, order, axis=0).reshape(half, 3 * hid)]
  transfers between devices with their start and end apart: 12 -> 29, of which waited for: 10 -> 10; matrix products, arithmetic and copies ran while one was open for 8% -> 18% of each run, Pallas kernels for 0% -> 0%
where the time goes in v1:
time: 256 us; the launch traced here: 255 us
  starting transfers between devices  118 us (46%)
  waiting for transfers between devices  82.6 us (32%)
  local copies, waits for them, and re-layouts  19.9 us (8%)
  other arithmetic  16.5 us (6%)
  matrix products  14.4 us (6%)
    ppermute x10, starting transfers between devices, ring(): left = lax.ppermute(left, axis, shift(axis, -1))  35.5 us
    ppermute x11, starting transfers between devices, ring(): right = lax.ppermute(right, axis, shift(axis, 1))  33.7 us
    all_to_all x1, waiting for transfers between devices, shards(): lax.all_to_all(flat.reshape(owners, -1, LANES), peers, split_axis=0, conc...  30 us
    all_to_all x1, starting transfers between devices, shards(): lax.all_to_all(flat.reshape(owners, -1, LANES), peers, split_axis=0, conc...  22.5 us
    ppermute x11, waiting for transfers between devices, ring(): right = lax.ppermute(right, axis, shift(axis, 1))  20.2 us
    all_to_all x1, waiting for transfers between devices, shards(): turned = lax.all_to_all(turned, 'y', split_axis=0, concat_axis=0)  14.7 us
    all_to_all x1, waiting for transfers between devices, shards(): lax.all_to_all(d_rows, peers, split_axis=0, concat_axis=0, tiled=True)  13.1 us
    all_to_all x1, starting transfers between devices, shards(): lax.all_to_all(d_rows, peers, split_axis=0, concat_axis=0, tiled=True)  8.7 us
  transfers between devices with their start and end apart: 29, of which 10 were waited for; matrix products, arithmetic and copies ran while one was open for 18% of the time, Pallas kernels for 0%

profile of v1, /device:TPU:6, one launch (start us, length us, event | category | flops | bytes accessed | tf_op | source)
XLA Modules:
  0.0 254.9 jit_solution(15469527597276529280)
XLA Ops:
  5.5 22.5 %all-to-all-start = ((bf16[64,40,128]{2,1,0:T(8,128)(2,1)}), bf16[64,40,128]{2,1,0:T(8,128)(2,1)S(1)}, u32[]{:S(2)}, u32[]{:S(2)}) async-start(bf16[64,40,128]{2,1,0:T(8,128)(2,1)} %bitcast.3), calls=%async_computation | async-start | bytes 1310720 | tf_op jit(solution)/shard_map/all_to_all | solution.py:149
  29.9 2.4 collective-permute-start.9
  35.1 30.0 %all-to-all-done = bf16[64,40,128]{2,1,0:T(8,128)(2,1)S(1)} async-done(((bf16[64,40,128]{2,1,0:T(8,128)(2,1)}), bf16[64,40,128]{2,1,0:T(8,128)(2,1)S(1)}, u32[]{:S(2)}, u32[]{:S(2)}) %all-to-all-start) | async-done | bytes 655392 | tf_op jit(solution)/shard_map/all_to_all | solution.py:149
  65.1 7.1 %all-to-all-start.1 = ((bf16[8,512,128]{2,1,0:T(8,128)(2,1)}), bf16[8,512,128]{2,1,0:T(8,128)(2,1)S(1)}, u32[]{:S(2)}, u32[]{:S(2)}) async-start(bf16[8,512,128]{2,1,0:T(8,128)(2,1)} %bitcast.123), calls=%async_computation.1 | async-start | bytes 2097152 | tf_op jit(solution)/shard_map/all_to_all | solution.py:156
  74.9 5.1 %collective-permute-start.11 = (bf16[320,512]{1,0:T(8,128)(2,1)S(1)}, bf16[320,512]{1,0:T(8,128)(2,1)S(1)}, u32[]{:S(2)}, u32[]{:S(2)}) collective-permute-start(bf16[320,512]{1,0:T(8,128)(2,1)S(1)} %get-tuple-element.12), channel_id=1, source_target_pairs={{0,7},{1,0},{2,1},{3,2},{4,3},{5,4},{6,5},{7,6},{8,15},{9,8},{10,9... | collective-permute-start | bytes 983048 | tf_op jit(solution)/shard_map/ppermute | solution.py:113
  80.0 3.1 %maximum_maximum_fusion = bf16[4096,256]{1,0:T(8,128)(2,1)} fusion(bf16[2048,128]{1,0:T(8,128)(2,1)} %copy-done.10, bf16[2048,128]{1,0:T(8,128)(2,1)} %copy-done.9, bf16[2048,128]{1,0:T(8,128)(2,1)} %bitcast.125, bf16[2048,128]{1,0:T(8,128)(2,1)} %bitcast.127), kind=kLoop, calls=%fused_computation.21 | loop fusion | flops 8388608 | bytes 4194304 | tf_op jit(solution)/shard_map/concatenate | solution.py:162
  83.1 14.7 %all-to-all-done.1 = bf16[8,512,128]{2,1,0:T(8,128)(2,1)S(1)} async-done(((bf16[8,512,128]{2,1,0:T(8,128)(2,1)}), bf16[8,512,128]{2,1,0:T(8,128)(2,1)S(1)}, u32[]{:S(2)}, u32[]{:S(2)}) %all-to-all-start.1) | async-done | bytes 1048608 | tf_op jit(solution)/shard_map/all_to_all | solution.py:156
  100.0 5.7 %collective-permute-start.10 = (bf16[320,512]{1,0:T(8,128)(2,1)S(1)}, bf16[320,512]{1,0:T(8,128)(2,1)S(1)}, u32[]{:S(2)}, u32[]{:S(2)}) collective-permute-start(bf16[320,512]{1,0:T(8,128)(2,1)S(1)} %get-tuple-element.12), channel_id=1, source_target_pairs={{0,1},{1,2},{2,3},{3,4},{4,5},{5,6},{6,7},{7,0},{8,9},{9,10},{10,1... | collective-permute-start | bytes 983048 | tf_op jit(solution)/shard_map/ppermute | solution.py:110
  107.8 3.9 %collective-permute-start.1 = (bf16[320,512]{1,0:T(8,128)(2,1)S(1)}, bf16[320,512]{1,0:T(8,128)(2,1)S(1)}, u32[]{:S(2)}, u32[]{:S(2)}) collective-permute-start(bf16[320,512]{1,0:T(8,128)(2,1)S(1)} %get-tuple-element.11), channel_id=1, source_target_pairs={{0,1},{1,2},{2,3},{3,4},{4,5},{5,6},{6,7},{7,0},{8,9},{9,10},{10,1... | collective-permute-start | bytes 983048 | tf_op jit(solution)/shard_map/ppermute | solution.py:110
  113.8 2.9 %collective-permute-start.13 = (bf16[320,512]{1,0:T(8,128)(2,1)S(1)}, bf16[320,512]{1,0:T(8,128)(2,1)S(1)}, u32[]{:S(2)}, u32[]{:S(2)}) collective-permute-start(bf16[320,512]{1,0:T(8,128)(2,1)S(1)} %collective-permute-done.11), channel_id=1, source_target_pairs={{0,7},{1,0},{2,1},{3,2},{4,3},{5,4},{6,5},{7,6},{8,15},{9,8},{10,9... | collective-permute-start | bytes 983048 | tf_op jit(solution)/shard_map/ppermute | solution.py:113
  117.9 3.4 %collective-permute-start.12 = (bf16[320,512]{1,0:T(8,128)(2,1)S(1)}, bf16[320,512]{1,0:T(8,128)(2,1)S(1)}, u32[]{:S(2)}, u32[]{:S(2)}) collective-permute-start(bf16[320,512]{1,0:T(8,128)(2,1)S(1)} %collective-permute-done.10), channel_id=1, source_target_pairs={{0,1},{1,2},{2,3},{3,4},{4,5},{5,6},{6,7},{7,0},{8,9},{9,10},{10,1... | collective-permute-start | bytes 983048 | tf_op jit(solution)/shard_map/ppermute | solution.py:110
  121.3 3.7 %collective-permute-start.4 = (bf16[320,512]{1,0:T(8,128)(2,1)S(1)}, bf16[320,512]{1,0:T(8,128)(2,1)S(1)}, u32[]{:S(2)}, u32[]{:S(2)}) collective-permute-start(bf16[320,512]{1,0:T(8,128)(2,1)S(1)} %collective-permute-done.2), channel_id=1, source_target_pairs={{0,7},{1,0},{2,1},{3,2},{4,3},{5,4},{6,5},{7,6},{8,15},{9,8},{10,9... | collective-permute-start | bytes 983048 | tf_op jit(solution)/shard_map/ppermute | solution.py:113
  129.6 4.9 %collective-permute-start.15 = (bf16[320,512]{1,0:T(8,128)(2,1)S(1)}, bf16[320,512]{1,0:T(8,128)(2,1)S(1)}, u32[]{:S(2)}, u32[]{:S(2)}) collective-permute-start(bf16[320,512]{1,0:T(8,128)(2,1)S(1)} %collective-permute-done.13), channel_id=1, source_target_pairs={{0,7},{1,0},{2,1},{3,2},{4,3},{5,4},{6,5},{7,6},{8,15},{9,8},{10,9... | collective-permute-start | bytes 983048 | tf_op jit(solution)/shard_map/ppermute | solution.py:113
  137.4 4.1 %collective-permute-start.14 = (bf16[320,512]{1,0:T(8,128)(2,1)S(1)}, bf16[320,512]{1,0:T(8,128)(2,1)S(1)}, u32[]{:S(2)}, u32[]{:S(2)}) collective-permute-start(bf16[320,512]{1,0:T(8,128)(2,1)S(1)} %collective-permute-done.12), channel_id=1, source_target_pairs={{0,1},{1,2},{2,3},{3,4},{4,5},{5,6},{6,7},{7,0},{8,9},{9,10},{10,1... | collective-permute-start | bytes 983048 | tf_op jit(solution)/shard_map/ppermute | solution.py:110
  144.6 2.2 collective-permute-done.6
  146.8 5.6 %collective-permute-start.7 = (bf16[320,512]{1,0:T(8,128)(2,1)S(1)}, bf16[320,512]{1,0:T(8,128)(2,1)S(1)}, u32[]{:S(2)}, u32[]{:S(2)}) collective-permute-start(bf16[320,512]{1,0:T(8,128)(2,1)S(1)} %collective-permute-done.6), channel_id=1, source_target_pairs={{0,7},{1,0},{2,1},{3,2},{4,3},{5,4},{6,5},{7,6},{8,15},{9,8},{10,9... | collective-permute-start | bytes 983048 | tf_op jit(solution)/shard_map/ppermute | solution.py:113
  156.3 7.2 %collective-permute-done.16 = bf16[320,512]{1,0:T(8,128)(2,1)S(1)} collective-permute-done((bf16[320,512]{1,0:T(8,128)(2,1)S(1)}, bf16[320,512]{1,0:T(8,128)(2,1)S(1)}, u32[]{:S(2)}, u32[]{:S(2)}) %collective-permute-start.16) | collective-permute-done | bytes 327712 | tf_op jit(solution)/shard_map/ppermute | solution.py:110
  166.4 4.1 %collective-permute-start.18 = (bf16[320,256]{1,0:T(8,128)(2,1)S(1)}, bf16[320,256]{1,0:T(8,128)(2,1)S(1)}, u32[]{:S(2)}, u32[]{:S(2)}) collective-permute-start(bf16[320,256]{1,0:T(8,128)(2,1)S(1)} %pad_maximum_fusion.2), channel_id=1, source_target_pairs={{0,1},{1,2},{2,3},{3,4},{4,5},{5,6},{6,7},{7,0},{8,9},{9,10},{10,1... | collective-permute-start | bytes 491528 | tf_op jit(solution)/shard_map/ppermute | solution.py:110
  174.9 3.7 %gather_fusion.1 = bf16[4,512,384]{1,2,0:T(8,128)(2,1)} fusion(bf16[8,512,384]{1,2,0:T(8,128)(2,1)} %pad_maximum_fusion, s32[1024]{0:T(1024)S(1)} %pad_clamp_fusion), kind=kCustom, calls=%fused_computation.1.clone | custom fusion | bytes 3145744 | tf_op jit(solution)/shard_map/jit(_take)/gather | solution.py:218
  178.6 2.8 %broadcast_select_fusion = bf16[4,512,384]{1,2,0:T(8,128)(2,1)} fusion(bf16[4,512,384]{1,2,0:T(8,128)(2,1)} %gather_fusion.1, pred[4]{0:T(512)(128)(4,1)S(1)} %get-tuple-element.24), kind=kLoop, calls=%fused_computation.40 | loop fusion | flops 786432 | bytes 3145732 | tf_op jit(solution)/shard_map/jit(_take)/select_n | solution.py:218
  181.4 3.8 %gather_fusion = bf16[4,512,384]{1,2,0:T(8,128)(2,1)} fusion(bf16[8,512,384]{1,2,0:T(8,128)(2,1)} %pad_maximum_fusion, s32[1024]{0:T(1024)S(1)} %pad_clamp_fusion.1), kind=kCustom, calls=%fused_computation.clone | custom fusion | bytes 3145744 | tf_op jit(solution)/shard_map/jit(_take)/gather | solution.py:218
  185.2 2.7 %copy.12 = bf16[4,512,384]{2,1,0:T(8,128)(2,1)} copy(bf16[4,512,384]{1,2,0:T(8,128)(2,1)} %broadcast_select_fusion) | data formatting | bytes 3145728 | tf_op jit(solution)/shard_map/jit(_take)/select_n | solution.py:218
  190.0 3.1 %collective-permute-start.21 = (bf16[320,256]{1,0:T(8,128)(2,1)S(1)}, bf16[320,256]{1,0:T(8,128)(2,1)S(1)}, u32[]{:S(2)}, u32[]{:S(2)}) collective-permute-start(bf16[320,256]{1,0:T(8,128)(2,1)S(1)} %collective-permute-done.19), channel_id=1, source_target_pairs={{0,7},{1,0},{2,1},{3,2},{4,3},{5,4},{6,5},{7,6},{8,15},{9,8},{10,9... | collective-permute-start | bytes 491528 | tf_op jit(solution)/shard_map/ppermute | solution.py:113
  193.2 2.7 %collective-permute-start.20 = (bf16[320,256]{1,0:T(8,128)(2,1)S(1)}, bf16[320,256]{1,0:T(8,128)(2,1)S(1)}, u32[]{:S(2)}, u32[]{:S(2)}) collective-permute-start(bf16[320,256]{1,0:T(8,128)(2,1)S(1)} %collective-permute-done.18), channel_id=1, source_target_pairs={{0,1},{1,2},{2,3},{3,4},{4,5},{5,6},{6,7},{7,0},{8,9},{9,10},{10,1... | collective-permute-start | bytes 491528 | tf_op jit(solution)/shard_map/ppermute | solution.py:110
  198.5 4.3 %collective-permute-start.23 = (bf16[320,256]{1,0:T(8,128)(2,1)S(1)}, bf16[320,256]{1,0:T(8,128)(2,1)S(1)}, u32[]{:S(2)}, u32[]{:S(2)}) collective-permute-start(bf16[320,256]{1,0:T(8,128)(2,1)S(1)} %collective-permute-done.21), channel_id=1, source_target_pairs={{0,7},{1,0},{2,1},{3,2},{4,3},{5,4},{6,5},{7,6},{8,15},{9,8},{10,9... | collective-permute-start | bytes 491528 | tf_op jit(solution)/shard_map/ppermute | solution.py:113
  205.4 6.1 %collective-permute-done.22 = bf16[320,256]{1,0:T(8,128)(2,1)S(1)} collective-permute-done((bf16[320,256]{1,0:T(8,128)(2,1)S(1)}, bf16[320,256]{1,0:T(8,128)(2,1)S(1)}, u32[]{:S(2)}, u32[]{:S(2)}) %collective-permute-start.22) | collective-permute-done | bytes 163872 | tf_op jit(solution)/shard_map/ppermute | solution.py:110
  214.0 5.9 %collective-permute-done.24 = bf16[320,256]{1,0:T(8,128)(2,1)S(1)} collective-permute-done((bf16[320,256]{1,0:T(8,128)(2,1)S(1)}, bf16[320,256]{1,0:T(8,128)(2,1)S(1)}, u32[]{:S(2)}, u32[]{:S(2)}) %collective-permute-start.24) | collective-permute-done | bytes 163872 | tf_op jit(solution)/shard_map/ppermute | solution.py:110
  221.3 8.7 %all-to-all-start.2 = ((bf16[64,20,128]{2,1,0:T(8,128)(2,1)}), bf16[64,20,128]{2,1,0:T(8,128)(2,1)S(1)}, u32[]{:S(2)}, u32[]{:S(2)}) async-start(bf16[64,20,128]{2,1,0:T(8,128)(2,1)} %reshape.37), calls=%async_computation.2 | async-start | bytes 786432 | tf_op jit(solution)/shard_map/all_to_all | solution.py:202
  230.0 3.4 %select_convert_fusion = f32[4,512,384]{1,2,0:T(8,128)} fusion(bf16[4,512,384]{1,2,0:T(8,128)(2,1)} %gather_fusion, pred[4]{0:T(512)(128)(4,1)S(1)} %get-tuple-element.25), kind=kLoop, calls=%fused_computation.39 | loop fusion | flops 1572864 | bytes 4718596 | tf_op jit(solution)/shard_map/convert_element_type | solution.py:221
  233.3 3.5 %copy.11 = f32[4,512,384]{2,1,0:T(8,128)} copy(f32[4,512,384]{1,2,0:T(8,128)} %select_convert_fusion) | data formatting | bytes 6291456 | tf_op jit(solution)/shard_map/convert_element_type | solution.py:221
  236.8 2.7 %fusion = bf16[2048,384]{1,0:T(8,128)(2,1)S(1)} fusion(f32[4,512,384]{2,1,0:T(8,128)} %copy.11, bf16[2048,384]{1,0:T(8,128)(2,1)} %collective-permute-done.25), kind=kLoop, calls=%fused_computation.20 | loop fusion | flops 2359296 | bytes 6291456 | tf_op jit(solution)/shard_map/convert_element_type | solution.py:221
  240.8 13.1 %all-to-all-done.2 = bf16[64,20,128]{2,1,0:T(8,128)(2,1)S(1)} async-done(((bf16[64,20,128]{2,1,0:T(8,128)(2,1)}), bf16[64,20,128]{2,1,0:T(8,128)(2,1)S(1)}, u32[]{:S(2)}, u32[]{:S(2)}) %all-to-all-start.2) | async-done | bytes 327712 | tf_op jit(solution)/shard_map/all_to_all | solution.py:202
  (117 shorter events, 54.1 us)
Async XLA Ops:
  3.9 30.1 %copy-start.8 = (bf16[1,2048,128]{2,1,0:T(8,128)(2,1)S(1)}, bf16[1,2048,128]{2,1,0:T(8,128)(2,1)}, u32[]{:S(2)}) copy-start(bf16[1,2048,128]{2,1,0:T(8,128)(2,1)} %param.13) | copy-start | bytes 1572868
  5.5 59.7 %all-to-all-start = ((bf16[64,40,128]{2,1,0:T(8,128)(2,1)}), bf16[64,40,128]{2,1,0:T(8,128)(2,1)S(1)}, u32[]{:S(2)}, u32[]{:S(2)}) async-start(bf16[64,40,128]{2,1,0:T(8,128)(2,1)} %bitcast.3), calls=%async_computation | async-start | bytes 1310720 | tf_op jit(solution)/shard_map/all_to_all | solution.py:149
  27.9 4.4 %collective-permute-start.8 = (bf16[2048,128]{1,0:T(8,128)(2,1)}, bf16[2048,128]{1,0:T(8,128)(2,1)S(1)}, u32[]{:S(2)}, u32[]{:S(2)}) collective-permute-start(bf16[2048,128]{1,0:T(8,128)(2,1)} %bitcast.126), channel_id=1, source_target_pairs={{0,512},{512,0},{1,513},{513,1},{2,514},{514,2},{3,515},{515,3},{4... | collective-permute-start | bytes 1572872 | tf_op jit(solution)/shard_map/ppermute | solution.py:134
  29.9 4.1 %collective-permute-start.9 = (bf16[2048,128]{1,0:T(8,128)(2,1)}, bf16[2048,128]{1,0:T(8,128)(2,1)S(1)}, u32[]{:S(2)}, u32[]{:S(2)}) collective-permute-start(bf16[2048,128]{1,0:T(8,128)(2,1)} %bitcast.124), channel_id=1, source_target_pairs={{0,512},{512,0},{1,513},{513,1},{2,514},{514,2},{3,515},{515,3},{4... | collective-permute-start | bytes 1572872 | tf_op jit(solution)/shard_map/ppermute | solution.py:135
  33.6 38.6 %copy-start.4 = (bf16[1,2048,128]{2,1,0:T(8,128)(2,1)S(1)}, bf16[1,2048,128]{2,1,0:T(8,128)(2,1)}, u32[]{:S(2)}) copy-start(bf16[1,2048,128]{2,1,0:T(8,128)(2,1)} %param.15) | copy-start | bytes 1572868
  34.0 31.1 %copy-start.10 = (bf16[2048,128]{1,0:T(8,128)(2,1)}, bf16[2048,128]{1,0:T(8,128)(2,1)S(1)}, u32[]{:S(2)}) copy-start(bf16[2048,128]{1,0:T(8,128)(2,1)S(1)} %collective-permute-done.9) | copy-start | bytes 1572868
  65.1 32.7 %all-to-all-start.1 = ((bf16[8,512,128]{2,1,0:T(8,128)(2,1)}), bf16[8,512,128]{2,1,0:T(8,128)(2,1)S(1)}, u32[]{:S(2)}, u32[]{:S(2)}) async-start(bf16[8,512,128]{2,1,0:T(8,128)(2,1)} %bitcast.123), calls=%async_computation.1 | async-start | bytes 2097152 | tf_op jit(solution)/shard_map/all_to_all | solution.py:156
  72.3 45.7 %collective-permute-start = (bf16[2048,128]{1,0:T(8,128)(2,1)S(1)}, bf16[2048,128]{1,0:T(8,128)(2,1)S(1)}, u32[]{:S(2)}, u32[]{:S(2)}) collective-permute-start(bf16[2048,128]{1,0:T(8,128)(2,1)S(1)} %bitcast.114), channel_id=1, source_target_pairs={{0,512},{512,0},{1,513},{513,1},{2,514},{514,2},{3,515},{515,3},{4... | collective-permute-start | bytes 1572872 | tf_op jit(solution)/shard_map/ppermute | solution.py:136
  74.9 32.8 %collective-permute-start.11 = (bf16[320,512]{1,0:T(8,128)(2,1)S(1)}, bf16[320,512]{1,0:T(8,128)(2,1)S(1)}, u32[]{:S(2)}, u32[]{:S(2)}) collective-permute-start(bf16[320,512]{1,0:T(8,128)(2,1)S(1)} %get-tuple-element.12), channel_id=1, source_target_pairs={{0,7},{1,0},{2,1},{3,2},{4,3},{5,4},{6,5},{7,6},{8,15},{9,8},{10,9... | collective-permute-start | bytes 983048 | tf_op jit(solution)/shard_map/ppermute | solution.py:113
  97.8 46.6 %collective-permute-start.17 = (bf16[8,512,128]{2,1,0:T(8,128)(2,1)S(1)}, bf16[8,512,128]{2,1,0:T(8,128)(2,1)S(1)}, u32[]{:S(2)}, u32[]{:S(2)}) collective-permute-start(bf16[8,512,128]{2,1,0:T(8,128)(2,1)S(1)} %all-to-all-done.1), channel_id=1, source_target_pairs={{0,512},{512,0},{1,513},{513,1},{2,514},{514,2},{3,515},{515,3},{4... | collective-permute-start | bytes 3145736 | tf_op jit(solution)/shard_map/ppermute | solution.py:157
  100.0 13.7 %collective-permute-start.10 = (bf16[320,512]{1,0:T(8,128)(2,1)S(1)}, bf16[320,512]{1,0:T(8,128)(2,1)S(1)}, u32[]{:S(2)}, u32[]{:S(2)}) collective-permute-start(bf16[320,512]{1,0:T(8,128)(2,1)S(1)} %get-tuple-element.12), channel_id=1, source_target_pairs={{0,1},{1,2},{2,3},{3,4},{4,5},{5,6},{6,7},{7,0},{8,9},{9,10},{10,1... | collective-permute-start | bytes 983048 | tf_op jit(solution)/shard_map/ppermute | solution.py:110
  105.8 15.5 %collective-permute-start.2 = (bf16[320,512]{1,0:T(8,128)(2,1)S(1)}, bf16[320,512]{1,0:T(8,128)(2,1)S(1)}, u32[]{:S(2)}, u32[]{:S(2)}) collective-permute-start(bf16[320,512]{1,0:T(8,128)(2,1)S(1)} %get-tuple-element.11), channel_id=1, source_target_pairs={{0,7},{1,0},{2,1},{3,2},{4,3},{5,4},{6,5},{7,6},{8,15},{9,8},{10,9... | collective-permute-start | bytes 983048 | tf_op jit(solution)/shard_map/ppermute | solution.py:113
  107.8 18.2 %collective-permute-start.1 = (bf16[320,512]{1,0:T(8,128)(2,1)S(1)}, bf16[320,512]{1,0:T(8,128)(2,1)S(1)}, u32[]{:S(2)}, u32[]{:S(2)}) collective-permute-start(bf16[320,512]{1,0:T(8,128)(2,1)S(1)} %get-tuple-element.11), channel_id=1, source_target_pairs={{0,1},{1,2},{2,3},{3,4},{4,5},{5,6},{6,7},{7,0},{8,9},{9,10},{10,1... | collective-permute-start | bytes 983048 | tf_op jit(solution)/shard_map/ppermute | solution.py:110
  113.8 15.8 %collective-permute-start.13 = (bf16[320,512]{1,0:T(8,128)(2,1)S(1)}, bf16[320,512]{1,0:T(8,128)(2,1)S(1)}, u32[]{:S(2)}, u32[]{:S(2)}) collective-permute-start(bf16[320,512]{1,0:T(8,128)(2,1)S(1)} %collective-permute-done.11), channel_id=1, source_target_pairs={{0,7},{1,0},{2,1},{3,2},{4,3},{5,4},{6,5},{7,6},{8,15},{9,8},{10,9... | collective-permute-start | bytes 983048 | tf_op jit(solution)/shard_map/ppermute | solution.py:113
  117.9 19.5 %collective-permute-start.12 = (bf16[320,512]{1,0:T(8,128)(2,1)S(1)}, bf16[320,512]{1,0:T(8,128)(2,1)S(1)}, u32[]{:S(2)}, u32[]{:S(2)}) collective-permute-start(bf16[320,512]{1,0:T(8,128)(2,1)S(1)} %collective-permute-done.10), channel_id=1, source_target_pairs={{0,1},{1,2},{2,3},{3,4},{4,5},{5,6},{6,7},{7,0},{8,9},{9,10},{10,1... | collective-permute-start | bytes 983048 | tf_op jit(solution)/shard_map/ppermute | solution.py:110
  121.3 13.4 %collective-permute-start.4 = (bf16[320,512]{1,0:T(8,128)(2,1)S(1)}, bf16[320,512]{1,0:T(8,128)(2,1)S(1)}, u32[]{:S(2)}, u32[]{:S(2)}) collective-permute-start(bf16[320,512]{1,0:T(8,128)(2,1)S(1)} %collective-permute-done.2), channel_id=1, source_target_pairs={{0,7},{1,0},{2,1},{3,2},{4,3},{5,4},{6,5},{7,6},{8,15},{9,8},{10,9... | collective-permute-start | bytes 983048 | tf_op jit(solution)/shard_map/ppermute | solution.py:113
  126.6 14.8 %collective-permute-start.3 = (bf16[320,512]{1,0:T(8,128)(2,1)S(1)}, bf16[320,512]{1,0:T(8,128)(2,1)S(1)}, u32[]{:S(2)}, u32[]{:S(2)}) collective-permute-start(bf16[320,512]{1,0:T(8,128)(2,1)S(1)} %collective-permute-done.1), channel_id=1, source_target_pairs={{0,1},{1,2},{2,3},{3,4},{4,5},{5,6},{6,7},{7,0},{8,9},{9,10},{10,1... | collective-permute-start | bytes 983048 | tf_op jit(solution)/shard_map/ppermute | solution.py:110
  129.6 23.5 %collective-permute-start.15 = (bf16[320,512]{1,0:T(8,128)(2,1)S(1)}, bf16[320,512]{1,0:T(8,128)(2,1)S(1)}, u32[]{:S(2)}, u32[]{:S(2)}) collective-permute-start(bf16[320,512]{1,0:T(8,128)(2,1)S(1)} %collective-permute-done.13), channel_id=1, source_target_pairs={{0,7},{1,0},{2,1},{3,2},{4,3},{5,4},{6,5},{7,6},{8,15},{9,8},{10,9... | collective-permute-start | bytes 983048 | tf_op jit(solution)/shard_map/ppermute | solution.py:113
  134.8 12.0 %collective-permute-start.6 = (bf16[320,512]{1,0:T(8,128)(2,1)S(1)}, bf16[320,512]{1,0:T(8,128)(2,1)S(1)}, u32[]{:S(2)}, u32[]{:S(2)}) collective-permute-start(bf16[320,512]{1,0:T(8,128)(2,1)S(1)} %collective-permute-done.4), channel_id=1, source_target_pairs={{0,7},{1,0},{2,1},{3,2},{4,3},{5,4},{6,5},{7,6},{8,15},{9,8},{10,9... | collective-permute-start | bytes 983048 | tf_op jit(solution)/shard_map/ppermute | solution.py:113
  137.4 16.0 %collective-permute-start.14 = (bf16[320,512]{1,0:T(8,128)(2,1)S(1)}, bf16[320,512]{1,0:T(8,128)(2,1)S(1)}, u32[]{:S(2)}, u32[]{:S(2)}) collective-permute-start(bf16[320,512]{1,0:T(8,128)(2,1)S(1)} %collective-permute-done.12), channel_id=1, source_target_pairs={{0,1},{1,2},{2,3},{3,4},{4,5},{5,6},{6,7},{7,0},{8,9},{9,10},{10,1... | collective-permute-start | bytes 983048 | tf_op jit(solution)/shard_map/ppermute | solution.py:110
  141.5 14.1 %collective-permute-start.5 = (bf16[320,512]{1,0:T(8,128)(2,1)S(1)}, bf16[320,512]{1,0:T(8,128)(2,1)S(1)}, u32[]{:S(2)}, u32[]{:S(2)}) collective-permute-start(bf16[320,512]{1,0:T(8,128)(2,1)S(1)} %collective-permute-done.3), channel_id=1, source_target_pairs={{0,1},{1,2},{2,3},{3,4},{4,5},{5,6},{6,7},{7,0},{8,9},{9,10},{10,1... | collective-permute-start | bytes 983048 | tf_op jit(solution)/shard_map/ppermute | solution.py:110
  146.8 17.0 %collective-permute-start.7 = (bf16[320,512]{1,0:T(8,128)(2,1)S(1)}, bf16[320,512]{1,0:T(8,128)(2,1)S(1)}, u32[]{:S(2)}, u32[]{:S(2)}) collective-permute-start(bf16[320,512]{1,0:T(8,128)(2,1)S(1)} %collective-permute-done.6), channel_id=1, source_target_pairs={{0,7},{1,0},{2,1},{3,2},{4,3},{5,4},{6,5},{7,6},{8,15},{9,8},{10,9... | collective-permute-start | bytes 983048 | tf_op jit(solution)/shard_map/ppermute | solution.py:113
  153.3 10.2 %collective-permute-start.16 = (bf16[320,512]{1,0:T(8,128)(2,1)S(1)}, bf16[320,512]{1,0:T(8,128)(2,1)S(1)}, u32[]{:S(2)}, u32[]{:S(2)}) collective-permute-start(bf16[320,512]{1,0:T(8,128)(2,1)S(1)} %collective-permute-done.14), channel_id=1, source_target_pairs={{0,1},{1,2},{2,3},{3,4},{4,5},{5,6},{6,7},{7,0},{8,9},{9,10},{10,1... | collective-permute-start | bytes 983048 | tf_op jit(solution)/shard_map/ppermute | solution.py:110
  164.5 25.5 %collective-permute-start.19 = (bf16[320,256]{1,0:T(8,128)(2,1)S(1)}, bf16[320,256]{1,0:T(8,128)(2,1)S(1)}, u32[]{:S(2)}, u32[]{:S(2)}) collective-permute-start(bf16[320,256]{1,0:T(8,128)(2,1)S(1)} %pad_maximum_fusion.2), channel_id=1, source_target_pairs={{0,7},{1,0},{2,1},{3,2},{4,3},{5,4},{6,5},{7,6},{8,15},{9,8},{10,9... | collective-permute-start | bytes 491528 | tf_op jit(solution)/shard_map/ppermute | solution.py:113
  166.4 26.7 %collective-permute-start.18 = (bf16[320,256]{1,0:T(8,128)(2,1)S(1)}, bf16[320,256]{1,0:T(8,128)(2,1)S(1)}, u32[]{:S(2)}, u32[]{:S(2)}) collective-permute-start(bf16[320,256]{1,0:T(8,128)(2,1)S(1)} %pad_maximum_fusion.2), channel_id=1, source_target_pairs={{0,1},{1,2},{2,3},{3,4},{4,5},{5,6},{6,7},{7,0},{8,9},{9,10},{10,1... | collective-permute-start | bytes 491528 | tf_op jit(solution)/shard_map/ppermute | solution.py:110
  187.8 49.0 %collective-permute-start.25 = (bf16[2048,384]{1,0:T(8,128)(2,1)}, bf16[2048,384]{1,0:T(8,128)(2,1)}, u32[]{:S(2)}, u32[]{:S(2)}) collective-permute-start(bf16[2048,384]{1,0:T(8,128)(2,1)} %bitcast.128), channel_id=1, source_target_pairs={{0,512},{512,0},{1,513},{513,1},{2,514},{514,2},{3,515},{515,3},{4... | collective-permute-start | bytes 4718600 | tf_op jit(solution)/shard_map/ppermute | solution.py:220
  190.0 8.5 %collective-permute-start.21 = (bf16[320,256]{1,0:T(8,128)(2,1)S(1)}, bf16[320,256]{1,0:T(8,128)(2,1)S(1)}, u32[]{:S(2)}, u32[]{:S(2)}) collective-permute-start(bf16[320,256]{1,0:T(8,128)(2,1)S(1)} %collective-permute-done.19), channel_id=1, source_target_pairs={{0,7},{1,0},{2,1},{3,2},{4,3},{5,4},{6,5},{7,6},{8,15},{9,8},{10,9... | collective-permute-start | bytes 491528 | tf_op jit(solution)/shard_map/ppermute | solution.py:113
  193.2 9.7 %collective-permute-start.20 = (bf16[320,256]{1,0:T(8,128)(2,1)S(1)}, bf16[320,256]{1,0:T(8,128)(2,1)S(1)}, u32[]{:S(2)}, u32[]{:S(2)}) collective-permute-start(bf16[320,256]{1,0:T(8,128)(2,1)S(1)} %collective-permute-done.18), channel_id=1, source_target_pairs={{0,1},{1,2},{2,3},{3,4},{4,5},{5,6},{6,7},{7,0},{8,9},{9,10},{10,1... | collective-permute-start | bytes 491528 | tf_op jit(solution)/shard_map/ppermute | solution.py:110
  198.5 14.9 %collective-permute-start.23 = (bf16[320,256]{1,0:T(8,128)(2,1)S(1)}, bf16[320,256]{1,0:T(8,128)(2,1)S(1)}, u32[]{:S(2)}, u32[]{:S(2)}) collective-permute-start(bf16[320,256]{1,0:T(8,128)(2,1)S(1)} %collective-permute-done.21), channel_id=1, source_target_pairs={{0,7},{1,0},{2,1},{3,2},{4,3},{5,4},{6,5},{7,6},{8,15},{9,8},{10,9... | collective-permute-start | bytes 491528 | tf_op jit(solution)/shard_map/ppermute | solution.py:113
  202.9 8.6 %collective-permute-start.22 = (bf16[320,256]{1,0:T(8,128)(2,1)S(1)}, bf16[320,256]{1,0:T(8,128)(2,1)S(1)}, u32[]{:S(2)}, u32[]{:S(2)}) collective-permute-start(bf16[320,256]{1,0:T(8,128)(2,1)S(1)} %collective-permute-done.20), channel_id=1, source_target_pairs={{0,1},{1,2},{2,3},{3,4},{4,5},{5,6},{6,7},{7,0},{8,9},{9,10},{10,1... | collective-permute-start | bytes 491528 | tf_op jit(solution)/shard_map/ppermute | solution.py:110
  211.5 8.4 %collective-permute-start.24 = (bf16[320,256]{1,0:T(8,128)(2,1)S(1)}, bf16[320,256]{1,0:T(8,128)(2,1)S(1)}, u32[]{:S(2)}, u32[]{:S(2)}) collective-permute-start(bf16[320,256]{1,0:T(8,128)(2,1)S(1)} %collective-permute-done.22), channel_id=1, source_target_pairs={{0,1},{1,2},{2,3},{3,4},{4,5},{5,6},{6,7},{7,0},{8,9},{9,10},{10,1... | collective-permute-start | bytes 491528 | tf_op jit(solution)/shard_map/ppermute | solution.py:110
  221.3 32.6 %all-to-all-start.2 = ((bf16[64,20,128]{2,1,0:T(8,128)(2,1)}), bf16[64,20,128]{2,1,0:T(8,128)(2,1)S(1)}, u32[]{:S(2)}, u32[]{:S(2)}) async-start(bf16[64,20,128]{2,1,0:T(8,128)(2,1)} %reshape.37), calls=%async_computation.2 | async-start | bytes 786432 | tf_op jit(solution)/shard_map/all_to_all | solution.py:202
  (10 other events, 87.4 us)

commit v2 on v1

--- a/solution.py
+++ b/solution.py
@@ -68,19 +68,18 @@
             jax.ShapeDtypeStruct((height, LANES), BF16),
             jax.ShapeDtypeStruct((rows, tok), BF16),
         ],
-        compiler_params=pltpu.CompilerParams(vmem_limit_bytes=32 << 20),
+        compiler_params=pltpu.CompilerParams(vmem_limit_bytes=60 << 20),
         name="pack",
     )(column, ids, probs, tokens, cotangent)
 
 
-def unpack_kernel(flat_ref, x_ref, dy_ref, flat):
-    rows, width = x_ref.shape
+def unpack_kernel(flat_ref, out_ref, flat):
+    rows, width = out_ref.shape
     chunks = width // LANES
     flat[...] = flat_ref[...].astype(F32)
     for c in range(chunks):
         cols = slice(c * LANES, (c + 1) * LANES)
-        x_ref[:, cols] = flat[pl.ds(c, rows, stride=2 * chunks), :].astype(BF16)
-        dy_ref[:, cols] = flat[pl.ds(chunks + c, rows, stride=2 * chunks), :].astype(BF16)
+        out_ref[:, cols] = flat[pl.ds(c, rows, stride=chunks), :].astype(BF16)
 
 
 def unpack(flat, rows, width):
@@ -88,37 +87,67 @@
     return pl.pallas_call(
         unpack_kernel,
         in_specs=[whole],
-        out_specs=[whole, whole],
+        out_specs=whole,
         scratch_shapes=[pltpu.VMEM(flat.shape, F32)],
-        out_shape=[jax.ShapeDtypeStruct((rows, width), BF16)] * 2,
-        compiler_params=pltpu.CompilerParams(vmem_limit_bytes=32 << 20),
+        out_shape=jax.ShapeDtypeStruct((rows, width), BF16),
+        compiler_params=pltpu.CompilerParams(vmem_limit_bytes=16 << 20),
         name="unpack",
     )(flat)
+
+
+def transposed_dot(left, right):
+    return lax.dot_general(left, right, (((0,), (0,)), ((), ())), preferred_element_type=F32)
+
+
+def grads_kernel(parts, position, *refs):
+    blocks, (x_mid, dy_mid, both_ref, hidden_ref, out_ref) = refs[: parts - 1], refs[parts - 1 :]
+    place, wanted = position[0], position[1]
+    width = x_mid.shape[1]
+    hid = hidden_ref.shape[1]
+    per_half = parts // 2
+    for d in range(parts):
+        source = lax.rem(place - d + parts, parts)
+
+        @pl.when(source // per_half == wanted)
+        def _():
+            if d == parts // 2:
+                x, dy = x_mid[...], dy_mid[...]
+            else:
+                block = blocks[d if d < parts // 2 else d - 1]
+                x, dy = block[:, :width], block[:, width:]
+            into = pl.ds(pl.multiple_of(lax.rem(source, per_half) * width, width), width)
+            out_ref[into, : 2 * hid] = transposed_dot(x, both_ref[...]).astype(BF16)
+            out_ref[into, 2 * hid :] = transposed_dot(dy, hidden_ref[...]).astype(BF16)
+
+
+def grads(place, which, blocks, x_mid, dy_mid, both, hidden):
+    parts = len(blocks) + 1
+    half = parts // 2 * x_mid.shape[1]
+    whole = pl.BlockSpec(memory_space=pltpu.VMEM)
+    out = jax.ShapeDtypeStruct((half, both.shape[1] + hidden.shape[1]), BF16)
+    return pl.pallas_call(
+        lambda *refs: grads_kernel(parts, *refs),
+        in_specs=[pl.BlockSpec(memory_space=pltpu.SMEM)] + [whole] * (parts + 3),
+        out_specs=whole,
+        out_shape=out,
+        cost_estimate=pl.CostEstimate(
+            flops=2 * both.shape[0] * half * out.shape[1], bytes_accessed=8 << 20, transcendentals=0
+        ),
+        compiler_params=pltpu.CompilerParams(vmem_limit_bytes=16 << 20),
+        name="grads",
+    )(jnp.stack((place, which)).astype(jnp.int32), *blocks, x_mid, dy_mid, both, hidden)
 
 
 def shift(axis, step):
     n = lax.axis_size(axis)
     return [(i, (i + step) % n) for i in range(n)]
-
-
-def ring(value, axis, rightward, leftward):
-    held = {0: value}
-    n = lax.axis_size(axis)
-    right = left = value
-    for s in range(1, max(rightward, leftward) + 1):
-        if s <= rightward:
-            right = lax.ppermute(right, axis, shift(axis, 1))
-            held[s] = right
-        if s <= leftward:
-            left = lax.ppermute(left, axis, shift(axis, -1))
-            held[n - s] = left
-    return held
 
 
 def shards(tokens, cotangent, expert_ids, probs, gate_weight, up_weight, down_weight):
     peers = ("x", "z")
     owners = lax.axis_size("x") * lax.axis_size("z")
     parts = lax.axis_size("y")
+    middle = parts // 2
     core, place = lax.axis_index("dp"), lax.axis_index("y")
     tok, model = tokens.shape
     choose = expert_ids.shape[1]
@@ -128,13 +157,11 @@
     hid = gate_weight.shape[2]
     capacity = min(tok, (5 * tok * choose + 4 * owners - 1) // (4 * owners))
     rows = owners * capacity
-
+    first = core == 0
     swap = shift("dp", 1)
-    gate_own, up_own, down_own = gate_weight[0], up_weight[0], down_weight[0]
-    gate_other = lax.ppermute(gate_own, "dp", swap)
-    up_other = lax.ppermute(up_own, "dp", swap)
-    down_other = lax.ppermute(down_own, "dp", swap)
-    first = core == 0
+
+    def block_of(distance):
+        return lax.rem(place - distance + 2 * parts, parts)
 
     flat, table = pack(
         expert_ids.T,
@@ -150,14 +177,19 @@
         flat.reshape(owners, -1, LANES), peers, split_axis=0, concat_axis=0, tiled=True
     )
 
+    gate_own, up_own, down_own = gate_weight[0], up_weight[0], down_weight[0]
+    gate_other = lax.ppermute(gate_own, "dp", swap)
+    up_other = lax.ppermute(up_own, "dp", swap)
+    down_other = lax.ppermute(down_own, "dp", swap)
+
     low = jnp.where(first, gate_own, up_other)
     high = jnp.where(first, gate_other, up_own)
-    turned = jnp.concatenate((low, high)).reshape(parts, width, hid)
-    turned = lax.all_to_all(turned, "y", split_axis=0, concat_axis=0)
-    turned_other = lax.ppermute(turned, "dp", swap)
-    columns = jnp.concatenate(
-        (jnp.where(first, turned, turned_other), jnp.where(first, turned_other, turned)), axis=2
-    )
+    turn = jnp.concatenate((low, high)).reshape(parts, width, hid)
+    turned = []
+    for d in range(parts):
+        piece = lax.dynamic_index_in_dim(turn, block_of(-d), 0, keepdims=False)
+        turned.append(lax.ppermute(piece, "y", shift("y", d)) if d else piece)
+    turned_other = lax.ppermute(jnp.concatenate(turned), "dp", swap)
 
     both = jnp.concatenate(
         (
@@ -166,59 +198,73 @@
         )
     )
     down = jnp.concatenate((down_own, down_other))
-
-    x_own, dy_own = unpack(flat.reshape(-1, LANES), rows, width)
-    x_ring = ring(x_own, "y", parts // 2, parts // 2 - 1)
-    dy_ring = ring(dy_own, "y", parts // 2 - 1, parts // 2)
-
-    def block_of(distance):
-        return lax.rem(place - distance + parts, parts)
+    flat, turned, turned_other, both, down = lax.optimization_barrier(
+        (flat, turned, turned_other, both, down)
+    )
+
+    own = unpack(flat.reshape(-1, LANES), rows, 2 * width)
+    blocks = {0: own}
+    right = left = own
+    for d in range(1, middle):
+        right = lax.ppermute(right, "y", shift("y", 1))
+        left = lax.ppermute(left, "y", shift("y", -1))
+        blocks[d], blocks[parts - d] = right, left
+    x_mid = lax.ppermute(right[:, :width], "y", shift("y", 1))
+    dy_mid = lax.ppermute(left[:, width:], "y", shift("y", -1))
 
     acc = jnp.zeros((rows, 2 * hid), F32)
     back = jnp.zeros((rows, hid), F32)
-    for d in sorted(x_ring, key=lambda d: min(d, parts - d)):
+    near = sorted(range(parts), key=lambda d: min(d, parts - d))
+    for d in near:
+        x, dy = (x_mid, dy_mid) if d == middle else (blocks[d][:, :width], blocks[d][:, width:])
         block = block_of(d)
         start = jnp.where(block // per_half == core, 0, half) + lax.rem(block, per_half) * width
         piece = lax.dynamic_slice_in_dim(both, start, width, 0)
-        acc = acc + jnp.dot(x_ring[d], piece, preferred_element_type=F32)
+        acc = acc + jnp.dot(x, piece, preferred_element_type=F32)
         piece = lax.dynamic_slice_in_dim(down, start, width, 0)
-        back = back + jnp.dot(dy_ring[d], piece, preferred_element_type=F32)
+        back = back + jnp.dot(dy, piece, preferred_element_type=F32)
     gate, up = acc[:, :hid], acc[:, hid:]
     sig = jax.nn.sigmoid(gate)
     act = gate * sig
     hidden = (act * up).astype(BF16)
     d_up = (back * act).astype(BF16)
     d_gate = (back * up * sig * (1.0 + gate * (1.0 - sig))).astype(BF16)
-    d_both = jnp.concatenate((d_gate, d_up), axis=1)
-
-    d_ring = ring(d_both, "y", parts // 2, parts // 2 - 1)
+    d_both = jnp.concatenate(
+        (jnp.where(first, d_gate, d_up), jnp.where(first, d_up, d_gate)), axis=1
+    )
+
+    d_ring = {0: d_both}
+    right = left = d_both
+    for d in range(1, middle + 1):
+        right = lax.ppermute(right, "y", shift("y", 1))
+        d_ring[d] = right
+        if d < middle:
+            left = lax.ppermute(left, "y", shift("y", -1))
+            d_ring[parts - d] = left
     d_rows = jnp.zeros((rows, width), F32)
-    for d in sorted(d_ring, key=lambda d: min(d, parts - d)):
-        piece = lax.dynamic_index_in_dim(columns, block_of(d), 0, keepdims=False)
+    contract = (((1,), (1,)), ((), ()))
+    for d in near:
+        other = turned_other[d * width : (d + 1) * width]
         d_rows = d_rows + lax.dot_general(
-            d_ring[d], piece, (((1,), (1,)), ((), ())), preferred_element_type=F32
+            d_ring[d][:, :hid], turned[d], contract, preferred_element_type=F32
+        )
+        d_rows = d_rows + lax.dot_general(
+            d_ring[d][:, hid:], other, contract, preferred_element_type=F32
         )
     d_rows = d_rows.astype(BF16).reshape(owners, -1, LANES)
+    operands = (
+        [blocks[d] for d in range(parts) if d != middle],
+        x_mid,
+        dy_mid,
+        jnp.concatenate((d_gate, d_up), axis=1),
+        hidden,
+    )
+    received = lax.ppermute(grads(place, 1 - core, *operands), "dp", swap)
+    d_rows, operands = lax.optimization_barrier((d_rows, operands))
     returned = lax.all_to_all(d_rows, peers, split_axis=0, concat_axis=0, tiled=True)
-    d_tokens = lax.dot_general(
-        table,
-        returned.reshape(rows, width),
-        (((0,), (0,)), ((), ())),
-        preferred_element_type=F32,
-    ).astype(BF16)
-
-    x_all = jnp.stack([x_ring[d] for d in range(parts)])
-    dy_all = jnp.stack([dy_ring[d] for d in range(parts)])
-    grads_both = jnp.einsum("prc,rf->pcf", x_all, d_both, preferred_element_type=F32).astype(BF16)
-    grads_down = jnp.einsum("prc,rf->pcf", dy_all, hidden, preferred_element_type=F32).astype(BF16)
-    grads = jnp.concatenate((grads_both, grads_down), axis=2)
-
-    def of_half(which):
-        order = lax.rem(place - which * per_half - jnp.arange(per_half) + 2 * parts, parts)
-        return jnp.take(grads, order, axis=0).reshape(half, 3 * hid)
-
-    received = lax.ppermute(of_half(1 - core), "dp", swap)
-    total = (of_half(core).astype(F32) + received.astype(F32)).astype(BF16)
+    d_tokens = transposed_dot(table, returned.reshape(rows, width)).astype(BF16)
+    mine = grads(place, core, *operands)
+    total = (mine.astype(F32) + received.astype(F32)).astype(BF16)
     return (
         d_tokens,
         total[None, :, :hid],

time: 256 us -> 253 us (0.988)
  starting transfers between devices: 118 us -> 131 us
  other arithmetic: 16.5 us -> 5.18 us
  waiting for transfers between devices: 82.6 us -> 73.6 us
  local copies, waits for them, and re-layouts: 19.9 us -> 11.3 us
  Pallas kernels: 1.91 us -> 8.9 us
  matrix products: 14.4 us -> 19.7 us
    ppermute x23 -> x24, waiting for transfers between devices: 24.5 us -> 59 us  [the longest x6 22.7 us: shards(): left = lax.ppermute(left, 'y', shift('y', -1))]
    all_to_all x1, waiting for transfers between devices: 30 us -> 0.01 us  [shards(): lax.all_to_all(flat.reshape(owners, -1, LANES), peers, split_axis=0, conc...]
    all_to_all x1 -> x0, waiting for transfers between devices: 14.7 us -> none  [shards(): turned = lax.all_to_all(turned, 'y', split_axis=0, concat_axis=0)]
    ppermute x23 -> x24, starting transfers between devices: 73.3 us -> 86.6 us  [the longest x7 30.5 us: shards(): turned.append(lax.ppermute(piece, 'y', shift('y', d)) if d else piece)]
    gather x2 -> x0, local copies, waits for them, and re-layouts: 7.44 us -> none  [of_half(): return jnp.take(grads, order, axis=0).reshape(half, 3 * hid)]
    all_to_all x1 -> x0, starting transfers between devices: 7.1 us -> none  [shards(): turned = lax.all_to_all(turned, 'y', split_axis=0, concat_axis=0)]
    all_to_all x1, starting transfers between devices: 8.7 us -> 15.3 us  [shards(): lax.all_to_all(d_rows, peers, split_axis=0, concat_axis=0, tiled=True)]
    pallas_call x1 -> x3, Pallas kernels: 0.36 us -> 6.53 us  [the longest x2 6.17 us: grads(): pl.pallas_call(lambda *refs: grads_kernel(parts, *refs), in_specs=[pl.Blo...]
  transfers between devices with their start and end apart: 29 -> 29, of which waited for: 10 -> 12; matrix products, arithmetic and copies ran while one was open for 18% -> 11% of each run, Pallas kernels for 0% -> 3%
where the time goes in v2:
time: 253 us; the launch traced here: 251 us
  starting transfers between devices  131 us (52%)
  waiting for transfers between devices  73.6 us (29%)
  matrix products  19.7 us (8%)
  local copies, waits for them, and re-layouts  11.3 us (4%)
  Pallas kernels  8.9 us (4%)
  other arithmetic  5.18 us (2%)
    ppermute x7, starting transfers between devices, shards(): turned.append(lax.ppermute(piece, 'y', shift('y', d)) if d else piece)  30.5 us
    ppermute x6, starting transfers between devices, shards(): left = lax.ppermute(left, 'y', shift('y', -1))  26.5 us
    ppermute x6, waiting for transfers between devices, shards(): left = lax.ppermute(left, 'y', shift('y', -1))  22.7 us
    all_to_all x1, starting transfers between devices, shards(): lax.all_to_all(flat.reshape(owners, -1, LANES), peers, split_axis=0, conc...  22.5 us
    ppermute x7, waiting for transfers between devices, shards(): right = lax.ppermute(right, 'y', shift('y', 1))  18 us
    ppermute x7, starting transfers between devices, shards(): right = lax.ppermute(right, 'y', shift('y', 1))  18 us
    all_to_all x1, starting transfers between devices, shards(): lax.all_to_all(d_rows, peers, split_axis=0, concat_axis=0, tiled=True)  15.3 us
    all_to_all x1, waiting for transfers between devices, shards(): lax.all_to_all(d_rows, peers, split_axis=0, concat_axis=0, tiled=True)  14.6 us
  transfers between devices with their start and end apart: 29, of which 12 were waited for; matrix products, arithmetic and copies ran while one was open for 11% of the time, Pallas kernels for 3%

profile of v2, /device:TPU:6, one launch (start us, length us, event | category | flops | bytes accessed | tf_op | source)
XLA Modules:
  0.0 251.5 jit_solution(4364106755924285395)
XLA Ops:
  2.7 2.4 collective-permute-start
  5.1 2.4 pack.1
  7.5 22.5 %all-to-all-start = ((bf16[64,40,128]{2,1,0:T(8,128)(2,1)}), bf16[64,40,128]{2,1,0:T(8,128)(2,1)S(1)}, u32[]{:S(2)}, u32[]{:S(2)}) async-start(bf16[64,40,128]{2,1,0:T(8,128)(2,1)} %bitcast.57), calls=%async_computation | async-start | bytes 1310720 | tf_op jit(solution)/shard_map/all_to_all | solution.py:176
  31.9 3.5 %collective-permute-start.2 = (bf16[512,128]{1,0:T(8,128)(2,1)}, bf16[512,128]{1,0:T(8,128)(2,1)S(1)}, u32[]{:S(2)}, u32[]{:S(2)}) collective-permute-start(bf16[512,128]{1,0:T(8,128)(2,1)} %get-tuple-element.70), channel_id=1, source_target_pairs={{0,1},{1,2},{2,3},{3,4},{4,5},{5,6},{6,7},{7,0},{8,9},{9,10},{10,1... | collective-permute-start | bytes 393224 | tf_op jit(solution)/shard_map/ppermute | solution.py:191
  37.4 4.6 %collective-permute-start.3 = (bf16[512,128]{1,0:T(8,128)(2,1)}, bf16[512,128]{1,0:T(8,128)(2,1)S(1)}, u32[]{:S(2)}, u32[]{:S(2)}) collective-permute-start(bf16[512,128]{1,0:T(8,128)(2,1)} %get-tuple-element.69), channel_id=1, source_target_pairs={{0,2},{1,3},{2,4},{3,5},{4,6},{5,7},{6,0},{7,1},{8,10},{9,11},{10,... | collective-permute-start | bytes 393224 | tf_op jit(solution)/shard_map/ppermute | solution.py:191
  42.7 4.9 %collective-permute-start.4 = (bf16[512,128]{1,0:T(8,128)(2,1)}, bf16[512,128]{1,0:T(8,128)(2,1)S(1)}, u32[]{:S(2)}, u32[]{:S(2)}) collective-permute-start(bf16[512,128]{1,0:T(8,128)(2,1)} %get-tuple-element.68), channel_id=1, source_target_pairs={{0,3},{1,4},{2,5},{3,6},{4,7},{5,0},{6,1},{7,2},{8,11},{9,12},{10,... | collective-permute-start | bytes 393224 | tf_op jit(solution)/shard_map/ppermute | solution.py:191
  47.6 3.8 %collective-permute-start.5 = (bf16[512,128]{1,0:T(8,128)(2,1)}, bf16[512,128]{1,0:T(8,128)(2,1)S(1)}, u32[]{:S(2)}, u32[]{:S(2)}) collective-permute-start(bf16[512,128]{1,0:T(8,128)(2,1)} %get-tuple-element.67), channel_id=1, source_target_pairs={{0,4},{1,5},{2,6},{3,7},{4,0},{5,1},{6,2},{7,3},{8,12},{9,13},{10,... | collective-permute-start | bytes 393224 | tf_op jit(solution)/shard_map/ppermute | solution.py:191
  51.5 5.1 %collective-permute-start.6 = (bf16[512,128]{1,0:T(8,128)(2,1)}, bf16[512,128]{1,0:T(8,128)(2,1)S(1)}, u32[]{:S(2)}, u32[]{:S(2)}) collective-permute-start(bf16[512,128]{1,0:T(8,128)(2,1)} %get-tuple-element.66), channel_id=1, source_target_pairs={{0,5},{1,6},{2,7},{3,0},{4,1},{5,2},{6,3},{7,4},{8,13},{9,14},{10,... | collective-permute-start | bytes 393224 | tf_op jit(solution)/shard_map/ppermute | solution.py:191
  56.7 5.3 %collective-permute-start.7 = (bf16[512,128]{1,0:T(8,128)(2,1)}, bf16[512,128]{1,0:T(8,128)(2,1)S(1)}, u32[]{:S(2)}, u32[]{:S(2)}) collective-permute-start(bf16[512,128]{1,0:T(8,128)(2,1)} %get-tuple-element.65), channel_id=1, source_target_pairs={{0,6},{1,7},{2,0},{3,1},{4,2},{5,3},{6,4},{7,5},{8,14},{9,15},{10,... | collective-permute-start | bytes 393224 | tf_op jit(solution)/shard_map/ppermute | solution.py:191
  62.0 3.3 %collective-permute-start.8 = (bf16[512,128]{1,0:T(8,128)(2,1)S(1)}, bf16[512,128]{1,0:T(8,128)(2,1)S(1)}, u32[]{:S(2)}, u32[]{:S(2)}) collective-permute-start(bf16[512,128]{1,0:T(8,128)(2,1)S(1)} %get-tuple-element.64), channel_id=1, source_target_pairs={{0,7},{1,0},{2,1},{3,2},{4,3},{5,4},{6,5},{7,6},{8,15},{9,8},{10,9... | collective-permute-start | bytes 393224 | tf_op jit(solution)/shard_map/ppermute | solution.py:191
  65.3 5.8 %collective-permute-done.6 = bf16[512,128]{1,0:T(8,128)(2,1)S(1)} collective-permute-done((bf16[512,128]{1,0:T(8,128)(2,1)}, bf16[512,128]{1,0:T(8,128)(2,1)S(1)}, u32[]{:S(2)}, u32[]{:S(2)}) %collective-permute-start.6) | collective-permute-done | bytes 131104 | tf_op jit(solution)/shard_map/ppermute | solution.py:191
  71.1 4.4 %collective-permute-done.7 = bf16[512,128]{1,0:T(8,128)(2,1)S(1)} collective-permute-done((bf16[512,128]{1,0:T(8,128)(2,1)}, bf16[512,128]{1,0:T(8,128)(2,1)S(1)}, u32[]{:S(2)}, u32[]{:S(2)}) %collective-permute-start.7) | collective-permute-done | bytes 131104 | tf_op jit(solution)/shard_map/ppermute | solution.py:191
  81.5 4.8 %collective-permute-start.11 = (bf16[320,1024]{1,0:T(8,128)(2,1)S(1)}, bf16[320,1024]{1,0:T(8,128)(2,1)S(1)}, u32[]{:S(2)}, u32[]{:S(2)}) collective-permute-start(bf16[320,1024]{1,0:T(8,128)(2,1)S(1)} %unpack.1.refs_1_), channel_id=1, source_target_pairs={{0,1},{1,2},{2,3},{3,4},{4,5},{5,6},{6,7},{7,0},{8,9},{9,10},{10,1... | collective-permute-start | bytes 1966088 | tf_op jit(solution)/shard_map/ppermute | solution.py:209
  86.7 2.4 collective-permute-start.12
  89.1 12.7 %collective-permute-done.11.refs_2_ = bf16[320,1024]{1,0:T(8,128)(2,1)S(1)} collective-permute-done((bf16[320,1024]{1,0:T(8,128)(2,1)S(1)}, bf16[320,1024]{1,0:T(8,128)(2,1)S(1)}, u32[]{:S(2)}, u32[]{:S(2)}) %collective-permute-start.11) | collective-permute-done | bytes 655392 | tf_op jit(solution)/shard_map/ppermute | solution.py:209
  101.8 3.6 %collective-permute-start.13 = (bf16[320,1024]{1,0:T(8,128)(2,1)S(1)}, bf16[320,1024]{1,0:T(8,128)(2,1)S(1)}, u32[]{:S(2)}, u32[]{:S(2)}) collective-permute-start(bf16[320,1024]{1,0:T(8,128)(2,1)S(1)} %collective-permute-done.11.refs_2_), channel_id=1, source_target_pairs={{0,1},{1,2},{2,3},{3,4},{4,5},{5,6},{6,7},{7,0},{8,9},{9,10},{10,1... | collective-permute-start | bytes 1966088 | tf_op jit(solution)/shard_map/ppermute | solution.py:209
  108.2 3.5 %collective-permute-start.14 = (bf16[320,1024]{1,0:T(8,128)(2,1)S(1)}, bf16[320,1024]{1,0:T(8,128)(2,1)S(1)}, u32[]{:S(2)}, u32[]{:S(2)}) collective-permute-start(bf16[320,1024]{1,0:T(8,128)(2,1)S(1)} %collective-permute-done.12.refs_7_), channel_id=1, source_target_pairs={{0,7},{1,0},{2,1},{3,2},{4,3},{5,4},{6,5},{7,6},{8,15},{9,8},{10,9... | collective-permute-start | bytes 1966088 | tf_op jit(solution)/shard_map/ppermute | solution.py:210
  113.4 12.8 %collective-permute-done.14.refs_6_ = bf16[320,1024]{1,0:T(8,128)(2,1)S(1)} collective-permute-done((bf16[320,1024]{1,0:T(8,128)(2,1)S(1)}, bf16[320,1024]{1,0:T(8,128)(2,1)S(1)}, u32[]{:S(2)}, u32[]{:S(2)}) %collective-permute-start.14) | collective-permute-done | bytes 655392 | tf_op jit(solution)/shard_map/ppermute | solution.py:210
  126.1 4.7 %collective-permute-start.16 = (bf16[320,1024]{1,0:T(8,128)(2,1)S(1)}, bf16[320,1024]{1,0:T(8,128)(2,1)S(1)}, u32[]{:S(2)}, u32[]{:S(2)}) collective-permute-start(bf16[320,1024]{1,0:T(8,128)(2,1)S(1)} %collective-permute-done.14.refs_6_), channel_id=1, source_target_pairs={{0,7},{1,0},{2,1},{3,2},{4,3},{5,4},{6,5},{7,6},{8,15},{9,8},{10,9... | collective-permute-start | bytes 1966088 | tf_op jit(solution)/shard_map/ppermute | solution.py:210
  133.8 9.7 %collective-permute-done.16.refs_5_ = bf16[320,1024]{1,0:T(8,128)(2,1)S(1)} collective-permute-done((bf16[320,1024]{1,0:T(8,128)(2,1)S(1)}, bf16[320,1024]{1,0:T(8,128)(2,1)S(1)}, u32[]{:S(2)}, u32[]{:S(2)}) %collective-permute-start.16) | collective-permute-done | bytes 655392 | tf_op jit(solution)/shard_map/ppermute | solution.py:210
  143.5 5.6 %collective-permute-start.17 = (bf16[320,512]{1,0:T(8,128)(2,1)S(1)}, bf16[320,512]{1,0:T(8,128)(2,1)S(1)}, u32[]{:S(2)}, u32[]{:S(2)}) collective-permute-start(bf16[320,512]{1,0:T(8,128)(2,1)S(1)} %slice.172), channel_id=1, source_target_pairs={{0,7},{1,0},{2,1},{3,2},{4,3},{5,4},{6,5},{7,6},{8,15},{9,8},{10,9... | collective-permute-start | bytes 983048 | tf_op jit(solution)/shard_map/ppermute | solution.py:213
  151.6 2.2 collective-permute-done.17.refs_9_
  154.0 5.3 %collective-permute-done.18.refs_8_ = bf16[320,512]{1,0:T(8,128)(2,1)S(1)} collective-permute-done((bf16[320,512]{1,0:T(8,128)(2,1)S(1)}, bf16[320,512]{1,0:T(8,128)(2,1)S(1)}, u32[]{:S(2)}, u32[]{:S(2)}) %collective-permute-start.18) | collective-permute-done | bytes 327712 | tf_op jit(solution)/shard_map/ppermute | solution.py:212
  162.1 5.1 %collective-permute-start.20 = (bf16[320,256]{1,0:T(8,128)(2,1)S(1)}, bf16[320,256]{1,0:T(8,128)(2,1)S(1)}, u32[]{:S(2)}, u32[]{:S(2)}) collective-permute-start(bf16[320,256]{1,0:T(8,128)(2,1)S(1)} %pad_maximum_fusion.2), channel_id=1, source_target_pairs={{0,7},{1,0},{2,1},{3,2},{4,3},{5,4},{6,5},{7,6},{8,15},{9,8},{10,9... | collective-permute-start | bytes 491528 | tf_op jit(solution)/shard_map/ppermute | solution.py:242
  167.4 3.7 %grads.3 = bf16[2048,384]{1,0:T(8,128)(2,1)} custom-call(s32[2]{0:T(128)S(1)} %pad_add_fusion.1.refs_0_, bf16[320,1024]{1,0:T(8,128)(2,1)S(1)} %unpack.1.refs_1_, bf16[320,1024]{1,0:T(8,128)(2,1)S(1)} %collective-permute-done.11.refs_2_, bf16[320,1024]{1,0:T(8,128)(2,1)S(1)} %collective-permute-done.13.refs_3_, ...), custom_call_target="tpu_custom_call" | custom-call | flops 503316480 | bytes 8388608 | tf_op jit(solution)/shard_map/grads/pallas_call | solution.py:128
  171.0 2.2 collective-permute-start.26
  179.5 5.3 %collective-permute-start.22 = (bf16[320,256]{1,0:T(8,128)(2,1)S(1)}, bf16[320,256]{1,0:T(8,128)(2,1)S(1)}, u32[]{:S(2)}, u32[]{:S(2)}) collective-permute-start(bf16[320,256]{1,0:T(8,128)(2,1)S(1)} %collective-permute-done.20), channel_id=1, source_target_pairs={{0,7},{1,0},{2,1},{3,2},{4,3},{5,4},{6,5},{7,6},{8,15},{9,8},{10,9... | collective-permute-start | bytes 491528 | tf_op jit(solution)/shard_map/ppermute | solution.py:242
  189.8 5.6 %collective-permute-start.24 = (bf16[320,256]{1,0:T(8,128)(2,1)S(1)}, bf16[320,256]{1,0:T(8,128)(2,1)S(1)}, u32[]{:S(2)}, u32[]{:S(2)}) collective-permute-start(bf16[320,256]{1,0:T(8,128)(2,1)S(1)} %collective-permute-done.22), channel_id=1, source_target_pairs={{0,7},{1,0},{2,1},{3,2},{4,3},{5,4},{6,5},{7,6},{8,15},{9,8},{10,9... | collective-permute-start | bytes 491528 | tf_op jit(solution)/shard_map/ppermute | solution.py:242
  200.8 4.8 %collective-permute-done.25 = bf16[320,256]{1,0:T(8,128)(2,1)S(1)} collective-permute-done((bf16[320,256]{1,0:T(8,128)(2,1)S(1)}, bf16[320,256]{1,0:T(8,128)(2,1)S(1)}, u32[]{:S(2)}, u32[]{:S(2)}) %collective-permute-start.25) | collective-permute-done | bytes 163872 | tf_op jit(solution)/shard_map/ppermute | solution.py:239
  209.7 15.3 %all-to-all-start.1 = ((bf16[64,20,128]{2,1,0:T(8,128)(2,1)}), bf16[64,20,128]{2,1,0:T(8,128)(2,1)}, u32[]{:S(2)}, u32[]{:S(2)}) async-start(bf16[64,20,128]{2,1,0:T(8,128)(2,1)} %reshape.26), calls=%async_computation.1 | async-start | bytes 786432 | tf_op jit(solution)/shard_map/all_to_all | solution.py:264
  229.2 2.5 grads.2
  234.8 14.6 %all-to-all-done.1 = bf16[64,20,128]{2,1,0:T(8,128)(2,1)} async-done(((bf16[64,20,128]{2,1,0:T(8,128)(2,1)}), bf16[64,20,128]{2,1,0:T(8,128)(2,1)}, u32[]{:S(2)}, u32[]{:S(2)}) %all-to-all-start.1) | async-done | bytes 327712 | tf_op jit(solution)/shard_map/all_to_all | solution.py:264
  (157 shorter events, 55.4 us)
Async XLA Ops:
  0.7 29.4 %collective-permute-start.1 = (bf16[2048,128]{1,0:T(8,128)(2,1)}, bf16[2048,128]{1,0:T(8,128)(2,1)S(1)}, u32[]{:S(2)}, u32[]{:S(2)}) collective-permute-start(bf16[2048,128]{1,0:T(8,128)(2,1)} %bitcast.53), channel_id=1, source_target_pairs={{0,512},{512,0},{1,513},{513,1},{2,514},{514,2},{3,515},{515,3},{4... | collective-permute-start | bytes 1572872 | tf_op jit(solution)/shard_map/ppermute | solution.py:181
  2.7 27.4 %collective-permute-start = (bf16[2048,128]{1,0:T(8,128)(2,1)}, bf16[2048,128]{1,0:T(8,128)(2,1)S(1)}, u32[]{:S(2)}, u32[]{:S(2)}) collective-permute-start(bf16[2048,128]{1,0:T(8,128)(2,1)} %bitcast.55), channel_id=1, source_target_pairs={{0,512},{512,0},{1,513},{513,1},{2,514},{514,2},{3,515},{515,3},{4... | collective-permute-start | bytes 1572872 | tf_op jit(solution)/shard_map/ppermute | solution.py:182
  7.5 73.7 %all-to-all-start = ((bf16[64,40,128]{2,1,0:T(8,128)(2,1)}), bf16[64,40,128]{2,1,0:T(8,128)(2,1)S(1)}, u32[]{:S(2)}, u32[]{:S(2)}) async-start(bf16[64,40,128]{2,1,0:T(8,128)(2,1)} %bitcast.57), calls=%async_computation | async-start | bytes 1310720 | tf_op jit(solution)/shard_map/all_to_all | solution.py:176
  31.9 19.5 %collective-permute-start.2 = (bf16[512,128]{1,0:T(8,128)(2,1)}, bf16[512,128]{1,0:T(8,128)(2,1)S(1)}, u32[]{:S(2)}, u32[]{:S(2)}) collective-permute-start(bf16[512,128]{1,0:T(8,128)(2,1)} %get-tuple-element.70), channel_id=1, source_target_pairs={{0,1},{1,2},{2,3},{3,4},{4,5},{5,6},{6,7},{7,0},{8,9},{9,10},{10,1... | collective-permute-start | bytes 393224 | tf_op jit(solution)/shard_map/ppermute | solution.py:191
  35.4 42.8 %collective-permute-start.10 = (bf16[2048,128]{1,0:T(8,128)(2,1)}, bf16[2048,128]{1,0:T(8,128)(2,1)}, u32[]{:S(2)}, u32[]{:S(2)}) collective-permute-start(bf16[2048,128]{1,0:T(8,128)(2,1)} %bitcast.15), channel_id=1, source_target_pairs={{0,512},{512,0},{1,513},{513,1},{2,514},{514,2},{3,515},{515,3},{4... | collective-permute-start | bytes 1572872 | tf_op jit(solution)/shard_map/ppermute | solution.py:183
  37.4 42.1 %copy-start.13 = (bf16[1,2048,128]{2,1,0:T(8,128)(2,1)S(1)}, bf16[1,2048,128]{2,1,0:T(8,128)(2,1)}, u32[]{:S(2)}) copy-start(bf16[1,2048,128]{2,1,0:T(8,128)(2,1)} %param.12) | copy-start | bytes 1572868
  37.4 42.1 %copy-start.15 = (bf16[2048,128]{1,0:T(8,128)(2,1)S(1)}, bf16[2048,128]{1,0:T(8,128)(2,1)}, u32[]{:S(2)}) copy-start(bf16[2048,128]{1,0:T(8,128)(2,1)} %copy-done.14) | copy-start | bytes 1572868
  37.4 19.3 %collective-permute-start.3 = (bf16[512,128]{1,0:T(8,128)(2,1)}, bf16[512,128]{1,0:T(8,128)(2,1)S(1)}, u32[]{:S(2)}, u32[]{:S(2)}) collective-permute-start(bf16[512,128]{1,0:T(8,128)(2,1)} %get-tuple-element.69), channel_id=1, source_target_pairs={{0,2},{1,3},{2,4},{3,5},{4,6},{5,7},{6,0},{7,1},{8,10},{9,11},{10,... | collective-permute-start | bytes 393224 | tf_op jit(solution)/shard_map/ppermute | solution.py:191
  42.7 19.3 %collective-permute-start.4 = (bf16[512,128]{1,0:T(8,128)(2,1)}, bf16[512,128]{1,0:T(8,128)(2,1)S(1)}, u32[]{:S(2)}, u32[]{:S(2)}) collective-permute-start(bf16[512,128]{1,0:T(8,128)(2,1)} %get-tuple-element.68), channel_id=1, source_target_pairs={{0,3},{1,4},{2,5},{3,6},{4,7},{5,0},{6,1},{7,2},{8,11},{9,12},{10,... | collective-permute-start | bytes 393224 | tf_op jit(solution)/shard_map/ppermute | solution.py:191
  47.6 17.7 %collective-permute-start.5 = (bf16[512,128]{1,0:T(8,128)(2,1)}, bf16[512,128]{1,0:T(8,128)(2,1)S(1)}, u32[]{:S(2)}, u32[]{:S(2)}) collective-permute-start(bf16[512,128]{1,0:T(8,128)(2,1)} %get-tuple-element.67), channel_id=1, source_target_pairs={{0,4},{1,5},{2,6},{3,7},{4,0},{5,1},{6,2},{7,3},{8,12},{9,13},{10,... | collective-permute-start | bytes 393224 | tf_op jit(solution)/shard_map/ppermute | solution.py:191
  51.5 19.7 %collective-permute-start.6 = (bf16[512,128]{1,0:T(8,128)(2,1)}, bf16[512,128]{1,0:T(8,128)(2,1)S(1)}, u32[]{:S(2)}, u32[]{:S(2)}) collective-permute-start(bf16[512,128]{1,0:T(8,128)(2,1)} %get-tuple-element.66), channel_id=1, source_target_pairs={{0,5},{1,6},{2,7},{3,0},{4,1},{5,2},{6,3},{7,4},{8,13},{9,14},{10,... | collective-permute-start | bytes 393224 | tf_op jit(solution)/shard_map/ppermute | solution.py:191
  56.7 18.9 %collective-permute-start.7 = (bf16[512,128]{1,0:T(8,128)(2,1)}, bf16[512,128]{1,0:T(8,128)(2,1)S(1)}, u32[]{:S(2)}, u32[]{:S(2)}) collective-permute-start(bf16[512,128]{1,0:T(8,128)(2,1)} %get-tuple-element.65), channel_id=1, source_target_pairs={{0,6},{1,7},{2,0},{3,1},{4,2},{5,3},{6,4},{7,5},{8,14},{9,15},{10,... | collective-permute-start | bytes 393224 | tf_op jit(solution)/shard_map/ppermute | solution.py:191
  62.0 14.2 %collective-permute-start.8 = (bf16[512,128]{1,0:T(8,128)(2,1)S(1)}, bf16[512,128]{1,0:T(8,128)(2,1)S(1)}, u32[]{:S(2)}, u32[]{:S(2)}) collective-permute-start(bf16[512,128]{1,0:T(8,128)(2,1)S(1)} %get-tuple-element.64), channel_id=1, source_target_pairs={{0,7},{1,0},{2,1},{3,2},{4,3},{5,4},{6,5},{7,6},{8,15},{9,8},{10,9... | collective-permute-start | bytes 393224 | tf_op jit(solution)/shard_map/ppermute | solution.py:191
  76.2 5.0 %collective-permute-start.9 = (bf16[4096,128]{1,0:T(8,128)(2,1)S(1)}, bf16[4096,128]{1,0:T(8,128)(2,1)}, u32[]{:S(2)}, u32[]{:S(2)}) collective-permute-start(bf16[4096,128]{1,0:T(8,128)(2,1)S(1)} %constant_dynamic-update-slice_fusion), channel_id=1, source_target_pairs={{0,512},{512,0},{1,513},{513,1},{2,514},{514,2},{3,515},{515,3},{4... | collective-permute-start | bytes 3145736 | tf_op jit(solution)/shard_map/ppermute | solution.py:192
  81.5 20.2 %collective-permute-start.11 = (bf16[320,1024]{1,0:T(8,128)(2,1)S(1)}, bf16[320,1024]{1,0:T(8,128)(2,1)S(1)}, u32[]{:S(2)}, u32[]{:S(2)}) collective-permute-start(bf16[320,1024]{1,0:T(8,128)(2,1)S(1)} %unpack.1.refs_1_), channel_id=1, source_target_pairs={{0,1},{1,2},{2,3},{3,4},{4,5},{5,6},{6,7},{7,0},{8,9},{9,10},{10,1... | collective-permute-start | bytes 1966088 | tf_op jit(solution)/shard_map/ppermute | solution.py:209
  86.7 21.5 %collective-permute-start.12 = (bf16[320,1024]{1,0:T(8,128)(2,1)S(1)}, bf16[320,1024]{1,0:T(8,128)(2,1)S(1)}, u32[]{:S(2)}, u32[]{:S(2)}) collective-permute-start(bf16[320,1024]{1,0:T(8,128)(2,1)S(1)} %unpack.1.refs_1_), channel_id=1, source_target_pairs={{0,7},{1,0},{2,1},{3,2},{4,3},{5,4},{6,5},{7,6},{8,15},{9,8},{10,9... | collective-permute-start | bytes 1966088 | tf_op jit(solution)/shard_map/ppermute | solution.py:210
  101.8 29.3 %collective-permute-start.13 = (bf16[320,1024]{1,0:T(8,128)(2,1)S(1)}, bf16[320,1024]{1,0:T(8,128)(2,1)S(1)}, u32[]{:S(2)}, u32[]{:S(2)}) collective-permute-start(bf16[320,1024]{1,0:T(8,128)(2,1)S(1)} %collective-permute-done.11.refs_2_), channel_id=1, source_target_pairs={{0,1},{1,2},{2,3},{3,4},{4,5},{5,6},{6,7},{7,0},{8,9},{9,10},{10,1... | collective-permute-start | bytes 1966088 | tf_op jit(solution)/shard_map/ppermute | solution.py:209
  108.2 59.2 %copy-start.2 = (bf16[320,1024]{1,0:T(8,128)(2,1)}, bf16[320,1024]{1,0:T(8,128)(2,1)S(1)}, u32[]{:S(2)}) copy-start(bf16[320,1024]{1,0:T(8,128)(2,1)S(1)} %collective-permute-done.12.refs_7_) | copy-start | bytes 1966084
  108.2 18.0 %collective-permute-start.14 = (bf16[320,1024]{1,0:T(8,128)(2,1)S(1)}, bf16[320,1024]{1,0:T(8,128)(2,1)S(1)}, u32[]{:S(2)}, u32[]{:S(2)}) collective-permute-start(bf16[320,1024]{1,0:T(8,128)(2,1)S(1)} %collective-permute-done.12.refs_7_), channel_id=1, source_target_pairs={{0,7},{1,0},{2,1},{3,2},{4,3},{5,4},{6,5},{7,6},{8,15},{9,8},{10,9... | collective-permute-start | bytes 1966088 | tf_op jit(solution)/shard_map/ppermute | solution.py:210
  126.1 17.3 %collective-permute-start.16 = (bf16[320,1024]{1,0:T(8,128)(2,1)S(1)}, bf16[320,1024]{1,0:T(8,128)(2,1)S(1)}, u32[]{:S(2)}, u32[]{:S(2)}) collective-permute-start(bf16[320,1024]{1,0:T(8,128)(2,1)S(1)} %collective-permute-done.14.refs_6_), channel_id=1, source_target_pairs={{0,7},{1,0},{2,1},{3,2},{4,3},{5,4},{6,5},{7,6},{8,15},{9,8},{10,9... | collective-permute-start | bytes 1966088 | tf_op jit(solution)/shard_map/ppermute | solution.py:210
  131.1 18.0 %collective-permute-start.15 = (bf16[320,1024]{1,0:T(8,128)(2,1)S(1)}, bf16[320,1024]{1,0:T(8,128)(2,1)S(1)}, u32[]{:S(2)}, u32[]{:S(2)}) collective-permute-start(bf16[320,1024]{1,0:T(8,128)(2,1)S(1)} %collective-permute-done.13.refs_3_), channel_id=1, source_target_pairs={{0,1},{1,2},{2,3},{3,4},{4,5},{5,6},{6,7},{7,0},{8,9},{9,10},{10,1... | collective-permute-start | bytes 1966088 | tf_op jit(solution)/shard_map/ppermute | solution.py:209
  143.5 10.3 %collective-permute-start.17 = (bf16[320,512]{1,0:T(8,128)(2,1)S(1)}, bf16[320,512]{1,0:T(8,128)(2,1)S(1)}, u32[]{:S(2)}, u32[]{:S(2)}) collective-permute-start(bf16[320,512]{1,0:T(8,128)(2,1)S(1)} %slice.172), channel_id=1, source_target_pairs={{0,7},{1,0},{2,1},{3,2},{4,3},{5,4},{6,5},{7,6},{8,15},{9,8},{10,9... | collective-permute-start | bytes 983048 | tf_op jit(solution)/shard_map/ppermute | solution.py:213
  149.1 10.2 %collective-permute-start.18 = (bf16[320,512]{1,0:T(8,128)(2,1)S(1)}, bf16[320,512]{1,0:T(8,128)(2,1)S(1)}, u32[]{:S(2)}, u32[]{:S(2)}) collective-permute-start(bf16[320,512]{1,0:T(8,128)(2,1)S(1)} %slice.178), channel_id=1, source_target_pairs={{0,1},{1,2},{2,3},{3,4},{4,5},{5,6},{6,7},{7,0},{8,9},{9,10},{10,1... | collective-permute-start | bytes 983048 | tf_op jit(solution)/shard_map/ppermute | solution.py:212
  160.2 14.2 %collective-permute-start.19 = (bf16[320,256]{1,0:T(8,128)(2,1)S(1)}, bf16[320,256]{1,0:T(8,128)(2,1)S(1)}, u32[]{:S(2)}, u32[]{:S(2)}) collective-permute-start(bf16[320,256]{1,0:T(8,128)(2,1)S(1)} %pad_maximum_fusion.2), channel_id=1, source_target_pairs={{0,1},{1,2},{2,3},{3,4},{4,5},{5,6},{6,7},{7,0},{8,9},{9,10},{10,1... | collective-permute-start | bytes 491528 | tf_op jit(solution)/shard_map/ppermute | solution.py:239
  162.1 15.7 %collective-permute-start.20 = (bf16[320,256]{1,0:T(8,128)(2,1)S(1)}, bf16[320,256]{1,0:T(8,128)(2,1)S(1)}, u32[]{:S(2)}, u32[]{:S(2)}) collective-permute-start(bf16[320,256]{1,0:T(8,128)(2,1)S(1)} %pad_maximum_fusion.2), channel_id=1, source_target_pairs={{0,7},{1,0},{2,1},{3,2},{4,3},{5,4},{6,5},{7,6},{8,15},{9,8},{10,9... | collective-permute-start | bytes 491528 | tf_op jit(solution)/shard_map/ppermute | solution.py:242
  171.0 60.7 %collective-permute-start.26 = (bf16[2048,384]{1,0:T(8,128)(2,1)}, bf16[2048,384]{1,0:T(8,128)(2,1)}, u32[]{:S(2)}, u32[]{:S(2)}) collective-permute-start(bf16[2048,384]{1,0:T(8,128)(2,1)} %grads.3), channel_id=1, source_target_pairs={{0,512},{512,0},{1,513},{513,1},{2,514},{514,2},{3,515},{515,3},{4... | collective-permute-start | bytes 4718600 | tf_op jit(solution)/shard_map/ppermute | solution.py:262
  175.6 9.7 %collective-permute-start.21 = (bf16[320,256]{1,0:T(8,128)(2,1)S(1)}, bf16[320,256]{1,0:T(8,128)(2,1)S(1)}, u32[]{:S(2)}, u32[]{:S(2)}) collective-permute-start(bf16[320,256]{1,0:T(8,128)(2,1)S(1)} %collective-permute-done.19), channel_id=1, source_target_pairs={{0,1},{1,2},{2,3},{3,4},{4,5},{5,6},{6,7},{7,0},{8,9},{9,10},{10,1... | collective-permute-start | bytes 491528 | tf_op jit(solution)/shard_map/ppermute | solution.py:239
  179.5 9.1 %collective-permute-start.22 = (bf16[320,256]{1,0:T(8,128)(2,1)S(1)}, bf16[320,256]{1,0:T(8,128)(2,1)S(1)}, u32[]{:S(2)}, u32[]{:S(2)}) collective-permute-start(bf16[320,256]{1,0:T(8,128)(2,1)S(1)} %collective-permute-done.20), channel_id=1, source_target_pairs={{0,7},{1,0},{2,1},{3,2},{4,3},{5,4},{6,5},{7,6},{8,15},{9,8},{10,9... | collective-permute-start | bytes 491528 | tf_op jit(solution)/shard_map/ppermute | solution.py:242
  185.3 10.7 %collective-permute-start.23 = (bf16[320,256]{1,0:T(8,128)(2,1)S(1)}, bf16[320,256]{1,0:T(8,128)(2,1)S(1)}, u32[]{:S(2)}, u32[]{:S(2)}) collective-permute-start(bf16[320,256]{1,0:T(8,128)(2,1)S(1)} %collective-permute-done.21), channel_id=1, source_target_pairs={{0,1},{1,2},{2,3},{3,4},{4,5},{5,6},{6,7},{7,0},{8,9},{9,10},{10,1... | collective-permute-start | bytes 491528 | tf_op jit(solution)/shard_map/ppermute | solution.py:239
  189.8 9.3 %collective-permute-start.24 = (bf16[320,256]{1,0:T(8,128)(2,1)S(1)}, bf16[320,256]{1,0:T(8,128)(2,1)S(1)}, u32[]{:S(2)}, u32[]{:S(2)}) collective-permute-start(bf16[320,256]{1,0:T(8,128)(2,1)S(1)} %collective-permute-done.22), channel_id=1, source_target_pairs={{0,7},{1,0},{2,1},{3,2},{4,3},{5,4},{6,5},{7,6},{8,15},{9,8},{10,9... | collective-permute-start | bytes 491528 | tf_op jit(solution)/shard_map/ppermute | solution.py:242
  197.1 8.4 %collective-permute-start.25 = (bf16[320,256]{1,0:T(8,128)(2,1)S(1)}, bf16[320,256]{1,0:T(8,128)(2,1)S(1)}, u32[]{:S(2)}, u32[]{:S(2)}) collective-permute-start(bf16[320,256]{1,0:T(8,128)(2,1)S(1)} %collective-permute-done.23), channel_id=1, source_target_pairs={{0,1},{1,2},{2,3},{3,4},{4,5},{5,6},{6,7},{7,0},{8,9},{9,10},{10,1... | collective-permute-start | bytes 491528 | tf_op jit(solution)/shard_map/ppermute | solution.py:239
  209.7 39.7 %all-to-all-start.1 = ((bf16[64,20,128]{2,1,0:T(8,128)(2,1)}), bf16[64,20,128]{2,1,0:T(8,128)(2,1)}, u32[]{:S(2)}, u32[]{:S(2)}) async-start(bf16[64,20,128]{2,1,0:T(8,128)(2,1)} %reshape.26), calls=%async_computation.1 | async-start | bytes 786432 | tf_op jit(solution)/shard_map/all_to_all | solution.py:264
  (31 other events, 373.7 us)

commit v3 on v2

v3 whole, which is shorter than its diff:
```python
import jax
import jax.numpy as jnp
from jax import lax
from jax.experimental import pallas as pl
from jax.experimental.pallas import tpu as pltpu
from jax.sharding import Mesh
from jax.sharding import PartitionSpec as P

F32 = jnp.float32
BF16 = jnp.bfloat16
LANES = 128
TILE = 8


def whole(shape):
    return pl.BlockSpec(
        shape, lambda *_: (0,) * len(shape), pipeline_mode=pl.Buffered(buffer_count=1)
    )


def local_call(kernel, name, scalars, operands, outs, scratch=(), flops=0, vmem=24):
    out_specs = jax.tree.map(lambda o: whole(o.shape), outs)
    return pl.pallas_call(
        kernel,
        grid=(1,),
        in_specs=[pl.BlockSpec(memory_space=pltpu.SMEM)] + [whole(o.shape) for o in operands],
        out_specs=out_specs,
        out_shape=outs,
        scratch_shapes=list(scratch),
        cost_estimate=pl.CostEstimate(flops=flops, bytes_accessed=1 << 20, transcendentals=0),
        compiler_params=pltpu.CompilerParams(vmem_limit_bytes=vmem << 20),
        name=name,
    )(scalars, *operands)


def transposed_dot(left, right):
    return lax.dot_general(left, right, (((0,), (0,)), ((), ())), preferred_element_type=F32)


def shift(axis, step):
    n = lax.axis_size(axis)
    return [(i, (i + step) % n) for i in range(n)]


def pack_kernel(capacity, col, ids_ref, probs_ref, x_ref, dy_ref, out_ref, table_ref, flat):
    choose, tok = ids_ref.shape
    rows = table_ref.shape[0]
    experts = rows // capacity
    chunks = x_ref.shape[1] // LANES
    stretch = flat.shape[0] // experts
    expert = lax.broadcasted_iota(jnp.int32, (experts, tok), 0)
    named = [expert == ids_ref[k : k + 1, :] for k in range(choose)]
    counts = sum(m.astype(F32) for m in named)
    earlier = lax.broadcasted_iota(jnp.int32, (tok, tok), 0) < lax.broadcasted_iota(
        jnp.int32, (tok, tok), 1
    )
    before = jnp.dot(
        counts.astype(BF16), earlier.astype(F32).astype(BF16), preferred_element_type=F32
    )
    row = lax.broadcasted_iota(jnp.int32, (rows, tok), 0)
    occupied = jnp.zeros((rows, tok), F32)
    weights = jnp.zeros((rows, tok), F32)
    for k in range(choose):
        slot = jnp.sum(jnp.where(named[k], before, 0.0), axis=0, keepdims=True)
        here = row == slot.astype(jnp.int32) * experts + ids_ref[k : k + 1, :]
        occupied = jnp.where(here, 1.0, occupied)
        weights = jnp.where(here, probs_ref[k : k + 1, :].astype(F32), weights)
    table = weights.astype(BF16)
    table_ref[...] = table
    placed = jnp.dot(occupied.astype(BF16), x_ref[...], preferred_element_type=F32)
    scaled = jnp.dot(table, dy_ref[...], preferred_element_type=F32)
    for s in range(capacity):
        of = slice(s * experts, (s + 1) * experts)
        for c in range(chunks):
            cols = slice(c * LANES, (c + 1) * LANES)
            at = s * 2 * chunks + c
            flat[pl.ds(at, experts, stride=stretch), :] = placed[of, cols]
            flat[pl.ds(at + chunks, experts, stride=stretch), :] = scaled[of, cols]
    out_ref[...] = flat[...].astype(BF16)


def pack(ids, probs, tokens, cotangent, column, width, experts, capacity):
    tok = tokens.shape[0]
    rows = experts * capacity
    height = rows * 2 * (width // LANES)
    wide = pl.BlockSpec((tok, width), lambda i, col: (0, col[0]))
    return pl.pallas_call(
        lambda *refs: pack_kernel(capacity, *refs),
        grid_spec=pltpu.PrefetchScalarGridSpec(
            num_scalar_prefetch=1,
            grid=(1,),
            in_specs=[whole(ids.shape), whole(probs.shape), wide, wide],
            out_specs=[whole((height, LANES)), whole((rows, tok))],
            scratch_shapes=[pltpu.VMEM((height, LANES), F32)],
        ),
        out_shape=[
            jax.ShapeDtypeStruct((height, LANES), BF16),
            jax.ShapeDtypeStruct((rows, tok), BF16),
        ],
        compiler_params=pltpu.CompilerParams(vmem_limit_bytes=60 << 20),
        name="pack",
    )(column, ids, probs, tokens, cotangent)


def unpack_kernel(capacity, _, flat_ref, out_ref, flat):
    rows, width = out_ref.shape
    owners, chunks = rows // capacity, width // LANES
    stretch = flat.shape[0] // owners
    flat[...] = flat_ref[...].astype(F32)
    for s in range(capacity):
        for c in range(chunks):
            out_ref[s * owners : (s + 1) * owners, c * LANES : (c + 1) * LANES] = flat[
                pl.ds(s * chunks + c, owners, stride=stretch), :
            ].astype(BF16)


def weights_at(parts, distance, position, width, weights):
    place, core = position[0], position[1]
    per_half = parts // 2
    source = lax.rem(place - distance + parts, parts)
    of = pl.ds(pl.multiple_of(lax.rem(source, per_half) * width, width), width)
    mine = source // per_half == core
    return jnp.concatenate(
        [
            jnp.where(mine, own[of, :], other[of, :])
            for own, other in zip(weights[::2], weights[1::2])
        ],
        axis=1,
    )


def forward_most(parts, distances, middle, position, *refs):
    blocks, weights = refs[: len(distances)], refs[len(distances) : -2]
    out, mid_ref = refs[-2:]
    rows, width = blocks[0].shape[0], blocks[0].shape[1] // 2
    hid = out.shape[1] // 3
    acc, back = jnp.zeros((rows, 2 * hid), F32), jnp.zeros((rows, hid), F32)
    for d, block in zip(distances, blocks):
        piece = weights_at(parts, d, position, width, weights)
        acc = acc + jnp.dot(block[:, :width], piece[:, : 2 * hid], preferred_element_type=F32)
        back = back + jnp.dot(block[:, width:], piece[:, 2 * hid :], preferred_element_type=F32)
    out[:, : 2 * hid] = acc
    out[:, 2 * hid :] = back
    mid_ref[...] = weights_at(parts, middle, position, width, weights)


def forward_last(position, x_ref, dy_ref, piece_ref, begun, ordered_ref, both_ref, hidden_ref):
    hid = hidden_ref.shape[1]
    acc = begun[:, : 2 * hid] + jnp.dot(
        x_ref[...], piece_ref[:, : 2 * hid], preferred_element_type=F32
    )
    back = begun[:, 2 * hid :] + jnp.dot(
        dy_ref[...], piece_ref[:, 2 * hid :], preferred_element_type=F32
    )
    gate, up = acc[:, :hid], acc[:, hid:]
    sig = 1.0 / (1.0 + jnp.exp(-gate))
    act = gate * sig
    hidden_ref[...] = (act * up).astype(BF16)
    d_up = back * act
    d_gate = back * up * sig * (1.0 + gate * (1.0 - sig))
    both_ref[:, :hid] = d_gate.astype(BF16)
    both_ref[:, hid:] = d_up.astype(BF16)
    first = position[1] == 0
    ordered_ref[:, :hid] = jnp.where(first, d_gate, d_up).astype(BF16)
    ordered_ref[:, hid:] = jnp.where(first, d_up, d_gate).astype(BF16)


def back_kernel(parts, capacity, _, *refs):
    blocks, turned = refs[:parts], refs[parts : 2 * parts]
    other_ref, out_ref, flat = refs[2 * parts :]
    rows, width = blocks[0].shape[0], turned[0].shape[0]
    owners, chunks = rows // capacity, width // LANES
    stretch = flat.shape[0] // owners
    total = jnp.zeros((rows, width), F32)
    for d in range(parts):
        weight = jnp.concatenate(
            (turned[d][...], other_ref[d * width : (d + 1) * width, :]), axis=1
        )
        total = total + lax.dot_general(
            blocks[d][...], weight, (((1,), (1,)), ((), ())), preferred_element_type=F32
        )
    for s in range(capacity):
        for c in range(chunks):
            flat[pl.ds(s * chunks + c, owners, stride=stretch), :] = total[
                s * owners : (s + 1) * owners, c * LANES : (c + 1) * LANES
            ]
    for pad in range(capacity * chunks, stretch):
        flat[pl.ds(pad, owners, stride=stretch), :] = jnp.zeros((owners, LANES), F32)
    out_ref[...] = flat[...].astype(BF16)


def combine_kernel(capacity, _, flat_ref, table_ref, out_ref, flat, rows_ref):
    rows, width = rows_ref.shape
    owners, chunks = rows // capacity, width // LANES
    stretch = flat.shape[0] // owners
    flat[...] = flat_ref[...].astype(F32)
    for s in range(capacity):
        for c in range(chunks):
            rows_ref[s * owners : (s + 1) * owners, c * LANES : (c + 1) * LANES] = flat[
                pl.ds(s * chunks + c, owners, stride=stretch), :
            ].astype(BF16)
    out_ref[...] = transposed_dot(table_ref[...], rows_ref[...]).astype(BF16)


def grads_kernel(parts, position, *refs):
    blocks, (x_mid, dy_mid, both_ref, hidden_ref, out_ref) = refs[: parts - 1], refs[parts - 1 :]
    place, wanted = position[0], position[1]
    width = x_mid.shape[1]
    hid = hidden_ref.shape[1]
    per_half = parts // 2
    for d in range(parts):
        source = lax.rem(place - d + parts, parts)

        @pl.when(source // per_half == wanted)
        def _():
            if d == parts // 2:
                x, dy = x_mid[...], dy_mid[...]
            else:
                block = blocks[d if d < parts // 2 else d - 1]
                x, dy = block[:, :width], block[:, width:]
            into = pl.ds(pl.multiple_of(lax.rem(source, per_half) * width, width), width)
            out_ref[into, : 2 * hid] = transposed_dot(x, both_ref[...]).astype(BF16)
            out_ref[into, 2 * hid :] = transposed_dot(dy, hidden_ref[...]).astype(BF16)


def grads(place, which, blocks, x_mid, dy_mid, both, hidden):
    parts = len(blocks) + 1
    half = parts // 2 * x_mid.shape[1]
    columns = both.shape[1] + hidden.shape[1]
    return local_call(
        lambda *refs: grads_kernel(parts, *refs),
        "grads",
        jnp.stack((place, which)).astype(jnp.int32),
        (*blocks, x_mid, dy_mid, both, hidden),
        jax.ShapeDtypeStruct((half, columns), BF16),
        flops=2 * both.shape[0] * half * columns,
    )


def add_kernel(_, mine, received, *outs):
    hid = outs[0].shape[2]
    for i, out in enumerate(outs):
        cols = slice(i * hid, (i + 1) * hid)
        out[0] = (mine[:, cols].astype(F32) + received[:, cols].astype(F32)).astype(BF16)


def shards(tokens, cotangent, expert_ids, probs, gate_weight, up_weight, down_weight):
    peers = ("x", "z")
    owners = lax.axis_size("x") * lax.axis_size("z")
    parts = lax.axis_size("y")
    middle = parts // 2
    core, place = lax.axis_index("dp"), lax.axis_index("y")
    tok, model = tokens.shape
    choose = expert_ids.shape[1]
    width = model // parts
    chunks = width // LANES
    hid = gate_weight.shape[2]
    capacity = min(tok, (5 * tok * choose + 4 * owners - 1) // (4 * owners))
    rows = owners * capacity
    first = core == 0
    swap = shift("dp", 1)
    place = place.astype(jnp.int32)
    position = jnp.stack((place, core.astype(jnp.int32)))

    def block_of(distance):
        return lax.rem(place - distance + 2 * parts, parts)

    flat, table = pack(
        expert_ids.T, probs.T, tokens, cotangent, place[None], width, owners, capacity
    )
    flat, gate_own, up_own, down_own = lax.optimization_barrier(
        (flat, gate_weight[0], up_weight[0], down_weight[0])
    )
    flat = lax.all_to_all(
        flat.reshape(owners, -1, LANES), peers, split_axis=0, concat_axis=0, tiled=True
    )

    gate_other = lax.ppermute(gate_own, "dp", swap)
    up_other = lax.ppermute(up_own, "dp", swap)
    down_other = lax.ppermute(down_own, "dp", swap)

    low = jnp.where(first, gate_own, up_other)
    high = jnp.where(first, gate_other, up_own)
    turn = jnp.concatenate((low, high)).reshape(parts, width, hid)
    turned = [None] * parts
    for d in sorted(range(parts), key=lambda d: -min(d, parts - d)):
        piece = lax.dynamic_index_in_dim(turn, block_of(-d), 0, keepdims=False)
        turned[d] = lax.ppermute(piece, "y", shift("y", d)) if d else piece
    turned_other = lax.ppermute(jnp.concatenate(turned), "dp", swap)

    flat, turned, turned_other, gate_other, up_other, down_other = lax.optimization_barrier(
        (flat, turned, turned_other, gate_other, up_other, down_other)
    )

    flat = flat.reshape(-1, LANES)
    own = local_call(
        lambda *refs: unpack_kernel(capacity, *refs),
        "unpack",
        position,
        (flat,),
        jax.ShapeDtypeStruct((rows, 2 * width), BF16),
        [pltpu.VMEM(flat.shape, F32)],
    )
    blocks = {0: own}
    right = left = own
    for d in range(1, middle):
        right = lax.ppermute(right, "y", shift("y", 1))
        left = lax.ppermute(left, "y", shift("y", -1))
        blocks[d], blocks[parts - d] = right, left
    x_mid = lax.ppermute(right[:, :width], "y", shift("y", 1))
    dy_mid = lax.ppermute(left[:, width:], "y", shift("y", -1))

    most = [d for d in range(parts) if d != middle]
    begun, piece = local_call(
        lambda *refs: forward_most(parts, most, middle, *refs),
        "forward_most",
        position,
        (
            *[blocks[d] for d in most],
            gate_own,
            gate_other,
            up_own,
            up_other,
            down_own,
            down_other,
        ),
        (
            jax.ShapeDtypeStruct((rows, 3 * hid), F32),
            jax.ShapeDtypeStruct((width, 3 * hid), BF16),
        ),
        flops=2 * rows * model * 3 * hid,
    )
    pair = jax.ShapeDtypeStruct((rows, 2 * hid), BF16)
    d_ordered, d_both, hidden = local_call(
        forward_last,
        "forward_last",
        position,
        (x_mid, dy_mid, piece, begun),
        (pair, pair, jax.ShapeDtypeStruct((rows, hid), BF16)),
        flops=2 * rows * width * 3 * hid,
    )

    d_ring = {0: d_ordered}
    right = left = d_ordered
    for d in range(1, middle + 1):
        right = lax.ppermute(right, "y", shift("y", 1))
        d_ring[d] = right
        if d < middle:
            left = lax.ppermute(left, "y", shift("y", -1))
            d_ring[parts - d] = left
    stretch = -(-capacity * chunks // TILE) * TILE
    d_rows = local_call(
        lambda *refs: back_kernel(parts, capacity, *refs),
        "back",
        position,
        (*[d_ring[d] for d in range(parts)], *turned, turned_other),
        jax.ShapeDtypeStruct((owners * stretch, LANES), BF16),
        [pltpu.VMEM((owners * stretch, LANES), F32)],
        flops=4 * rows * width * parts * hid,
    )
    operands = ([blocks[d] for d in most], x_mid, dy_mid, d_both, hidden)
    d_rows, operands = lax.optimization_barrier((d_rows, operands))
    returned = lax.all_to_all(
        d_rows.reshape(owners, -1, LANES), peers, split_axis=0, concat_axis=0, tiled=True
    )
    d_tokens = local_call(
        lambda *refs: combine_kernel(capacity, *refs),
        "combine",
        position,
        (returned.reshape(-1, LANES), table),
        jax.ShapeDtypeStruct((tok, width), BF16),
        [pltpu.VMEM((owners * stretch, LANES), F32), pltpu.VMEM((rows, width), BF16)],
        flops=1 << 37,
    )
    received = lax.ppermute(grads(place, 1 - core, *operands), "dp", swap)
    mine = grads(place, core, *operands)
    grad = jax.ShapeDtypeStruct(gate_weight.shape, BF16)
    return d_tokens, *local_call(
        add_kernel, "add", position, (mine, received), (grad, grad, grad)
    )


def solution(mesh):
    dp, experts, etp = mesh.devices.shape
    inner = min(16, experts)
    grid = Mesh(mesh.devices.reshape(dp, experts // inner, inner, etp), ("dp", "x", "z", "y"))
    row = P(("dp", "x", "z"), None)
    weight = P(("x", "z"), "dp", "y")
    return jax.shard_map(
        shards,
        mesh=grid,
        in_specs=(row, row, row, row, weight, weight, weight),
        out_specs=(P(("dp", "x", "z"), "y"), weight, weight, weight),
        check_vma=False,
    )
```

time: 253 us -> 236 us (0.933)
  matrix products: 19.7 us -> 0 us
  waiting for transfers between devices: 73.6 us -> 61.8 us
  local copies, waits for them, and re-layouts: 11.3 us -> 21.6 us
  Pallas kernels: 8.9 us -> 18.7 us
  other arithmetic: 5.18 us -> 0.34 us
    ppermute x7, waiting for transfers between devices: 18 us -> 47.6 us  [shards(): right = lax.ppermute(right, 'y', shift('y', 1))]
    ppermute x6, waiting for transfers between devices: 22.7 us -> 0.02 us  [shards(): left = lax.ppermute(left, 'y', shift('y', -1))]
    dot_general x33 -> x0, matrix products: 19.7 us -> none  [the longest x8 9.19 us: shards(): lax.dot_general(d_ring[d][:, hid:], other, contract, preferred_element_ty...]
    unnamed x75 -> x107, local copies, waits for them, and re-layouts: 5.74 us -> 21.5 us
    all_to_all x1, waiting for transfers between devices: 14.6 us -> 2.43 us  [shards(): lax.all_to_all(d_rows.reshape(owners, -1, LANES), peers, split_axis=0, co...]
    pallas_call x4 -> x9, Pallas kernels: 8.9 us -> 18.7 us  [the longest x8 16.3 us: local_call(): pl.pallas_call(kernel, grid=(1,), in_specs=[pl.BlockSpec(memory_space=plt...]
    ppermute x1, waiting for transfers between devices: 5.28 us -> 0.01 us  [shards(): x_mid = lax.ppermute(right[:, :width], 'y', shift('y', 1))]
    reshape x2 -> x0, local copies, waits for them, and re-layouts: 3.28 us -> none  [the longest x1 2.01 us: shards(): d_rows = d_rows.astype(BF16).reshape(owners, -1, LANES)]
  transfers between devices with their start and end apart: 29 -> 29, of which waited for: 12 -> 12; matrix products, arithmetic and copies ran while one was open for 11% -> 1% of each run, Pallas kernels for 3% -> 4%
where the time goes in v3:
time: 236 us; the launch traced here: 234 us
  starting transfers between devices  130 us (55%)
  waiting for transfers between devices  61.8 us (26%)
  local copies, waits for them, and re-layouts  21.6 us (9%)
  Pallas kernels  18.7 us (8%)
    ppermute x7, waiting for transfers between devices, shards(): right = lax.ppermute(right, 'y', shift('y', 1))  47.6 us
    ppermute x7, starting transfers between devices, shards(): turned[d] = lax.ppermute(piece, 'y', shift('y', d)) if d else piece  30.5 us
    ppermute x6, starting transfers between devices, shards(): left = lax.ppermute(left, 'y', shift('y', -1))  27.9 us
    all_to_all x1, starting transfers between devices, shards(): lax.all_to_all(flat.reshape(owners, -1, LANES), peers, split_axis=0, conc...  22.5 us
    unnamed x107, local copies, waits for them, and re-layouts  21.5 us
    pallas_call x8, Pallas kernels, local_call(): pl.pallas_call(kernel, grid=(1,), in_specs=[pl.BlockSpec(memory_space=plt...  16.3 us
    ppermute x7, starting transfers between devices, shards(): right = lax.ppermute(right, 'y', shift('y', 1))  16.3 us
    all_to_all x1, starting transfers between devices, shards(): lax.all_to_all(d_rows.reshape(owners, -1, LANES), peers, split_axis=0, co...  15.3 us
  transfers between devices with their start and end apart: 29, of which 12 were waited for; matrix products, arithmetic and copies ran while one was open for 1% of the time, Pallas kernels for 4%

profile of v3, /device:TPU:6, one launch (start us, length us, event | category | flops | bytes accessed | tf_op | source)
XLA Modules:
  0.0 234.1 jit_solution(18398013588410198276)
XLA Ops:
  0.6 2.4 %pack.1 = (bf16[2560,128]{1,0:T(8,128)(2,1)}, bf16[320,32]{1,0:T(8,128)(2,1)}) custom-call(s32[1]{0:T(128)} %bitcast.refs_0_, s32[8,32]{1,0:T(8,128)} %bitcast.43, bf16[8,32]{1,0:T(8,128)(2,1)} %bitcast.44, bf16[32,4096]{1,0:T(8,128)(2,1)} %refs_3_.1, bf16[32,4096]{1,0:T(8,128)(2,1)} %refs_4_.1), custom_call_target="tpu_custom_call" | custom-call | tf_op jit(solution)/shard_map/pack/pallas_call | solution.py:87
  3.1 2.0 collective-permute-start
  5.1 2.4 %collective-permute-start.1 = (bf16[2048,128]{1,0:T(8,128)(2,1)}, bf16[2048,128]{1,0:T(8,128)(2,1)S(1)}, u32[]{:S(2)}, u32[]{:S(2)}) collective-permute-start(bf16[2048,128]{1,0:T(8,128)(2,1)} %bitcast.31), channel_id=1, source_target_pairs={{0,512},{512,0},{1,513},{513,1},{2,514},{514,2},{3,515},{515,3},{4... | collective-permute-start | bytes 1572872 | tf_op jit(solution)/shard_map/ppermute | solution.py:278
  7.5 22.5 %all-to-all-start = ((bf16[64,40,128]{2,1,0:T(8,128)(2,1)}), bf16[64,40,128]{2,1,0:T(8,128)(2,1)S(1)}, u32[]{:S(2)}, u32[]{:S(2)}) async-start(bf16[64,40,128]{2,1,0:T(8,128)(2,1)} %bitcast.42), calls=%async_computation | async-start | bytes 1310720 | tf_op jit(solution)/shard_map/all_to_all | solution.py:274
  32.0 3.6 %collective-permute-start.2 = (bf16[512,128]{1,0:T(8,128)(2,1)S(1)}, bf16[512,128]{1,0:T(8,128)(2,1)S(1)}, u32[]{:S(2)}, u32[]{:S(2)}) collective-permute-start(bf16[512,128]{1,0:T(8,128)(2,1)S(1)} %get-tuple-element.90), channel_id=1, source_target_pairs={{0,1},{1,2},{2,3},{3,4},{4,5},{5,6},{6,7},{7,0},{8,9},{9,10},{10,1... | collective-permute-start | bytes 393224 | tf_op jit(solution)/shard_map/ppermute | solution.py:288
  35.6 4.5 %collective-permute-start.3 = (bf16[512,128]{1,0:T(8,128)(2,1)S(1)}, bf16[512,128]{1,0:T(8,128)(2,1)S(1)}, u32[]{:S(2)}, u32[]{:S(2)}) collective-permute-start(bf16[512,128]{1,0:T(8,128)(2,1)S(1)} %get-tuple-element.89), channel_id=1, source_target_pairs={{0,2},{1,3},{2,4},{3,5},{4,6},{5,7},{6,0},{7,1},{8,10},{9,11},{10,... | collective-permute-start | bytes 393224 | tf_op jit(solution)/shard_map/ppermute | solution.py:288
  41.8 4.9 %collective-permute-start.4 = (bf16[512,128]{1,0:T(8,128)(2,1)S(1)}, bf16[512,128]{1,0:T(8,128)(2,1)S(1)}, u32[]{:S(2)}, u32[]{:S(2)}) collective-permute-start(bf16[512,128]{1,0:T(8,128)(2,1)S(1)} %get-tuple-element.88), channel_id=1, source_target_pairs={{0,3},{1,4},{2,5},{3,6},{4,7},{5,0},{6,1},{7,2},{8,11},{9,12},{10,... | collective-permute-start | bytes 393224 | tf_op jit(solution)/shard_map/ppermute | solution.py:288
  46.7 3.8 %collective-permute-start.5 = (bf16[512,128]{1,0:T(8,128)(2,1)S(1)}, bf16[512,128]{1,0:T(8,128)(2,1)S(1)}, u32[]{:S(2)}, u32[]{:S(2)}) collective-permute-start(bf16[512,128]{1,0:T(8,128)(2,1)S(1)} %get-tuple-element.87), channel_id=1, source_target_pairs={{0,4},{1,5},{2,6},{3,7},{4,0},{5,1},{6,2},{7,3},{8,12},{9,13},{10,... | collective-permute-start | bytes 393224 | tf_op jit(solution)/shard_map/ppermute | solution.py:288
  50.5 5.2 %collective-permute-start.6 = (bf16[512,128]{1,0:T(8,128)(2,1)S(1)}, bf16[512,128]{1,0:T(8,128)(2,1)S(1)}, u32[]{:S(2)}, u32[]{:S(2)}) collective-permute-start(bf16[512,128]{1,0:T(8,128)(2,1)S(1)} %get-tuple-element.86), channel_id=1, source_target_pairs={{0,5},{1,6},{2,7},{3,0},{4,1},{5,2},{6,3},{7,4},{8,13},{9,14},{10,... | collective-permute-start | bytes 393224 | tf_op jit(solution)/shard_map/ppermute | solution.py:288
  55.7 5.3 %collective-permute-start.7 = (bf16[512,128]{1,0:T(8,128)(2,1)S(1)}, bf16[512,128]{1,0:T(8,128)(2,1)S(1)}, u32[]{:S(2)}, u32[]{:S(2)}) collective-permute-start(bf16[512,128]{1,0:T(8,128)(2,1)S(1)} %get-tuple-element.85), channel_id=1, source_target_pairs={{0,6},{1,7},{2,0},{3,1},{4,2},{5,3},{6,4},{7,5},{8,14},{9,15},{10,... | collective-permute-start | bytes 393224 | tf_op jit(solution)/shard_map/ppermute | solution.py:288
  61.0 3.3 %collective-permute-start.8 = (bf16[512,128]{1,0:T(8,128)(2,1)S(1)}, bf16[512,128]{1,0:T(8,128)(2,1)S(1)}, u32[]{:S(2)}, u32[]{:S(2)}) collective-permute-start(bf16[512,128]{1,0:T(8,128)(2,1)S(1)} %get-tuple-element.84), channel_id=1, source_target_pairs={{0,7},{1,0},{2,1},{3,2},{4,3},{5,4},{6,5},{7,6},{8,15},{9,8},{10,9... | collective-permute-start | bytes 393224 | tf_op jit(solution)/shard_map/ppermute | solution.py:288
  64.4 5.7 %collective-permute-done.6.refs_14_ = bf16[512,128]{1,0:T(8,128)(2,1)S(1)} collective-permute-done((bf16[512,128]{1,0:T(8,128)(2,1)S(1)}, bf16[512,128]{1,0:T(8,128)(2,1)S(1)}, u32[]{:S(2)}, u32[]{:S(2)}) %collective-permute-start.6) | collective-permute-done | bytes 131104 | tf_op jit(solution)/shard_map/ppermute | solution.py:288
  70.1 2.7 %collective-permute-done.7.refs_15_ = bf16[512,128]{1,0:T(8,128)(2,1)S(1)} collective-permute-done((bf16[512,128]{1,0:T(8,128)(2,1)S(1)}, bf16[512,128]{1,0:T(8,128)(2,1)S(1)}, u32[]{:S(2)}, u32[]{:S(2)}) %collective-permute-start.7) | collective-permute-done | bytes 131104 | tf_op jit(solution)/shard_map/ppermute | solution.py:288
  77.2 2.4 %collective-permute-start.10 = (bf16[2048,128]{1,0:T(8,128)(2,1)S(1)}, bf16[2048,128]{1,0:T(8,128)(2,1)S(1)}, u32[]{:S(2)}, u32[]{:S(2)}) collective-permute-start(bf16[2048,128]{1,0:T(8,128)(2,1)S(1)} %bitcast.38), channel_id=1, source_target_pairs={{0,512},{512,0},{1,513},{513,1},{2,514},{514,2},{3,515},{515,3},{4... | collective-permute-start | bytes 1572872 | tf_op jit(solution)/shard_map/ppermute | solution.py:280
  83.9 4.0 %collective-permute-start.11 = (bf16[320,1024]{1,0:T(8,128)(2,1)S(1)}, bf16[320,1024]{1,0:T(8,128)(2,1)S(1)}, u32[]{:S(2)}, u32[]{:S(2)}) collective-permute-start(bf16[320,1024]{1,0:T(8,128)(2,1)S(1)} %unpack.1.refs_1_), channel_id=1, source_target_pairs={{0,1},{1,2},{2,3},{3,4},{4,5},{5,6},{6,7},{7,0},{8,9},{9,10},{10,1... | collective-permute-start | bytes 1966088 | tf_op jit(solution)/shard_map/ppermute | solution.py:307
  87.8 3.1 %collective-permute-start.15 = (bf16[320,1024]{1,0:T(8,128)(2,1)S(1)}, bf16[320,1024]{1,0:T(8,128)(2,1)S(1)}, u32[]{:S(2)}, u32[]{:S(2)}) collective-permute-start(bf16[320,1024]{1,0:T(8,128)(2,1)S(1)} %unpack.1.refs_1_), channel_id=1, source_target_pairs={{0,7},{1,0},{2,1},{3,2},{4,3},{5,4},{6,5},{7,6},{8,15},{9,8},{10,9... | collective-permute-start | bytes 1966088 | tf_op jit(solution)/shard_map/ppermute | solution.py:308
  90.9 13.0 %collective-permute-done.11.refs_2_ = bf16[320,1024]{1,0:T(8,128)(2,1)S(1)} collective-permute-done((bf16[320,1024]{1,0:T(8,128)(2,1)S(1)}, bf16[320,1024]{1,0:T(8,128)(2,1)S(1)}, u32[]{:S(2)}, u32[]{:S(2)}) %collective-permute-start.11) | collective-permute-done | bytes 655392 | tf_op jit(solution)/shard_map/ppermute | solution.py:307
  104.0 2.7 %collective-permute-start.12 = (bf16[320,1024]{1,0:T(8,128)(2,1)S(1)}, bf16[320,1024]{1,0:T(8,128)(2,1)S(1)}, u32[]{:S(2)}, u32[]{:S(2)}) collective-permute-start(bf16[320,1024]{1,0:T(8,128)(2,1)S(1)} %collective-permute-done.11.refs_2_), channel_id=1, source_target_pairs={{0,1},{1,2},{2,3},{3,4},{4,5},{5,6},{6,7},{7,0},{8,9},{9,10},{10,1... | collective-permute-start | bytes 1966088 | tf_op jit(solution)/shard_map/ppermute | solution.py:307
  106.7 4.3 %collective-permute-start.16 = (bf16[320,1024]{1,0:T(8,128)(2,1)S(1)}, bf16[320,1024]{1,0:T(8,128)(2,1)S(1)}, u32[]{:S(2)}, u32[]{:S(2)}) collective-permute-start(bf16[320,1024]{1,0:T(8,128)(2,1)S(1)} %collective-permute-done.15.refs_7_), channel_id=1, source_target_pairs={{0,7},{1,0},{2,1},{3,2},{4,3},{5,4},{6,5},{7,6},{8,15},{9,8},{10,9... | collective-permute-start | bytes 1966088 | tf_op jit(solution)/shard_map/ppermute | solution.py:308
  111.0 12.2 %collective-permute-done.12.refs_3_ = bf16[320,1024]{1,0:T(8,128)(2,1)S(1)} collective-permute-done((bf16[320,1024]{1,0:T(8,128)(2,1)S(1)}, bf16[320,1024]{1,0:T(8,128)(2,1)S(1)}, u32[]{:S(2)}, u32[]{:S(2)}) %collective-permute-start.12) | collective-permute-done | bytes 655392 | tf_op jit(solution)/shard_map/ppermute | solution.py:307
  125.2 5.1 %collective-permute-start.17 = (bf16[320,1024]{1,0:T(8,128)(2,1)S(1)}, bf16[320,1024]{1,0:T(8,128)(2,1)S(1)}, u32[]{:S(2)}, u32[]{:S(2)}) collective-permute-start(bf16[320,1024]{1,0:T(8,128)(2,1)S(1)} %collective-permute-done.16.refs_6_), channel_id=1, source_target_pairs={{0,7},{1,0},{2,1},{3,2},{4,3},{5,4},{6,5},{7,6},{8,15},{9,8},{10,9... | collective-permute-start | bytes 1966088 | tf_op jit(solution)/shard_map/ppermute | solution.py:308
  130.3 11.3 %collective-permute-done.13.refs_4_ = bf16[320,1024]{1,0:T(8,128)(2,1)S(1)} collective-permute-done((bf16[320,1024]{1,0:T(8,128)(2,1)S(1)}, bf16[320,1024]{1,0:T(8,128)(2,1)S(1)}, u32[]{:S(2)}, u32[]{:S(2)}) %collective-permute-start.13) | collective-permute-done | bytes 655392 | tf_op jit(solution)/shard_map/ppermute | solution.py:307
  143.6 5.1 %collective-permute-start.18 = (bf16[320,512]{1,0:T(8,128)(2,1)S(1)}, bf16[320,512]{1,0:T(8,128)(2,1)S(1)}, u32[]{:S(2)}, u32[]{:S(2)}) collective-permute-start(bf16[320,512]{1,0:T(8,128)(2,1)S(1)} %slice.9), channel_id=1, source_target_pairs={{0,7},{1,0},{2,1},{3,2},{4,3},{5,4},{6,5},{7,6},{8,15},{9,8},{10,9... | collective-permute-start | bytes 983048 | tf_op jit(solution)/shard_map/ppermute | solution.py:311
  159.8 5.1 %collective-permute-start.23 = (bf16[320,256]{1,0:T(8,128)(2,1)S(1)}, bf16[320,256]{1,0:T(8,128)(2,1)S(1)}, u32[]{:S(2)}, u32[]{:S(2)}) collective-permute-start(bf16[320,256]{1,0:T(8,128)(2,1)S(1)} %get-tuple-element.54.refs_1_), channel_id=1, source_target_pairs={{0,7},{1,0},{2,1},{3,2},{4,3},{5,4},{6,5},{7,6},{8,15},{9,8},{10,9... | collective-permute-start | bytes 491528 | tf_op jit(solution)/shard_map/ppermute | solution.py:349
  168.2 5.1 %collective-permute-start.24 = (bf16[320,256]{1,0:T(8,128)(2,1)S(1)}, bf16[320,256]{1,0:T(8,128)(2,1)S(1)}, u32[]{:S(2)}, u32[]{:S(2)}) collective-permute-start(bf16[320,256]{1,0:T(8,128)(2,1)S(1)} %collective-permute-done.23.refs_8_), channel_id=1, source_target_pairs={{0,7},{1,0},{2,1},{3,2},{4,3},{5,4},{6,5},{7,6},{8,15},{9,8},{10,9... | collective-permute-start | bytes 491528 | tf_op jit(solution)/shard_map/ppermute | solution.py:349
  176.6 5.1 %collective-permute-start.25 = (bf16[320,256]{1,0:T(8,128)(2,1)S(1)}, bf16[320,256]{1,0:T(8,128)(2,1)S(1)}, u32[]{:S(2)}, u32[]{:S(2)}) collective-permute-start(bf16[320,256]{1,0:T(8,128)(2,1)S(1)} %collective-permute-done.24.refs_7_), channel_id=1, source_target_pairs={{0,7},{1,0},{2,1},{3,2},{4,3},{5,4},{6,5},{7,6},{8,15},{9,8},{10,9... | collective-permute-start | bytes 491528 | tf_op jit(solution)/shard_map/ppermute | solution.py:349
  185.6 6.5 %collective-permute-done.22.refs_5_ = bf16[320,256]{1,0:T(8,128)(2,1)S(1)} collective-permute-done((bf16[320,256]{1,0:T(8,128)(2,1)S(1)}, bf16[320,256]{1,0:T(8,128)(2,1)S(1)}, u32[]{:S(2)}, u32[]{:S(2)}) %collective-permute-start.22) | collective-permute-done | bytes 163872 | tf_op jit(solution)/shard_map/ppermute | solution.py:346
  194.4 15.3 %all-to-all-start.1 = ((bf16[64,24,128]{2,1,0:T(8,128)(2,1)}), bf16[64,24,128]{2,1,0:T(8,128)(2,1)}, u32[]{:S(2)}, u32[]{:S(2)}) async-start(bf16[64,24,128]{2,1,0:T(8,128)(2,1)} %bitcast.37), calls=%async_computation.1 | async-start | bytes 786432 | tf_op jit(solution)/shard_map/all_to_all | solution.py:363
  213.9 3.8 %grads.3 = bf16[2048,384]{1,0:T(8,128)(2,1)} custom-call(s32[2]{0:T(128)S(1)} %pad_add_fusion.1.refs_0_, bf16[320,1024]{1,0:T(8,128)(2,1)S(1)} %unpack.1.refs_1_, bf16[320,1024]{1,0:T(8,128)(2,1)S(1)} %collective-permute-done.11.refs_2_, bf16[320,1024]{1,0:T(8,128)(2,1)S(1)} %copy-done.5, bf16[320,1024]{1,0:T(8,128)(2,1)S(1)} %collective-permute-done.13.refs_4_, ...), custom_call_target="tpu_custom_call" | custom-call | flops 503316480 | bytes 1048576 | tf_op jit(solution)/shard_map/grads/pallas_call | solution.py:23
  223.6 2.5 %grads.2.mine = bf16[2048,384]{1,0:T(8,128)(2,1)S(1)} custom-call(s32[2]{0:T(128)S(1)} %pad_add_fusion.refs_0_.position._, bf16[320,1024]{1,0:T(8,128)(2,1)S(1)} %unpack.1.refs_1_, bf16[320,1024]{1,0:T(8,128)(2,1)S(1)} %copy-done.1, bf16[320,1024]{1,0:T(8,128)(2,1)S(1)} %copy-done.6, bf16[320,1024]{1,0:T(8,128)(2,1)S(1)} %collective-permute-done.13.refs_4_, ...), custom_call_target="tpu_custom_call" | custom-call | flops 503316480 | bytes 1048576 | tf_op jit(solution)/shard_map/grads/pallas_call | solution.py:23
  226.2 2.4 %all-to-all-done.1 = bf16[64,24,128]{2,1,0:T(8,128)(2,1)} async-done(((bf16[64,24,128]{2,1,0:T(8,128)(2,1)}), bf16[64,24,128]{2,1,0:T(8,128)(2,1)}, u32[]{:S(2)}, u32[]{:S(2)}) %all-to-all-start.1) | async-done | bytes 393248 | tf_op jit(solution)/shard_map/all_to_all | solution.py:363
  231.4 2.7 %add.91 = (bf16[1,2048,128]{2,1,0:T(8,128)(2,1)}, bf16[1,2048,128]{2,1,0:T(8,128)(2,1)}, bf16[1,2048,128]{2,1,0:T(8,128)(2,1)}) custom-call(s32[2]{0:T(128)S(1)} %pad_add_fusion.refs_0_.position._, bf16[2048,384]{1,0:T(8,128)(2,1)S(1)} %grads.2.mine, bf16[2048,384]{1,0:T(8,128)(2,1)} %collective-permute-done.26.received), custom_call_target="tpu_custom_call" | custom-call | bytes 1048576 | tf_op jit(solution)/shard_map/add/pallas_call | solution.py:23
  (151 shorter events, 52.5 us)
Async XLA Ops:
  3.1 27.0 %collective-permute-start = (bf16[2048,128]{1,0:T(8,128)(2,1)}, bf16[2048,128]{1,0:T(8,128)(2,1)S(1)}, u32[]{:S(2)}, u32[]{:S(2)}) collective-permute-start(bf16[2048,128]{1,0:T(8,128)(2,1)} %bitcast.34), channel_id=1, source_target_pairs={{0,512},{512,0},{1,513},{513,1},{2,514},{514,2},{3,515},{515,3},{4... | collective-permute-start | bytes 1572872 | tf_op jit(solution)/shard_map/ppermute | solution.py:279
  5.1 25.1 %collective-permute-start.1 = (bf16[2048,128]{1,0:T(8,128)(2,1)}, bf16[2048,128]{1,0:T(8,128)(2,1)S(1)}, u32[]{:S(2)}, u32[]{:S(2)}) collective-permute-start(bf16[2048,128]{1,0:T(8,128)(2,1)} %bitcast.31), channel_id=1, source_target_pairs={{0,512},{512,0},{1,513},{513,1},{2,514},{514,2},{3,515},{515,3},{4... | collective-permute-start | bytes 1572872 | tf_op jit(solution)/shard_map/ppermute | solution.py:278
  7.5 75.4 %all-to-all-start = ((bf16[64,40,128]{2,1,0:T(8,128)(2,1)}), bf16[64,40,128]{2,1,0:T(8,128)(2,1)S(1)}, u32[]{:S(2)}, u32[]{:S(2)}) async-start(bf16[64,40,128]{2,1,0:T(8,128)(2,1)} %bitcast.42), calls=%async_computation | async-start | bytes 1310720 | tf_op jit(solution)/shard_map/all_to_all | solution.py:274
  32.0 23.6 %collective-permute-start.2 = (bf16[512,128]{1,0:T(8,128)(2,1)S(1)}, bf16[512,128]{1,0:T(8,128)(2,1)S(1)}, u32[]{:S(2)}, u32[]{:S(2)}) collective-permute-start(bf16[512,128]{1,0:T(8,128)(2,1)S(1)} %get-tuple-element.90), channel_id=1, source_target_pairs={{0,1},{1,2},{2,3},{3,4},{4,5},{5,6},{6,7},{7,0},{8,9},{9,10},{10,1... | collective-permute-start | bytes 393224 | tf_op jit(solution)/shard_map/ppermute | solution.py:288
  35.6 25.3 %collective-permute-start.3 = (bf16[512,128]{1,0:T(8,128)(2,1)S(1)}, bf16[512,128]{1,0:T(8,128)(2,1)S(1)}, u32[]{:S(2)}, u32[]{:S(2)}) collective-permute-start(bf16[512,128]{1,0:T(8,128)(2,1)S(1)} %get-tuple-element.89), channel_id=1, source_target_pairs={{0,2},{1,3},{2,4},{3,5},{4,6},{5,7},{6,0},{7,1},{8,10},{9,11},{10,... | collective-permute-start | bytes 393224 | tf_op jit(solution)/shard_map/ppermute | solution.py:288
  41.8 22.5 %collective-permute-start.4 = (bf16[512,128]{1,0:T(8,128)(2,1)S(1)}, bf16[512,128]{1,0:T(8,128)(2,1)S(1)}, u32[]{:S(2)}, u32[]{:S(2)}) collective-permute-start(bf16[512,128]{1,0:T(8,128)(2,1)S(1)} %get-tuple-element.88), channel_id=1, source_target_pairs={{0,3},{1,4},{2,5},{3,6},{4,7},{5,0},{6,1},{7,2},{8,11},{9,12},{10,... | collective-permute-start | bytes 393224 | tf_op jit(solution)/shard_map/ppermute | solution.py:288
  46.7 17.7 %collective-permute-start.5 = (bf16[512,128]{1,0:T(8,128)(2,1)S(1)}, bf16[512,128]{1,0:T(8,128)(2,1)S(1)}, u32[]{:S(2)}, u32[]{:S(2)}) collective-permute-start(bf16[512,128]{1,0:T(8,128)(2,1)S(1)} %get-tuple-element.87), channel_id=1, source_target_pairs={{0,4},{1,5},{2,6},{3,7},{4,0},{5,1},{6,2},{7,3},{8,12},{9,13},{10,... | collective-permute-start | bytes 393224 | tf_op jit(solution)/shard_map/ppermute | solution.py:288
  50.5 19.6 %collective-permute-start.6 = (bf16[512,128]{1,0:T(8,128)(2,1)S(1)}, bf16[512,128]{1,0:T(8,128)(2,1)S(1)}, u32[]{:S(2)}, u32[]{:S(2)}) collective-permute-start(bf16[512,128]{1,0:T(8,128)(2,1)S(1)} %get-tuple-element.86), channel_id=1, source_target_pairs={{0,5},{1,6},{2,7},{3,0},{4,1},{5,2},{6,3},{7,4},{8,13},{9,14},{10,... | collective-permute-start | bytes 393224 | tf_op jit(solution)/shard_map/ppermute | solution.py:288
  55.7 17.1 %collective-permute-start.7 = (bf16[512,128]{1,0:T(8,128)(2,1)S(1)}, bf16[512,128]{1,0:T(8,128)(2,1)S(1)}, u32[]{:S(2)}, u32[]{:S(2)}) collective-permute-start(bf16[512,128]{1,0:T(8,128)(2,1)S(1)} %get-tuple-element.85), channel_id=1, source_target_pairs={{0,6},{1,7},{2,0},{3,1},{4,2},{5,3},{6,4},{7,5},{8,14},{9,15},{10,... | collective-permute-start | bytes 393224 | tf_op jit(solution)/shard_map/ppermute | solution.py:288
  61.0 13.7 %collective-permute-start.8 = (bf16[512,128]{1,0:T(8,128)(2,1)S(1)}, bf16[512,128]{1,0:T(8,128)(2,1)S(1)}, u32[]{:S(2)}, u32[]{:S(2)}) collective-permute-start(bf16[512,128]{1,0:T(8,128)(2,1)S(1)} %get-tuple-element.84), channel_id=1, source_target_pairs={{0,7},{1,0},{2,1},{3,2},{4,3},{5,4},{6,5},{7,6},{8,15},{9,8},{10,9... | collective-permute-start | bytes 393224 | tf_op jit(solution)/shard_map/ppermute | solution.py:288
  75.3 6.7 %collective-permute-start.9 = (bf16[4096,128]{1,0:T(8,128)(2,1)S(1)}, bf16[4096,128]{1,0:T(8,128)(2,1)S(1)}, u32[]{:S(2)}, u32[]{:S(2)}) collective-permute-start(bf16[4096,128]{1,0:T(8,128)(2,1)S(1)} %constant_dynamic-update-slice_fusion), channel_id=1, source_target_pairs={{0,512},{512,0},{1,513},{513,1},{2,514},{514,2},{3,515},{515,3},{4... | collective-permute-start | bytes 3145736 | tf_op jit(solution)/shard_map/ppermute | solution.py:289
  77.2 3.9 %collective-permute-start.10 = (bf16[2048,128]{1,0:T(8,128)(2,1)S(1)}, bf16[2048,128]{1,0:T(8,128)(2,1)S(1)}, u32[]{:S(2)}, u32[]{:S(2)}) collective-permute-start(bf16[2048,128]{1,0:T(8,128)(2,1)S(1)} %bitcast.38), channel_id=1, source_target_pairs={{0,512},{512,0},{1,513},{513,1},{2,514},{514,2},{3,515},{515,3},{4... | collective-permute-start | bytes 1572872 | tf_op jit(solution)/shard_map/ppermute | solution.py:280
  82.9 65.8 %copy-start.45 = (bf16[2048,128]{1,0:T(8,128)(2,1)S(1)}, bf16[2048,128]{1,0:T(8,128)(2,1)}, u32[]{:S(2)}) copy-start(bf16[2048,128]{1,0:T(8,128)(2,1)} %copy-done.44) | copy-start | bytes 1572868
  83.9 20.1 %collective-permute-start.11 = (bf16[320,1024]{1,0:T(8,128)(2,1)S(1)}, bf16[320,1024]{1,0:T(8,128)(2,1)S(1)}, u32[]{:S(2)}, u32[]{:S(2)}) collective-permute-start(bf16[320,1024]{1,0:T(8,128)(2,1)S(1)} %unpack.1.refs_1_), channel_id=1, source_target_pairs={{0,1},{1,2},{2,3},{3,4},{4,5},{5,6},{6,7},{7,0},{8,9},{9,10},{10,1... | collective-permute-start | bytes 1966088 | tf_op jit(solution)/shard_map/ppermute | solution.py:307
  87.8 18.9 %collective-permute-start.15 = (bf16[320,1024]{1,0:T(8,128)(2,1)S(1)}, bf16[320,1024]{1,0:T(8,128)(2,1)S(1)}, u32[]{:S(2)}, u32[]{:S(2)}) collective-permute-start(bf16[320,1024]{1,0:T(8,128)(2,1)S(1)} %unpack.1.refs_1_), channel_id=1, source_target_pairs={{0,7},{1,0},{2,1},{3,2},{4,3},{5,4},{6,5},{7,6},{8,15},{9,8},{10,9... | collective-permute-start | bytes 1966088 | tf_op jit(solution)/shard_map/ppermute | solution.py:308
  104.0 105.8 %copy-start = (bf16[320,1024]{1,0:T(8,128)(2,1)}, bf16[320,1024]{1,0:T(8,128)(2,1)S(1)}, u32[]{:S(2)}) copy-start(bf16[320,1024]{1,0:T(8,128)(2,1)S(1)} %collective-permute-done.11.refs_2_) | copy-start | bytes 1966084
  104.0 19.3 %collective-permute-start.12 = (bf16[320,1024]{1,0:T(8,128)(2,1)S(1)}, bf16[320,1024]{1,0:T(8,128)(2,1)S(1)}, u32[]{:S(2)}, u32[]{:S(2)}) collective-permute-start(bf16[320,1024]{1,0:T(8,128)(2,1)S(1)} %collective-permute-done.11.refs_2_), channel_id=1, source_target_pairs={{0,1},{1,2},{2,3},{3,4},{4,5},{5,6},{6,7},{7,0},{8,9},{9,10},{10,1... | collective-permute-start | bytes 1966088 | tf_op jit(solution)/shard_map/ppermute | solution.py:307
  106.7 103.0 %copy-start.2 = (bf16[320,1024]{1,0:T(8,128)(2,1)}, bf16[320,1024]{1,0:T(8,128)(2,1)S(1)}, u32[]{:S(2)}) copy-start(bf16[320,1024]{1,0:T(8,128)(2,1)S(1)} %collective-permute-done.15.refs_7_) | copy-start | bytes 1966084
  106.7 18.4 %collective-permute-start.16 = (bf16[320,1024]{1,0:T(8,128)(2,1)S(1)}, bf16[320,1024]{1,0:T(8,128)(2,1)S(1)}, u32[]{:S(2)}, u32[]{:S(2)}) collective-permute-start(bf16[320,1024]{1,0:T(8,128)(2,1)S(1)} %collective-permute-done.15.refs_7_), channel_id=1, source_target_pairs={{0,7},{1,0},{2,1},{3,2},{4,3},{5,4},{6,5},{7,6},{8,15},{9,8},{10,9... | collective-permute-start | bytes 1966088 | tf_op jit(solution)/shard_map/ppermute | solution.py:308
  123.3 18.4 %collective-permute-start.13 = (bf16[320,1024]{1,0:T(8,128)(2,1)S(1)}, bf16[320,1024]{1,0:T(8,128)(2,1)S(1)}, u32[]{:S(2)}, u32[]{:S(2)}) collective-permute-start(bf16[320,1024]{1,0:T(8,128)(2,1)S(1)} %collective-permute-done.12.refs_3_), channel_id=1, source_target_pairs={{0,1},{1,2},{2,3},{3,4},{4,5},{5,6},{6,7},{7,0},{8,9},{9,10},{10,1... | collective-permute-start | bytes 1966088 | tf_op jit(solution)/shard_map/ppermute | solution.py:307
  125.2 18.4 %collective-permute-start.17 = (bf16[320,1024]{1,0:T(8,128)(2,1)S(1)}, bf16[320,1024]{1,0:T(8,128)(2,1)S(1)}, u32[]{:S(2)}, u32[]{:S(2)}) collective-permute-start(bf16[320,1024]{1,0:T(8,128)(2,1)S(1)} %collective-permute-done.16.refs_6_), channel_id=1, source_target_pairs={{0,7},{1,0},{2,1},{3,2},{4,3},{5,4},{6,5},{7,6},{8,15},{9,8},{10,9... | collective-permute-start | bytes 1966088 | tf_op jit(solution)/shard_map/ppermute | solution.py:308
  141.7 14.5 %collective-permute-start.14 = (bf16[320,512]{1,0:T(8,128)(2,1)S(1)}, bf16[320,512]{1,0:T(8,128)(2,1)S(1)}, u32[]{:S(2)}, u32[]{:S(2)}) collective-permute-start(bf16[320,512]{1,0:T(8,128)(2,1)S(1)} %slice.8), channel_id=1, source_target_pairs={{0,1},{1,2},{2,3},{3,4},{4,5},{5,6},{6,7},{7,0},{8,9},{9,10},{10,1... | collective-permute-start | bytes 983048 | tf_op jit(solution)/shard_map/ppermute | solution.py:310
  143.6 12.5 %collective-permute-start.18 = (bf16[320,512]{1,0:T(8,128)(2,1)S(1)}, bf16[320,512]{1,0:T(8,128)(2,1)S(1)}, u32[]{:S(2)}, u32[]{:S(2)}) collective-permute-start(bf16[320,512]{1,0:T(8,128)(2,1)S(1)} %slice.9), channel_id=1, source_target_pairs={{0,7},{1,0},{2,1},{3,2},{4,3},{5,4},{6,5},{7,6},{8,15},{9,8},{10,9... | collective-permute-start | bytes 983048 | tf_op jit(solution)/shard_map/ppermute | solution.py:311
  157.9 8.4 %collective-permute-start.19 = (bf16[320,256]{1,0:T(8,128)(2,1)S(1)}, bf16[320,256]{1,0:T(8,128)(2,1)S(1)}, u32[]{:S(2)}, u32[]{:S(2)}) collective-permute-start(bf16[320,256]{1,0:T(8,128)(2,1)S(1)} %get-tuple-element.54.refs_1_), channel_id=1, source_target_pairs={{0,1},{1,2},{2,3},{3,4},{4,5},{5,6},{6,7},{7,0},{8,9},{9,10},{10,1... | collective-permute-start | bytes 491528 | tf_op jit(solution)/shard_map/ppermute | solution.py:346
  159.8 8.4 %collective-permute-start.23 = (bf16[320,256]{1,0:T(8,128)(2,1)S(1)}, bf16[320,256]{1,0:T(8,128)(2,1)S(1)}, u32[]{:S(2)}, u32[]{:S(2)}) collective-permute-start(bf16[320,256]{1,0:T(8,128)(2,1)S(1)} %get-tuple-element.54.refs_1_), channel_id=1, source_target_pairs={{0,7},{1,0},{2,1},{3,2},{4,3},{5,4},{6,5},{7,6},{8,15},{9,8},{10,9... | collective-permute-start | bytes 491528 | tf_op jit(solution)/shard_map/ppermute | solution.py:349
  166.3 8.4 %collective-permute-start.20 = (bf16[320,256]{1,0:T(8,128)(2,1)S(1)}, bf16[320,256]{1,0:T(8,128)(2,1)S(1)}, u32[]{:S(2)}, u32[]{:S(2)}) collective-permute-start(bf16[320,256]{1,0:T(8,128)(2,1)S(1)} %collective-permute-done.19.refs_2_), channel_id=1, source_target_pairs={{0,1},{1,2},{2,3},{3,4},{4,5},{5,6},{6,7},{7,0},{8,9},{9,10},{10,1... | collective-permute-start | bytes 491528 | tf_op jit(solution)/shard_map/ppermute | solution.py:346
  168.2 8.4 %collective-permute-start.24 = (bf16[320,256]{1,0:T(8,128)(2,1)S(1)}, bf16[320,256]{1,0:T(8,128)(2,1)S(1)}, u32[]{:S(2)}, u32[]{:S(2)}) collective-permute-start(bf16[320,256]{1,0:T(8,128)(2,1)S(1)} %collective-permute-done.23.refs_8_), channel_id=1, source_target_pairs={{0,7},{1,0},{2,1},{3,2},{4,3},{5,4},{6,5},{7,6},{8,15},{9,8},{10,9... | collective-permute-start | bytes 491528 | tf_op jit(solution)/shard_map/ppermute | solution.py:349
  174.7 9.0 %collective-permute-start.21 = (bf16[320,256]{1,0:T(8,128)(2,1)S(1)}, bf16[320,256]{1,0:T(8,128)(2,1)S(1)}, u32[]{:S(2)}, u32[]{:S(2)}) collective-permute-start(bf16[320,256]{1,0:T(8,128)(2,1)S(1)} %collective-permute-done.20.refs_3_), channel_id=1, source_target_pairs={{0,1},{1,2},{2,3},{3,4},{4,5},{5,6},{6,7},{7,0},{8,9},{9,10},{10,1... | collective-permute-start | bytes 491528 | tf_op jit(solution)/shard_map/ppermute | solution.py:346
  176.6 9.0 %collective-permute-start.25 = (bf16[320,256]{1,0:T(8,128)(2,1)S(1)}, bf16[320,256]{1,0:T(8,128)(2,1)S(1)}, u32[]{:S(2)}, u32[]{:S(2)}) collective-permute-start(bf16[320,256]{1,0:T(8,128)(2,1)S(1)} %collective-permute-done.24.refs_7_), channel_id=1, source_target_pairs={{0,7},{1,0},{2,1},{3,2},{4,3},{5,4},{6,5},{7,6},{8,15},{9,8},{10,9... | collective-permute-start | bytes 491528 | tf_op jit(solution)/shard_map/ppermute | solution.py:349
  183.7 8.4 %collective-permute-start.22 = (bf16[320,256]{1,0:T(8,128)(2,1)S(1)}, bf16[320,256]{1,0:T(8,128)(2,1)S(1)}, u32[]{:S(2)}, u32[]{:S(2)}) collective-permute-start(bf16[320,256]{1,0:T(8,128)(2,1)S(1)} %collective-permute-done.21.refs_4_), channel_id=1, source_target_pairs={{0,1},{1,2},{2,3},{3,4},{4,5},{5,6},{6,7},{7,0},{8,9},{9,10},{10,1... | collective-permute-start | bytes 491528 | tf_op jit(solution)/shard_map/ppermute | solution.py:346
  194.4 34.2 %all-to-all-start.1 = ((bf16[64,24,128]{2,1,0:T(8,128)(2,1)}), bf16[64,24,128]{2,1,0:T(8,128)(2,1)}, u32[]{:S(2)}, u32[]{:S(2)}) async-start(bf16[64,24,128]{2,1,0:T(8,128)(2,1)} %bitcast.37), calls=%async_computation.1 | async-start | bytes 786432 | tf_op jit(solution)/shard_map/all_to_all | solution.py:363
  217.7 13.7 %collective-permute-start.26 = (bf16[2048,384]{1,0:T(8,128)(2,1)}, bf16[2048,384]{1,0:T(8,128)(2,1)}, u32[]{:S(2)}, u32[]{:S(2)}) collective-permute-start(bf16[2048,384]{1,0:T(8,128)(2,1)} %grads.3), channel_id=1, source_target_pairs={{0,512},{512,0},{1,513},{513,1},{2,514},{514,2},{3,515},{515,3},{4... | collective-permute-start | bytes 4718600 | tf_op jit(solution)/shard_map/ppermute | solution.py:375
  (47 other events, 738.2 us)

commit v4 on v3

v4 whole, which is shorter than its diff:
```python
import jax
import jax.numpy as jnp
from jax import lax
from jax.experimental import pallas as pl
from jax.experimental.pallas import tpu as pltpu
from jax.sharding import Mesh
from jax.sharding import PartitionSpec as P

F32 = jnp.float32
BF16 = jnp.bfloat16
LANES = 128
TILE = 8


def whole(shape):
    return pl.BlockSpec(
        shape, lambda *_: (0,) * len(shape), pipeline_mode=pl.Buffered(buffer_count=1)
    )


def local_call(kernel, name, scalars, operands, outs, scratch=(), flops=0, vmem=24):
    out_specs = jax.tree.map(lambda o: whole(o.shape), outs)
    return pl.pallas_call(
        kernel,
        grid=(1,),
        in_specs=[pl.BlockSpec(memory_space=pltpu.SMEM)] + [whole(o.shape) for o in operands],
        out_specs=out_specs,
        out_shape=outs,
        scratch_shapes=list(scratch),
        cost_estimate=pl.CostEstimate(flops=flops, bytes_accessed=1 << 20, transcendentals=0),
        compiler_params=pltpu.CompilerParams(vmem_limit_bytes=vmem << 20),
        name=name,
    )(scalars, *operands)


def transposed_dot(left, right):
    return lax.dot_general(left, right, (((0,), (0,)), ((), ())), preferred_element_type=F32)


def shift(axis, step):
    n = lax.axis_size(axis)
    return [(i, (i + step) % n) for i in range(n)]


def pack_kernel(capacity, col, ids_ref, probs_ref, x_ref, dy_ref, out_ref, table_ref, flat):
    choose, tok = ids_ref.shape
    rows = table_ref.shape[0]
    experts = rows // capacity
    chunks = x_ref.shape[1] // LANES
    stretch = flat.shape[0] // experts
    expert = lax.broadcasted_iota(jnp.int32, (experts, tok), 0)
    named = [expert == ids_ref[k : k + 1, :] for k in range(choose)]
    counts = sum(m.astype(F32) for m in named)
    earlier = lax.broadcasted_iota(jnp.int32, (tok, tok), 0) < lax.broadcasted_iota(
        jnp.int32, (tok, tok), 1
    )
    before = jnp.dot(
        counts.astype(BF16), earlier.astype(F32).astype(BF16), preferred_element_type=F32
    )
    row = lax.broadcasted_iota(jnp.int32, (rows, tok), 0)
    occupied = jnp.zeros((rows, tok), F32)
    weights = jnp.zeros((rows, tok), F32)
    for k in range(choose):
        slot = jnp.sum(jnp.where(named[k], before, 0.0), axis=0, keepdims=True)
        here = row == slot.astype(jnp.int32) * experts + ids_ref[k : k + 1, :]
        occupied = jnp.where(here, 1.0, occupied)
        weights = jnp.where(here, probs_ref[k : k + 1, :].astype(F32), weights)
    table = weights.astype(BF16)
    table_ref[...] = table
    placed = jnp.dot(occupied.astype(BF16), x_ref[...], preferred_element_type=F32)
    scaled = jnp.dot(table, dy_ref[...], preferred_element_type=F32)
    for s in range(capacity):
        of = slice(s * experts, (s + 1) * experts)
        for c in range(chunks):
            cols = slice(c * LANES, (c + 1) * LANES)
            at = s * 2 * chunks + c
            flat[pl.ds(at, experts, stride=stretch), :] = placed[of, cols]
            flat[pl.ds(at + chunks, experts, stride=stretch), :] = scaled[of, cols]
    out_ref[...] = flat[...].astype(BF16)


def pack(ids, probs, tokens, cotangent, column, width, experts, capacity):
    tok = tokens.shape[0]
    rows = experts * capacity
    height = rows * 2 * (width // LANES)
    wide = pl.BlockSpec((tok, width), lambda i, col: (0, col[0]))
    return pl.pallas_call(
        lambda *refs: pack_kernel(capacity, *refs),
        grid_spec=pltpu.PrefetchScalarGridSpec(
            num_scalar_prefetch=1,
            grid=(1,),
            in_specs=[whole(ids.shape), whole(probs.shape), wide, wide],
            out_specs=[whole((height, LANES)), whole((rows, tok))],
            scratch_shapes=[pltpu.VMEM((height, LANES), F32)],
        ),
        out_shape=[
            jax.ShapeDtypeStruct((height, LANES), BF16),
            jax.ShapeDtypeStruct((rows, tok), BF16),
        ],
        compiler_params=pltpu.CompilerParams(vmem_limit_bytes=60 << 20),
        name="pack",
    )(column, ids, probs, tokens, cotangent)


def unpack_kernel(capacity, _, flat_ref, x_ref, dy_ref, flat):
    rows, width = x_ref.shape
    owners, chunks = rows // capacity, width // LANES
    stretch = flat.shape[0] // owners
    flat[...] = flat_ref[...].astype(F32)
    for s in range(capacity):
        of = slice(s * owners, (s + 1) * owners)
        for c in range(chunks):
            cols = slice(c * LANES, (c + 1) * LANES)
            at = s * 2 * chunks + c
            x_ref[of, cols] = flat[pl.ds(at, owners, stride=stretch), :].astype(BF16)
            dy_ref[of, cols] = flat[pl.ds(at + chunks, owners, stride=stretch), :].astype(BF16)


def weights_at(parts, distance, position, width, weights):
    per_half = parts // 2
    source = lax.rem(position[0] - distance + parts, parts)
    of = pl.ds(pl.multiple_of(lax.rem(source, per_half) * width, width), width)
    half = source // per_half
    return jnp.concatenate([weights[half, i, of, :] for i in range(3)], axis=1)


def forward_most(parts, distances, middle, position, *refs):
    xs, dys = refs[: len(distances)], refs[len(distances) : 2 * len(distances)]
    weights, out, mid_ref = refs[2 * len(distances) :]
    rows, width = xs[0].shape
    hid = out.shape[1] // 3
    acc, back = jnp.zeros((rows, 2 * hid), F32), jnp.zeros((rows, hid), F32)
    for d, x, dy in zip(distances, xs, dys):
        piece = weights_at(parts, d, position, width, weights)
        acc = acc + jnp.dot(x[...], piece[:, : 2 * hid], preferred_element_type=F32)
        back = back + jnp.dot(dy[...], piece[:, 2 * hid :], preferred_element_type=F32)
    out[:, : 2 * hid] = acc
    out[:, 2 * hid :] = back
    mid_ref[...] = weights_at(parts, middle, position, width, weights)


def forward_last(_, x_ref, dy_ref, piece_ref, begun, both_ref, hidden_ref):
    hid = hidden_ref.shape[1]
    acc = begun[:, : 2 * hid] + jnp.dot(
        x_ref[...], piece_ref[:, : 2 * hid], preferred_element_type=F32
    )
    back = begun[:, 2 * hid :] + jnp.dot(
        dy_ref[...], piece_ref[:, 2 * hid :], preferred_element_type=F32
    )
    gate, up = acc[:, :hid], acc[:, hid:]
    sig = 1.0 / (1.0 + jnp.exp(-gate))
    act = gate * sig
    hidden_ref[...] = (act * up).astype(BF16)
    both_ref[:, :hid] = (back * up * sig * (1.0 + gate * (1.0 - sig))).astype(BF16)
    both_ref[:, hid:] = (back * act).astype(BF16)


def back_kernel(parts, capacity, position, *refs):
    blocks, (own_ref, other_ref, out_ref, flat) = refs[:parts], refs[parts:]
    place, core = position[0], position[1]
    per_half = parts // 2
    sub = own_ref.shape[0] // parts
    rows, width = blocks[0].shape[0], 2 * sub
    owners, chunks = rows // capacity, width // LANES
    stretch = flat.shape[0] // owners
    ahead = lax.rem(core + place // per_half, 2)
    own, other = jnp.zeros((rows, sub), F32), jnp.zeros((rows, sub), F32)
    contract = (((1,), (1,)), ((), ()))
    for d in range(parts):
        block = blocks[d][...]
        at = pl.multiple_of(lax.rem(d + per_half * ahead, parts) * sub, sub)
        own = own + lax.dot_general(
            block, own_ref[pl.ds(at, sub), :], contract, preferred_element_type=F32
        )
        at = pl.multiple_of(lax.rem(d + per_half * (1 - ahead), parts) * sub, sub)
        other = other + lax.dot_general(
            block, other_ref[pl.ds(at, sub), :], contract, preferred_element_type=F32
        )
    first = core == 0
    total = jnp.concatenate((jnp.where(first, own, other), jnp.where(first, other, own)), axis=1)
    for s in range(capacity):
        for c in range(chunks):
            flat[pl.ds(s * chunks + c, owners, stride=stretch), :] = total[
                s * owners : (s + 1) * owners, c * LANES : (c + 1) * LANES
            ]
    for pad in range(capacity * chunks, stretch):
        flat[pl.ds(pad, owners, stride=stretch), :] = jnp.zeros((owners, LANES), F32)
    out_ref[...] = flat[...].astype(BF16)


def combine_kernel(capacity, _, flat_ref, table_ref, out_ref, flat, rows_ref):
    rows, width = rows_ref.shape
    owners, chunks = rows // capacity, width // LANES
    stretch = flat.shape[0] // owners
    flat[...] = flat_ref[...].astype(F32)
    for s in range(capacity):
        for c in range(chunks):
            rows_ref[s * owners : (s + 1) * owners, c * LANES : (c + 1) * LANES] = flat[
                pl.ds(s * chunks + c, owners, stride=stretch), :
            ].astype(BF16)
    out_ref[...] = transposed_dot(table_ref[...], rows_ref[...]).astype(BF16)


def grads_kernel(parts, position, *refs):
    xs, dys, both_ref, hidden_ref = refs[:parts], refs[parts : 2 * parts], *refs[2 * parts :][:2]
    rest = refs[2 * parts + 2 :]
    place, wanted = position[0], position[1]
    width = xs[0].shape[1]
    hid = hidden_ref.shape[1]
    per_half = parts // 2
    for d in range(parts):
        source = lax.rem(place - d + parts, parts)

        @pl.when(source // per_half == wanted)
        def _():
            into = pl.ds(pl.multiple_of(lax.rem(source, per_half) * width, width), width)
            both = transposed_dot(xs[d][...], both_ref[...]).astype(BF16)
            down = transposed_dot(dys[d][...], hidden_ref[...]).astype(BF16)
            if len(rest) == 1:
                rest[0][into, : 2 * hid] = both
                rest[0][into, 2 * hid :] = down
            else:
                received, outs = rest[0], rest[1:]
                for i, share in enumerate((both[:, :hid], both[:, hid:], down)):
                    more = received[into, i * hid : (i + 1) * hid].astype(F32)
                    outs[i][0, into, :] = (share.astype(F32) + more).astype(BF16)


def grads(place, which, operands, outs):
    xs, dys, both, hidden, *received = operands
    parts = len(xs)
    half = parts // 2 * xs[0].shape[1]
    return local_call(
        lambda *refs: grads_kernel(parts, *refs),
        "grads",
        jnp.stack((place, which)).astype(jnp.int32),
        (*xs, *dys, both, hidden, *received),
        outs,
        flops=2 * both.shape[0] * half * (both.shape[1] + hidden.shape[1]),
    )


def shards(tokens, cotangent, expert_ids, probs, gate_weight, up_weight, down_weight):
    peers = ("x", "z")
    owners = lax.axis_size("x") * lax.axis_size("z")
    parts = lax.axis_size("y")
    core, place = lax.axis_index("dp"), lax.axis_index("y")
    tok, model = tokens.shape
    choose = expert_ids.shape[1]
    width = model // parts
    chunks = width // LANES
    hid = gate_weight.shape[2]
    capacity = min(tok, (5 * tok * choose + 4 * owners - 1) // (4 * owners))
    rows = owners * capacity
    half = parts // 2
    swap = shift("dp", 1)
    place, core = place.astype(jnp.int32), core.astype(jnp.int32)
    position = jnp.stack((place, core))

    flat, table = pack(
        expert_ids.T, probs.T, tokens, cotangent, place[None], width, owners, capacity
    )
    flat, own_weights = lax.optimization_barrier(
        (flat, (gate_weight[0], up_weight[0], down_weight[0]))
    )
    flat = lax.all_to_all(
        flat.reshape(owners, -1, LANES), peers, split_axis=0, concat_axis=0, tiled=True
    )
    weights = lax.all_gather(jnp.stack(own_weights), "dp")

    sub = width // 2
    turned = []
    for k in range(parts):
        target = lax.rem(place + k, parts)
        start = lax.rem(target, half) * width + target // half * sub
        piece = jnp.concatenate(
            [lax.dynamic_slice_in_dim(w, start, sub, 0) for w in own_weights[:2]], axis=1
        )
        perm = []
        for h in range(2):
            for p in range(parts):
                t = (p + k) % parts
                perm.append((h * parts + p, t // half * parts + h * half + t % half))
        turned.append(lax.ppermute(piece, ("dp", "y"), perm))
    flat, turned = lax.optimization_barrier((flat, turned))
    turned = jnp.concatenate(turned)
    turned_other = lax.ppermute(turned, "dp", swap)

    flat = flat.reshape(-1, LANES)
    pair = jax.ShapeDtypeStruct((rows, width), BF16)
    own = local_call(
        lambda *refs: unpack_kernel(capacity, *refs),
        "unpack",
        position,
        (flat,),
        (pair, pair),
        [pltpu.VMEM(flat.shape, F32)],
    )

    def ring(value, rightward):
        held = {0: value}
        right = left = value
        for d in range(1, half + 1):
            if d < half or rightward:
                right = lax.ppermute(right, "y", shift("y", 1))
                held[d] = right
            if d < half or not rightward:
                left = lax.ppermute(left, "y", shift("y", -1))
                held[parts - d] = left
        return [held[d] for d in range(parts)]

    xs, dys = ring(own[0], True), ring(own[1], False)
    most = [d for d in range(parts) if d != half]
    begun, piece = local_call(
        lambda *refs: forward_most(parts, most, half, *refs),
        "forward_most",
        position,
        (*[xs[d] for d in most], *[dys[d] for d in most], weights),
        (
            jax.ShapeDtypeStruct((rows, 3 * hid), F32),
            jax.ShapeDtypeStruct((width, 3 * hid), BF16),
        ),
        flops=2 * rows * model * 3 * hid,
    )
    d_both, hidden = local_call(
        forward_last,
        "forward_last",
        position,
        (xs[half], dys[half], piece, begun),
        (
            jax.ShapeDtypeStruct((rows, 2 * hid), BF16),
            jax.ShapeDtypeStruct((rows, hid), BF16),
        ),
        flops=2 * rows * width * 3 * hid,
    )

    stretch = -(-capacity * chunks // TILE) * TILE
    d_rows = local_call(
        lambda *refs: back_kernel(parts, capacity, *refs),
        "back",
        position,
        (*ring(d_both, True), turned, turned_other),
        jax.ShapeDtypeStruct((owners * stretch, LANES), BF16),
        [pltpu.VMEM((owners * stretch, LANES), F32)],
        flops=4 * rows * width * parts * hid,
    )
    d_rows, operands = lax.optimization_barrier((d_rows, (xs, dys, d_both, hidden)))
    returned = lax.all_to_all(
        d_rows.reshape(owners, -1, LANES), peers, split_axis=0, concat_axis=0, tiled=True
    )
    d_tokens = local_call(
        lambda *refs: combine_kernel(capacity, *refs),
        "combine",
        position,
        (returned.reshape(-1, LANES), table),
        jax.ShapeDtypeStruct((tok, width), BF16),
        [pltpu.VMEM((owners * stretch, LANES), F32), pltpu.VMEM((rows, width), BF16)],
        flops=1 << 37,
    )
    send = jax.ShapeDtypeStruct((model // 2, 3 * hid), BF16)
    received = lax.ppermute(grads(place, 1 - core, operands, send), "dp", swap)
    grad = jax.ShapeDtypeStruct(gate_weight.shape, BF16)
    return d_tokens, *grads(place, core, (*operands, received), (grad, grad, grad))


def solution(mesh):
    dp, experts, etp = mesh.devices.shape
    inner = min(16, experts)
    grid = Mesh(mesh.devices.reshape(dp, experts // inner, inner, etp), ("dp", "x", "z", "y"))
    row = P(("dp", "x", "z"), None)
    weight = P(("x", "z"), "dp", "y")
    return jax.shard_map(
        shards,
        mesh=grid,
        in_specs=(row, row, row, row, weight, weight, weight),
        out_specs=(P(("dp", "x", "z"), "y"), weight, weight, weight),
        check_vma=False,
    )
```

time: 236 us -> 228 us (0.966)
  waiting for transfers between devices: 61.8 us -> 33.9 us
  starting transfers between devices: 130 us -> 145 us
  between operations: 1.52 us -> 14.9 us
  local copies, waits for them, and re-layouts: 21.6 us -> 9.85 us
  Pallas kernels: 18.7 us -> 21.5 us
    ppermute x27 -> x31, waiting for transfers between devices: 59.3 us -> 18.5 us  [the longest x11 13.6 us: ring(): right = lax.ppermute(right, 'y', shift('y', 1))]
    ppermute x27 -> x31, starting transfers between devices: 92.4 us -> 107 us  [the longest x10 49.4 us: ring(): left = lax.ppermute(left, 'y', shift('y', -1))]
    all_to_all x1, waiting for transfers between devices: 2.43 us -> 15.3 us  [shards(): lax.all_to_all(d_rows.reshape(owners, -1, LANES), peers, split_axis=0, co...]
    unnamed x107 -> x29, local copies, waits for them, and re-layouts: 21.5 us -> 9.09 us
    pallas_call x8 -> x7, Pallas kernels: 16.3 us -> 19.1 us  [local_call(): pl.pallas_call(kernel, grid=(1,), in_specs=[pl.BlockSpec(memory_space=plt...]
  transfers between devices with their start and end apart: 29 -> 34, of which waited for: 12 -> 9; matrix products, arithmetic and copies ran while one was open for 1% -> 3% of each run, Pallas kernels for 4% -> 5%
where the time goes in v4:
time: 228 us; the launch traced here: 227 us
  starting transfers between devices  145 us (64%)
  waiting for transfers between devices  33.9 us (15%)
  Pallas kernels  21.5 us (9%)
  between operations  14.9 us (7%)
  local copies, waits for them, and re-layouts  9.85 us (4%)
    ppermute x10, starting transfers between devices, ring(): left = lax.ppermute(left, 'y', shift('y', -1))  49.4 us
    ppermute x8, starting transfers between devices, shards(): turned.append(lax.ppermute(piece, ('dp', 'y'), perm))  31.8 us
    all_to_all x1, starting transfers between devices, shards(): lax.all_to_all(flat.reshape(owners, -1, LANES), peers, split_axis=0, conc...  22.5 us
    ppermute x11, starting transfers between devices, ring(): right = lax.ppermute(right, 'y', shift('y', 1))  22.3 us
    pallas_call x7, Pallas kernels, local_call(): pl.pallas_call(kernel, grid=(1,), in_specs=[pl.BlockSpec(memory_space=plt...  19.1 us
    all_to_all x1, waiting for transfers between devices, shards(): lax.all_to_all(d_rows.reshape(owners, -1, LANES), peers, split_axis=0, co...  15.3 us
    all_to_all x1, starting transfers between devices, shards(): lax.all_to_all(d_rows.reshape(owners, -1, LANES), peers, split_axis=0, co...  15.3 us
    ppermute x11, waiting for transfers between devices, ring(): right = lax.ppermute(right, 'y', shift('y', 1))  13.6 us
  transfers between devices with their start and end apart: 34, of which 9 were waited for; matrix products, arithmetic and copies ran while one was open for 3% of the time, Pallas kernels for 5%

profile of v4, /device:TPU:6, one launch (start us, length us, event | category | flops | bytes accessed | tf_op | source)
XLA Modules:
  0.0 227.0 jit_solution(17520662066959423217)
XLA Ops:
  7.2 2.5 %pack.1 = (bf16[2560,128]{1,0:T(8,128)(2,1)}, bf16[320,32]{1,0:T(8,128)(2,1)}) custom-call(s32[1]{0:T(128)} %bitcast.refs_0_, s32[8,32]{1,0:T(8,128)} %bitcast.22, bf16[8,32]{1,0:T(8,128)(2,1)} %bitcast.23, bf16[32,4096]{1,0:T(8,128)(2,1)} %refs_3_.1, bf16[32,4096]{1,0:T(8,128)(2,1)} %refs_4_.1), custom_call_target="tpu_custom_call" | custom-call | tf_op jit(solution)/shard_map/pack/pallas_call | solution.py:87
  9.7 22.5 %all-to-all-start = ((bf16[64,40,128]{2,1,0:T(8,128)(2,1)}), bf16[64,40,128]{2,1,0:T(8,128)(2,1)S(1)}, u32[]{:S(2)}, u32[]{:S(2)}) async-start(bf16[64,40,128]{2,1,0:T(8,128)(2,1)} %bitcast.21), calls=%async_computation | async-start | bytes 1310720 | tf_op jit(solution)/shard_map/all_to_all | solution.py:266
  34.6 3.5 %collective-permute-start.1 = (bf16[256,256]{1,0:T(8,128)(2,1)S(1)}, bf16[256,256]{1,0:T(8,128)(2,1)S(1)}, u32[]{:S(2)}, u32[]{:S(2)}) collective-permute-start(bf16[256,256]{1,0:T(8,128)(2,1)S(1)} %pad_maximum_fusion.2), channel_id=1, source_target_pairs={{0,1},{1,2},{2,3},{3,512},{4,513},{5,514},{6,515},{7,0},{512,5},{5... | collective-permute-start | bytes 393224 | tf_op jit(solution)/shard_map/ppermute | solution.py:284
  38.1 4.5 %collective-permute-start.2 = (bf16[256,256]{1,0:T(8,128)(2,1)S(1)}, bf16[256,256]{1,0:T(8,128)(2,1)S(1)}, u32[]{:S(2)}, u32[]{:S(2)}) collective-permute-start(bf16[256,256]{1,0:T(8,128)(2,1)S(1)} %pad_maximum_fusion.3), channel_id=1, source_target_pairs={{0,2},{1,3},{2,512},{3,513},{4,514},{5,515},{6,0},{7,1},{512,6},{5... | collective-permute-start | bytes 393224 | tf_op jit(solution)/shard_map/ppermute | solution.py:284
  42.7 8.4 %collective-permute-start.3 = (bf16[256,256]{1,0:T(8,128)(2,1)S(1)}, bf16[256,256]{1,0:T(8,128)(2,1)S(1)}, u32[]{:S(2)}, u32[]{:S(2)}) collective-permute-start(bf16[256,256]{1,0:T(8,128)(2,1)S(1)} %pad_maximum_fusion.4), channel_id=1, source_target_pairs={{0,3},{1,512},{2,513},{3,514},{4,515},{5,0},{6,1},{7,2},{512,7},{5... | collective-permute-start | bytes 393224 | tf_op jit(solution)/shard_map/ppermute | solution.py:284
  53.1 4.8 %collective-permute-start.5 = (bf16[256,256]{1,0:T(8,128)(2,1)S(1)}, bf16[256,256]{1,0:T(8,128)(2,1)S(1)}, u32[]{:S(2)}, u32[]{:S(2)}) collective-permute-start(bf16[256,256]{1,0:T(8,128)(2,1)S(1)} %pad_maximum_fusion.6), channel_id=1, source_target_pairs={{0,513},{1,514},{2,515},{3,0},{4,1},{5,2},{6,3},{7,512},{512,517},... | collective-permute-start | bytes 393224 | tf_op jit(solution)/shard_map/ppermute | solution.py:284
  57.9 3.0 %collective-permute-start.6 = (bf16[256,256]{1,0:T(8,128)(2,1)S(1)}, bf16[256,256]{1,0:T(8,128)(2,1)S(1)}, u32[]{:S(2)}, u32[]{:S(2)}) collective-permute-start(bf16[256,256]{1,0:T(8,128)(2,1)S(1)} %pad_maximum_fusion.7), channel_id=1, source_target_pairs={{0,514},{1,515},{2,0},{3,1},{4,2},{5,3},{6,512},{7,513},{512,518},... | collective-permute-start | bytes 393224 | tf_op jit(solution)/shard_map/ppermute | solution.py:284
  60.9 5.1 %collective-permute-start.7 = (bf16[256,256]{1,0:T(8,128)(2,1)S(1)}, bf16[256,256]{1,0:T(8,128)(2,1)S(1)}, u32[]{:S(2)}, u32[]{:S(2)}) collective-permute-start(bf16[256,256]{1,0:T(8,128)(2,1)S(1)} %pad_maximum_fusion.8), channel_id=1, source_target_pairs={{0,515},{1,0},{2,1},{3,2},{4,3},{5,512},{6,513},{7,514},{512,519},... | collective-permute-start | bytes 393224 | tf_op jit(solution)/shard_map/ppermute | solution.py:284
  66.1 2.6 %collective-permute-done.6 = bf16[256,256]{1,0:T(8,128)(2,1)S(1)} collective-permute-done((bf16[256,256]{1,0:T(8,128)(2,1)S(1)}, bf16[256,256]{1,0:T(8,128)(2,1)S(1)}, u32[]{:S(2)}, u32[]{:S(2)}) %collective-permute-start.6) | collective-permute-done | bytes 131104 | tf_op jit(solution)/shard_map/ppermute | solution.py:284
  70.8 2.9 %collective-permute-start.8 = (bf16[320,512]{1,0:T(8,128)(2,1)S(1)}, bf16[320,512]{1,0:T(8,128)(2,1)S(1)}, u32[]{:S(2)}, u32[]{:S(2)}) collective-permute-start(bf16[320,512]{1,0:T(8,128)(2,1)S(1)} %get-tuple-element.69.refs_1_), channel_id=1, source_target_pairs={{0,1},{1,2},{2,3},{3,4},{4,5},{5,6},{6,7},{7,0},{8,9},{9,10},{10,1... | collective-permute-start | bytes 983048 | tf_op jit(solution)/shard_map/ppermute | solution.py:305
  73.7 5.4 %collective-permute-start.12 = (bf16[320,512]{1,0:T(8,128)(2,1)S(1)}, bf16[320,512]{1,0:T(8,128)(2,1)S(1)}, u32[]{:S(2)}, u32[]{:S(2)}) collective-permute-start(bf16[320,512]{1,0:T(8,128)(2,1)S(1)} %get-tuple-element.77.refs_8_.refs_9_), channel_id=1, source_target_pairs={{0,7},{1,0},{2,1},{3,2},{4,3},{5,4},{6,5},{7,6},{8,15},{9,8},{10,9... | collective-permute-start | bytes 983048 | tf_op jit(solution)/shard_map/ppermute | solution.py:308
  79.1 3.9 %collective-permute-start.16 = (bf16[320,512]{1,0:T(8,128)(2,1)S(1)}, bf16[320,512]{1,0:T(8,128)(2,1)S(1)}, u32[]{:S(2)}, u32[]{:S(2)}) collective-permute-start(bf16[320,512]{1,0:T(8,128)(2,1)S(1)} %get-tuple-element.69.refs_1_), channel_id=1, source_target_pairs={{0,7},{1,0},{2,1},{3,2},{4,3},{5,4},{6,5},{7,6},{8,15},{9,8},{10,9... | collective-permute-start | bytes 983048 | tf_op jit(solution)/shard_map/ppermute | solution.py:308
  88.2 5.1 %collective-permute-start.13 = (bf16[320,512]{1,0:T(8,128)(2,1)S(1)}, bf16[320,512]{1,0:T(8,128)(2,1)S(1)}, u32[]{:S(2)}, u32[]{:S(2)}) collective-permute-start(bf16[320,512]{1,0:T(8,128)(2,1)S(1)} %collective-permute-done.12.refs_14_.refs_16_), channel_id=1, source_target_pairs={{0,7},{1,0},{2,1},{3,2},{4,3},{5,4},{6,5},{7,6},{8,15},{9,8},{10,9... | collective-permute-start | bytes 983048 | tf_op jit(solution)/shard_map/ppermute | solution.py:308
  94.7 5.1 %collective-permute-start.17 = (bf16[320,512]{1,0:T(8,128)(2,1)S(1)}, bf16[320,512]{1,0:T(8,128)(2,1)S(1)}, u32[]{:S(2)}, u32[]{:S(2)}) collective-permute-start(bf16[320,512]{1,0:T(8,128)(2,1)S(1)} %collective-permute-done.16.refs_7_.refs_8_), channel_id=1, source_target_pairs={{0,7},{1,0},{2,1},{3,2},{4,3},{5,4},{6,5},{7,6},{8,15},{9,8},{10,9... | collective-permute-start | bytes 983048 | tf_op jit(solution)/shard_map/ppermute | solution.py:308
  104.4 5.1 %collective-permute-start.14 = (bf16[320,512]{1,0:T(8,128)(2,1)S(1)}, bf16[320,512]{1,0:T(8,128)(2,1)}, u32[]{:S(2)}, u32[]{:S(2)}) collective-permute-start(bf16[320,512]{1,0:T(8,128)(2,1)S(1)} %collective-permute-done.13.refs_13_.refs_15_), channel_id=1, source_target_pairs={{0,7},{1,0},{2,1},{3,2},{4,3},{5,4},{6,5},{7,6},{8,15},{9,8},{10,9... | collective-permute-start | bytes 983048 | tf_op jit(solution)/shard_map/ppermute | solution.py:308
  111.7 3.9 %collective-permute-start.18 = (bf16[320,512]{1,0:T(8,128)(2,1)S(1)}, bf16[320,512]{1,0:T(8,128)(2,1)}, u32[]{:S(2)}, u32[]{:S(2)}) collective-permute-start(bf16[320,512]{1,0:T(8,128)(2,1)S(1)} %collective-permute-done.17.refs_6_.refs_7_), channel_id=1, source_target_pairs={{0,7},{1,0},{2,1},{3,2},{4,3},{5,4},{6,5},{7,6},{8,15},{9,8},{10,9... | collective-permute-start | bytes 983048 | tf_op jit(solution)/shard_map/ppermute | solution.py:308
  122.1 5.1 %collective-permute-start.15 = (bf16[320,512]{1,0:T(8,128)(2,1)}, bf16[320,512]{1,0:T(8,128)(2,1)}, u32[]{:S(2)}, u32[]{:S(2)}) collective-permute-start(bf16[320,512]{1,0:T(8,128)(2,1)} %collective-permute-done.14.refs_12_.refs_14_), channel_id=1, source_target_pairs={{0,7},{1,0},{2,1},{3,2},{4,3},{5,4},{6,5},{7,6},{8,15},{9,8},{10,9... | collective-permute-start | bytes 983048 | tf_op jit(solution)/shard_map/ppermute | solution.py:308
  129.2 2.6 %forward_most.1 = (f32[320,384]{1,0:T(8,128)S(1)}, bf16[512,384]{1,0:T(8,128)(2,1)S(1)}) custom-call(s32[2]{0:T(128)S(1)} %pad_add_fusion.refs_0_._, bf16[320,512]{1,0:T(8,128)(2,1)S(1)} %get-tuple-element.69.refs_1_, bf16[320,512]{1,0:T(8,128)(2,1)S(1)} %collective-permute-done.8.refs_2_, bf16[320,512]{1,0:T(8,128)(2,1)S(1)} %collective-permute-done.9.refs_3_, ...), custom_call_target="tpu_custom_call" | custom-call | flops 1006632960 | bytes 1048576 | tf_op jit(solution)/shard_map/forward_most/pallas_call | solution.py:23
  131.9 2.3 collective-permute-done.11.x_ref.refs_5_
  136.7 2.1 collective-permute-start.22
  138.8 5.4 %collective-permute-start.26 = (bf16[320,256]{1,0:T(8,128)(2,1)S(1)}, bf16[320,256]{1,0:T(8,128)(2,1)S(1)}, u32[]{:S(2)}, u32[]{:S(2)}) collective-permute-start(bf16[320,256]{1,0:T(8,128)(2,1)S(1)} %get-tuple-element.85.refs_1_.refs_17_), channel_id=1, source_target_pairs={{0,7},{1,0},{2,1},{3,2},{4,3},{5,4},{6,5},{7,6},{8,15},{9,8},{10,9... | collective-permute-start | bytes 491528 | tf_op jit(solution)/shard_map/ppermute | solution.py:308
  144.2 2.1 collective-permute-done.22.refs_2_
  148.3 5.1 %collective-permute-start.27 = (bf16[320,256]{1,0:T(8,128)(2,1)S(1)}, bf16[320,256]{1,0:T(8,128)(2,1)S(1)}, u32[]{:S(2)}, u32[]{:S(2)}) collective-permute-start(bf16[320,256]{1,0:T(8,128)(2,1)S(1)} %collective-permute-done.26.refs_8_), channel_id=1, source_target_pairs={{0,7},{1,0},{2,1},{3,2},{4,3},{5,4},{6,5},{7,6},{8,15},{9,8},{10,9... | collective-permute-start | bytes 491528 | tf_op jit(solution)/shard_map/ppermute | solution.py:308
  156.7 5.1 %collective-permute-start.28 = (bf16[320,256]{1,0:T(8,128)(2,1)S(1)}, bf16[320,256]{1,0:T(8,128)(2,1)S(1)}, u32[]{:S(2)}, u32[]{:S(2)}) collective-permute-start(bf16[320,256]{1,0:T(8,128)(2,1)S(1)} %collective-permute-done.27.refs_7_), channel_id=1, source_target_pairs={{0,7},{1,0},{2,1},{3,2},{4,3},{5,4},{6,5},{7,6},{8,15},{9,8},{10,9... | collective-permute-start | bytes 491528 | tf_op jit(solution)/shard_map/ppermute | solution.py:308
  165.1 6.5 %collective-permute-done.25.refs_5_ = bf16[320,256]{1,0:T(8,128)(2,1)S(1)} collective-permute-done((bf16[320,256]{1,0:T(8,128)(2,1)S(1)}, bf16[320,256]{1,0:T(8,128)(2,1)S(1)}, u32[]{:S(2)}, u32[]{:S(2)}) %collective-permute-start.25) | collective-permute-done | bytes 163872 | tf_op jit(solution)/shard_map/ppermute | solution.py:305
  171.6 2.5 %back.1 = bf16[1536,128]{1,0:T(8,128)(2,1)S(1)} custom-call(s32[2]{0:T(128)S(1)} %pad_add_fusion.refs_0_._, bf16[320,256]{1,0:T(8,128)(2,1)S(1)} %get-tuple-element.85.refs_1_.refs_17_, bf16[320,256]{1,0:T(8,128)(2,1)S(1)} %collective-permute-done.22.refs_2_, bf16[320,256]{1,0:T(8,128)(2,1)S(1)} %collective-permute-done.23.refs_3_, ...), custom_call_target="tpu_custom_call" | custom-call | flops 671088640 | bytes 1048576 | tf_op jit(solution)/shard_map/back/pallas_call | solution.py:23
  174.8 15.3 %all-to-all-start.1 = ((bf16[64,24,128]{2,1,0:T(8,128)(2,1)}), bf16[64,24,128]{2,1,0:T(8,128)(2,1)}, u32[]{:S(2)}, u32[]{:S(2)}) async-start(bf16[64,24,128]{2,1,0:T(8,128)(2,1)} %bitcast.18), calls=%async_computation.1 | async-start | bytes 786432 | tf_op jit(solution)/shard_map/all_to_all | solution.py:348
  190.2 4.5 %grads.2 = bf16[2048,384]{1,0:T(8,128)(2,1)} custom-call(s32[2]{0:T(128)S(1)} %pad_add_fusion.1.refs_0_, bf16[320,512]{1,0:T(8,128)(2,1)S(1)} %get-tuple-element.69.refs_1_, bf16[320,512]{1,0:T(8,128)(2,1)S(1)} %collective-permute-done.8.refs_2_, bf16[320,512]{1,0:T(8,128)(2,1)S(1)} %collective-permute-done.9.refs_3_, ...), custom_call_target="tpu_custom_call" | custom-call | flops 503316480 | bytes 1048576 | tf_op jit(solution)/shard_map/grads/pallas_call | solution.py:23
  194.8 2.1 collective-permute-start.30
  196.8 15.3 %all-to-all-done.1 = bf16[64,24,128]{2,1,0:T(8,128)(2,1)} async-done(((bf16[64,24,128]{2,1,0:T(8,128)(2,1)}), bf16[64,24,128]{2,1,0:T(8,128)(2,1)}, u32[]{:S(2)}, u32[]{:S(2)}) %all-to-all-start.1) | async-done | bytes 393248 | tf_op jit(solution)/shard_map/all_to_all | solution.py:348
  213.1 1.9 combine.1
  215.0 5.1 %grads.3 = (bf16[1,2048,128]{2,1,0:T(8,128)(2,1)}, bf16[1,2048,128]{2,1,0:T(8,128)(2,1)}, bf16[1,2048,128]{2,1,0:T(8,128)(2,1)}) custom-call(s32[2]{0:T(128)S(1)} %pad_add_fusion.refs_0_._, bf16[320,512]{1,0:T(8,128)(2,1)S(1)} %get-tuple-element.69.refs_1_, bf16[320,512]{1,0:T(8,128)(2,1)S(1)} %collective-permute-done.8.refs_2_, ...), custom_call_target="tpu_custom_call" | custom-call | flops 503316480 | bytes 1048576 | tf_op jit(solution)/shard_map/grads/pallas_call | solution.py:23
  (87 shorter events, 40.6 us)
Async XLA Ops:
  9.7 60.2 %all-to-all-start = ((bf16[64,40,128]{2,1,0:T(8,128)(2,1)}), bf16[64,40,128]{2,1,0:T(8,128)(2,1)S(1)}, u32[]{:S(2)}, u32[]{:S(2)}) async-start(bf16[64,40,128]{2,1,0:T(8,128)(2,1)} %bitcast.21), calls=%async_computation | async-start | bytes 1310720 | tf_op jit(solution)/shard_map/all_to_all | solution.py:266
  32.1 95.2 %all-gather.3.cloned.1.call-start = ((), (), s32[]{:S(2)}) async-start(), calls=%async_computation.2 | async-start | bytes 4718592 | tf_op jit(solution)/shard_map/all_gather | solution.py:269
  33.9 19.2 %collective-permute-start = (bf16[256,256]{1,0:T(8,128)(2,1)S(1)}, bf16[256,256]{1,0:T(8,128)(2,1)S(1)}, u32[]{:S(2)}, u32[]{:S(2)}) collective-permute-start(bf16[256,256]{1,0:T(8,128)(2,1)S(1)} %pad_maximum_fusion.1), channel_id=1, source_target_pairs={{0,0},{1,1},{2,2},{3,3},{4,512},{5,513},{6,514},{7,515},{512,4},{5... | collective-permute-start | bytes 393224 | tf_op jit(solution)/shard_map/ppermute | solution.py:284
  34.6 23.3 %collective-permute-start.1 = (bf16[256,256]{1,0:T(8,128)(2,1)S(1)}, bf16[256,256]{1,0:T(8,128)(2,1)S(1)}, u32[]{:S(2)}, u32[]{:S(2)}) collective-permute-start(bf16[256,256]{1,0:T(8,128)(2,1)S(1)} %pad_maximum_fusion.2), channel_id=1, source_target_pairs={{0,1},{1,2},{2,3},{3,512},{4,513},{5,514},{6,515},{7,0},{512,5},{5... | collective-permute-start | bytes 393224 | tf_op jit(solution)/shard_map/ppermute | solution.py:284
  38.1 22.7 %collective-permute-start.2 = (bf16[256,256]{1,0:T(8,128)(2,1)S(1)}, bf16[256,256]{1,0:T(8,128)(2,1)S(1)}, u32[]{:S(2)}, u32[]{:S(2)}) collective-permute-start(bf16[256,256]{1,0:T(8,128)(2,1)S(1)} %pad_maximum_fusion.3), channel_id=1, source_target_pairs={{0,2},{1,3},{2,512},{3,513},{4,514},{5,515},{6,0},{7,1},{512,6},{5... | collective-permute-start | bytes 393224 | tf_op jit(solution)/shard_map/ppermute | solution.py:284
  42.7 23.4 %collective-permute-start.3 = (bf16[256,256]{1,0:T(8,128)(2,1)S(1)}, bf16[256,256]{1,0:T(8,128)(2,1)S(1)}, u32[]{:S(2)}, u32[]{:S(2)}) collective-permute-start(bf16[256,256]{1,0:T(8,128)(2,1)S(1)} %pad_maximum_fusion.4), channel_id=1, source_target_pairs={{0,3},{1,512},{2,513},{3,514},{4,515},{5,0},{6,1},{7,2},{512,7},{5... | collective-permute-start | bytes 393224 | tf_op jit(solution)/shard_map/ppermute | solution.py:284
  51.1 15.0 %collective-permute-start.4 = (bf16[256,256]{1,0:T(8,128)(2,1)S(1)}, bf16[256,256]{1,0:T(8,128)(2,1)S(1)}, u32[]{:S(2)}, u32[]{:S(2)}) collective-permute-start(bf16[256,256]{1,0:T(8,128)(2,1)S(1)} %pad_maximum_fusion.5), channel_id=1, source_target_pairs={{0,512},{1,513},{2,514},{3,515},{4,0},{5,1},{6,2},{7,3},{512,516},... | collective-permute-start | bytes 393224 | tf_op jit(solution)/shard_map/ppermute | solution.py:284
  53.1 13.0 %collective-permute-start.5 = (bf16[256,256]{1,0:T(8,128)(2,1)S(1)}, bf16[256,256]{1,0:T(8,128)(2,1)S(1)}, u32[]{:S(2)}, u32[]{:S(2)}) collective-permute-start(bf16[256,256]{1,0:T(8,128)(2,1)S(1)} %pad_maximum_fusion.6), channel_id=1, source_target_pairs={{0,513},{1,514},{2,515},{3,0},{4,1},{5,2},{6,3},{7,512},{512,517},... | collective-permute-start | bytes 393224 | tf_op jit(solution)/shard_map/ppermute | solution.py:284
  57.9 10.8 %collective-permute-start.6 = (bf16[256,256]{1,0:T(8,128)(2,1)S(1)}, bf16[256,256]{1,0:T(8,128)(2,1)S(1)}, u32[]{:S(2)}, u32[]{:S(2)}) collective-permute-start(bf16[256,256]{1,0:T(8,128)(2,1)S(1)} %pad_maximum_fusion.7), channel_id=1, source_target_pairs={{0,514},{1,515},{2,0},{3,1},{4,2},{5,3},{6,512},{7,513},{512,518},... | collective-permute-start | bytes 393224 | tf_op jit(solution)/shard_map/ppermute | solution.py:284
  60.9 9.0 %collective-permute-start.7 = (bf16[256,256]{1,0:T(8,128)(2,1)S(1)}, bf16[256,256]{1,0:T(8,128)(2,1)S(1)}, u32[]{:S(2)}, u32[]{:S(2)}) collective-permute-start(bf16[256,256]{1,0:T(8,128)(2,1)S(1)} %pad_maximum_fusion.8), channel_id=1, source_target_pairs={{0,515},{1,0},{2,1},{3,2},{4,3},{5,512},{6,513},{7,514},{512,519},... | collective-permute-start | bytes 393224 | tf_op jit(solution)/shard_map/ppermute | solution.py:284
  70.8 15.5 %collective-permute-start.8 = (bf16[320,512]{1,0:T(8,128)(2,1)S(1)}, bf16[320,512]{1,0:T(8,128)(2,1)S(1)}, u32[]{:S(2)}, u32[]{:S(2)}) collective-permute-start(bf16[320,512]{1,0:T(8,128)(2,1)S(1)} %get-tuple-element.69.refs_1_), channel_id=1, source_target_pairs={{0,1},{1,2},{2,3},{3,4},{4,5},{5,6},{6,7},{7,0},{8,9},{9,10},{10,1... | collective-permute-start | bytes 983048 | tf_op jit(solution)/shard_map/ppermute | solution.py:305
  73.7 14.5 %collective-permute-start.12 = (bf16[320,512]{1,0:T(8,128)(2,1)S(1)}, bf16[320,512]{1,0:T(8,128)(2,1)S(1)}, u32[]{:S(2)}, u32[]{:S(2)}) collective-permute-start(bf16[320,512]{1,0:T(8,128)(2,1)S(1)} %get-tuple-element.77.refs_8_.refs_9_), channel_id=1, source_target_pairs={{0,7},{1,0},{2,1},{3,2},{4,3},{5,4},{6,5},{7,6},{8,15},{9,8},{10,9... | collective-permute-start | bytes 983048 | tf_op jit(solution)/shard_map/ppermute | solution.py:308
  79.1 15.6 %collective-permute-start.16 = (bf16[320,512]{1,0:T(8,128)(2,1)S(1)}, bf16[320,512]{1,0:T(8,128)(2,1)S(1)}, u32[]{:S(2)}, u32[]{:S(2)}) collective-permute-start(bf16[320,512]{1,0:T(8,128)(2,1)S(1)} %get-tuple-element.69.refs_1_), channel_id=1, source_target_pairs={{0,7},{1,0},{2,1},{3,2},{4,3},{5,4},{6,5},{7,6},{8,15},{9,8},{10,9... | collective-permute-start | bytes 983048 | tf_op jit(solution)/shard_map/ppermute | solution.py:308
  83.0 16.8 %collective-permute-start.19 = (bf16[320,512]{1,0:T(8,128)(2,1)S(1)}, bf16[320,512]{1,0:T(8,128)(2,1)S(1)}, u32[]{:S(2)}, u32[]{:S(2)}) collective-permute-start(bf16[320,512]{1,0:T(8,128)(2,1)S(1)} %get-tuple-element.77.refs_8_.refs_9_), channel_id=1, source_target_pairs={{0,1},{1,2},{2,3},{3,4},{4,5},{5,6},{6,7},{7,0},{8,9},{9,10},{10,1... | collective-permute-start | bytes 983048 | tf_op jit(solution)/shard_map/ppermute | solution.py:305
  86.3 16.1 %collective-permute-start.9 = (bf16[320,512]{1,0:T(8,128)(2,1)S(1)}, bf16[320,512]{1,0:T(8,128)(2,1)S(1)}, u32[]{:S(2)}, u32[]{:S(2)}) collective-permute-start(bf16[320,512]{1,0:T(8,128)(2,1)S(1)} %collective-permute-done.8.refs_2_), channel_id=1, source_target_pairs={{0,1},{1,2},{2,3},{3,4},{4,5},{5,6},{6,7},{7,0},{8,9},{9,10},{10,1... | collective-permute-start | bytes 983048 | tf_op jit(solution)/shard_map/ppermute | solution.py:305
  88.2 16.1 %collective-permute-start.13 = (bf16[320,512]{1,0:T(8,128)(2,1)S(1)}, bf16[320,512]{1,0:T(8,128)(2,1)S(1)}, u32[]{:S(2)}, u32[]{:S(2)}) collective-permute-start(bf16[320,512]{1,0:T(8,128)(2,1)S(1)} %collective-permute-done.12.refs_14_.refs_16_), channel_id=1, source_target_pairs={{0,7},{1,0},{2,1},{3,2},{4,3},{5,4},{6,5},{7,6},{8,15},{9,8},{10,9... | collective-permute-start | bytes 983048 | tf_op jit(solution)/shard_map/ppermute | solution.py:308
  94.7 17.1 %collective-permute-start.17 = (bf16[320,512]{1,0:T(8,128)(2,1)S(1)}, bf16[320,512]{1,0:T(8,128)(2,1)S(1)}, u32[]{:S(2)}, u32[]{:S(2)}) collective-permute-start(bf16[320,512]{1,0:T(8,128)(2,1)S(1)} %collective-permute-done.16.refs_7_.refs_8_), channel_id=1, source_target_pairs={{0,7},{1,0},{2,1},{3,2},{4,3},{5,4},{6,5},{7,6},{8,15},{9,8},{10,9... | collective-permute-start | bytes 983048 | tf_op jit(solution)/shard_map/ppermute | solution.py:308
  99.8 15.8 %collective-permute-start.20 = (bf16[320,512]{1,0:T(8,128)(2,1)S(1)}, bf16[320,512]{1,0:T(8,128)(2,1)S(1)}, u32[]{:S(2)}, u32[]{:S(2)}) collective-permute-start(bf16[320,512]{1,0:T(8,128)(2,1)S(1)} %collective-permute-done.19.refs_9_.refs_10_), channel_id=1, source_target_pairs={{0,1},{1,2},{2,3},{3,4},{4,5},{5,6},{6,7},{7,0},{8,9},{9,10},{10,1... | collective-permute-start | bytes 983048 | tf_op jit(solution)/shard_map/ppermute | solution.py:305
  102.4 17.7 %collective-permute-start.10 = (bf16[320,512]{1,0:T(8,128)(2,1)S(1)}, bf16[320,512]{1,0:T(8,128)(2,1)}, u32[]{:S(2)}, u32[]{:S(2)}) collective-permute-start(bf16[320,512]{1,0:T(8,128)(2,1)S(1)} %collective-permute-done.9.refs_3_), channel_id=1, source_target_pairs={{0,1},{1,2},{2,3},{3,4},{4,5},{5,6},{6,7},{7,0},{8,9},{9,10},{10,1... | collective-permute-start | bytes 983048 | tf_op jit(solution)/shard_map/ppermute | solution.py:305
  104.4 17.8 %collective-permute-start.14 = (bf16[320,512]{1,0:T(8,128)(2,1)S(1)}, bf16[320,512]{1,0:T(8,128)(2,1)}, u32[]{:S(2)}, u32[]{:S(2)}) collective-permute-start(bf16[320,512]{1,0:T(8,128)(2,1)S(1)} %collective-permute-done.13.refs_13_.refs_15_), channel_id=1, source_target_pairs={{0,7},{1,0},{2,1},{3,2},{4,3},{5,4},{6,5},{7,6},{8,15},{9,8},{10,9... | collective-permute-start | bytes 983048 | tf_op jit(solution)/shard_map/ppermute | solution.py:308
  111.7 15.6 %collective-permute-start.18 = (bf16[320,512]{1,0:T(8,128)(2,1)S(1)}, bf16[320,512]{1,0:T(8,128)(2,1)}, u32[]{:S(2)}, u32[]{:S(2)}) collective-permute-start(bf16[320,512]{1,0:T(8,128)(2,1)S(1)} %collective-permute-done.17.refs_6_.refs_7_), channel_id=1, source_target_pairs={{0,7},{1,0},{2,1},{3,2},{4,3},{5,4},{6,5},{7,6},{8,15},{9,8},{10,9... | collective-permute-start | bytes 983048 | tf_op jit(solution)/shard_map/ppermute | solution.py:308
  115.7 11.6 %collective-permute-start.21 = (bf16[320,512]{1,0:T(8,128)(2,1)S(1)}, bf16[320,512]{1,0:T(8,128)(2,1)}, u32[]{:S(2)}, u32[]{:S(2)}) collective-permute-start(bf16[320,512]{1,0:T(8,128)(2,1)S(1)} %collective-permute-done.20.refs_10_.refs_11_), channel_id=1, source_target_pairs={{0,1},{1,2},{2,3},{3,4},{4,5},{5,6},{6,7},{7,0},{8,9},{9,10},{10,1... | collective-permute-start | bytes 983048 | tf_op jit(solution)/shard_map/ppermute | solution.py:305
  118.3 46.8 %collective-permute-start.29 = (bf16[2048,256]{1,0:T(8,128)(2,1)}, bf16[2048,256]{1,0:T(8,128)(2,1)}, u32[]{:S(2)}, u32[]{:S(2)}) collective-permute-start(bf16[2048,256]{1,0:T(8,128)(2,1)} %constant_dynamic-update-slice_fusion.refs_9_), channel_id=1, source_target_pairs={{0,512},{512,0},{1,513},{513,1},{2,514},{514,2},{3,515},{515,3},{4... | collective-permute-start | bytes 3145736 | tf_op jit(solution)/shard_map/ppermute | solution.py:287
  120.2 13.9 %collective-permute-start.11 = (bf16[320,512]{1,0:T(8,128)(2,1)}, bf16[320,512]{1,0:T(8,128)(2,1)}, u32[]{:S(2)}, u32[]{:S(2)}) collective-permute-start(bf16[320,512]{1,0:T(8,128)(2,1)} %collective-permute-done.10.refs_4_), channel_id=1, source_target_pairs={{0,1},{1,2},{2,3},{3,4},{4,5},{5,6},{6,7},{7,0},{8,9},{9,10},{10,1... | collective-permute-start | bytes 983048 | tf_op jit(solution)/shard_map/ppermute | solution.py:305
  122.1 13.1 %collective-permute-start.15 = (bf16[320,512]{1,0:T(8,128)(2,1)}, bf16[320,512]{1,0:T(8,128)(2,1)}, u32[]{:S(2)}, u32[]{:S(2)}) collective-permute-start(bf16[320,512]{1,0:T(8,128)(2,1)} %collective-permute-done.14.refs_12_.refs_14_), channel_id=1, source_target_pairs={{0,7},{1,0},{2,1},{3,2},{4,3},{5,4},{6,5},{7,6},{8,15},{9,8},{10,9... | collective-permute-start | bytes 983048 | tf_op jit(solution)/shard_map/ppermute | solution.py:308
  136.7 9.7 %collective-permute-start.22 = (bf16[320,256]{1,0:T(8,128)(2,1)S(1)}, bf16[320,256]{1,0:T(8,128)(2,1)S(1)}, u32[]{:S(2)}, u32[]{:S(2)}) collective-permute-start(bf16[320,256]{1,0:T(8,128)(2,1)S(1)} %get-tuple-element.85.refs_1_.refs_17_), channel_id=1, source_target_pairs={{0,1},{1,2},{2,3},{3,4},{4,5},{5,6},{6,7},{7,0},{8,9},{9,10},{10,1... | collective-permute-start | bytes 491528 | tf_op jit(solution)/shard_map/ppermute | solution.py:305
  138.8 9.5 %collective-permute-start.26 = (bf16[320,256]{1,0:T(8,128)(2,1)S(1)}, bf16[320,256]{1,0:T(8,128)(2,1)S(1)}, u32[]{:S(2)}, u32[]{:S(2)}) collective-permute-start(bf16[320,256]{1,0:T(8,128)(2,1)S(1)} %get-tuple-element.85.refs_1_.refs_17_), channel_id=1, source_target_pairs={{0,7},{1,0},{2,1},{3,2},{4,3},{5,4},{6,5},{7,6},{8,15},{9,8},{10,9... | collective-permute-start | bytes 491528 | tf_op jit(solution)/shard_map/ppermute | solution.py:308
  146.3 8.4 %collective-permute-start.23 = (bf16[320,256]{1,0:T(8,128)(2,1)S(1)}, bf16[320,256]{1,0:T(8,128)(2,1)S(1)}, u32[]{:S(2)}, u32[]{:S(2)}) collective-permute-start(bf16[320,256]{1,0:T(8,128)(2,1)S(1)} %collective-permute-done.22.refs_2_), channel_id=1, source_target_pairs={{0,1},{1,2},{2,3},{3,4},{4,5},{5,6},{6,7},{7,0},{8,9},{9,10},{10,1... | collective-permute-start | bytes 491528 | tf_op jit(solution)/shard_map/ppermute | solution.py:305
  154.7 8.4 %collective-permute-start.24 = (bf16[320,256]{1,0:T(8,128)(2,1)S(1)}, bf16[320,256]{1,0:T(8,128)(2,1)S(1)}, u32[]{:S(2)}, u32[]{:S(2)}) collective-permute-start(bf16[320,256]{1,0:T(8,128)(2,1)S(1)} %collective-permute-done.23.refs_3_), channel_id=1, source_target_pairs={{0,1},{1,2},{2,3},{3,4},{4,5},{5,6},{6,7},{7,0},{8,9},{9,10},{10,1... | collective-permute-start | bytes 491528 | tf_op jit(solution)/shard_map/ppermute | solution.py:305
  156.7 8.4 %collective-permute-start.28 = (bf16[320,256]{1,0:T(8,128)(2,1)S(1)}, bf16[320,256]{1,0:T(8,128)(2,1)S(1)}, u32[]{:S(2)}, u32[]{:S(2)}) collective-permute-start(bf16[320,256]{1,0:T(8,128)(2,1)S(1)} %collective-permute-done.27.refs_7_), channel_id=1, source_target_pairs={{0,7},{1,0},{2,1},{3,2},{4,3},{5,4},{6,5},{7,6},{8,15},{9,8},{10,9... | collective-permute-start | bytes 491528 | tf_op jit(solution)/shard_map/ppermute | solution.py:308
  174.8 37.4 %all-to-all-start.1 = ((bf16[64,24,128]{2,1,0:T(8,128)(2,1)}), bf16[64,24,128]{2,1,0:T(8,128)(2,1)}, u32[]{:S(2)}, u32[]{:S(2)}) async-start(bf16[64,24,128]{2,1,0:T(8,128)(2,1)} %bitcast.18), calls=%async_computation.1 | async-start | bytes 786432 | tf_op jit(solution)/shard_map/all_to_all | solution.py:348
  194.8 20.3 %collective-permute-start.30 = (bf16[2048,384]{1,0:T(8,128)(2,1)}, bf16[2048,384]{1,0:T(8,128)(2,1)}, u32[]{:S(2)}, u32[]{:S(2)}) collective-permute-start(bf16[2048,384]{1,0:T(8,128)(2,1)} %grads.2), channel_id=1, source_target_pairs={{0,512},{512,0},{1,513},{513,1},{2,514},{514,2},{3,515},{515,3},{4... | collective-permute-start | bytes 4718600 | tf_op jit(solution)/shard_map/ppermute | solution.py:361
  (13 other events, 200.4 us)
Sparse Core Ops, SparseCore 0:
  35.6 25.9 all-gather.2

commit v5 on v4

--- a/solution.py
+++ b/solution.py
@@ -18,19 +18,24 @@
     )
 
 
-def local_call(kernel, name, scalars, operands, outs, scratch=(), flops=0, vmem=24):
+HBM = pl.BlockSpec(memory_space=pltpu.HBM)
+
+
+def local_call(kernel, name, scalars, operands, outs, scratch=(), flops=0, far=(), vmem=24):
     out_specs = jax.tree.map(lambda o: whole(o.shape), outs)
     return pl.pallas_call(
         kernel,
         grid=(1,),
-        in_specs=[pl.BlockSpec(memory_space=pltpu.SMEM)] + [whole(o.shape) for o in operands],
+        in_specs=[pl.BlockSpec(memory_space=pltpu.SMEM)]
+        + [whole(o.shape) for o in operands]
+        + [HBM] * len(far),
         out_specs=out_specs,
         out_shape=outs,
         scratch_shapes=list(scratch),
         cost_estimate=pl.CostEstimate(flops=flops, bytes_accessed=1 << 20, transcendentals=0),
         compiler_params=pltpu.CompilerParams(vmem_limit_bytes=vmem << 20),
         name=name,
-    )(scalars, *operands)
+    )(scalars, *operands, *far)
 
 
 def transposed_dot(left, right):
@@ -116,27 +121,48 @@
             dy_ref[of, cols] = flat[pl.ds(at + chunks, owners, stride=stretch), :].astype(BF16)
 
 
-def weights_at(parts, distance, position, width, weights):
+def bundle_kernel(_, *refs):
+    pieces, weights, out = refs[:-4], refs[-4:-1], refs[-1]
+    sub, wide = pieces[0].shape
+    hid = weights[0].shape[1]
+    for i, piece in enumerate(pieces):
+        out[i * sub : (i + 1) * sub, :wide] = piece[...]
+    for i, weight in enumerate(weights):
+        out[:, wide + i * hid : wide + (i + 1) * hid] = weight[...]
+
+
+def fetch(bundles, columns, held, sems):
+    copies = [
+        pltpu.make_async_copy(bundle.at[:, columns], held.at[i], sems.at[i])
+        for i, bundle in enumerate(bundles)
+    ]
+    for copy in copies:
+        copy.start()
+    for copy in copies:
+        copy.wait()
+
+
+def weights_at(parts, distance, position, width, held):
     per_half = parts // 2
     source = lax.rem(position[0] - distance + parts, parts)
     of = pl.ds(pl.multiple_of(lax.rem(source, per_half) * width, width), width)
-    half = source // per_half
-    return jnp.concatenate([weights[half, i, of, :] for i in range(3)], axis=1)
+    return held[jnp.where(source // per_half == position[1], 0, 1), of, :]
 
 
 def forward_most(parts, distances, middle, position, *refs):
     xs, dys = refs[: len(distances)], refs[len(distances) : 2 * len(distances)]
-    weights, out, mid_ref = refs[2 * len(distances) :]
+    own_bundle, other_bundle, out, mid_ref, held, sems = refs[2 * len(distances) :]
     rows, width = xs[0].shape
     hid = out.shape[1] // 3
+    fetch((own_bundle, other_bundle), pl.ds(2 * hid, 3 * hid), held, sems)
     acc, back = jnp.zeros((rows, 2 * hid), F32), jnp.zeros((rows, hid), F32)
     for d, x, dy in zip(distances, xs, dys):
-        piece = weights_at(parts, d, position, width, weights)
+        piece = weights_at(parts, d, position, width, held)
         acc = acc + jnp.dot(x[...], piece[:, : 2 * hid], preferred_element_type=F32)
         back = back + jnp.dot(dy[...], piece[:, 2 * hid :], preferred_element_type=F32)
     out[:, : 2 * hid] = acc
     out[:, 2 * hid :] = back
-    mid_ref[...] = weights_at(parts, middle, position, width, weights)
+    mid_ref[...] = weights_at(parts, middle, position, width, held)
 
 
 def forward_last(_, x_ref, dy_ref, piece_ref, begun, both_ref, hidden_ref):
@@ -156,10 +182,11 @@
 
 
 def back_kernel(parts, capacity, position, *refs):
-    blocks, (own_ref, other_ref, out_ref, flat) = refs[:parts], refs[parts:]
+    blocks, (own_bundle, other_bundle, out_ref, flat, held, sems) = refs[:parts], refs[parts:]
+    fetch((own_bundle, other_bundle), pl.ds(0, held.shape[2]), held, sems)
     place, core = position[0], position[1]
     per_half = parts // 2
-    sub = own_ref.shape[0] // parts
+    sub = held.shape[1] // parts
     rows, width = blocks[0].shape[0], 2 * sub
     owners, chunks = rows // capacity, width // LANES
     stretch = flat.shape[0] // owners
@@ -170,11 +197,11 @@
         block = blocks[d][...]
         at = pl.multiple_of(lax.rem(d + per_half * ahead, parts) * sub, sub)
         own = own + lax.dot_general(
-            block, own_ref[pl.ds(at, sub), :], contract, preferred_element_type=F32
+            block, held[0, pl.ds(at, sub), :], contract, preferred_element_type=F32
         )
         at = pl.multiple_of(lax.rem(d + per_half * (1 - ahead), parts) * sub, sub)
         other = other + lax.dot_general(
-            block, other_ref[pl.ds(at, sub), :], contract, preferred_element_type=F32
+            block, held[1, pl.ds(at, sub), :], contract, preferred_element_type=F32
         )
     first = core == 0
     total = jnp.concatenate((jnp.where(first, own, other), jnp.where(first, other, own)), axis=1)
@@ -216,14 +243,11 @@
             into = pl.ds(pl.multiple_of(lax.rem(source, per_half) * width, width), width)
             both = transposed_dot(xs[d][...], both_ref[...]).astype(BF16)
             down = transposed_dot(dys[d][...], hidden_ref[...]).astype(BF16)
-            if len(rest) == 1:
-                rest[0][into, : 2 * hid] = both
-                rest[0][into, 2 * hid :] = down
-            else:
-                received, outs = rest[0], rest[1:]
-                for i, share in enumerate((both[:, :hid], both[:, hid:], down)):
-                    more = received[into, i * hid : (i + 1) * hid].astype(F32)
-                    outs[i][0, into, :] = (share.astype(F32) + more).astype(BF16)
+            for i, share in enumerate((both[:, :hid], both[:, hid:], down)):
+                if len(rest) > 3:
+                    more = rest[i][0, into, :].astype(F32)
+                    share = (share.astype(F32) + more).astype(BF16)
+                rest[i - 3][0, into, :] = share
 
 
 def grads(place, which, operands, outs):
@@ -266,8 +290,6 @@
     flat = lax.all_to_all(
         flat.reshape(owners, -1, LANES), peers, split_axis=0, concat_axis=0, tiled=True
     )
-    weights = lax.all_gather(jnp.stack(own_weights), "dp")
-
     sub = width // 2
     turned = []
     for k in range(parts):
@@ -283,8 +305,14 @@
                 perm.append((h * parts + p, t // half * parts + h * half + t % half))
         turned.append(lax.ppermute(piece, ("dp", "y"), perm))
     flat, turned = lax.optimization_barrier((flat, turned))
-    turned = jnp.concatenate(turned)
-    turned_other = lax.ppermute(turned, "dp", swap)
+    bundle = local_call(
+        bundle_kernel,
+        "bundle",
+        position,
+        (*turned, *own_weights),
+        jax.ShapeDtypeStruct((model // 2, 5 * hid), BF16),
+    )
+    bundles = (bundle, lax.ppermute(bundle, "dp", swap))
 
     flat = flat.reshape(-1, LANES)
     pair = jax.ShapeDtypeStruct((rows, width), BF16)
@@ -315,12 +343,14 @@
         lambda *refs: forward_most(parts, most, half, *refs),
         "forward_most",
         position,
-        (*[xs[d] for d in most], *[dys[d] for d in most], weights),
+        (*[xs[d] for d in most], *[dys[d] for d in most]),
         (
             jax.ShapeDtypeStruct((rows, 3 * hid), F32),
             jax.ShapeDtypeStruct((width, 3 * hid), BF16),
         ),
+        [pltpu.VMEM((2, model // 2, 3 * hid), BF16), pltpu.SemaphoreType.DMA((2,))],
         flops=2 * rows * model * 3 * hid,
+        far=bundles,
     )
     d_both, hidden = local_call(
         forward_last,
@@ -339,15 +369,26 @@
         lambda *refs: back_kernel(parts, capacity, *refs),
         "back",
         position,
-        (*ring(d_both, True), turned, turned_other),
+        ring(d_both, True),
         jax.ShapeDtypeStruct((owners * stretch, LANES), BF16),
-        [pltpu.VMEM((owners * stretch, LANES), F32)],
+        [
+            pltpu.VMEM((owners * stretch, LANES), F32),
+            pltpu.VMEM((2, model // 2, 2 * hid), BF16),
+            pltpu.SemaphoreType.DMA((2,)),
+        ],
         flops=4 * rows * width * parts * hid,
+        far=bundles,
     )
     d_rows, operands = lax.optimization_barrier((d_rows, (xs, dys, d_both, hidden)))
     returned = lax.all_to_all(
         d_rows.reshape(owners, -1, LANES), peers, split_axis=0, concat_axis=0, tiled=True
     )
+    outs = (jax.ShapeDtypeStruct(gate_weight.shape, BF16),) * 3
+    received = [
+        lax.ppermute(share, "dp", swap) for share in grads(place, 1 - core, operands, outs)
+    ]
+    final = grads(place, core, (*operands, *received), outs)
+    returned, final = lax.optimization_barrier((returned, final))
     d_tokens = local_call(
         lambda *refs: combine_kernel(capacity, *refs),
         "combine",
@@ -357,10 +398,7 @@
         [pltpu.VMEM((owners * stretch, LANES), F32), pltpu.VMEM((rows, width), BF16)],
         flops=1 << 37,
     )
-    send = jax.ShapeDtypeStruct((model // 2, 3 * hid), BF16)
-    received = lax.ppermute(grads(place, 1 - core, operands, send), "dp", swap)
-    grad = jax.ShapeDtypeStruct(gate_weight.shape, BF16)
-    return d_tokens, *grads(place, core, (*operands, received), (grad, grad, grad))
+    return d_tokens, *final
 
 
 def solution(mesh):

time: 228 us -> 209 us (0.917)
  between operations: 14.9 us -> 1.47 us
  waiting for transfers between devices: 33.9 us -> 28.6 us
  Pallas kernels: 21.5 us -> 17.3 us
  starting transfers between devices: 145 us -> 148 us
    all_to_all x1, waiting for transfers between devices: 15.3 us -> 0.01 us  [shards(): lax.all_to_all(d_rows.reshape(owners, -1, LANES), peers, split_axis=0, co...]
    ppermute x10, starting transfers between devices: 49.4 us -> 38.3 us  [ring(): left = lax.ppermute(left, 'y', shift('y', -1))]
    ppermute x11, starting transfers between devices: 22.3 us -> 30.6 us  [ring(): right = lax.ppermute(right, 'y', shift('y', 1))]
    ppermute x2 -> x4, starting transfers between devices: 4 us -> 9.2 us  [the longest x3 6.25 us: shards(): lax.ppermute(share, 'dp', swap)]
    ppermute x10, waiting for transfers between devices: 1.11 us -> 6.06 us  [ring(): left = lax.ppermute(left, 'y', shift('y', -1))]
    pallas_call x7 -> x8, Pallas kernels: 19.1 us -> 14.8 us  [local_call(): pl.pallas_call(kernel, grid=(1,), in_specs=[pl.BlockSpec(memory_space=plt...]
    ppermute x11, waiting for transfers between devices: 13.6 us -> 16.5 us  [ring(): right = lax.ppermute(right, 'y', shift('y', 1))]
    unnamed x29 -> x44, local copies, waits for them, and re-layouts: 9.09 us -> 9.02 us
  transfers between devices with their start and end apart: 34 -> 35, of which waited for: 9 -> 15; matrix products, arithmetic and copies ran while one was open for 3% -> 1% of each run, Pallas kernels for 5% -> 5%
where the time goes in v5:
time: 209 us; the launch traced here: 206 us
  starting transfers between devices  148 us (71%)
  waiting for transfers between devices  28.6 us (14%)
  Pallas kernels  17.3 us (8%)
  local copies, waits for them, and re-layouts  9.13 us (4%)
  other arithmetic  2.25 us (1%)
    ppermute x10, starting transfers between devices, ring(): left = lax.ppermute(left, 'y', shift('y', -1))  38.3 us
    ppermute x8, starting transfers between devices, shards(): turned.append(lax.ppermute(piece, ('dp', 'y'), perm))  31.8 us
    ppermute x11, starting transfers between devices, ring(): right = lax.ppermute(right, 'y', shift('y', 1))  30.6 us
    all_to_all x1, starting transfers between devices, shards(): lax.all_to_all(flat.reshape(owners, -1, LANES), peers, split_axis=0, conc...  22.5 us
    ppermute x11, waiting for transfers between devices, ring(): right = lax.ppermute(right, 'y', shift('y', 1))  16.5 us
    all_to_all x1, starting transfers between devices, shards(): lax.all_to_all(d_rows.reshape(owners, -1, LANES), peers, split_axis=0, co...  15.3 us
    pallas_call x8, Pallas kernels, local_call(): pl.pallas_call(kernel, grid=(1,), in_specs=[pl.BlockSpec(memory_space=plt...  14.8 us
    unnamed x44, local copies, waits for them, and re-layouts  9.02 us
  transfers between devices with their start and end apart: 35, of which 15 were waited for; matrix products, arithmetic and copies ran while one was open for 1% of the time, Pallas kernels for 5%

profile of v5, /device:TPU:6, one launch (start us, length us, event | category | flops | bytes accessed | tf_op | source)
XLA Modules:
  0.0 206.4 jit_solution(8251888951395182130)
XLA Ops:
  0.7 2.4 %pack.1 = (bf16[2560,128]{1,0:T(8,128)(2,1)}, bf16[320,32]{1,0:T(8,128)(2,1)}) custom-call(s32[1]{0:T(128)} %bitcast.refs_0_, s32[8,32]{1,0:T(8,128)} %bitcast.20, bf16[8,32]{1,0:T(8,128)(2,1)} %bitcast.21, bf16[32,4096]{1,0:T(8,128)(2,1)} %refs_3_.1, bf16[32,4096]{1,0:T(8,128)(2,1)} %refs_4_.1), custom_call_target="tpu_custom_call" | custom-call | tf_op jit(solution)/shard_map/pack/pallas_call | solution.py:92
  3.1 22.5 %all-to-all-start = ((bf16[64,40,128]{2,1,0:T(8,128)(2,1)}), bf16[64,40,128]{2,1,0:T(8,128)(2,1)S(1)}, u32[]{:S(2)}, u32[]{:S(2)}) async-start(bf16[64,40,128]{2,1,0:T(8,128)(2,1)} %bitcast.19), calls=%async_computation | async-start | bytes 1310720 | tf_op jit(solution)/shard_map/all_to_all | solution.py:290
  26.7 3.5 %collective-permute-start.1 = (bf16[256,256]{1,0:T(8,128)(2,1)S(1)}, bf16[256,256]{1,0:T(8,128)(2,1)S(1)}, u32[]{:S(2)}, u32[]{:S(2)}) collective-permute-start(bf16[256,256]{1,0:T(8,128)(2,1)S(1)} %pad_maximum_fusion.1), channel_id=1, source_target_pairs={{0,1},{1,2},{2,3},{3,512},{4,513},{5,514},{6,515},{7,0},{512,5},{5... | collective-permute-start | bytes 393224 | tf_op jit(solution)/shard_map/ppermute | solution.py:306
  30.2 4.5 %collective-permute-start.2 = (bf16[256,256]{1,0:T(8,128)(2,1)S(1)}, bf16[256,256]{1,0:T(8,128)(2,1)S(1)}, u32[]{:S(2)}, u32[]{:S(2)}) collective-permute-start(bf16[256,256]{1,0:T(8,128)(2,1)S(1)} %pad_maximum_fusion.2), channel_id=1, source_target_pairs={{0,2},{1,3},{2,512},{3,513},{4,514},{5,515},{6,0},{7,1},{512,6},{5... | collective-permute-start | bytes 393224 | tf_op jit(solution)/shard_map/ppermute | solution.py:306
  34.7 8.4 %collective-permute-start.3 = (bf16[256,256]{1,0:T(8,128)(2,1)S(1)}, bf16[256,256]{1,0:T(8,128)(2,1)S(1)}, u32[]{:S(2)}, u32[]{:S(2)}) collective-permute-start(bf16[256,256]{1,0:T(8,128)(2,1)S(1)} %pad_maximum_fusion.3), channel_id=1, source_target_pairs={{0,3},{1,512},{2,513},{3,514},{4,515},{5,0},{6,1},{7,2},{512,7},{5... | collective-permute-start | bytes 393224 | tf_op jit(solution)/shard_map/ppermute | solution.py:306
  47.0 4.8 %collective-permute-start.5 = (bf16[256,256]{1,0:T(8,128)(2,1)}, bf16[256,256]{1,0:T(8,128)(2,1)S(1)}, u32[]{:S(2)}, u32[]{:S(2)}) collective-permute-start(bf16[256,256]{1,0:T(8,128)(2,1)} %pad_maximum_fusion.5), channel_id=1, source_target_pairs={{0,513},{1,514},{2,515},{3,0},{4,1},{5,2},{6,3},{7,512},{512,517},... | collective-permute-start | bytes 393224 | tf_op jit(solution)/shard_map/ppermute | solution.py:306
  51.8 3.0 %collective-permute-start.6 = (bf16[256,256]{1,0:T(8,128)(2,1)}, bf16[256,256]{1,0:T(8,128)(2,1)S(1)}, u32[]{:S(2)}, u32[]{:S(2)}) collective-permute-start(bf16[256,256]{1,0:T(8,128)(2,1)} %pad_maximum_fusion.6), channel_id=1, source_target_pairs={{0,514},{1,515},{2,0},{3,1},{4,2},{5,3},{6,512},{7,513},{512,518},... | collective-permute-start | bytes 393224 | tf_op jit(solution)/shard_map/ppermute | solution.py:306
  54.8 5.1 %collective-permute-start.7 = (bf16[256,256]{1,0:T(8,128)(2,1)S(1)}, bf16[256,256]{1,0:T(8,128)(2,1)S(1)}, u32[]{:S(2)}, u32[]{:S(2)}) collective-permute-start(bf16[256,256]{1,0:T(8,128)(2,1)S(1)} %pad_maximum_fusion.7), channel_id=1, source_target_pairs={{0,515},{1,0},{2,1},{3,2},{4,3},{5,512},{6,513},{7,514},{512,519},... | collective-permute-start | bytes 393224 | tf_op jit(solution)/shard_map/ppermute | solution.py:306
  60.0 2.8 %collective-permute-done.6.refs_6_ = bf16[256,256]{1,0:T(8,128)(2,1)S(1)} collective-permute-done((bf16[256,256]{1,0:T(8,128)(2,1)}, bf16[256,256]{1,0:T(8,128)(2,1)S(1)}, u32[]{:S(2)}, u32[]{:S(2)}) %collective-permute-start.6) | collective-permute-done | bytes 131104 | tf_op jit(solution)/shard_map/ppermute | solution.py:306
  65.1 3.0 %collective-permute-start.22 = (bf16[2048,640]{1,0:T(8,128)(2,1)S(1)}, bf16[2048,640]{1,0:T(8,128)(2,1)S(1)}, u32[]{:S(2)}, u32[]{:S(2)}) collective-permute-start(bf16[2048,640]{1,0:T(8,128)(2,1)S(1)} %bundle.1.refs_15_.refs_9_), channel_id=1, source_target_pairs={{0,512},{512,0},{1,513},{513,1},{2,514},{514,2},{3,515},{515,3},{4... | collective-permute-start | bytes 7864328 | tf_op jit(solution)/shard_map/ppermute | solution.py:315
  69.0 6.0 %collective-permute-start.8 = (bf16[320,512]{1,0:T(8,128)(2,1)S(1)}, bf16[320,512]{1,0:T(8,128)(2,1)S(1)}, u32[]{:S(2)}, u32[]{:S(2)}) collective-permute-start(bf16[320,512]{1,0:T(8,128)(2,1)S(1)} %get-tuple-element.75.refs_1_), channel_id=1, source_target_pairs={{0,1},{1,2},{2,3},{3,4},{4,5},{5,6},{6,7},{7,0},{8,9},{9,10},{10,1... | collective-permute-start | bytes 983048 | tf_op jit(solution)/shard_map/ppermute | solution.py:333
  77.0 2.8 %collective-permute-start.16 = (bf16[320,512]{1,0:T(8,128)(2,1)S(1)}, bf16[320,512]{1,0:T(8,128)(2,1)S(1)}, u32[]{:S(2)}, u32[]{:S(2)}) collective-permute-start(bf16[320,512]{1,0:T(8,128)(2,1)S(1)} %get-tuple-element.75.refs_1_), channel_id=1, source_target_pairs={{0,7},{1,0},{2,1},{3,2},{4,3},{5,4},{6,5},{7,6},{8,15},{9,8},{10,9... | collective-permute-start | bytes 983048 | tf_op jit(solution)/shard_map/ppermute | solution.py:336
  79.8 3.0 %collective-permute-start.19 = (bf16[320,512]{1,0:T(8,128)(2,1)S(1)}, bf16[320,512]{1,0:T(8,128)(2,1)S(1)}, u32[]{:S(2)}, u32[]{:S(2)}) collective-permute-start(bf16[320,512]{1,0:T(8,128)(2,1)S(1)} %get-tuple-element.83.refs_8_.refs_9_), channel_id=1, source_target_pairs={{0,1},{1,2},{2,3},{3,4},{4,5},{5,6},{6,7},{7,0},{8,9},{9,10},{10,1... | collective-permute-start | bytes 983048 | tf_op jit(solution)/shard_map/ppermute | solution.py:333
  82.8 3.9 %collective-permute-start.9 = (bf16[320,512]{1,0:T(8,128)(2,1)S(1)}, bf16[320,512]{1,0:T(8,128)(2,1)S(1)}, u32[]{:S(2)}, u32[]{:S(2)}) collective-permute-start(bf16[320,512]{1,0:T(8,128)(2,1)S(1)} %collective-permute-done.8.refs_2_), channel_id=1, source_target_pairs={{0,1},{1,2},{2,3},{3,4},{4,5},{5,6},{6,7},{7,0},{8,9},{9,10},{10,1... | collective-permute-start | bytes 983048 | tf_op jit(solution)/shard_map/ppermute | solution.py:333
  87.5 3.1 %collective-permute-start.13 = (bf16[320,512]{1,0:T(8,128)(2,1)S(1)}, bf16[320,512]{1,0:T(8,128)(2,1)S(1)}, u32[]{:S(2)}, u32[]{:S(2)}) collective-permute-start(bf16[320,512]{1,0:T(8,128)(2,1)S(1)} %collective-permute-done.12.refs_14_.refs_16_), channel_id=1, source_target_pairs={{0,7},{1,0},{2,1},{3,2},{4,3},{5,4},{6,5},{7,6},{8,15},{9,8},{10,9... | collective-permute-start | bytes 983048 | tf_op jit(solution)/shard_map/ppermute | solution.py:336
  90.6 3.9 %collective-permute-done.16.refs_7_.refs_8_ = bf16[320,512]{1,0:T(8,128)(2,1)S(1)} collective-permute-done((bf16[320,512]{1,0:T(8,128)(2,1)S(1)}, bf16[320,512]{1,0:T(8,128)(2,1)S(1)}, u32[]{:S(2)}, u32[]{:S(2)}) %collective-permute-start.16) | collective-permute-done | bytes 327712 | tf_op jit(solution)/shard_map/ppermute | solution.py:336
  94.6 3.1 %collective-permute-start.17 = (bf16[320,512]{1,0:T(8,128)(2,1)S(1)}, bf16[320,512]{1,0:T(8,128)(2,1)S(1)}, u32[]{:S(2)}, u32[]{:S(2)}) collective-permute-start(bf16[320,512]{1,0:T(8,128)(2,1)S(1)} %collective-permute-done.16.refs_7_.refs_8_), channel_id=1, source_target_pairs={{0,7},{1,0},{2,1},{3,2},{4,3},{5,4},{6,5},{7,6},{8,15},{9,8},{10,9... | collective-permute-start | bytes 983048 | tf_op jit(solution)/shard_map/ppermute | solution.py:336
  97.7 2.7 %collective-permute-start.20 = (bf16[320,512]{1,0:T(8,128)(2,1)S(1)}, bf16[320,512]{1,0:T(8,128)(2,1)S(1)}, u32[]{:S(2)}, u32[]{:S(2)}) collective-permute-start(bf16[320,512]{1,0:T(8,128)(2,1)S(1)} %collective-permute-done.19.refs_9_.refs_10_), channel_id=1, source_target_pairs={{0,1},{1,2},{2,3},{3,4},{4,5},{5,6},{6,7},{7,0},{8,9},{9,10},{10,1... | collective-permute-start | bytes 983048 | tf_op jit(solution)/shard_map/ppermute | solution.py:333
  100.4 2.3 %collective-permute-start.10 = (bf16[320,512]{1,0:T(8,128)(2,1)S(1)}, bf16[320,512]{1,0:T(8,128)(2,1)S(1)}, u32[]{:S(2)}, u32[]{:S(2)}) collective-permute-start(bf16[320,512]{1,0:T(8,128)(2,1)S(1)} %collective-permute-done.9.refs_3_), channel_id=1, source_target_pairs={{0,1},{1,2},{2,3},{3,4},{4,5},{5,6},{6,7},{7,0},{8,9},{9,10},{10,1... | collective-permute-start | bytes 983048 | tf_op jit(solution)/shard_map/ppermute | solution.py:333
  102.7 4.8 %collective-permute-start.14 = (bf16[320,512]{1,0:T(8,128)(2,1)S(1)}, bf16[320,512]{1,0:T(8,128)(2,1)S(1)}, u32[]{:S(2)}, u32[]{:S(2)}) collective-permute-start(bf16[320,512]{1,0:T(8,128)(2,1)S(1)} %collective-permute-done.13.refs_13_.refs_15_), channel_id=1, source_target_pairs={{0,7},{1,0},{2,1},{3,2},{4,3},{5,4},{6,5},{7,6},{8,15},{9,8},{10,9... | collective-permute-start | bytes 983048 | tf_op jit(solution)/shard_map/ppermute | solution.py:336
  111.4 3.0 %collective-permute-start.21 = (bf16[320,512]{1,0:T(8,128)(2,1)S(1)}, bf16[320,512]{1,0:T(8,128)(2,1)S(1)}, u32[]{:S(2)}, u32[]{:S(2)}) collective-permute-start(bf16[320,512]{1,0:T(8,128)(2,1)S(1)} %collective-permute-done.20.refs_10_.refs_11_), channel_id=1, source_target_pairs={{0,1},{1,2},{2,3},{3,4},{4,5},{5,6},{6,7},{7,0},{8,9},{9,10},{10,1... | collective-permute-start | bytes 983048 | tf_op jit(solution)/shard_map/ppermute | solution.py:333
  117.3 5.1 %collective-permute-start.15 = (bf16[320,512]{1,0:T(8,128)(2,1)S(1)}, bf16[320,512]{1,0:T(8,128)(2,1)S(1)}, u32[]{:S(2)}, u32[]{:S(2)}) collective-permute-start(bf16[320,512]{1,0:T(8,128)(2,1)S(1)} %collective-permute-done.14.refs_12_.refs_14_), channel_id=1, source_target_pairs={{0,7},{1,0},{2,1},{3,2},{4,3},{5,4},{6,5},{7,6},{8,15},{9,8},{10,9... | collective-permute-start | bytes 983048 | tf_op jit(solution)/shard_map/ppermute | solution.py:336
  122.6 2.5 %collective-permute-done.21.refs_11_.refs_12_ = bf16[320,512]{1,0:T(8,128)(2,1)S(1)} collective-permute-done((bf16[320,512]{1,0:T(8,128)(2,1)S(1)}, bf16[320,512]{1,0:T(8,128)(2,1)S(1)}, u32[]{:S(2)}, u32[]{:S(2)}) %collective-permute-start.21) | collective-permute-done | bytes 327712 | tf_op jit(solution)/shard_map/ppermute | solution.py:333
  125.2 2.3 %forward_most.1 = (f32[320,384]{1,0:T(8,128)S(1)}, bf16[512,384]{1,0:T(8,128)(2,1)S(1)}) custom-call(s32[2]{0:T(128)S(1)} %pad_add_fusion.refs_0_._, bf16[320,512]{1,0:T(8,128)(2,1)S(1)} %get-tuple-element.75.refs_1_, bf16[320,512]{1,0:T(8,128)(2,1)S(1)} %collective-permute-done.8.refs_2_, bf16[320,512]{1,0:T(8,128)(2,1)S(1)} %collective-permute-done.9.refs_3_, ...), custom_call_target="tpu_custom_call" | custom-call | flops 1006632960 | bytes 1048576 | tf_op jit(solution)/shard_map/forward_most/pallas_call | solution.py:26
  132.9 5.1 %collective-permute-start.27 = (bf16[320,256]{1,0:T(8,128)(2,1)S(1)}, bf16[320,256]{1,0:T(8,128)(2,1)S(1)}, u32[]{:S(2)}, u32[]{:S(2)}) collective-permute-start(bf16[320,256]{1,0:T(8,128)(2,1)S(1)} %get-tuple-element.91.refs_1_.refs_17_), channel_id=1, source_target_pairs={{0,7},{1,0},{2,1},{3,2},{4,3},{5,4},{6,5},{7,6},{8,15},{9,8},{10,9... | collective-permute-start | bytes 491528 | tf_op jit(solution)/shard_map/ppermute | solution.py:336
  141.3 5.1 %collective-permute-start.28 = (bf16[320,256]{1,0:T(8,128)(2,1)S(1)}, bf16[320,256]{1,0:T(8,128)(2,1)S(1)}, u32[]{:S(2)}, u32[]{:S(2)}) collective-permute-start(bf16[320,256]{1,0:T(8,128)(2,1)S(1)} %collective-permute-done.27.refs_8_), channel_id=1, source_target_pairs={{0,7},{1,0},{2,1},{3,2},{4,3},{5,4},{6,5},{7,6},{8,15},{9,8},{10,9... | collective-permute-start | bytes 491528 | tf_op jit(solution)/shard_map/ppermute | solution.py:336
  149.7 5.1 %collective-permute-start.29 = (bf16[320,256]{1,0:T(8,128)(2,1)S(1)}, bf16[320,256]{1,0:T(8,128)(2,1)S(1)}, u32[]{:S(2)}, u32[]{:S(2)}) collective-permute-start(bf16[320,256]{1,0:T(8,128)(2,1)S(1)} %collective-permute-done.28.refs_7_), channel_id=1, source_target_pairs={{0,7},{1,0},{2,1},{3,2},{4,3},{5,4},{6,5},{7,6},{8,15},{9,8},{10,9... | collective-permute-start | bytes 491528 | tf_op jit(solution)/shard_map/ppermute | solution.py:336
  158.1 6.5 %collective-permute-done.26.refs_5_ = bf16[320,256]{1,0:T(8,128)(2,1)S(1)} collective-permute-done((bf16[320,256]{1,0:T(8,128)(2,1)S(1)}, bf16[320,256]{1,0:T(8,128)(2,1)S(1)}, u32[]{:S(2)}, u32[]{:S(2)}) %collective-permute-start.26) | collective-permute-done | bytes 163872 | tf_op jit(solution)/shard_map/ppermute | solution.py:333
  167.0 15.3 %all-to-all-start.1 = ((bf16[64,24,128]{2,1,0:T(8,128)(2,1)}), bf16[64,24,128]{2,1,0:T(8,128)(2,1)}, u32[]{:S(2)}, u32[]{:S(2)}) async-start(bf16[64,24,128]{2,1,0:T(8,128)(2,1)} %bitcast.17), calls=%async_computation.1 | async-start | bytes 786432 | tf_op jit(solution)/shard_map/all_to_all | solution.py:383
  189.1 2.6 %grads.2 = (bf16[1,2048,128]{2,1,0:T(8,128)(2,1)S(1)}, bf16[1,2048,128]{2,1,0:T(8,128)(2,1)S(1)}, bf16[1,2048,128]{2,1,0:T(8,128)(2,1)S(1)}) custom-call(s32[2]{0:T(128)S(1)} %pad_add_fusion.1.refs_0_, bf16[320,512]{1,0:T(8,128)(2,1)S(1)} %get-tuple-element.75.refs_1_, bf16[320,512]{1,0:T(8,128)(2,1)S(1)} %collective-permute-done.8.refs_2_, ...), custom_call_target="tpu_custom_call" | custom-call | flops 503316480 | bytes 1048576 | tf_op jit(solution)/shard_map/grads/pallas_call | solution.py:26
  193.7 2.4 %collective-permute-start.31 = (bf16[1,2048,128]{2,1,0:T(8,128)(2,1)S(1)}, bf16[1,2048,128]{2,1,0:T(8,128)(2,1)S(1)}, u32[]{:S(2)}, u32[]{:S(2)}) collective-permute-start(bf16[1,2048,128]{2,1,0:T(8,128)(2,1)S(1)} %get-tuple-element.94), channel_id=1, source_target_pairs={{0,512},{512,0},{1,513},{513,1},{2,514},{514,2},{3,515},{515,3},{4... | collective-permute-start | bytes 1572872 | tf_op jit(solution)/shard_map/ppermute | solution.py:388
  199.9 3.6 %grads.3 = (bf16[1,2048,128]{2,1,0:T(8,128)(2,1)}, bf16[1,2048,128]{2,1,0:T(8,128)(2,1)}, bf16[1,2048,128]{2,1,0:T(8,128)(2,1)}) custom-call(s32[2]{0:T(128)S(1)} %pad_add_fusion.refs_0_._, bf16[320,512]{1,0:T(8,128)(2,1)S(1)} %get-tuple-element.75.refs_1_, bf16[320,512]{1,0:T(8,128)(2,1)S(1)} %collective-permute-done.8.refs_2_, ...), custom_call_target="tpu_custom_call" | custom-call | flops 503316480 | bytes 1048576 | tf_op jit(solution)/shard_map/grads/pallas_call | solution.py:26
  (102 shorter events, 50.6 us)
Async XLA Ops:
  3.1 61.1 %all-to-all-start = ((bf16[64,40,128]{2,1,0:T(8,128)(2,1)}), bf16[64,40,128]{2,1,0:T(8,128)(2,1)S(1)}, u32[]{:S(2)}, u32[]{:S(2)}) async-start(bf16[64,40,128]{2,1,0:T(8,128)(2,1)} %bitcast.19), calls=%async_computation | async-start | bytes 1310720 | tf_op jit(solution)/shard_map/all_to_all | solution.py:290
  26.0 21.1 %collective-permute-start = (bf16[256,256]{1,0:T(8,128)(2,1)S(1)}, bf16[256,256]{1,0:T(8,128)(2,1)S(1)}, u32[]{:S(2)}, u32[]{:S(2)}) collective-permute-start(bf16[256,256]{1,0:T(8,128)(2,1)S(1)} %pad_maximum_fusion), channel_id=1, source_target_pairs={{0,0},{1,1},{2,2},{3,3},{4,512},{5,513},{6,514},{7,515},{512,4},{5... | collective-permute-start | bytes 393224 | tf_op jit(solution)/shard_map/ppermute | solution.py:306
  26.7 25.2 %collective-permute-start.1 = (bf16[256,256]{1,0:T(8,128)(2,1)S(1)}, bf16[256,256]{1,0:T(8,128)(2,1)S(1)}, u32[]{:S(2)}, u32[]{:S(2)}) collective-permute-start(bf16[256,256]{1,0:T(8,128)(2,1)S(1)} %pad_maximum_fusion.1), channel_id=1, source_target_pairs={{0,1},{1,2},{2,3},{3,512},{4,513},{5,514},{6,515},{7,0},{512,5},{5... | collective-permute-start | bytes 393224 | tf_op jit(solution)/shard_map/ppermute | solution.py:306
  30.2 24.7 %collective-permute-start.2 = (bf16[256,256]{1,0:T(8,128)(2,1)S(1)}, bf16[256,256]{1,0:T(8,128)(2,1)S(1)}, u32[]{:S(2)}, u32[]{:S(2)}) collective-permute-start(bf16[256,256]{1,0:T(8,128)(2,1)S(1)} %pad_maximum_fusion.2), channel_id=1, source_target_pairs={{0,2},{1,3},{2,512},{3,513},{4,514},{5,515},{6,0},{7,1},{512,6},{5... | collective-permute-start | bytes 393224 | tf_op jit(solution)/shard_map/ppermute | solution.py:306
  34.7 25.3 %collective-permute-start.3 = (bf16[256,256]{1,0:T(8,128)(2,1)S(1)}, bf16[256,256]{1,0:T(8,128)(2,1)S(1)}, u32[]{:S(2)}, u32[]{:S(2)}) collective-permute-start(bf16[256,256]{1,0:T(8,128)(2,1)S(1)} %pad_maximum_fusion.3), channel_id=1, source_target_pairs={{0,3},{1,512},{2,513},{3,514},{4,515},{5,0},{6,1},{7,2},{512,7},{5... | collective-permute-start | bytes 393224 | tf_op jit(solution)/shard_map/ppermute | solution.py:306
  43.7 16.3 %collective-permute-start.4 = (bf16[256,256]{1,0:T(8,128)(2,1)}, bf16[256,256]{1,0:T(8,128)(2,1)S(1)}, u32[]{:S(2)}, u32[]{:S(2)}) collective-permute-start(bf16[256,256]{1,0:T(8,128)(2,1)} %pad_maximum_fusion.4), channel_id=1, source_target_pairs={{0,512},{1,513},{2,514},{3,515},{4,0},{5,1},{6,2},{7,3},{512,516},... | collective-permute-start | bytes 393224 | tf_op jit(solution)/shard_map/ppermute | solution.py:306
  47.0 13.0 %collective-permute-start.5 = (bf16[256,256]{1,0:T(8,128)(2,1)}, bf16[256,256]{1,0:T(8,128)(2,1)S(1)}, u32[]{:S(2)}, u32[]{:S(2)}) collective-permute-start(bf16[256,256]{1,0:T(8,128)(2,1)} %pad_maximum_fusion.5), channel_id=1, source_target_pairs={{0,513},{1,514},{2,515},{3,0},{4,1},{5,2},{6,3},{7,512},{512,517},... | collective-permute-start | bytes 393224 | tf_op jit(solution)/shard_map/ppermute | solution.py:306
  51.8 11.0 %collective-permute-start.6 = (bf16[256,256]{1,0:T(8,128)(2,1)}, bf16[256,256]{1,0:T(8,128)(2,1)S(1)}, u32[]{:S(2)}, u32[]{:S(2)}) collective-permute-start(bf16[256,256]{1,0:T(8,128)(2,1)} %pad_maximum_fusion.6), channel_id=1, source_target_pairs={{0,514},{1,515},{2,0},{3,1},{4,2},{5,3},{6,512},{7,513},{512,518},... | collective-permute-start | bytes 393224 | tf_op jit(solution)/shard_map/ppermute | solution.py:306
  54.8 9.4 %collective-permute-start.7 = (bf16[256,256]{1,0:T(8,128)(2,1)S(1)}, bf16[256,256]{1,0:T(8,128)(2,1)S(1)}, u32[]{:S(2)}, u32[]{:S(2)}) collective-permute-start(bf16[256,256]{1,0:T(8,128)(2,1)S(1)} %pad_maximum_fusion.7), channel_id=1, source_target_pairs={{0,515},{1,0},{2,1},{3,2},{4,3},{5,512},{6,513},{7,514},{512,519},... | collective-permute-start | bytes 393224 | tf_op jit(solution)/shard_map/ppermute | solution.py:306
  65.1 60.0 %collective-permute-start.22 = (bf16[2048,640]{1,0:T(8,128)(2,1)S(1)}, bf16[2048,640]{1,0:T(8,128)(2,1)S(1)}, u32[]{:S(2)}, u32[]{:S(2)}) collective-permute-start(bf16[2048,640]{1,0:T(8,128)(2,1)S(1)} %bundle.1.refs_15_.refs_9_), channel_id=1, source_target_pairs={{0,512},{512,0},{1,513},{513,1},{2,514},{514,2},{3,515},{515,3},{4... | collective-permute-start | bytes 7864328 | tf_op jit(solution)/shard_map/ppermute | solution.py:315
  69.0 13.8 %collective-permute-start.8 = (bf16[320,512]{1,0:T(8,128)(2,1)S(1)}, bf16[320,512]{1,0:T(8,128)(2,1)S(1)}, u32[]{:S(2)}, u32[]{:S(2)}) collective-permute-start(bf16[320,512]{1,0:T(8,128)(2,1)S(1)} %get-tuple-element.75.refs_1_), channel_id=1, source_target_pairs={{0,1},{1,2},{2,3},{3,4},{4,5},{5,6},{6,7},{7,0},{8,9},{9,10},{10,1... | collective-permute-start | bytes 983048 | tf_op jit(solution)/shard_map/ppermute | solution.py:333
  75.0 12.5 %collective-permute-start.12 = (bf16[320,512]{1,0:T(8,128)(2,1)S(1)}, bf16[320,512]{1,0:T(8,128)(2,1)S(1)}, u32[]{:S(2)}, u32[]{:S(2)}) collective-permute-start(bf16[320,512]{1,0:T(8,128)(2,1)S(1)} %get-tuple-element.83.refs_8_.refs_9_), channel_id=1, source_target_pairs={{0,7},{1,0},{2,1},{3,2},{4,3},{5,4},{6,5},{7,6},{8,15},{9,8},{10,9... | collective-permute-start | bytes 983048 | tf_op jit(solution)/shard_map/ppermute | solution.py:336
  77.0 17.6 %collective-permute-start.16 = (bf16[320,512]{1,0:T(8,128)(2,1)S(1)}, bf16[320,512]{1,0:T(8,128)(2,1)S(1)}, u32[]{:S(2)}, u32[]{:S(2)}) collective-permute-start(bf16[320,512]{1,0:T(8,128)(2,1)S(1)} %get-tuple-element.75.refs_1_), channel_id=1, source_target_pairs={{0,7},{1,0},{2,1},{3,2},{4,3},{5,4},{6,5},{7,6},{8,15},{9,8},{10,9... | collective-permute-start | bytes 983048 | tf_op jit(solution)/shard_map/ppermute | solution.py:336
  79.8 17.9 %collective-permute-start.19 = (bf16[320,512]{1,0:T(8,128)(2,1)S(1)}, bf16[320,512]{1,0:T(8,128)(2,1)S(1)}, u32[]{:S(2)}, u32[]{:S(2)}) collective-permute-start(bf16[320,512]{1,0:T(8,128)(2,1)S(1)} %get-tuple-element.83.refs_8_.refs_9_), channel_id=1, source_target_pairs={{0,1},{1,2},{2,3},{3,4},{4,5},{5,6},{6,7},{7,0},{8,9},{9,10},{10,1... | collective-permute-start | bytes 983048 | tf_op jit(solution)/shard_map/ppermute | solution.py:333
  82.8 17.6 %collective-permute-start.9 = (bf16[320,512]{1,0:T(8,128)(2,1)S(1)}, bf16[320,512]{1,0:T(8,128)(2,1)S(1)}, u32[]{:S(2)}, u32[]{:S(2)}) collective-permute-start(bf16[320,512]{1,0:T(8,128)(2,1)S(1)} %collective-permute-done.8.refs_2_), channel_id=1, source_target_pairs={{0,1},{1,2},{2,3},{3,4},{4,5},{5,6},{6,7},{7,0},{8,9},{9,10},{10,1... | collective-permute-start | bytes 983048 | tf_op jit(solution)/shard_map/ppermute | solution.py:333
  87.5 15.2 %collective-permute-start.13 = (bf16[320,512]{1,0:T(8,128)(2,1)S(1)}, bf16[320,512]{1,0:T(8,128)(2,1)S(1)}, u32[]{:S(2)}, u32[]{:S(2)}) collective-permute-start(bf16[320,512]{1,0:T(8,128)(2,1)S(1)} %collective-permute-done.12.refs_14_.refs_16_), channel_id=1, source_target_pairs={{0,7},{1,0},{2,1},{3,2},{4,3},{5,4},{6,5},{7,6},{8,15},{9,8},{10,9... | collective-permute-start | bytes 983048 | tf_op jit(solution)/shard_map/ppermute | solution.py:336
  94.6 14.0 %collective-permute-start.17 = (bf16[320,512]{1,0:T(8,128)(2,1)S(1)}, bf16[320,512]{1,0:T(8,128)(2,1)S(1)}, u32[]{:S(2)}, u32[]{:S(2)}) collective-permute-start(bf16[320,512]{1,0:T(8,128)(2,1)S(1)} %collective-permute-done.16.refs_7_.refs_8_), channel_id=1, source_target_pairs={{0,7},{1,0},{2,1},{3,2},{4,3},{5,4},{6,5},{7,6},{8,15},{9,8},{10,9... | collective-permute-start | bytes 983048 | tf_op jit(solution)/shard_map/ppermute | solution.py:336
  97.7 13.8 %collective-permute-start.20 = (bf16[320,512]{1,0:T(8,128)(2,1)S(1)}, bf16[320,512]{1,0:T(8,128)(2,1)S(1)}, u32[]{:S(2)}, u32[]{:S(2)}) collective-permute-start(bf16[320,512]{1,0:T(8,128)(2,1)S(1)} %collective-permute-done.19.refs_9_.refs_10_), channel_id=1, source_target_pairs={{0,1},{1,2},{2,3},{3,4},{4,5},{5,6},{6,7},{7,0},{8,9},{9,10},{10,1... | collective-permute-start | bytes 983048 | tf_op jit(solution)/shard_map/ppermute | solution.py:333
  100.4 14.9 %collective-permute-start.10 = (bf16[320,512]{1,0:T(8,128)(2,1)S(1)}, bf16[320,512]{1,0:T(8,128)(2,1)S(1)}, u32[]{:S(2)}, u32[]{:S(2)}) collective-permute-start(bf16[320,512]{1,0:T(8,128)(2,1)S(1)} %collective-permute-done.9.refs_3_), channel_id=1, source_target_pairs={{0,1},{1,2},{2,3},{3,4},{4,5},{5,6},{6,7},{7,0},{8,9},{9,10},{10,1... | collective-permute-start | bytes 983048 | tf_op jit(solution)/shard_map/ppermute | solution.py:333
  102.7 14.5 %collective-permute-start.14 = (bf16[320,512]{1,0:T(8,128)(2,1)S(1)}, bf16[320,512]{1,0:T(8,128)(2,1)S(1)}, u32[]{:S(2)}, u32[]{:S(2)}) collective-permute-start(bf16[320,512]{1,0:T(8,128)(2,1)S(1)} %collective-permute-done.13.refs_13_.refs_15_), channel_id=1, source_target_pairs={{0,7},{1,0},{2,1},{3,2},{4,3},{5,4},{6,5},{7,6},{8,15},{9,8},{10,9... | collective-permute-start | bytes 983048 | tf_op jit(solution)/shard_map/ppermute | solution.py:336
  108.6 14.0 %collective-permute-start.18 = (bf16[320,512]{1,0:T(8,128)(2,1)S(1)}, bf16[320,512]{1,0:T(8,128)(2,1)S(1)}, u32[]{:S(2)}, u32[]{:S(2)}) collective-permute-start(bf16[320,512]{1,0:T(8,128)(2,1)S(1)} %collective-permute-done.17.refs_6_.refs_7_), channel_id=1, source_target_pairs={{0,7},{1,0},{2,1},{3,2},{4,3},{5,4},{6,5},{7,6},{8,15},{9,8},{10,9... | collective-permute-start | bytes 983048 | tf_op jit(solution)/shard_map/ppermute | solution.py:336
  111.4 13.7 %collective-permute-start.21 = (bf16[320,512]{1,0:T(8,128)(2,1)S(1)}, bf16[320,512]{1,0:T(8,128)(2,1)S(1)}, u32[]{:S(2)}, u32[]{:S(2)}) collective-permute-start(bf16[320,512]{1,0:T(8,128)(2,1)S(1)} %collective-permute-done.20.refs_10_.refs_11_), channel_id=1, source_target_pairs={{0,1},{1,2},{2,3},{3,4},{4,5},{5,6},{6,7},{7,0},{8,9},{9,10},{10,1... | collective-permute-start | bytes 983048 | tf_op jit(solution)/shard_map/ppermute | solution.py:333
  115.3 14.0 %collective-permute-start.11 = (bf16[320,512]{1,0:T(8,128)(2,1)S(1)}, bf16[320,512]{1,0:T(8,128)(2,1)S(1)}, u32[]{:S(2)}, u32[]{:S(2)}) collective-permute-start(bf16[320,512]{1,0:T(8,128)(2,1)S(1)} %collective-permute-done.10.refs_4_), channel_id=1, source_target_pairs={{0,1},{1,2},{2,3},{3,4},{4,5},{5,6},{6,7},{7,0},{8,9},{9,10},{10,1... | collective-permute-start | bytes 983048 | tf_op jit(solution)/shard_map/ppermute | solution.py:333
  117.3 12.1 %collective-permute-start.15 = (bf16[320,512]{1,0:T(8,128)(2,1)S(1)}, bf16[320,512]{1,0:T(8,128)(2,1)S(1)}, u32[]{:S(2)}, u32[]{:S(2)}) collective-permute-start(bf16[320,512]{1,0:T(8,128)(2,1)S(1)} %collective-permute-done.14.refs_12_.refs_14_), channel_id=1, source_target_pairs={{0,7},{1,0},{2,1},{3,2},{4,3},{5,4},{6,5},{7,6},{8,15},{9,8},{10,9... | collective-permute-start | bytes 983048 | tf_op jit(solution)/shard_map/ppermute | solution.py:336
  130.9 8.4 %collective-permute-start.23 = (bf16[320,256]{1,0:T(8,128)(2,1)S(1)}, bf16[320,256]{1,0:T(8,128)(2,1)S(1)}, u32[]{:S(2)}, u32[]{:S(2)}) collective-permute-start(bf16[320,256]{1,0:T(8,128)(2,1)S(1)} %get-tuple-element.91.refs_1_.refs_17_), channel_id=1, source_target_pairs={{0,1},{1,2},{2,3},{3,4},{4,5},{5,6},{6,7},{7,0},{8,9},{9,10},{10,1... | collective-permute-start | bytes 491528 | tf_op jit(solution)/shard_map/ppermute | solution.py:333
  132.9 8.4 %collective-permute-start.27 = (bf16[320,256]{1,0:T(8,128)(2,1)S(1)}, bf16[320,256]{1,0:T(8,128)(2,1)S(1)}, u32[]{:S(2)}, u32[]{:S(2)}) collective-permute-start(bf16[320,256]{1,0:T(8,128)(2,1)S(1)} %get-tuple-element.91.refs_1_.refs_17_), channel_id=1, source_target_pairs={{0,7},{1,0},{2,1},{3,2},{4,3},{5,4},{6,5},{7,6},{8,15},{9,8},{10,9... | collective-permute-start | bytes 491528 | tf_op jit(solution)/shard_map/ppermute | solution.py:336
  139.3 8.4 %collective-permute-start.24 = (bf16[320,256]{1,0:T(8,128)(2,1)S(1)}, bf16[320,256]{1,0:T(8,128)(2,1)S(1)}, u32[]{:S(2)}, u32[]{:S(2)}) collective-permute-start(bf16[320,256]{1,0:T(8,128)(2,1)S(1)} %collective-permute-done.23.refs_2_), channel_id=1, source_target_pairs={{0,1},{1,2},{2,3},{3,4},{4,5},{5,6},{6,7},{7,0},{8,9},{9,10},{10,1... | collective-permute-start | bytes 491528 | tf_op jit(solution)/shard_map/ppermute | solution.py:333
  141.3 8.4 %collective-permute-start.28 = (bf16[320,256]{1,0:T(8,128)(2,1)S(1)}, bf16[320,256]{1,0:T(8,128)(2,1)S(1)}, u32[]{:S(2)}, u32[]{:S(2)}) collective-permute-start(bf16[320,256]{1,0:T(8,128)(2,1)S(1)} %collective-permute-done.27.refs_8_), channel_id=1, source_target_pairs={{0,7},{1,0},{2,1},{3,2},{4,3},{5,4},{6,5},{7,6},{8,15},{9,8},{10,9... | collective-permute-start | bytes 491528 | tf_op jit(solution)/shard_map/ppermute | solution.py:336
  147.8 8.4 %collective-permute-start.25 = (bf16[320,256]{1,0:T(8,128)(2,1)S(1)}, bf16[320,256]{1,0:T(8,128)(2,1)S(1)}, u32[]{:S(2)}, u32[]{:S(2)}) collective-permute-start(bf16[320,256]{1,0:T(8,128)(2,1)S(1)} %collective-permute-done.24.refs_3_), channel_id=1, source_target_pairs={{0,1},{1,2},{2,3},{3,4},{4,5},{5,6},{6,7},{7,0},{8,9},{9,10},{10,1... | collective-permute-start | bytes 491528 | tf_op jit(solution)/shard_map/ppermute | solution.py:333
  149.7 8.4 %collective-permute-start.29 = (bf16[320,256]{1,0:T(8,128)(2,1)S(1)}, bf16[320,256]{1,0:T(8,128)(2,1)S(1)}, u32[]{:S(2)}, u32[]{:S(2)}) collective-permute-start(bf16[320,256]{1,0:T(8,128)(2,1)S(1)} %collective-permute-done.28.refs_7_), channel_id=1, source_target_pairs={{0,7},{1,0},{2,1},{3,2},{4,3},{5,4},{6,5},{7,6},{8,15},{9,8},{10,9... | collective-permute-start | bytes 491528 | tf_op jit(solution)/shard_map/ppermute | solution.py:336
  156.2 8.4 %collective-permute-start.26 = (bf16[320,256]{1,0:T(8,128)(2,1)S(1)}, bf16[320,256]{1,0:T(8,128)(2,1)S(1)}, u32[]{:S(2)}, u32[]{:S(2)}) collective-permute-start(bf16[320,256]{1,0:T(8,128)(2,1)S(1)} %collective-permute-done.25.refs_4_), channel_id=1, source_target_pairs={{0,1},{1,2},{2,3},{3,4},{4,5},{5,6},{6,7},{7,0},{8,9},{9,10},{10,1... | collective-permute-start | bytes 491528 | tf_op jit(solution)/shard_map/ppermute | solution.py:333
  167.0 36.6 %all-to-all-start.1 = ((bf16[64,24,128]{2,1,0:T(8,128)(2,1)}), bf16[64,24,128]{2,1,0:T(8,128)(2,1)}, u32[]{:S(2)}, u32[]{:S(2)}) async-start(bf16[64,24,128]{2,1,0:T(8,128)(2,1)} %bitcast.17), calls=%async_computation.1 | async-start | bytes 786432 | tf_op jit(solution)/shard_map/all_to_all | solution.py:383
  (25 other events, 248.0 us)

commit v6 on v5

--- a/solution.py
+++ b/solution.py
@@ -42,9 +42,16 @@
     return lax.dot_general(left, right, (((0,), (0,)), ((), ())), preferred_element_type=F32)
 
 
-def shift(axis, step):
-    n = lax.axis_size(axis)
-    return [(i, (i + step) % n) for i in range(n)]
+def around(parts, step):
+    pairs = []
+    for p in range(parts):
+        pairs.append((p, (p + step) % parts))
+        pairs.append((parts + p, parts + (p - step) % parts))
+    return pairs
+
+
+def source_of(parts, position, distance):
+    return lax.rem(position[0] - position[2] * distance + 2 * parts, parts)
 
 
 def pack_kernel(capacity, col, ids_ref, probs_ref, x_ref, dy_ref, out_ref, table_ref, flat):
@@ -144,7 +151,7 @@
 
 def weights_at(parts, distance, position, width, held):
     per_half = parts // 2
-    source = lax.rem(position[0] - distance + parts, parts)
+    source = source_of(parts, position, distance)
     of = pl.ds(pl.multiple_of(lax.rem(source, per_half) * width, width), width)
     return held[jnp.where(source // per_half == position[1], 0, 1), of, :]
 
@@ -195,11 +202,11 @@
     contract = (((1,), (1,)), ((), ()))
     for d in range(parts):
         block = blocks[d][...]
-        at = pl.multiple_of(lax.rem(d + per_half * ahead, parts) * sub, sub)
+        at = pl.multiple_of(lax.rem(position[2] * d + parts + per_half * ahead, parts) * sub, sub)
         own = own + lax.dot_general(
             block, held[0, pl.ds(at, sub), :], contract, preferred_element_type=F32
         )
-        at = pl.multiple_of(lax.rem(d + per_half * (1 - ahead), parts) * sub, sub)
+        at = pl.multiple_of(lax.rem(position[2] * d + parts + per_half * (1 - ahead), parts) * sub, sub)
         other = other + lax.dot_general(
             block, held[1, pl.ds(at, sub), :], contract, preferred_element_type=F32
         )
@@ -215,7 +222,9 @@
     out_ref[...] = flat[...].astype(BF16)
 
 
-def combine_kernel(capacity, _, flat_ref, table_ref, out_ref, flat, rows_ref):
+def combine_kernel(capacity, _, flat_ref, table_far, out_ref, flat, rows_ref, table, sem):
+    copy = pltpu.make_async_copy(table_far, table, sem)
+    copy.start()
     rows, width = rows_ref.shape
     owners, chunks = rows // capacity, width // LANES
     stretch = flat.shape[0] // owners
@@ -225,18 +234,19 @@
             rows_ref[s * owners : (s + 1) * owners, c * LANES : (c + 1) * LANES] = flat[
                 pl.ds(s * chunks + c, owners, stride=stretch), :
             ].astype(BF16)
-    out_ref[...] = transposed_dot(table_ref[...], rows_ref[...]).astype(BF16)
+    copy.wait()
+    out_ref[...] = transposed_dot(table[...], rows_ref[...]).astype(BF16)
 
 
 def grads_kernel(parts, position, *refs):
     xs, dys, both_ref, hidden_ref = refs[:parts], refs[parts : 2 * parts], *refs[2 * parts :][:2]
     rest = refs[2 * parts + 2 :]
-    place, wanted = position[0], position[1]
+    wanted = position[1]
     width = xs[0].shape[1]
     hid = hidden_ref.shape[1]
     per_half = parts // 2
     for d in range(parts):
-        source = lax.rem(place - d + parts, parts)
+        source = source_of(parts, position, d)
 
         @pl.when(source // per_half == wanted)
         def _():
@@ -250,14 +260,14 @@
                 rest[i - 3][0, into, :] = share
 
 
-def grads(place, which, operands, outs):
+def grads(position, which, operands, outs):
     xs, dys, both, hidden, *received = operands
     parts = len(xs)
     half = parts // 2 * xs[0].shape[1]
     return local_call(
         lambda *refs: grads_kernel(parts, *refs),
         "grads",
-        jnp.stack((place, which)).astype(jnp.int32),
+        position.at[1].set(which),
         (*xs, *dys, both, hidden, *received),
         outs,
         flops=2 * both.shape[0] * half * (both.shape[1] + hidden.shape[1]),
@@ -277,9 +287,9 @@
     capacity = min(tok, (5 * tok * choose + 4 * owners - 1) // (4 * owners))
     rows = owners * capacity
     half = parts // 2
-    swap = shift("dp", 1)
+    swap = [(0, 1), (1, 0)]
     place, core = place.astype(jnp.int32), core.astype(jnp.int32)
-    position = jnp.stack((place, core))
+    position = jnp.stack((place, core, 1 - 2 * core))
 
     flat, table = pack(
         expert_ids.T, probs.T, tokens, cotangent, place[None], width, owners, capacity
@@ -313,7 +323,6 @@
         jax.ShapeDtypeStruct((model // 2, 5 * hid), BF16),
     )
     bundles = (bundle, lax.ppermute(bundle, "dp", swap))
-
     flat = flat.reshape(-1, LANES)
     pair = jax.ShapeDtypeStruct((rows, width), BF16)
     own = local_call(
@@ -330,10 +339,10 @@
         right = left = value
         for d in range(1, half + 1):
             if d < half or rightward:
-                right = lax.ppermute(right, "y", shift("y", 1))
+                right = lax.ppermute(right, ("dp", "y"), around(parts, 1))
                 held[d] = right
             if d < half or not rightward:
-                left = lax.ppermute(left, "y", shift("y", -1))
+                left = lax.ppermute(left, ("dp", "y"), around(parts, -1))
                 held[parts - d] = left
         return [held[d] for d in range(parts)]
 
@@ -385,18 +394,24 @@
     )
     outs = (jax.ShapeDtypeStruct(gate_weight.shape, BF16),) * 3
     received = [
-        lax.ppermute(share, "dp", swap) for share in grads(place, 1 - core, operands, outs)
+        lax.ppermute(share, "dp", swap) for share in grads(position, 1 - core, operands, outs)
     ]
-    final = grads(place, core, (*operands, *received), outs)
+    final = grads(position, core, (*operands, *received), outs)
     returned, final = lax.optimization_barrier((returned, final))
     d_tokens = local_call(
         lambda *refs: combine_kernel(capacity, *refs),
         "combine",
         position,
-        (returned.reshape(-1, LANES), table),
+        (returned.reshape(-1, LANES),),
         jax.ShapeDtypeStruct((tok, width), BF16),
-        [pltpu.VMEM((owners * stretch, LANES), F32), pltpu.VMEM((rows, width), BF16)],
-        flops=1 << 37,
+        [
+            pltpu.VMEM((owners * stretch, LANES), F32),
+            pltpu.VMEM((rows, width), BF16),
+            pltpu.VMEM(table.shape, BF16),
+            pltpu.SemaphoreType.DMA(()),
+        ],
+        far=(table,),
+        vmem=60,
     )
     return d_tokens, *final
 

time: 209 us -> 210 us (level)
    ppermute x1, starting transfers between devices: 2.95 us -> 7.29 us  [shards(): bundles = (bundle, lax.ppermute(bundle, 'dp', swap))]
    all_to_all x1, waiting for transfers between devices: 0.01 us -> 4.1 us  [shards(): lax.all_to_all(flat.reshape(owners, -1, LANES), peers, split_axis=0, conc...]
    ppermute x8, starting transfers between devices: 31.8 us -> 29 us  [shards(): turned.append(lax.ppermute(piece, ('dp', 'y'), perm))]
    ppermute x8, waiting for transfers between devices: 4.22 us -> 1.47 us  [shards(): turned.append(lax.ppermute(piece, ('dp', 'y'), perm))]
    unnamed x44 -> x40, local copies, waits for them, and re-layouts: 9.02 us -> 8.14 us
  transfers between devices with their start and end apart: 35 -> 35, of which waited for: 15 -> 12; matrix products, arithmetic and copies ran while one was open for 1% -> 1% of each run, Pallas kernels for 5% -> 5%
where the time goes in v6:
time: 210 us; the launch traced here: 207 us
  starting transfers between devices  149 us (71%)
  waiting for transfers between devices  28.2 us (13%)
  Pallas kernels  18.1 us (9%)
  local copies, waits for them, and re-layouts  8.28 us (4%)
  other arithmetic  2.17 us (1%)
    ppermute x10, starting transfers between devices, ring(): left = lax.ppermute(left, ('dp', 'y'), around(parts, -1))  43.6 us
    ppermute x8, starting transfers between devices, shards(): turned.append(lax.ppermute(piece, ('dp', 'y'), perm))  29 us
    ppermute x11, starting transfers between devices, ring(): right = lax.ppermute(right, ('dp', 'y'), around(parts, 1))  25.1 us
    all_to_all x1, starting transfers between devices, shards(): lax.all_to_all(flat.reshape(owners, -1, LANES), peers, split_axis=0, conc...  22.5 us
    ppermute x11, waiting for transfers between devices, ring(): right = lax.ppermute(right, ('dp', 'y'), around(parts, 1))  20.8 us
    pallas_call x8, Pallas kernels, local_call(): pl.pallas_call(kernel, grid=(1,), in_specs=[pl.BlockSpec(memory_space=plt...  15.7 us
    all_to_all x1, starting transfers between devices, shards(): lax.all_to_all(d_rows.reshape(owners, -1, LANES), peers, split_axis=0, co...  15.3 us
    unnamed x40, local copies, waits for them, and re-layouts  8.14 us
  transfers between devices with their start and end apart: 35, of which 12 were waited for; matrix products, arithmetic and copies ran while one was open for 1% of the time, Pallas kernels for 5%

profile of v6, /device:TPU:6, one launch (start us, length us, event | category | flops | bytes accessed | tf_op | source)
XLA Modules:
  0.0 207.4 jit_solution(11321153225410474877)
XLA Ops:
  0.7 2.4 %pack.1 = (bf16[2560,128]{1,0:T(8,128)(2,1)}, bf16[320,32]{1,0:T(8,128)(2,1)}) custom-call(s32[1]{0:T(128)} %bitcast.refs_0_, s32[8,32]{1,0:T(8,128)} %bitcast.21, bf16[8,32]{1,0:T(8,128)(2,1)} %bitcast.22, bf16[32,4096]{1,0:T(8,128)(2,1)} %refs_3_.1, bf16[32,4096]{1,0:T(8,128)(2,1)} %refs_4_.1), custom_call_target="tpu_custom_call" | custom-call | tf_op jit(solution)/shard_map/pack/pallas_call | solution.py:99
  3.1 22.5 %all-to-all-start = ((bf16[64,40,128]{2,1,0:T(8,128)(2,1)}), bf16[64,40,128]{2,1,0:T(8,128)(2,1)S(1)}, u32[]{:S(2)}, u32[]{:S(2)}) async-start(bf16[64,40,128]{2,1,0:T(8,128)(2,1)} %bitcast.20), calls=%async_computation | async-start | bytes 1310720 | tf_op jit(solution)/shard_map/all_to_all | solution.py:300
  25.9 4.4 %collective-permute-start.7 = (bf16[256,256]{1,0:T(8,128)(2,1)S(1)}, bf16[256,256]{1,0:T(8,128)(2,1)S(1)}, u32[]{:S(2)}, u32[]{:S(2)}) collective-permute-start(bf16[256,256]{1,0:T(8,128)(2,1)S(1)} %pad_maximum_fusion.7), channel_id=1, source_target_pairs={{0,515},{1,0},{2,1},{3,2},{4,3},{5,512},{6,513},{7,514},{512,519},... | collective-permute-start | bytes 393224 | tf_op jit(solution)/shard_map/ppermute | solution.py:316
  30.4 5.7 %collective-permute-start.6 = (bf16[256,256]{1,0:T(8,128)(2,1)S(1)}, bf16[256,256]{1,0:T(8,128)(2,1)S(1)}, u32[]{:S(2)}, u32[]{:S(2)}) collective-permute-start(bf16[256,256]{1,0:T(8,128)(2,1)S(1)} %pad_maximum_fusion.6), channel_id=1, source_target_pairs={{0,514},{1,515},{2,0},{3,1},{4,2},{5,3},{6,512},{7,513},{512,518},... | collective-permute-start | bytes 393224 | tf_op jit(solution)/shard_map/ppermute | solution.py:316
  38.0 2.0 collective-permute-start.4
  40.0 5.6 %collective-permute-start.3 = (bf16[256,256]{1,0:T(8,128)(2,1)S(1)}, bf16[256,256]{1,0:T(8,128)(2,1)S(1)}, u32[]{:S(2)}, u32[]{:S(2)}) collective-permute-start(bf16[256,256]{1,0:T(8,128)(2,1)S(1)} %pad_maximum_fusion.3), channel_id=1, source_target_pairs={{0,3},{1,512},{2,513},{3,514},{4,515},{5,0},{6,1},{7,2},{512,7},{5... | collective-permute-start | bytes 393224 | tf_op jit(solution)/shard_map/ppermute | solution.py:316
  49.6 5.9 %collective-permute-start.1 = (bf16[256,256]{1,0:T(8,128)(2,1)}, bf16[256,256]{1,0:T(8,128)(2,1)S(1)}, u32[]{:S(2)}, u32[]{:S(2)}) collective-permute-start(bf16[256,256]{1,0:T(8,128)(2,1)} %pad_maximum_fusion.1), channel_id=1, source_target_pairs={{0,1},{1,2},{2,3},{3,512},{4,513},{5,514},{6,515},{7,0},{512,5},{5... | collective-permute-start | bytes 393224 | tf_op jit(solution)/shard_map/ppermute | solution.py:316
  58.7 4.1 %all-to-all-done = bf16[64,40,128]{2,1,0:T(8,128)(2,1)S(1)} async-done(((bf16[64,40,128]{2,1,0:T(8,128)(2,1)}), bf16[64,40,128]{2,1,0:T(8,128)(2,1)S(1)}, u32[]{:S(2)}, u32[]{:S(2)}) %all-to-all-start) | async-done | bytes 655392 | tf_op jit(solution)/shard_map/all_to_all | solution.py:300
  63.6 7.3 %collective-permute-start.22 = (bf16[2048,640]{1,0:T(8,128)(2,1)S(1)}, bf16[2048,640]{1,0:T(8,128)(2,1)S(1)}, u32[]{:S(2)}, u32[]{:S(2)}) collective-permute-start(bf16[2048,640]{1,0:T(8,128)(2,1)S(1)} %bundle.1.refs_15_.refs_9_), channel_id=1, source_target_pairs={{0,512},{512,0},{1,513},{513,1},{2,514},{514,2},{3,515},{515,3},{4... | collective-permute-start | bytes 7864328 | tf_op jit(solution)/shard_map/ppermute | solution.py:325
  73.7 5.1 %collective-permute-start.12 = (bf16[320,512]{1,0:T(8,128)(2,1)S(1)}, bf16[320,512]{1,0:T(8,128)(2,1)S(1)}, u32[]{:S(2)}, u32[]{:S(2)}) collective-permute-start(bf16[320,512]{1,0:T(8,128)(2,1)S(1)} %get-tuple-element.107.refs_8_.refs_9_), channel_id=1, source_target_pairs={{0,7},{512,513},{1,0},{513,514},{2,1},{514,515},{3,2},{515,516},{4... | collective-permute-start | bytes 983048 | tf_op jit(solution)/shard_map/ppermute | solution.py:345
  80.8 3.9 %collective-permute-start.19 = (bf16[320,512]{1,0:T(8,128)(2,1)S(1)}, bf16[320,512]{1,0:T(8,128)(2,1)S(1)}, u32[]{:S(2)}, u32[]{:S(2)}) collective-permute-start(bf16[320,512]{1,0:T(8,128)(2,1)S(1)} %get-tuple-element.107.refs_8_.refs_9_), channel_id=1, source_target_pairs={{0,1},{512,519},{1,2},{513,512},{2,3},{514,513},{3,4},{515,514},{4... | collective-permute-start | bytes 983048 | tf_op jit(solution)/shard_map/ppermute | solution.py:342
  86.7 5.1 %collective-permute-start.13 = (bf16[320,512]{1,0:T(8,128)(2,1)S(1)}, bf16[320,512]{1,0:T(8,128)(2,1)S(1)}, u32[]{:S(2)}, u32[]{:S(2)}) collective-permute-start(bf16[320,512]{1,0:T(8,128)(2,1)S(1)} %collective-permute-done.12.refs_14_.refs_16_), channel_id=1, source_target_pairs={{0,7},{512,513},{1,0},{513,514},{2,1},{514,515},{3,2},{515,516},{4... | collective-permute-start | bytes 983048 | tf_op jit(solution)/shard_map/ppermute | solution.py:345
  91.8 3.6 %collective-permute-start.17 = (bf16[320,512]{1,0:T(8,128)(2,1)S(1)}, bf16[320,512]{1,0:T(8,128)(2,1)S(1)}, u32[]{:S(2)}, u32[]{:S(2)}) collective-permute-start(bf16[320,512]{1,0:T(8,128)(2,1)S(1)} %collective-permute-done.16.refs_7_.refs_8_), channel_id=1, source_target_pairs={{0,7},{512,513},{1,0},{513,514},{2,1},{514,515},{3,2},{515,516},{4... | collective-permute-start | bytes 983048 | tf_op jit(solution)/shard_map/ppermute | solution.py:345
  95.5 2.2 %collective-permute-start.20 = (bf16[320,512]{1,0:T(8,128)(2,1)S(1)}, bf16[320,512]{1,0:T(8,128)(2,1)S(1)}, u32[]{:S(2)}, u32[]{:S(2)}) collective-permute-start(bf16[320,512]{1,0:T(8,128)(2,1)S(1)} %collective-permute-done.19.refs_9_.refs_10_), channel_id=1, source_target_pairs={{0,1},{512,519},{1,2},{513,512},{2,3},{514,513},{3,4},{515,514},{4... | collective-permute-start | bytes 983048 | tf_op jit(solution)/shard_map/ppermute | solution.py:342
  97.7 3.0 %collective-permute-done.9.refs_3_ = bf16[320,512]{1,0:T(8,128)(2,1)S(1)} collective-permute-done((bf16[320,512]{1,0:T(8,128)(2,1)S(1)}, bf16[320,512]{1,0:T(8,128)(2,1)S(1)}, u32[]{:S(2)}, u32[]{:S(2)}) %collective-permute-start.9) | collective-permute-done | bytes 327712 | tf_op jit(solution)/shard_map/ppermute | solution.py:342
  102.7 5.1 %collective-permute-start.14 = (bf16[320,512]{1,0:T(8,128)(2,1)S(1)}, bf16[320,512]{1,0:T(8,128)(2,1)S(1)}, u32[]{:S(2)}, u32[]{:S(2)}) collective-permute-start(bf16[320,512]{1,0:T(8,128)(2,1)S(1)} %collective-permute-done.13.refs_13_.refs_15_), channel_id=1, source_target_pairs={{0,7},{512,513},{1,0},{513,514},{2,1},{514,515},{3,2},{515,516},{4... | collective-permute-start | bytes 983048 | tf_op jit(solution)/shard_map/ppermute | solution.py:345
  107.8 2.3 %collective-permute-start.18 = (bf16[320,512]{1,0:T(8,128)(2,1)S(1)}, bf16[320,512]{1,0:T(8,128)(2,1)S(1)}, u32[]{:S(2)}, u32[]{:S(2)}) collective-permute-start(bf16[320,512]{1,0:T(8,128)(2,1)S(1)} %collective-permute-done.17.refs_6_.refs_7_), channel_id=1, source_target_pairs={{0,7},{512,513},{1,0},{513,514},{2,1},{514,515},{3,2},{515,516},{4... | collective-permute-start | bytes 983048 | tf_op jit(solution)/shard_map/ppermute | solution.py:345
  110.1 3.6 %collective-permute-start.21 = (bf16[320,512]{1,0:T(8,128)(2,1)S(1)}, bf16[320,512]{1,0:T(8,128)(2,1)S(1)}, u32[]{:S(2)}, u32[]{:S(2)}) collective-permute-start(bf16[320,512]{1,0:T(8,128)(2,1)S(1)} %collective-permute-done.20.refs_10_.refs_11_), channel_id=1, source_target_pairs={{0,1},{512,519},{1,2},{513,512},{2,3},{514,513},{3,4},{515,514},{4... | collective-permute-start | bytes 983048 | tf_op jit(solution)/shard_map/ppermute | solution.py:342
  116.4 5.1 %collective-permute-start.15 = (bf16[320,512]{1,0:T(8,128)(2,1)S(1)}, bf16[320,512]{1,0:T(8,128)(2,1)S(1)}, u32[]{:S(2)}, u32[]{:S(2)}) collective-permute-start(bf16[320,512]{1,0:T(8,128)(2,1)S(1)} %collective-permute-done.14.refs_12_.refs_14_), channel_id=1, source_target_pairs={{0,7},{512,513},{1,0},{513,514},{2,1},{514,515},{3,2},{515,516},{4... | collective-permute-start | bytes 983048 | tf_op jit(solution)/shard_map/ppermute | solution.py:345
  122.3 2.3 %forward_most.1 = (f32[320,384]{1,0:T(8,128)S(1)}, bf16[512,384]{1,0:T(8,128)(2,1)S(1)}) custom-call(s32[3]{0:T(128)S(1)} %pad_add_fusion.refs_0_._, bf16[320,512]{1,0:T(8,128)(2,1)S(1)} %get-tuple-element.99.refs_1_, bf16[320,512]{1,0:T(8,128)(2,1)S(1)} %collective-permute-done.8.refs_2_, bf16[320,512]{1,0:T(8,128)(2,1)S(1)} %collective-permute-done.9.refs_3_, ...), custom_call_target="tpu_custom_call" | custom-call | flops 1006632960 | bytes 1048576 | tf_op jit(solution)/shard_map/forward_most/pallas_call | solution.py:26
  124.6 3.0 %collective-permute-done.11.x_ref.refs_5_ = bf16[320,512]{1,0:T(8,128)(2,1)S(1)} collective-permute-done((bf16[320,512]{1,0:T(8,128)(2,1)S(1)}, bf16[320,512]{1,0:T(8,128)(2,1)S(1)}, u32[]{:S(2)}, u32[]{:S(2)}) %collective-permute-start.11) | collective-permute-done | bytes 327712 | tf_op jit(solution)/shard_map/ppermute | solution.py:342
  131.2 5.0 %collective-permute-start.27 = (bf16[320,256]{1,0:T(8,128)(2,1)S(1)}, bf16[320,256]{1,0:T(8,128)(2,1)S(1)}, u32[]{:S(2)}, u32[]{:S(2)}) collective-permute-start(bf16[320,256]{1,0:T(8,128)(2,1)S(1)} %get-tuple-element.115.refs_1_.refs_17_), channel_id=1, source_target_pairs={{0,7},{512,513},{1,0},{513,514},{2,1},{514,515},{3,2},{515,516},{4... | collective-permute-start | bytes 491528 | tf_op jit(solution)/shard_map/ppermute | solution.py:345
  136.3 3.1 %collective-permute-done.23.refs_2_ = bf16[320,256]{1,0:T(8,128)(2,1)S(1)} collective-permute-done((bf16[320,256]{1,0:T(8,128)(2,1)S(1)}, bf16[320,256]{1,0:T(8,128)(2,1)S(1)}, u32[]{:S(2)}, u32[]{:S(2)}) %collective-permute-start.23) | collective-permute-done | bytes 163872 | tf_op jit(solution)/shard_map/ppermute | solution.py:342
  141.3 5.1 %collective-permute-start.28 = (bf16[320,256]{1,0:T(8,128)(2,1)S(1)}, bf16[320,256]{1,0:T(8,128)(2,1)S(1)}, u32[]{:S(2)}, u32[]{:S(2)}) collective-permute-start(bf16[320,256]{1,0:T(8,128)(2,1)S(1)} %collective-permute-done.27.refs_8_), channel_id=1, source_target_pairs={{0,7},{512,513},{1,0},{513,514},{2,1},{514,515},{3,2},{515,516},{4... | collective-permute-start | bytes 491528 | tf_op jit(solution)/shard_map/ppermute | solution.py:345
  146.4 2.2 %collective-permute-done.24.refs_3_ = bf16[320,256]{1,0:T(8,128)(2,1)S(1)} collective-permute-done((bf16[320,256]{1,0:T(8,128)(2,1)S(1)}, bf16[320,256]{1,0:T(8,128)(2,1)S(1)}, u32[]{:S(2)}, u32[]{:S(2)}) %collective-permute-start.24) | collective-permute-done | bytes 163872 | tf_op jit(solution)/shard_map/ppermute | solution.py:342
  150.6 5.1 %collective-permute-start.29 = (bf16[320,256]{1,0:T(8,128)(2,1)S(1)}, bf16[320,256]{1,0:T(8,128)(2,1)S(1)}, u32[]{:S(2)}, u32[]{:S(2)}) collective-permute-start(bf16[320,256]{1,0:T(8,128)(2,1)S(1)} %collective-permute-done.28.refs_7_), channel_id=1, source_target_pairs={{0,7},{512,513},{1,0},{513,514},{2,1},{514,515},{3,2},{515,516},{4... | collective-permute-start | bytes 491528 | tf_op jit(solution)/shard_map/ppermute | solution.py:345
  159.0 6.5 %collective-permute-done.26.refs_5_ = bf16[320,256]{1,0:T(8,128)(2,1)S(1)} collective-permute-done((bf16[320,256]{1,0:T(8,128)(2,1)S(1)}, bf16[320,256]{1,0:T(8,128)(2,1)S(1)}, u32[]{:S(2)}, u32[]{:S(2)}) %collective-permute-start.26) | collective-permute-done | bytes 163872 | tf_op jit(solution)/shard_map/ppermute | solution.py:342
  168.0 15.3 %all-to-all-start.1 = ((bf16[64,24,128]{2,1,0:T(8,128)(2,1)}), bf16[64,24,128]{2,1,0:T(8,128)(2,1)}, u32[]{:S(2)}, u32[]{:S(2)}) async-start(bf16[64,24,128]{2,1,0:T(8,128)(2,1)} %bitcast.18), calls=%async_computation.1 | async-start | bytes 786432 | tf_op jit(solution)/shard_map/all_to_all | solution.py:392
  190.0 2.7 %grads.2 = (bf16[1,2048,128]{2,1,0:T(8,128)(2,1)S(1)}, bf16[1,2048,128]{2,1,0:T(8,128)(2,1)S(1)}, bf16[1,2048,128]{2,1,0:T(8,128)(2,1)S(1)}) custom-call(s32[3]{0:T(128)S(1)} %constant_dynamic-update-slice_fusion.refs_0_, bf16[320,512]{1,0:T(8,128)(2,1)S(1)} %get-tuple-element.99.refs_1_, bf16[320,512]{1,0:T(8,128)(2,1)S(1)} %collective-permute-done.8.refs_2_, ...), custom_call_target="tpu_custom_call" | custom-call | flops 503316480 | bytes 1048576 | tf_op jit(solution)/shard_map/grads/pallas_call | solution.py:26
  194.6 2.4 %collective-permute-start.31 = (bf16[1,2048,128]{2,1,0:T(8,128)(2,1)S(1)}, bf16[1,2048,128]{2,1,0:T(8,128)(2,1)S(1)}, u32[]{:S(2)}, u32[]{:S(2)}) collective-permute-start(bf16[1,2048,128]{2,1,0:T(8,128)(2,1)S(1)} %get-tuple-element.118), channel_id=1, source_target_pairs={{0,512},{512,0},{1,513},{513,1},{2,514},{514,2},{3,515},{515,3},{4... | collective-permute-start | bytes 1572872 | tf_op jit(solution)/shard_map/ppermute | solution.py:397
  200.9 3.7 %grads.3 = (bf16[1,2048,128]{2,1,0:T(8,128)(2,1)}, bf16[1,2048,128]{2,1,0:T(8,128)(2,1)}, bf16[1,2048,128]{2,1,0:T(8,128)(2,1)}) custom-call(s32[3]{0:T(128)S(1)} %constant_dynamic-update-slice_fusion.1.refs_0_, bf16[320,512]{1,0:T(8,128)(2,1)S(1)} %get-tuple-element.99.refs_1_, bf16[320,512]{1,0:T(8,128)(2,1)S(1)} %collective-permute-done.8.refs_2_, ...), custom_call_target="tpu_custom_call" | custom-call | flops 503316480 | bytes 1048576 | tf_op jit(solution)/shard_map/grads/pallas_call | solution.py:26
  204.5 2.7 %combine.1 = bf16[32,512]{1,0:T(8,128)(2,1)} custom-call(s32[3]{0:T(128)} %copy-done.18, bf16[1536,128]{1,0:T(8,128)(2,1)} %bitcast.12.refs_1_, bf16[320,32]{1,0:T(8,128)(2,1)} %get-tuple-element.124.refs_2_), custom_call_target="tpu_custom_call" | custom-call | bytes 1048576 | tf_op jit(solution)/shard_map/combine/pallas_call | solution.py:26
  (99 shorter events, 47.5 us)
Async XLA Ops:
  3.1 59.7 %all-to-all-start = ((bf16[64,40,128]{2,1,0:T(8,128)(2,1)}), bf16[64,40,128]{2,1,0:T(8,128)(2,1)S(1)}, u32[]{:S(2)}, u32[]{:S(2)}) async-start(bf16[64,40,128]{2,1,0:T(8,128)(2,1)} %bitcast.20), calls=%async_computation | async-start | bytes 1310720 | tf_op jit(solution)/shard_map/all_to_all | solution.py:300
  25.9 21.8 %collective-permute-start.7 = (bf16[256,256]{1,0:T(8,128)(2,1)S(1)}, bf16[256,256]{1,0:T(8,128)(2,1)S(1)}, u32[]{:S(2)}, u32[]{:S(2)}) collective-permute-start(bf16[256,256]{1,0:T(8,128)(2,1)S(1)} %pad_maximum_fusion.7), channel_id=1, source_target_pairs={{0,515},{1,0},{2,1},{3,2},{4,3},{5,512},{6,513},{7,514},{512,519},... | collective-permute-start | bytes 393224 | tf_op jit(solution)/shard_map/ppermute | solution.py:316
  30.4 19.3 %collective-permute-start.6 = (bf16[256,256]{1,0:T(8,128)(2,1)S(1)}, bf16[256,256]{1,0:T(8,128)(2,1)S(1)}, u32[]{:S(2)}, u32[]{:S(2)}) collective-permute-start(bf16[256,256]{1,0:T(8,128)(2,1)S(1)} %pad_maximum_fusion.6), channel_id=1, source_target_pairs={{0,514},{1,515},{2,0},{3,1},{4,2},{5,3},{6,512},{7,513},{512,518},... | collective-permute-start | bytes 393224 | tf_op jit(solution)/shard_map/ppermute | solution.py:316
  36.0 19.5 %collective-permute-start.5 = (bf16[256,256]{1,0:T(8,128)(2,1)S(1)}, bf16[256,256]{1,0:T(8,128)(2,1)S(1)}, u32[]{:S(2)}, u32[]{:S(2)}) collective-permute-start(bf16[256,256]{1,0:T(8,128)(2,1)S(1)} %pad_maximum_fusion.5), channel_id=1, source_target_pairs={{0,513},{1,514},{2,515},{3,0},{4,1},{5,2},{6,3},{7,512},{512,517},... | collective-permute-start | bytes 393224 | tf_op jit(solution)/shard_map/ppermute | solution.py:316
  38.0 19.2 %collective-permute-start.4 = (bf16[256,256]{1,0:T(8,128)(2,1)S(1)}, bf16[256,256]{1,0:T(8,128)(2,1)S(1)}, u32[]{:S(2)}, u32[]{:S(2)}) collective-permute-start(bf16[256,256]{1,0:T(8,128)(2,1)S(1)} %pad_maximum_fusion.4), channel_id=1, source_target_pairs={{0,512},{1,513},{2,514},{3,515},{4,0},{5,1},{6,2},{7,3},{512,516},... | collective-permute-start | bytes 393224 | tf_op jit(solution)/shard_map/ppermute | solution.py:316
  40.0 17.2 %collective-permute-start.3 = (bf16[256,256]{1,0:T(8,128)(2,1)S(1)}, bf16[256,256]{1,0:T(8,128)(2,1)S(1)}, u32[]{:S(2)}, u32[]{:S(2)}) collective-permute-start(bf16[256,256]{1,0:T(8,128)(2,1)S(1)} %pad_maximum_fusion.3), channel_id=1, source_target_pairs={{0,3},{1,512},{2,513},{3,514},{4,515},{5,0},{6,1},{7,2},{512,7},{5... | collective-permute-start | bytes 393224 | tf_op jit(solution)/shard_map/ppermute | solution.py:316
  47.7 10.6 %collective-permute-start.2 = (bf16[256,256]{1,0:T(8,128)(2,1)}, bf16[256,256]{1,0:T(8,128)(2,1)S(1)}, u32[]{:S(2)}, u32[]{:S(2)}) collective-permute-start(bf16[256,256]{1,0:T(8,128)(2,1)} %pad_maximum_fusion.2), channel_id=1, source_target_pairs={{0,2},{1,3},{2,512},{3,513},{4,514},{5,515},{6,0},{7,1},{512,6},{5... | collective-permute-start | bytes 393224 | tf_op jit(solution)/shard_map/ppermute | solution.py:316
  49.6 9.0 %collective-permute-start.1 = (bf16[256,256]{1,0:T(8,128)(2,1)}, bf16[256,256]{1,0:T(8,128)(2,1)S(1)}, u32[]{:S(2)}, u32[]{:S(2)}) collective-permute-start(bf16[256,256]{1,0:T(8,128)(2,1)} %pad_maximum_fusion.1), channel_id=1, source_target_pairs={{0,1},{1,2},{2,3},{3,512},{4,513},{5,514},{6,515},{7,0},{512,5},{5... | collective-permute-start | bytes 393224 | tf_op jit(solution)/shard_map/ppermute | solution.py:316
  63.6 58.6 %collective-permute-start.22 = (bf16[2048,640]{1,0:T(8,128)(2,1)S(1)}, bf16[2048,640]{1,0:T(8,128)(2,1)S(1)}, u32[]{:S(2)}, u32[]{:S(2)}) collective-permute-start(bf16[2048,640]{1,0:T(8,128)(2,1)S(1)} %bundle.1.refs_15_.refs_9_), channel_id=1, source_target_pairs={{0,512},{512,0},{1,513},{513,1},{2,514},{514,2},{3,515},{515,3},{4... | collective-permute-start | bytes 7864328 | tf_op jit(solution)/shard_map/ppermute | solution.py:325
  71.8 12.9 %collective-permute-start.8 = (bf16[320,512]{1,0:T(8,128)(2,1)S(1)}, bf16[320,512]{1,0:T(8,128)(2,1)S(1)}, u32[]{:S(2)}, u32[]{:S(2)}) collective-permute-start(bf16[320,512]{1,0:T(8,128)(2,1)S(1)} %get-tuple-element.99.refs_1_), channel_id=1, source_target_pairs={{0,1},{512,519},{1,2},{513,512},{2,3},{514,513},{3,4},{515,514},{4... | collective-permute-start | bytes 983048 | tf_op jit(solution)/shard_map/ppermute | solution.py:342
  73.7 12.9 %collective-permute-start.12 = (bf16[320,512]{1,0:T(8,128)(2,1)S(1)}, bf16[320,512]{1,0:T(8,128)(2,1)S(1)}, u32[]{:S(2)}, u32[]{:S(2)}) collective-permute-start(bf16[320,512]{1,0:T(8,128)(2,1)S(1)} %get-tuple-element.107.refs_8_.refs_9_), channel_id=1, source_target_pairs={{0,7},{512,513},{1,0},{513,514},{2,1},{514,515},{3,2},{515,516},{4... | collective-permute-start | bytes 983048 | tf_op jit(solution)/shard_map/ppermute | solution.py:345
  78.9 13.0 %collective-permute-start.16 = (bf16[320,512]{1,0:T(8,128)(2,1)S(1)}, bf16[320,512]{1,0:T(8,128)(2,1)S(1)}, u32[]{:S(2)}, u32[]{:S(2)}) collective-permute-start(bf16[320,512]{1,0:T(8,128)(2,1)S(1)} %get-tuple-element.99.refs_1_), channel_id=1, source_target_pairs={{0,7},{512,513},{1,0},{513,514},{2,1},{514,515},{3,2},{515,516},{4... | collective-permute-start | bytes 983048 | tf_op jit(solution)/shard_map/ppermute | solution.py:345
  80.8 14.6 %collective-permute-start.19 = (bf16[320,512]{1,0:T(8,128)(2,1)S(1)}, bf16[320,512]{1,0:T(8,128)(2,1)S(1)}, u32[]{:S(2)}, u32[]{:S(2)}) collective-permute-start(bf16[320,512]{1,0:T(8,128)(2,1)S(1)} %get-tuple-element.107.refs_8_.refs_9_), channel_id=1, source_target_pairs={{0,1},{512,519},{1,2},{513,512},{2,3},{514,513},{3,4},{515,514},{4... | collective-permute-start | bytes 983048 | tf_op jit(solution)/shard_map/ppermute | solution.py:342
  84.8 16.0 %collective-permute-start.9 = (bf16[320,512]{1,0:T(8,128)(2,1)S(1)}, bf16[320,512]{1,0:T(8,128)(2,1)S(1)}, u32[]{:S(2)}, u32[]{:S(2)}) collective-permute-start(bf16[320,512]{1,0:T(8,128)(2,1)S(1)} %collective-permute-done.8.refs_2_), channel_id=1, source_target_pairs={{0,1},{512,519},{1,2},{513,512},{2,3},{514,513},{3,4},{515,514},{4... | collective-permute-start | bytes 983048 | tf_op jit(solution)/shard_map/ppermute | solution.py:342
  86.7 16.0 %collective-permute-start.13 = (bf16[320,512]{1,0:T(8,128)(2,1)S(1)}, bf16[320,512]{1,0:T(8,128)(2,1)S(1)}, u32[]{:S(2)}, u32[]{:S(2)}) collective-permute-start(bf16[320,512]{1,0:T(8,128)(2,1)S(1)} %collective-permute-done.12.refs_14_.refs_16_), channel_id=1, source_target_pairs={{0,7},{512,513},{1,0},{513,514},{2,1},{514,515},{3,2},{515,516},{4... | collective-permute-start | bytes 983048 | tf_op jit(solution)/shard_map/ppermute | solution.py:345
  91.8 16.0 %collective-permute-start.17 = (bf16[320,512]{1,0:T(8,128)(2,1)S(1)}, bf16[320,512]{1,0:T(8,128)(2,1)S(1)}, u32[]{:S(2)}, u32[]{:S(2)}) collective-permute-start(bf16[320,512]{1,0:T(8,128)(2,1)S(1)} %collective-permute-done.16.refs_7_.refs_8_), channel_id=1, source_target_pairs={{0,7},{512,513},{1,0},{513,514},{2,1},{514,515},{3,2},{515,516},{4... | collective-permute-start | bytes 983048 | tf_op jit(solution)/shard_map/ppermute | solution.py:345
  95.5 14.6 %collective-permute-start.20 = (bf16[320,512]{1,0:T(8,128)(2,1)S(1)}, bf16[320,512]{1,0:T(8,128)(2,1)S(1)}, u32[]{:S(2)}, u32[]{:S(2)}) collective-permute-start(bf16[320,512]{1,0:T(8,128)(2,1)S(1)} %collective-permute-done.19.refs_9_.refs_10_), channel_id=1, source_target_pairs={{0,1},{512,519},{1,2},{513,512},{2,3},{514,513},{3,4},{515,514},{4... | collective-permute-start | bytes 983048 | tf_op jit(solution)/shard_map/ppermute | solution.py:342
  100.7 13.7 %collective-permute-start.10 = (bf16[320,512]{1,0:T(8,128)(2,1)S(1)}, bf16[320,512]{1,0:T(8,128)(2,1)S(1)}, u32[]{:S(2)}, u32[]{:S(2)}) collective-permute-start(bf16[320,512]{1,0:T(8,128)(2,1)S(1)} %collective-permute-done.9.refs_3_), channel_id=1, source_target_pairs={{0,1},{512,519},{1,2},{513,512},{2,3},{514,513},{3,4},{515,514},{4... | collective-permute-start | bytes 983048 | tf_op jit(solution)/shard_map/ppermute | solution.py:342
  102.7 13.7 %collective-permute-start.14 = (bf16[320,512]{1,0:T(8,128)(2,1)S(1)}, bf16[320,512]{1,0:T(8,128)(2,1)S(1)}, u32[]{:S(2)}, u32[]{:S(2)}) collective-permute-start(bf16[320,512]{1,0:T(8,128)(2,1)S(1)} %collective-permute-done.13.refs_13_.refs_15_), channel_id=1, source_target_pairs={{0,7},{512,513},{1,0},{513,514},{2,1},{514,515},{3,2},{515,516},{4... | collective-permute-start | bytes 983048 | tf_op jit(solution)/shard_map/ppermute | solution.py:345
  107.8 13.7 %collective-permute-start.18 = (bf16[320,512]{1,0:T(8,128)(2,1)S(1)}, bf16[320,512]{1,0:T(8,128)(2,1)S(1)}, u32[]{:S(2)}, u32[]{:S(2)}) collective-permute-start(bf16[320,512]{1,0:T(8,128)(2,1)S(1)} %collective-permute-done.17.refs_6_.refs_7_), channel_id=1, source_target_pairs={{0,7},{512,513},{1,0},{513,514},{2,1},{514,515},{3,2},{515,516},{4... | collective-permute-start | bytes 983048 | tf_op jit(solution)/shard_map/ppermute | solution.py:345
  110.1 12.2 %collective-permute-start.21 = (bf16[320,512]{1,0:T(8,128)(2,1)S(1)}, bf16[320,512]{1,0:T(8,128)(2,1)S(1)}, u32[]{:S(2)}, u32[]{:S(2)}) collective-permute-start(bf16[320,512]{1,0:T(8,128)(2,1)S(1)} %collective-permute-done.20.refs_10_.refs_11_), channel_id=1, source_target_pairs={{0,1},{512,519},{1,2},{513,512},{2,3},{514,513},{3,4},{515,514},{4... | collective-permute-start | bytes 983048 | tf_op jit(solution)/shard_map/ppermute | solution.py:342
  114.4 13.2 %collective-permute-start.11 = (bf16[320,512]{1,0:T(8,128)(2,1)S(1)}, bf16[320,512]{1,0:T(8,128)(2,1)S(1)}, u32[]{:S(2)}, u32[]{:S(2)}) collective-permute-start(bf16[320,512]{1,0:T(8,128)(2,1)S(1)} %collective-permute-done.10.refs_4_), channel_id=1, source_target_pairs={{0,1},{512,519},{1,2},{513,512},{2,3},{514,513},{3,4},{515,514},{4... | collective-permute-start | bytes 983048 | tf_op jit(solution)/shard_map/ppermute | solution.py:342
  116.4 11.3 %collective-permute-start.15 = (bf16[320,512]{1,0:T(8,128)(2,1)S(1)}, bf16[320,512]{1,0:T(8,128)(2,1)S(1)}, u32[]{:S(2)}, u32[]{:S(2)}) collective-permute-start(bf16[320,512]{1,0:T(8,128)(2,1)S(1)} %collective-permute-done.14.refs_12_.refs_14_), channel_id=1, source_target_pairs={{0,7},{512,513},{1,0},{513,514},{2,1},{514,515},{3,2},{515,516},{4... | collective-permute-start | bytes 983048 | tf_op jit(solution)/shard_map/ppermute | solution.py:345
  129.2 10.2 %collective-permute-start.23 = (bf16[320,256]{1,0:T(8,128)(2,1)S(1)}, bf16[320,256]{1,0:T(8,128)(2,1)S(1)}, u32[]{:S(2)}, u32[]{:S(2)}) collective-permute-start(bf16[320,256]{1,0:T(8,128)(2,1)S(1)} %get-tuple-element.115.refs_1_.refs_17_), channel_id=1, source_target_pairs={{0,1},{512,519},{1,2},{513,512},{2,3},{514,513},{3,4},{515,514},{4... | collective-permute-start | bytes 491528 | tf_op jit(solution)/shard_map/ppermute | solution.py:342
  131.2 10.1 %collective-permute-start.27 = (bf16[320,256]{1,0:T(8,128)(2,1)S(1)}, bf16[320,256]{1,0:T(8,128)(2,1)S(1)}, u32[]{:S(2)}, u32[]{:S(2)}) collective-permute-start(bf16[320,256]{1,0:T(8,128)(2,1)S(1)} %get-tuple-element.115.refs_1_.refs_17_), channel_id=1, source_target_pairs={{0,7},{512,513},{1,0},{513,514},{2,1},{514,515},{3,2},{515,516},{4... | collective-permute-start | bytes 491528 | tf_op jit(solution)/shard_map/ppermute | solution.py:345
  139.4 9.3 %collective-permute-start.24 = (bf16[320,256]{1,0:T(8,128)(2,1)S(1)}, bf16[320,256]{1,0:T(8,128)(2,1)S(1)}, u32[]{:S(2)}, u32[]{:S(2)}) collective-permute-start(bf16[320,256]{1,0:T(8,128)(2,1)S(1)} %collective-permute-done.23.refs_2_), channel_id=1, source_target_pairs={{0,1},{512,519},{1,2},{513,512},{2,3},{514,513},{3,4},{515,514},{4... | collective-permute-start | bytes 491528 | tf_op jit(solution)/shard_map/ppermute | solution.py:342
  141.3 9.3 %collective-permute-start.28 = (bf16[320,256]{1,0:T(8,128)(2,1)S(1)}, bf16[320,256]{1,0:T(8,128)(2,1)S(1)}, u32[]{:S(2)}, u32[]{:S(2)}) collective-permute-start(bf16[320,256]{1,0:T(8,128)(2,1)S(1)} %collective-permute-done.27.refs_8_), channel_id=1, source_target_pairs={{0,7},{512,513},{1,0},{513,514},{2,1},{514,515},{3,2},{515,516},{4... | collective-permute-start | bytes 491528 | tf_op jit(solution)/shard_map/ppermute | solution.py:345
  148.6 8.5 %collective-permute-start.25 = (bf16[320,256]{1,0:T(8,128)(2,1)S(1)}, bf16[320,256]{1,0:T(8,128)(2,1)S(1)}, u32[]{:S(2)}, u32[]{:S(2)}) collective-permute-start(bf16[320,256]{1,0:T(8,128)(2,1)S(1)} %collective-permute-done.24.refs_3_), channel_id=1, source_target_pairs={{0,1},{512,519},{1,2},{513,512},{2,3},{514,513},{3,4},{515,514},{4... | collective-permute-start | bytes 491528 | tf_op jit(solution)/shard_map/ppermute | solution.py:342
  150.6 8.5 %collective-permute-start.29 = (bf16[320,256]{1,0:T(8,128)(2,1)S(1)}, bf16[320,256]{1,0:T(8,128)(2,1)S(1)}, u32[]{:S(2)}, u32[]{:S(2)}) collective-permute-start(bf16[320,256]{1,0:T(8,128)(2,1)S(1)} %collective-permute-done.28.refs_7_), channel_id=1, source_target_pairs={{0,7},{512,513},{1,0},{513,514},{2,1},{514,515},{3,2},{515,516},{4... | collective-permute-start | bytes 491528 | tf_op jit(solution)/shard_map/ppermute | solution.py:345
  157.1 8.4 %collective-permute-start.26 = (bf16[320,256]{1,0:T(8,128)(2,1)S(1)}, bf16[320,256]{1,0:T(8,128)(2,1)S(1)}, u32[]{:S(2)}, u32[]{:S(2)}) collective-permute-start(bf16[320,256]{1,0:T(8,128)(2,1)S(1)} %collective-permute-done.25.refs_4_), channel_id=1, source_target_pairs={{0,1},{512,519},{1,2},{513,512},{2,3},{514,513},{3,4},{515,514},{4... | collective-permute-start | bytes 491528 | tf_op jit(solution)/shard_map/ppermute | solution.py:342
  168.0 36.6 %all-to-all-start.1 = ((bf16[64,24,128]{2,1,0:T(8,128)(2,1)}), bf16[64,24,128]{2,1,0:T(8,128)(2,1)}, u32[]{:S(2)}, u32[]{:S(2)}) async-start(bf16[64,24,128]{2,1,0:T(8,128)(2,1)} %bitcast.18), calls=%async_computation.1 | async-start | bytes 786432 | tf_op jit(solution)/shard_map/all_to_all | solution.py:392
  192.7 6.3 %collective-permute-start.30 = (bf16[1,2048,128]{2,1,0:T(8,128)(2,1)S(1)}, bf16[1,2048,128]{2,1,0:T(8,128)(2,1)S(1)}, u32[]{:S(2)}, u32[]{:S(2)}) collective-permute-start(bf16[1,2048,128]{2,1,0:T(8,128)(2,1)S(1)} %get-tuple-element.117), channel_id=1, source_target_pairs={{0,512},{512,0},{1,513},{513,1},{2,514},{514,2},{3,515},{515,3},{4... | collective-permute-start | bytes 1572872 | tf_op jit(solution)/shard_map/ppermute | solution.py:397
  (22 other events, 351.6 us)

commit v7 on v6

--- a/solution.py
+++ b/solution.py
@@ -40,6 +40,10 @@
 
 def transposed_dot(left, right):
     return lax.dot_general(left, right, (((0,), (0,)), ((), ())), preferred_element_type=F32)
+
+
+def shift(parts, step):
+    return [(p, (p + step) % parts) for p in range(parts)]
 
 
 def around(parts, step):
@@ -114,18 +118,16 @@
     )(column, ids, probs, tokens, cotangent)
 
 
-def unpack_kernel(capacity, _, flat_ref, x_ref, dy_ref, flat):
-    rows, width = x_ref.shape
+def unpack_kernel(capacity, _, flat_ref, out_ref, flat):
+    rows, width = out_ref.shape
     owners, chunks = rows // capacity, width // LANES
     stretch = flat.shape[0] // owners
     flat[...] = flat_ref[...].astype(F32)
     for s in range(capacity):
-        of = slice(s * owners, (s + 1) * owners)
         for c in range(chunks):
-            cols = slice(c * LANES, (c + 1) * LANES)
-            at = s * 2 * chunks + c
-            x_ref[of, cols] = flat[pl.ds(at, owners, stride=stretch), :].astype(BF16)
-            dy_ref[of, cols] = flat[pl.ds(at + chunks, owners, stride=stretch), :].astype(BF16)
+            out_ref[s * owners : (s + 1) * owners, c * LANES : (c + 1) * LANES] = flat[
+                pl.ds(s * chunks + c, owners, stride=stretch), :
+            ].astype(BF16)
 
 
 def bundle_kernel(_, *refs):
@@ -157,28 +159,30 @@
 
 
 def forward_most(parts, distances, middle, position, *refs):
-    xs, dys = refs[: len(distances)], refs[len(distances) : 2 * len(distances)]
-    own_bundle, other_bundle, out, mid_ref, held, sems = refs[2 * len(distances) :]
-    rows, width = xs[0].shape
+    blocks, (own_bundle, other_bundle, out, mid_ref, held, sems) = (
+        refs[: len(distances)],
+        refs[len(distances) :],
+    )
+    rows, width = blocks[0].shape[0], blocks[0].shape[1] // 2
     hid = out.shape[1] // 3
     fetch((own_bundle, other_bundle), pl.ds(2 * hid, 3 * hid), held, sems)
     acc, back = jnp.zeros((rows, 2 * hid), F32), jnp.zeros((rows, hid), F32)
-    for d, x, dy in zip(distances, xs, dys):
+    for d, block in zip(distances, blocks):
         piece = weights_at(parts, d, position, width, held)
-        acc = acc + jnp.dot(x[...], piece[:, : 2 * hid], preferred_element_type=F32)
-        back = back + jnp.dot(dy[...], piece[:, 2 * hid :], preferred_element_type=F32)
+        acc = acc + jnp.dot(block[:, :width], piece[:, : 2 * hid], preferred_element_type=F32)
+        back = back + jnp.dot(block[:, width:], piece[:, 2 * hid :], preferred_element_type=F32)
     out[:, : 2 * hid] = acc
     out[:, 2 * hid :] = back
     mid_ref[...] = weights_at(parts, middle, position, width, held)
 
 
-def forward_last(_, x_ref, dy_ref, piece_ref, begun, both_ref, hidden_ref):
-    hid = hidden_ref.shape[1]
+def forward_last(_, block, piece_ref, begun, both_ref, hidden_ref):
+    hid, width = hidden_ref.shape[1], block.shape[1] // 2
     acc = begun[:, : 2 * hid] + jnp.dot(
-        x_ref[...], piece_ref[:, : 2 * hid], preferred_element_type=F32
+        block[:, :width], piece_ref[:, : 2 * hid], preferred_element_type=F32
     )
     back = begun[:, 2 * hid :] + jnp.dot(
-        dy_ref[...], piece_ref[:, 2 * hid :], preferred_element_type=F32
+        block[:, width:], piece_ref[:, 2 * hid :], preferred_element_type=F32
     )
     gate, up = acc[:, :hid], acc[:, hid:]
     sig = 1.0 / (1.0 + jnp.exp(-gate))
@@ -239,10 +243,9 @@
 
 
 def grads_kernel(parts, position, *refs):
-    xs, dys, both_ref, hidden_ref = refs[:parts], refs[parts : 2 * parts], *refs[2 * parts :][:2]
-    rest = refs[2 * parts + 2 :]
+    blocks, (both_ref, hidden_ref, *rest) = refs[:parts], refs[parts:]
     wanted = position[1]
-    width = xs[0].shape[1]
+    width = blocks[0].shape[1] // 2
     hid = hidden_ref.shape[1]
     per_half = parts // 2
     for d in range(parts):
@@ -251,8 +254,8 @@
         @pl.when(source // per_half == wanted)
         def _():
             into = pl.ds(pl.multiple_of(lax.rem(source, per_half) * width, width), width)
-            both = transposed_dot(xs[d][...], both_ref[...]).astype(BF16)
-            down = transposed_dot(dys[d][...], hidden_ref[...]).astype(BF16)
+            both = transposed_dot(blocks[d][:, :width], both_ref[...]).astype(BF16)
+            down = transposed_dot(blocks[d][:, width:], hidden_ref[...]).astype(BF16)
             for i, share in enumerate((both[:, :hid], both[:, hid:], down)):
                 if len(rest) > 3:
                     more = rest[i][0, into, :].astype(F32)
@@ -261,14 +264,14 @@
 
 
 def grads(position, which, operands, outs):
-    xs, dys, both, hidden, *received = operands
-    parts = len(xs)
-    half = parts // 2 * xs[0].shape[1]
+    blocks, both, hidden, *received = operands
+    parts = len(blocks)
+    half = parts // 2 * (blocks[0].shape[1] // 2)
     return local_call(
         lambda *refs: grads_kernel(parts, *refs),
         "grads",
         position.at[1].set(which),
-        (*xs, *dys, both, hidden, *received),
+        (*blocks, both, hidden, *received),
         outs,
         flops=2 * both.shape[0] * half * (both.shape[1] + hidden.shape[1]),
     )
@@ -324,35 +327,33 @@
     )
     bundles = (bundle, lax.ppermute(bundle, "dp", swap))
     flat = flat.reshape(-1, LANES)
-    pair = jax.ShapeDtypeStruct((rows, width), BF16)
     own = local_call(
         lambda *refs: unpack_kernel(capacity, *refs),
         "unpack",
         position,
         (flat,),
-        (pair, pair),
+        jax.ShapeDtypeStruct((rows, 2 * width), BF16),
         [pltpu.VMEM(flat.shape, F32)],
     )
 
-    def ring(value, rightward):
+    def ring(value, axes, on, back):
         held = {0: value}
-        right = left = value
+        ahead = behind = value
         for d in range(1, half + 1):
-            if d < half or rightward:
-                right = lax.ppermute(right, ("dp", "y"), around(parts, 1))
-                held[d] = right
-            if d < half or not rightward:
-                left = lax.ppermute(left, ("dp", "y"), around(parts, -1))
-                held[parts - d] = left
+            ahead = lax.ppermute(ahead, axes, on)
+            held[d] = ahead
+            if d < half:
+                behind = lax.ppermute(behind, axes, back)
+                held[parts - d] = behind
         return [held[d] for d in range(parts)]
 
-    xs, dys = ring(own[0], True), ring(own[1], False)
+    blocks = ring(own, ("dp", "y"), around(parts, 1), around(parts, -1))
     most = [d for d in range(parts) if d != half]
     begun, piece = local_call(
         lambda *refs: forward_most(parts, most, half, *refs),
         "forward_most",
         position,
-        (*[xs[d] for d in most], *[dys[d] for d in most]),
+        [blocks[d] for d in most],
         (
             jax.ShapeDtypeStruct((rows, 3 * hid), F32),
             jax.ShapeDtypeStruct((width, 3 * hid), BF16),
@@ -365,7 +366,7 @@
         forward_last,
         "forward_last",
         position,
-        (xs[half], dys[half], piece, begun),
+        (blocks[half], piece, begun),
         (
             jax.ShapeDtypeStruct((rows, 2 * hid), BF16),
             jax.ShapeDtypeStruct((rows, hid), BF16),
@@ -377,8 +378,8 @@
     d_rows = local_call(
         lambda *refs: back_kernel(parts, capacity, *refs),
         "back",
-        position,
-        ring(d_both, True),
+        position.at[2].set(1),
+        ring(d_both, "y", shift(parts, 1), shift(parts, -1)),
         jax.ShapeDtypeStruct((owners * stretch, LANES), BF16),
         [
             pltpu.VMEM((owners * stretch, LANES), F32),
@@ -388,7 +389,7 @@
         flops=4 * rows * width * parts * hid,
         far=bundles,
     )
-    d_rows, operands = lax.optimization_barrier((d_rows, (xs, dys, d_both, hidden)))
+    d_rows, operands = lax.optimization_barrier((d_rows, (blocks, d_both, hidden)))
     returned = lax.all_to_all(
         d_rows.reshape(owners, -1, LANES), peers, split_axis=0, concat_axis=0, tiled=True
     )

time: 210 us -> 224 us (1.067)
  waiting for transfers between devices: 28.2 us -> 70.1 us
  starting transfers between devices: 149 us -> 127 us
  local copies, waits for them, and re-layouts: 8.28 us -> 4.19 us
    ppermute x21 -> x14, waiting for transfers between devices: 20.8 us -> 61.4 us  [the longest x8 61.4 us: ring(): ahead = lax.ppermute(ahead, axes, on)]
    ppermute x21 -> x14, starting transfers between devices: 68.8 us -> 46.4 us  [the longest x6 31.1 us: ring(): behind = lax.ppermute(behind, axes, back)]
    unnamed x40 -> x25, local copies, waits for them, and re-layouts: 8.14 us -> 4.03 us
  transfers between devices with their start and end apart: 35 -> 28, of which waited for: 12 -> 13; matrix products, arithmetic and copies ran while one was open for 1% -> 1% of each run, Pallas kernels for 5% -> 4%
where the time goes in v7:
time: 224 us; the launch traced here: 223 us
  starting transfers between devices  127 us (57%)
  waiting for transfers between devices  70.1 us (31%)
  Pallas kernels  18.1 us (8%)
  local copies, waits for them, and re-layouts  4.19 us (2%)
    ppermute x8, waiting for transfers between devices, ring(): ahead = lax.ppermute(ahead, axes, on)  61.4 us
    ppermute x6, starting transfers between devices, ring(): behind = lax.ppermute(behind, axes, back)  31.1 us
    ppermute x8, starting transfers between devices, shards(): turned.append(lax.ppermute(piece, ('dp', 'y'), perm))  29 us
    all_to_all x1, starting transfers between devices, shards(): lax.all_to_all(flat.reshape(owners, -1, LANES), peers, split_axis=0, conc...  22.5 us
    pallas_call x8, Pallas kernels, local_call(): pl.pallas_call(kernel, grid=(1,), in_specs=[pl.BlockSpec(memory_space=plt...  15.7 us
    ppermute x8, starting transfers between devices, ring(): ahead = lax.ppermute(ahead, axes, on)  15.3 us
    all_to_all x1, starting transfers between devices, shards(): lax.all_to_all(d_rows.reshape(owners, -1, LANES), peers, split_axis=0, co...  15.3 us
    ppermute x1, starting transfers between devices, shards(): bundles = (bundle, lax.ppermute(bundle, 'dp', swap))  7.29 us
  transfers between devices with their start and end apart: 28, of which 13 were waited for; matrix products, arithmetic and copies ran while one was open for 1% of the time, Pallas kernels for 4%

profile of v7, /device:TPU:6, one launch (start us, length us, event | category | flops | bytes accessed | tf_op | source)
XLA Modules:
  0.0 222.7 jit_solution(15800726463933924524)
XLA Ops:
  0.7 2.4 %pack.1 = (bf16[2560,128]{1,0:T(8,128)(2,1)}, bf16[320,32]{1,0:T(8,128)(2,1)}) custom-call(s32[1]{0:T(128)} %bitcast.refs_0_, s32[8,32]{1,0:T(8,128)} %bitcast.21, bf16[8,32]{1,0:T(8,128)(2,1)} %bitcast.22, bf16[32,4096]{1,0:T(8,128)(2,1)} %refs_3_.1, bf16[32,4096]{1,0:T(8,128)(2,1)} %refs_4_.1), custom_call_target="tpu_custom_call" | custom-call | tf_op jit(solution)/shard_map/pack/pallas_call | solution.py:103
  3.1 22.5 %all-to-all-start = ((bf16[64,40,128]{2,1,0:T(8,128)(2,1)}), bf16[64,40,128]{2,1,0:T(8,128)(2,1)S(1)}, u32[]{:S(2)}, u32[]{:S(2)}) async-start(bf16[64,40,128]{2,1,0:T(8,128)(2,1)} %bitcast.20), calls=%async_computation | async-start | bytes 1310720 | tf_op jit(solution)/shard_map/all_to_all | solution.py:303
  25.9 4.4 %collective-permute-start.7 = (bf16[256,256]{1,0:T(8,128)(2,1)S(1)}, bf16[256,256]{1,0:T(8,128)(2,1)S(1)}, u32[]{:S(2)}, u32[]{:S(2)}) collective-permute-start(bf16[256,256]{1,0:T(8,128)(2,1)S(1)} %pad_maximum_fusion.7), channel_id=1, source_target_pairs={{0,515},{1,0},{2,1},{3,2},{4,3},{5,512},{6,513},{7,514},{512,519},... | collective-permute-start | bytes 393224 | tf_op jit(solution)/shard_map/ppermute | solution.py:319
  30.4 5.7 %collective-permute-start.6 = (bf16[256,256]{1,0:T(8,128)(2,1)S(1)}, bf16[256,256]{1,0:T(8,128)(2,1)S(1)}, u32[]{:S(2)}, u32[]{:S(2)}) collective-permute-start(bf16[256,256]{1,0:T(8,128)(2,1)S(1)} %pad_maximum_fusion.6), channel_id=1, source_target_pairs={{0,514},{1,515},{2,0},{3,1},{4,2},{5,3},{6,512},{7,513},{512,518},... | collective-permute-start | bytes 393224 | tf_op jit(solution)/shard_map/ppermute | solution.py:319
  36.0 1.9 collective-permute-start.5
  38.0 2.0 collective-permute-start.4
  40.0 5.6 %collective-permute-start.3 = (bf16[256,256]{1,0:T(8,128)(2,1)S(1)}, bf16[256,256]{1,0:T(8,128)(2,1)S(1)}, u32[]{:S(2)}, u32[]{:S(2)}) collective-permute-start(bf16[256,256]{1,0:T(8,128)(2,1)S(1)} %pad_maximum_fusion.3), channel_id=1, source_target_pairs={{0,3},{1,512},{2,513},{3,514},{4,515},{5,0},{6,1},{7,2},{512,7},{5... | collective-permute-start | bytes 393224 | tf_op jit(solution)/shard_map/ppermute | solution.py:319
  49.6 5.9 %collective-permute-start.1 = (bf16[256,256]{1,0:T(8,128)(2,1)}, bf16[256,256]{1,0:T(8,128)(2,1)S(1)}, u32[]{:S(2)}, u32[]{:S(2)}) collective-permute-start(bf16[256,256]{1,0:T(8,128)(2,1)} %pad_maximum_fusion.1), channel_id=1, source_target_pairs={{0,1},{1,2},{2,3},{3,512},{4,513},{5,514},{6,515},{7,0},{512,5},{5... | collective-permute-start | bytes 393224 | tf_op jit(solution)/shard_map/ppermute | solution.py:319
  58.7 4.1 %all-to-all-done = bf16[64,40,128]{2,1,0:T(8,128)(2,1)S(1)} async-done(((bf16[64,40,128]{2,1,0:T(8,128)(2,1)}), bf16[64,40,128]{2,1,0:T(8,128)(2,1)S(1)}, u32[]{:S(2)}, u32[]{:S(2)}) %all-to-all-start) | async-done | bytes 655392 | tf_op jit(solution)/shard_map/all_to_all | solution.py:303
  63.6 7.3 %collective-permute-start.15 = (bf16[2048,640]{1,0:T(8,128)(2,1)S(1)}, bf16[2048,640]{1,0:T(8,128)(2,1)S(1)}, u32[]{:S(2)}, u32[]{:S(2)}) collective-permute-start(bf16[2048,640]{1,0:T(8,128)(2,1)S(1)} %bundle.1.refs_8_.refs_9_), channel_id=1, source_target_pairs={{0,512},{512,0},{1,513},{513,1},{2,514},{514,2},{3,515},{515,3},{4... | collective-permute-start | bytes 7864328 | tf_op jit(solution)/shard_map/ppermute | solution.py:328
  71.8 1.9 collective-permute-start.8
  73.7 5.1 %collective-permute-start.12 = (bf16[320,1024]{1,0:T(8,128)(2,1)S(1)}, bf16[320,1024]{1,0:T(8,128)(2,1)S(1)}, u32[]{:S(2)}, u32[]{:S(2)}) collective-permute-start(bf16[320,1024]{1,0:T(8,128)(2,1)S(1)} %unpack.1.refs_1_), channel_id=1, source_target_pairs={{0,7},{512,513},{1,0},{513,514},{2,1},{514,515},{3,2},{515,516},{4... | collective-permute-start | bytes 1966088 | tf_op jit(solution)/shard_map/ppermute | solution.py:346
  78.9 12.7 %collective-permute-done.8.refs_2_ = bf16[320,1024]{1,0:T(8,128)(2,1)S(1)} collective-permute-done((bf16[320,1024]{1,0:T(8,128)(2,1)S(1)}, bf16[320,1024]{1,0:T(8,128)(2,1)S(1)}, u32[]{:S(2)}, u32[]{:S(2)}) %collective-permute-start.8) | collective-permute-done | bytes 655392 | tf_op jit(solution)/shard_map/ppermute | solution.py:343
  93.5 5.1 %collective-permute-start.13 = (bf16[320,1024]{1,0:T(8,128)(2,1)S(1)}, bf16[320,1024]{1,0:T(8,128)(2,1)S(1)}, u32[]{:S(2)}, u32[]{:S(2)}) collective-permute-start(bf16[320,1024]{1,0:T(8,128)(2,1)S(1)} %collective-permute-done.12.refs_7_.refs_8_), channel_id=1, source_target_pairs={{0,7},{512,513},{1,0},{513,514},{2,1},{514,515},{3,2},{515,516},{4... | collective-permute-start | bytes 1966088 | tf_op jit(solution)/shard_map/ppermute | solution.py:346
  98.6 13.4 %collective-permute-done.9.refs_3_ = bf16[320,1024]{1,0:T(8,128)(2,1)S(1)} collective-permute-done((bf16[320,1024]{1,0:T(8,128)(2,1)S(1)}, bf16[320,1024]{1,0:T(8,128)(2,1)S(1)}, u32[]{:S(2)}, u32[]{:S(2)}) %collective-permute-start.9) | collective-permute-done | bytes 655392 | tf_op jit(solution)/shard_map/ppermute | solution.py:343
  114.0 5.1 %collective-permute-start.14 = (bf16[320,1024]{1,0:T(8,128)(2,1)S(1)}, bf16[320,1024]{1,0:T(8,128)(2,1)S(1)}, u32[]{:S(2)}, u32[]{:S(2)}) collective-permute-start(bf16[320,1024]{1,0:T(8,128)(2,1)S(1)} %collective-permute-done.13.refs_6_.refs_7_), channel_id=1, source_target_pairs={{0,7},{512,513},{1,0},{513,514},{2,1},{514,515},{3,2},{515,516},{4... | collective-permute-start | bytes 1966088 | tf_op jit(solution)/shard_map/ppermute | solution.py:346
  119.2 12.6 %collective-permute-done.10.refs_4_ = bf16[320,1024]{1,0:T(8,128)(2,1)S(1)} collective-permute-done((bf16[320,1024]{1,0:T(8,128)(2,1)S(1)}, bf16[320,1024]{1,0:T(8,128)(2,1)S(1)}, u32[]{:S(2)}, u32[]{:S(2)}) %collective-permute-start.10) | collective-permute-done | bytes 655392 | tf_op jit(solution)/shard_map/ppermute | solution.py:343
  133.7 2.3 %forward_most.1 = (f32[320,384]{1,0:T(8,128)S(1)}, bf16[512,384]{1,0:T(8,128)(2,1)S(1)}) custom-call(s32[3]{0:T(128)S(1)} %pad_add_fusion.refs_0_._, bf16[320,1024]{1,0:T(8,128)(2,1)S(1)} %unpack.1.refs_1_, bf16[320,1024]{1,0:T(8,128)(2,1)S(1)} %collective-permute-done.8.refs_2_, bf16[320,1024]{1,0:T(8,128)(2,1)S(1)} %collective-permute-done.9.refs_3_, ...), custom_call_target="tpu_custom_call" | custom-call | flops 1006632960 | bytes 1048576 | tf_op jit(solution)/shard_map/forward_most/pallas_call | solution.py:26
  136.0 11.2 %collective-permute-done.11.block.refs_5_ = bf16[320,1024]{1,0:T(8,128)(2,1)S(1)} collective-permute-done((bf16[320,1024]{1,0:T(8,128)(2,1)S(1)}, bf16[320,1024]{1,0:T(8,128)(2,1)S(1)}, u32[]{:S(2)}, u32[]{:S(2)}) %collective-permute-start.11) | collective-permute-done | bytes 655392 | tf_op jit(solution)/shard_map/ppermute | solution.py:343
  148.1 1.9 collective-permute-start.16
  150.0 5.1 %collective-permute-start.20 = (bf16[320,256]{1,0:T(8,128)(2,1)S(1)}, bf16[320,256]{1,0:T(8,128)(2,1)S(1)}, u32[]{:S(2)}, u32[]{:S(2)}) collective-permute-start(bf16[320,256]{1,0:T(8,128)(2,1)S(1)} %get-tuple-element.107.refs_1_.refs_9_), channel_id=1, source_target_pairs={{0,7},{1,0},{2,1},{3,2},{4,3},{5,4},{6,5},{7,6},{8,15},{9,8},{10,9... | collective-permute-start | bytes 491528 | tf_op jit(solution)/shard_map/ppermute | solution.py:346
  158.5 5.4 %collective-permute-start.21 = (bf16[320,256]{1,0:T(8,128)(2,1)S(1)}, bf16[320,256]{1,0:T(8,128)(2,1)S(1)}, u32[]{:S(2)}, u32[]{:S(2)}) collective-permute-start(bf16[320,256]{1,0:T(8,128)(2,1)S(1)} %collective-permute-done.20.refs_8_), channel_id=1, source_target_pairs={{0,7},{1,0},{2,1},{3,2},{4,3},{5,4},{6,5},{7,6},{8,15},{9,8},{10,9... | collective-permute-start | bytes 491528 | tf_op jit(solution)/shard_map/ppermute | solution.py:346
  163.9 2.3 %collective-permute-done.17.refs_3_ = bf16[320,256]{1,0:T(8,128)(2,1)S(1)} collective-permute-done((bf16[320,256]{1,0:T(8,128)(2,1)S(1)}, bf16[320,256]{1,0:T(8,128)(2,1)S(1)}, u32[]{:S(2)}, u32[]{:S(2)}) %collective-permute-start.17) | collective-permute-done | bytes 163872 | tf_op jit(solution)/shard_map/ppermute | solution.py:343
  168.1 5.1 %collective-permute-start.22 = (bf16[320,256]{1,0:T(8,128)(2,1)S(1)}, bf16[320,256]{1,0:T(8,128)(2,1)S(1)}, u32[]{:S(2)}, u32[]{:S(2)}) collective-permute-start(bf16[320,256]{1,0:T(8,128)(2,1)S(1)} %collective-permute-done.21.refs_7_), channel_id=1, source_target_pairs={{0,7},{1,0},{2,1},{3,2},{4,3},{5,4},{6,5},{7,6},{8,15},{9,8},{10,9... | collective-permute-start | bytes 491528 | tf_op jit(solution)/shard_map/ppermute | solution.py:346
  176.5 6.5 %collective-permute-done.19.refs_5_ = bf16[320,256]{1,0:T(8,128)(2,1)S(1)} collective-permute-done((bf16[320,256]{1,0:T(8,128)(2,1)S(1)}, bf16[320,256]{1,0:T(8,128)(2,1)S(1)}, u32[]{:S(2)}, u32[]{:S(2)}) %collective-permute-start.19) | collective-permute-done | bytes 163872 | tf_op jit(solution)/shard_map/ppermute | solution.py:343
  185.4 15.3 %all-to-all-start.1 = ((bf16[64,24,128]{2,1,0:T(8,128)(2,1)}), bf16[64,24,128]{2,1,0:T(8,128)(2,1)}, u32[]{:S(2)}, u32[]{:S(2)}) async-start(bf16[64,24,128]{2,1,0:T(8,128)(2,1)} %bitcast.18), calls=%async_computation.1 | async-start | bytes 786432 | tf_op jit(solution)/shard_map/all_to_all | solution.py:393
  204.0 2.7 %grads.2 = (bf16[1,2048,128]{2,1,0:T(8,128)(2,1)S(1)}, bf16[1,2048,128]{2,1,0:T(8,128)(2,1)S(1)}, bf16[1,2048,128]{2,1,0:T(8,128)(2,1)S(1)}) custom-call(s32[3]{0:T(128)S(1)} %constant_dynamic-update-slice_fusion.refs_0_, bf16[320,1024]{1,0:T(8,128)(2,1)S(1)} %unpack.1.refs_1_, bf16[320,1024]{1,0:T(8,128)(2,1)S(1)} %collective-permute-done.8.refs_2_, ...), custom_call_target="tpu_custom_call" | custom-call | flops 503316480 | bytes 1048576 | tf_op jit(solution)/shard_map/grads/pallas_call | solution.py:26
  206.7 1.9 collective-permute-start.23
  208.7 2.4 %collective-permute-start.24 = (bf16[1,2048,128]{2,1,0:T(8,128)(2,1)S(1)}, bf16[1,2048,128]{2,1,0:T(8,128)(2,1)S(1)}, u32[]{:S(2)}, u32[]{:S(2)}) collective-permute-start(bf16[1,2048,128]{2,1,0:T(8,128)(2,1)S(1)} %get-tuple-element.110), channel_id=1, source_target_pairs={{0,512},{512,0},{1,513},{513,1},{2,514},{514,2},{3,515},{515,3},{4... | collective-permute-start | bytes 1572872 | tf_op jit(solution)/shard_map/ppermute | solution.py:398
  211.1 1.9 collective-permute-start.25
  214.9 3.7 %grads.3 = (bf16[1,2048,128]{2,1,0:T(8,128)(2,1)}, bf16[1,2048,128]{2,1,0:T(8,128)(2,1)}, bf16[1,2048,128]{2,1,0:T(8,128)(2,1)}) custom-call(s32[3]{0:T(128)S(1)} %constant_dynamic-update-slice_fusion.1.refs_0_, bf16[320,1024]{1,0:T(8,128)(2,1)S(1)} %unpack.1.refs_1_, bf16[320,1024]{1,0:T(8,128)(2,1)S(1)} %collective-permute-done.8.refs_2_, ...), custom_call_target="tpu_custom_call" | custom-call | flops 503316480 | bytes 1048576 | tf_op jit(solution)/shard_map/grads/pallas_call | solution.py:26
  219.9 2.7 %combine.1 = bf16[32,512]{1,0:T(8,128)(2,1)} custom-call(s32[3]{0:T(128)} %copy-done.10, bf16[1536,128]{1,0:T(8,128)(2,1)} %bitcast.12.refs_1_, bf16[320,32]{1,0:T(8,128)(2,1)} %get-tuple-element.116.refs_2_), custom_call_target="tpu_custom_call" | custom-call | bytes 1048576 | tf_op jit(solution)/shard_map/combine/pallas_call | solution.py:26
  (71 shorter events, 33.0 us)
Async XLA Ops:
  0.6 25.1 %copy-start.7 = (bf16[1,2048,128]{2,1,0:T(8,128)(2,1)S(1)}, bf16[1,2048,128]{2,1,0:T(8,128)(2,1)}, u32[]{:S(2)}) copy-start(bf16[1,2048,128]{2,1,0:T(8,128)(2,1)} %param.17) | copy-start | bytes 1572868
  3.1 59.7 %all-to-all-start = ((bf16[64,40,128]{2,1,0:T(8,128)(2,1)}), bf16[64,40,128]{2,1,0:T(8,128)(2,1)S(1)}, u32[]{:S(2)}, u32[]{:S(2)}) async-start(bf16[64,40,128]{2,1,0:T(8,128)(2,1)} %bitcast.20), calls=%async_computation | async-start | bytes 1310720 | tf_op jit(solution)/shard_map/all_to_all | solution.py:303
  25.5 37.2 %copy-start.9 = (bf16[1,2048,128]{2,1,0:T(8,128)(2,1)S(1)}, bf16[1,2048,128]{2,1,0:T(8,128)(2,1)}, u32[]{:S(2)}) copy-start(bf16[1,2048,128]{2,1,0:T(8,128)(2,1)} %param.19) | copy-start | bytes 1572868
  25.9 21.8 %collective-permute-start.7 = (bf16[256,256]{1,0:T(8,128)(2,1)S(1)}, bf16[256,256]{1,0:T(8,128)(2,1)S(1)}, u32[]{:S(2)}, u32[]{:S(2)}) collective-permute-start(bf16[256,256]{1,0:T(8,128)(2,1)S(1)} %pad_maximum_fusion.7), channel_id=1, source_target_pairs={{0,515},{1,0},{2,1},{3,2},{4,3},{5,512},{6,513},{7,514},{512,519},... | collective-permute-start | bytes 393224 | tf_op jit(solution)/shard_map/ppermute | solution.py:319
  30.4 19.3 %collective-permute-start.6 = (bf16[256,256]{1,0:T(8,128)(2,1)S(1)}, bf16[256,256]{1,0:T(8,128)(2,1)S(1)}, u32[]{:S(2)}, u32[]{:S(2)}) collective-permute-start(bf16[256,256]{1,0:T(8,128)(2,1)S(1)} %pad_maximum_fusion.6), channel_id=1, source_target_pairs={{0,514},{1,515},{2,0},{3,1},{4,2},{5,3},{6,512},{7,513},{512,518},... | collective-permute-start | bytes 393224 | tf_op jit(solution)/shard_map/ppermute | solution.py:319
  36.0 19.5 %collective-permute-start.5 = (bf16[256,256]{1,0:T(8,128)(2,1)S(1)}, bf16[256,256]{1,0:T(8,128)(2,1)S(1)}, u32[]{:S(2)}, u32[]{:S(2)}) collective-permute-start(bf16[256,256]{1,0:T(8,128)(2,1)S(1)} %pad_maximum_fusion.5), channel_id=1, source_target_pairs={{0,513},{1,514},{2,515},{3,0},{4,1},{5,2},{6,3},{7,512},{512,517},... | collective-permute-start | bytes 393224 | tf_op jit(solution)/shard_map/ppermute | solution.py:319
  38.0 19.2 %collective-permute-start.4 = (bf16[256,256]{1,0:T(8,128)(2,1)S(1)}, bf16[256,256]{1,0:T(8,128)(2,1)S(1)}, u32[]{:S(2)}, u32[]{:S(2)}) collective-permute-start(bf16[256,256]{1,0:T(8,128)(2,1)S(1)} %pad_maximum_fusion.4), channel_id=1, source_target_pairs={{0,512},{1,513},{2,514},{3,515},{4,0},{5,1},{6,2},{7,3},{512,516},... | collective-permute-start | bytes 393224 | tf_op jit(solution)/shard_map/ppermute | solution.py:319
  40.0 17.2 %collective-permute-start.3 = (bf16[256,256]{1,0:T(8,128)(2,1)S(1)}, bf16[256,256]{1,0:T(8,128)(2,1)S(1)}, u32[]{:S(2)}, u32[]{:S(2)}) collective-permute-start(bf16[256,256]{1,0:T(8,128)(2,1)S(1)} %pad_maximum_fusion.3), channel_id=1, source_target_pairs={{0,3},{1,512},{2,513},{3,514},{4,515},{5,0},{6,1},{7,2},{512,7},{5... | collective-permute-start | bytes 393224 | tf_op jit(solution)/shard_map/ppermute | solution.py:319
  47.7 10.6 %collective-permute-start.2 = (bf16[256,256]{1,0:T(8,128)(2,1)}, bf16[256,256]{1,0:T(8,128)(2,1)S(1)}, u32[]{:S(2)}, u32[]{:S(2)}) collective-permute-start(bf16[256,256]{1,0:T(8,128)(2,1)} %pad_maximum_fusion.2), channel_id=1, source_target_pairs={{0,2},{1,3},{2,512},{3,513},{4,514},{5,515},{6,0},{7,1},{512,6},{5... | collective-permute-start | bytes 393224 | tf_op jit(solution)/shard_map/ppermute | solution.py:319
  49.6 9.0 %collective-permute-start.1 = (bf16[256,256]{1,0:T(8,128)(2,1)}, bf16[256,256]{1,0:T(8,128)(2,1)S(1)}, u32[]{:S(2)}, u32[]{:S(2)}) collective-permute-start(bf16[256,256]{1,0:T(8,128)(2,1)} %pad_maximum_fusion.1), channel_id=1, source_target_pairs={{0,1},{1,2},{2,3},{3,512},{4,513},{5,514},{6,515},{7,0},{512,5},{5... | collective-permute-start | bytes 393224 | tf_op jit(solution)/shard_map/ppermute | solution.py:319
  55.5 3.1 %collective-permute-start = (bf16[256,256]{1,0:T(8,128)(2,1)}, bf16[256,256]{1,0:T(8,128)(2,1)S(1)}, u32[]{:S(2)}, u32[]{:S(2)}) collective-permute-start(bf16[256,256]{1,0:T(8,128)(2,1)} %pad_maximum_fusion), channel_id=1, source_target_pairs={{0,0},{1,1},{2,2},{3,3},{4,512},{5,513},{6,514},{7,515},{512,4},{5... | collective-permute-start | bytes 393224 | tf_op jit(solution)/shard_map/ppermute | solution.py:319
  57.2 155.8 %copy-start.10 = (s32[3]{0:T(128)}, s32[3]{0:T(128)S(1)}, u32[]{:S(2)}) copy-start(s32[3]{0:T(128)S(1)} %pad_add_fusion.refs_0_._) | copy-start | bytes 40
  63.6 70.0 %collective-permute-start.15 = (bf16[2048,640]{1,0:T(8,128)(2,1)S(1)}, bf16[2048,640]{1,0:T(8,128)(2,1)S(1)}, u32[]{:S(2)}, u32[]{:S(2)}) collective-permute-start(bf16[2048,640]{1,0:T(8,128)(2,1)S(1)} %bundle.1.refs_8_.refs_9_), channel_id=1, source_target_pairs={{0,512},{512,0},{1,513},{513,1},{2,514},{514,2},{3,515},{515,3},{4... | collective-permute-start | bytes 7864328 | tf_op jit(solution)/shard_map/ppermute | solution.py:328
  71.8 19.7 %collective-permute-start.8 = (bf16[320,1024]{1,0:T(8,128)(2,1)S(1)}, bf16[320,1024]{1,0:T(8,128)(2,1)S(1)}, u32[]{:S(2)}, u32[]{:S(2)}) collective-permute-start(bf16[320,1024]{1,0:T(8,128)(2,1)S(1)} %unpack.1.refs_1_), channel_id=1, source_target_pairs={{0,1},{512,519},{1,2},{513,512},{2,3},{514,513},{3,4},{515,514},{4... | collective-permute-start | bytes 1966088 | tf_op jit(solution)/shard_map/ppermute | solution.py:343
  73.7 19.7 %collective-permute-start.12 = (bf16[320,1024]{1,0:T(8,128)(2,1)S(1)}, bf16[320,1024]{1,0:T(8,128)(2,1)S(1)}, u32[]{:S(2)}, u32[]{:S(2)}) collective-permute-start(bf16[320,1024]{1,0:T(8,128)(2,1)S(1)} %unpack.1.refs_1_), channel_id=1, source_target_pairs={{0,7},{512,513},{1,0},{513,514},{2,1},{514,515},{3,2},{515,516},{4... | collective-permute-start | bytes 1966088 | tf_op jit(solution)/shard_map/ppermute | solution.py:346
  91.6 20.5 %collective-permute-start.9 = (bf16[320,1024]{1,0:T(8,128)(2,1)S(1)}, bf16[320,1024]{1,0:T(8,128)(2,1)S(1)}, u32[]{:S(2)}, u32[]{:S(2)}) collective-permute-start(bf16[320,1024]{1,0:T(8,128)(2,1)S(1)} %collective-permute-done.8.refs_2_), channel_id=1, source_target_pairs={{0,1},{512,519},{1,2},{513,512},{2,3},{514,513},{3,4},{515,514},{4... | collective-permute-start | bytes 1966088 | tf_op jit(solution)/shard_map/ppermute | solution.py:343
  93.5 20.5 %collective-permute-start.13 = (bf16[320,1024]{1,0:T(8,128)(2,1)S(1)}, bf16[320,1024]{1,0:T(8,128)(2,1)S(1)}, u32[]{:S(2)}, u32[]{:S(2)}) collective-permute-start(bf16[320,1024]{1,0:T(8,128)(2,1)S(1)} %collective-permute-done.12.refs_7_.refs_8_), channel_id=1, source_target_pairs={{0,7},{512,513},{1,0},{513,514},{2,1},{514,515},{3,2},{515,516},{4... | collective-permute-start | bytes 1966088 | tf_op jit(solution)/shard_map/ppermute | solution.py:346
  112.1 19.7 %collective-permute-start.10 = (bf16[320,1024]{1,0:T(8,128)(2,1)S(1)}, bf16[320,1024]{1,0:T(8,128)(2,1)S(1)}, u32[]{:S(2)}, u32[]{:S(2)}) collective-permute-start(bf16[320,1024]{1,0:T(8,128)(2,1)S(1)} %collective-permute-done.9.refs_3_), channel_id=1, source_target_pairs={{0,1},{512,519},{1,2},{513,512},{2,3},{514,513},{3,4},{515,514},{4... | collective-permute-start | bytes 1966088 | tf_op jit(solution)/shard_map/ppermute | solution.py:343
  114.0 19.7 %collective-permute-start.14 = (bf16[320,1024]{1,0:T(8,128)(2,1)S(1)}, bf16[320,1024]{1,0:T(8,128)(2,1)S(1)}, u32[]{:S(2)}, u32[]{:S(2)}) collective-permute-start(bf16[320,1024]{1,0:T(8,128)(2,1)S(1)} %collective-permute-done.13.refs_6_.refs_7_), channel_id=1, source_target_pairs={{0,7},{512,513},{1,0},{513,514},{2,1},{514,515},{3,2},{515,516},{4... | collective-permute-start | bytes 1966088 | tf_op jit(solution)/shard_map/ppermute | solution.py:346
  131.7 15.4 %collective-permute-start.11 = (bf16[320,1024]{1,0:T(8,128)(2,1)S(1)}, bf16[320,1024]{1,0:T(8,128)(2,1)S(1)}, u32[]{:S(2)}, u32[]{:S(2)}) collective-permute-start(bf16[320,1024]{1,0:T(8,128)(2,1)S(1)} %collective-permute-done.10.refs_4_), channel_id=1, source_target_pairs={{0,1},{512,519},{1,2},{513,512},{2,3},{514,513},{3,4},{515,514},{4... | collective-permute-start | bytes 1966088 | tf_op jit(solution)/shard_map/ppermute | solution.py:343
  147.2 37.5 %copy-start.4 = (bf16[320,1024]{1,0:T(8,128)(2,1)}, bf16[320,1024]{1,0:T(8,128)(2,1)S(1)}, u32[]{:S(2)}) copy-start(bf16[320,1024]{1,0:T(8,128)(2,1)S(1)} %collective-permute-done.11.block.refs_5_) | copy-start | bytes 1966084
  148.1 8.4 %collective-permute-start.16 = (bf16[320,256]{1,0:T(8,128)(2,1)S(1)}, bf16[320,256]{1,0:T(8,128)(2,1)S(1)}, u32[]{:S(2)}, u32[]{:S(2)}) collective-permute-start(bf16[320,256]{1,0:T(8,128)(2,1)S(1)} %get-tuple-element.107.refs_1_.refs_9_), channel_id=1, source_target_pairs={{0,1},{1,2},{2,3},{3,4},{4,5},{5,6},{6,7},{7,0},{8,9},{9,10},{10,1... | collective-permute-start | bytes 491528 | tf_op jit(solution)/shard_map/ppermute | solution.py:343
  150.0 8.4 %collective-permute-start.20 = (bf16[320,256]{1,0:T(8,128)(2,1)S(1)}, bf16[320,256]{1,0:T(8,128)(2,1)S(1)}, u32[]{:S(2)}, u32[]{:S(2)}) collective-permute-start(bf16[320,256]{1,0:T(8,128)(2,1)S(1)} %get-tuple-element.107.refs_1_.refs_9_), channel_id=1, source_target_pairs={{0,7},{1,0},{2,1},{3,2},{4,3},{5,4},{6,5},{7,6},{8,15},{9,8},{10,9... | collective-permute-start | bytes 491528 | tf_op jit(solution)/shard_map/ppermute | solution.py:346
  156.5 9.6 %collective-permute-start.17 = (bf16[320,256]{1,0:T(8,128)(2,1)S(1)}, bf16[320,256]{1,0:T(8,128)(2,1)S(1)}, u32[]{:S(2)}, u32[]{:S(2)}) collective-permute-start(bf16[320,256]{1,0:T(8,128)(2,1)S(1)} %collective-permute-done.16.refs_2_), channel_id=1, source_target_pairs={{0,1},{1,2},{2,3},{3,4},{4,5},{5,6},{6,7},{7,0},{8,9},{9,10},{10,1... | collective-permute-start | bytes 491528 | tf_op jit(solution)/shard_map/ppermute | solution.py:343
  158.5 9.6 %collective-permute-start.21 = (bf16[320,256]{1,0:T(8,128)(2,1)S(1)}, bf16[320,256]{1,0:T(8,128)(2,1)S(1)}, u32[]{:S(2)}, u32[]{:S(2)}) collective-permute-start(bf16[320,256]{1,0:T(8,128)(2,1)S(1)} %collective-permute-done.20.refs_8_), channel_id=1, source_target_pairs={{0,7},{1,0},{2,1},{3,2},{4,3},{5,4},{6,5},{7,6},{8,15},{9,8},{10,9... | collective-permute-start | bytes 491528 | tf_op jit(solution)/shard_map/ppermute | solution.py:346
  166.2 8.4 %collective-permute-start.18 = (bf16[320,256]{1,0:T(8,128)(2,1)S(1)}, bf16[320,256]{1,0:T(8,128)(2,1)S(1)}, u32[]{:S(2)}, u32[]{:S(2)}) collective-permute-start(bf16[320,256]{1,0:T(8,128)(2,1)S(1)} %collective-permute-done.17.refs_3_), channel_id=1, source_target_pairs={{0,1},{1,2},{2,3},{3,4},{4,5},{5,6},{6,7},{7,0},{8,9},{9,10},{10,1... | collective-permute-start | bytes 491528 | tf_op jit(solution)/shard_map/ppermute | solution.py:343
  168.1 8.4 %collective-permute-start.22 = (bf16[320,256]{1,0:T(8,128)(2,1)S(1)}, bf16[320,256]{1,0:T(8,128)(2,1)S(1)}, u32[]{:S(2)}, u32[]{:S(2)}) collective-permute-start(bf16[320,256]{1,0:T(8,128)(2,1)S(1)} %collective-permute-done.21.refs_7_), channel_id=1, source_target_pairs={{0,7},{1,0},{2,1},{3,2},{4,3},{5,4},{6,5},{7,6},{8,15},{9,8},{10,9... | collective-permute-start | bytes 491528 | tf_op jit(solution)/shard_map/ppermute | solution.py:346
  174.6 8.4 %collective-permute-start.19 = (bf16[320,256]{1,0:T(8,128)(2,1)S(1)}, bf16[320,256]{1,0:T(8,128)(2,1)S(1)}, u32[]{:S(2)}, u32[]{:S(2)}) collective-permute-start(bf16[320,256]{1,0:T(8,128)(2,1)S(1)} %collective-permute-done.18.refs_4_), channel_id=1, source_target_pairs={{0,1},{1,2},{2,3},{3,4},{4,5},{5,6},{6,7},{7,0},{8,9},{9,10},{10,1... | collective-permute-start | bytes 491528 | tf_op jit(solution)/shard_map/ppermute | solution.py:343
  185.4 34.5 %all-to-all-start.1 = ((bf16[64,24,128]{2,1,0:T(8,128)(2,1)}), bf16[64,24,128]{2,1,0:T(8,128)(2,1)}, u32[]{:S(2)}, u32[]{:S(2)}) async-start(bf16[64,24,128]{2,1,0:T(8,128)(2,1)} %bitcast.18), calls=%async_computation.1 | async-start | bytes 786432 | tf_op jit(solution)/shard_map/all_to_all | solution.py:393
  206.7 6.3 %collective-permute-start.23 = (bf16[1,2048,128]{2,1,0:T(8,128)(2,1)S(1)}, bf16[1,2048,128]{2,1,0:T(8,128)(2,1)S(1)}, u32[]{:S(2)}, u32[]{:S(2)}) collective-permute-start(bf16[1,2048,128]{2,1,0:T(8,128)(2,1)S(1)} %get-tuple-element.109), channel_id=1, source_target_pairs={{0,512},{512,0},{1,513},{513,1},{2,514},{514,2},{3,515},{515,3},{4... | collective-permute-start | bytes 1572872 | tf_op jit(solution)/shard_map/ppermute | solution.py:398
  208.7 4.4 %collective-permute-start.24 = (bf16[1,2048,128]{2,1,0:T(8,128)(2,1)S(1)}, bf16[1,2048,128]{2,1,0:T(8,128)(2,1)S(1)}, u32[]{:S(2)}, u32[]{:S(2)}) collective-permute-start(bf16[1,2048,128]{2,1,0:T(8,128)(2,1)S(1)} %get-tuple-element.110), channel_id=1, source_target_pairs={{0,512},{512,0},{1,513},{513,1},{2,514},{514,2},{3,515},{515,3},{4... | collective-permute-start | bytes 1572872 | tf_op jit(solution)/shard_map/ppermute | solution.py:398
  211.1 3.8 %collective-permute-start.25 = (bf16[1,2048,128]{2,1,0:T(8,128)(2,1)S(1)}, bf16[1,2048,128]{2,1,0:T(8,128)(2,1)S(1)}, u32[]{:S(2)}, u32[]{:S(2)}) collective-permute-start(bf16[1,2048,128]{2,1,0:T(8,128)(2,1)S(1)} %get-tuple-element.111), channel_id=1, source_target_pairs={{0,512},{512,0},{1,513},{513,1},{2,514},{514,2},{3,515},{515,3},{4... | collective-permute-start | bytes 1572872 | tf_op jit(solution)/shard_map/ppermute | solution.py:398
  (7 other events, 35.7 us)

commit v8 on v6

--- a/solution.py
+++ b/solution.py
@@ -40,6 +40,10 @@
 
 def transposed_dot(left, right):
     return lax.dot_general(left, right, (((0,), (0,)), ((), ())), preferred_element_type=F32)
+
+
+def shift(parts, step):
+    return [(p, (p + step) % parts) for p in range(parts)]
 
 
 def around(parts, step):
@@ -271,6 +275,7 @@
         (*xs, *dys, both, hidden, *received),
         outs,
         flops=2 * both.shape[0] * half * (both.shape[1] + hidden.shape[1]),
+        vmem=56,
     )
 
 
@@ -301,8 +306,8 @@
         flat.reshape(owners, -1, LANES), peers, split_axis=0, concat_axis=0, tiled=True
     )
     sub = width // 2
-    turned = []
-    for k in range(parts):
+    turned = [None] * parts
+    for k in reversed(range(parts)):
         target = lax.rem(place + k, parts)
         start = lax.rem(target, half) * width + target // half * sub
         piece = jnp.concatenate(
@@ -313,8 +318,9 @@
             for p in range(parts):
                 t = (p + k) % parts
                 perm.append((h * parts + p, t // half * parts + h * half + t % half))
-        turned.append(lax.ppermute(piece, ("dp", "y"), perm))
-    flat, turned = lax.optimization_barrier((flat, turned))
+        turned[k] = lax.ppermute(piece, ("dp", "y"), perm)
+    flat, turned = lax.optimization_barrier((flat, turned[::-1]))
+    turned = turned[::-1]
     bundle = local_call(
         bundle_kernel,
         "bundle",
@@ -334,19 +340,20 @@
         [pltpu.VMEM(flat.shape, F32)],
     )
 
-    def ring(value, rightward):
+    def ring(value, rightward, axes, on, back):
         held = {0: value}
         right = left = value
         for d in range(1, half + 1):
             if d < half or rightward:
-                right = lax.ppermute(right, ("dp", "y"), around(parts, 1))
+                right = lax.ppermute(right, axes, on)
                 held[d] = right
             if d < half or not rightward:
-                left = lax.ppermute(left, ("dp", "y"), around(parts, -1))
+                left = lax.ppermute(left, axes, back)
                 held[parts - d] = left
         return [held[d] for d in range(parts)]
 
-    xs, dys = ring(own[0], True), ring(own[1], False)
+    two_way = ("dp", "y"), around(parts, 1), around(parts, -1)
+    xs, dys = ring(own[0], True, *two_way), ring(own[1], False, *two_way)
     most = [d for d in range(parts) if d != half]
     begun, piece = local_call(
         lambda *refs: forward_most(parts, most, half, *refs),
@@ -377,8 +384,8 @@
     d_rows = local_call(
         lambda *refs: back_kernel(parts, capacity, *refs),
         "back",
-        position,
-        ring(d_both, True),
+        position.at[2].set(1),
+        ring(d_both, True, "y", shift(parts, 1), shift(parts, -1)),
         jax.ShapeDtypeStruct((owners * stretch, LANES), BF16),
         [
             pltpu.VMEM((owners * stretch, LANES), F32),

time: 210 us -> 206 us (0.981)
  Pallas kernels: 18.1 us -> 24.4 us
  local copies, waits for them, and re-layouts: 8.28 us -> 2.39 us
  waiting for transfers between devices: 28.2 us -> 24.5 us
    pallas_call x8, Pallas kernels: 15.7 us -> 22 us  [local_call(): pl.pallas_call(kernel, grid=(1,), in_specs=[pl.BlockSpec(memory_space=plt...]
    unnamed x40 -> x59, local copies, waits for them, and re-layouts: 8.14 us -> 2.23 us
    ppermute x1, starting transfers between devices: 7.29 us -> 3 us  [shards(): bundles = (bundle, lax.ppermute(bundle, 'dp', swap))]
    all_to_all x1, waiting for transfers between devices: 4.1 us -> 0.01 us  [shards(): lax.all_to_all(flat.reshape(owners, -1, LANES), peers, split_axis=0, conc...]
    ppermute x29, starting transfers between devices: 97.7 us -> 101 us  [the longest x11 37.6 us: ring(): right = lax.ppermute(right, axes, on)]
  transfers between devices with their start and end apart: 35 -> 35, of which waited for: 12 -> 13; matrix products, arithmetic and copies ran while one was open for 1% -> 1% of each run, Pallas kernels for 5% -> 7%
where the time goes in v8:
time: 206 us; the launch traced here: 204 us
  starting transfers between devices  148 us (72%)
  waiting for transfers between devices  24.5 us (12%)
  Pallas kernels  24.4 us (12%)
  local copies, waits for them, and re-layouts  2.39 us (1%)
  other arithmetic  2.17 us (1%)
    ppermute x11, starting transfers between devices, ring(): right = lax.ppermute(right, axes, on)  37.6 us
    ppermute x10, starting transfers between devices, ring(): left = lax.ppermute(left, axes, back)  32.1 us
    ppermute x8, starting transfers between devices, shards(): turned[k] = lax.ppermute(piece, ('dp', 'y'), perm)  31.8 us
    all_to_all x1, starting transfers between devices, shards(): lax.all_to_all(flat.reshape(owners, -1, LANES), peers, split_axis=0, conc...  22.5 us
    pallas_call x8, Pallas kernels, local_call(): pl.pallas_call(kernel, grid=(1,), in_specs=[pl.BlockSpec(memory_space=plt...  22 us
    ppermute x11, waiting for transfers between devices, ring(): right = lax.ppermute(right, axes, on)  17.4 us
    all_to_all x1, starting transfers between devices, shards(): lax.all_to_all(d_rows.reshape(owners, -1, LANES), peers, split_axis=0, co...  15.1 us
    ppermute x3, starting transfers between devices, shards(): lax.ppermute(share, 'dp', swap)  6.23 us
  transfers between devices with their start and end apart: 35, of which 13 were waited for; matrix products, arithmetic and copies ran while one was open for 1% of the time, Pallas kernels for 7%

profile of v8, /device:TPU:6, one launch (start us, length us, event | category | flops | bytes accessed | tf_op | source)
XLA Modules:
  0.0 203.7 jit_solution(10659386026789705582)
XLA Ops:
  0.7 2.5 %pack.1 = (bf16[2560,128]{1,0:T(8,128)(2,1)}, bf16[320,32]{1,0:T(8,128)(2,1)}) custom-call(s32[1]{0:T(128)} %bitcast.refs_0_, s32[8,32]{1,0:T(8,128)} %bitcast.21, bf16[8,32]{1,0:T(8,128)(2,1)} %bitcast.22, bf16[32,4096]{1,0:T(8,128)(2,1)} %refs_3_.1, bf16[32,4096]{1,0:T(8,128)(2,1)} %refs_4_.1), custom_call_target="tpu_custom_call" | custom-call | tf_op jit(solution)/shard_map/pack/pallas_call | solution.py:103
  3.1 22.5 %all-to-all-start = ((bf16[64,40,128]{2,1,0:T(8,128)(2,1)}), bf16[64,40,128]{2,1,0:T(8,128)(2,1)S(1)}, u32[]{:S(2)}, u32[]{:S(2)}) async-start(bf16[64,40,128]{2,1,0:T(8,128)(2,1)} %bitcast.20), calls=%async_computation | async-start | bytes 1310720 | tf_op jit(solution)/shard_map/all_to_all | solution.py:305
  26.7 3.5 %collective-permute-start.6 = (bf16[256,256]{1,0:T(8,128)(2,1)S(1)}, bf16[256,256]{1,0:T(8,128)(2,1)S(1)}, u32[]{:S(2)}, u32[]{:S(2)}) collective-permute-start(bf16[256,256]{1,0:T(8,128)(2,1)S(1)} %pad_maximum_fusion.6), channel_id=1, source_target_pairs={{0,1},{1,2},{2,3},{3,512},{4,513},{5,514},{6,515},{7,0},{512,5},{5... | collective-permute-start | bytes 393224 | tf_op jit(solution)/shard_map/ppermute | solution.py:321
  30.2 4.5 %collective-permute-start.5 = (bf16[256,256]{1,0:T(8,128)(2,1)S(1)}, bf16[256,256]{1,0:T(8,128)(2,1)S(1)}, u32[]{:S(2)}, u32[]{:S(2)}) collective-permute-start(bf16[256,256]{1,0:T(8,128)(2,1)S(1)} %pad_maximum_fusion.5), channel_id=1, source_target_pairs={{0,2},{1,3},{2,512},{3,513},{4,514},{5,515},{6,0},{7,1},{512,6},{5... | collective-permute-start | bytes 393224 | tf_op jit(solution)/shard_map/ppermute | solution.py:321
  34.7 8.4 %collective-permute-start.4 = (bf16[256,256]{1,0:T(8,128)(2,1)S(1)}, bf16[256,256]{1,0:T(8,128)(2,1)S(1)}, u32[]{:S(2)}, u32[]{:S(2)}) collective-permute-start(bf16[256,256]{1,0:T(8,128)(2,1)S(1)} %pad_maximum_fusion.4), channel_id=1, source_target_pairs={{0,3},{1,512},{2,513},{3,514},{4,515},{5,0},{6,1},{7,2},{512,7},{5... | collective-permute-start | bytes 393224 | tf_op jit(solution)/shard_map/ppermute | solution.py:321
  47.1 4.8 %collective-permute-start.2 = (bf16[256,256]{1,0:T(8,128)(2,1)}, bf16[256,256]{1,0:T(8,128)(2,1)S(1)}, u32[]{:S(2)}, u32[]{:S(2)}) collective-permute-start(bf16[256,256]{1,0:T(8,128)(2,1)} %pad_maximum_fusion.2), channel_id=1, source_target_pairs={{0,513},{1,514},{2,515},{3,0},{4,1},{5,2},{6,3},{7,512},{512,517},... | collective-permute-start | bytes 393224 | tf_op jit(solution)/shard_map/ppermute | solution.py:321
  51.9 3.0 %collective-permute-start.1 = (bf16[256,256]{1,0:T(8,128)(2,1)}, bf16[256,256]{1,0:T(8,128)(2,1)S(1)}, u32[]{:S(2)}, u32[]{:S(2)}) collective-permute-start(bf16[256,256]{1,0:T(8,128)(2,1)} %pad_maximum_fusion.1), channel_id=1, source_target_pairs={{0,514},{1,515},{2,0},{3,1},{4,2},{5,3},{6,512},{7,513},{512,518},... | collective-permute-start | bytes 393224 | tf_op jit(solution)/shard_map/ppermute | solution.py:321
  54.9 5.1 %collective-permute-start = (bf16[256,256]{1,0:T(8,128)(2,1)}, bf16[256,256]{1,0:T(8,128)(2,1)S(1)}, u32[]{:S(2)}, u32[]{:S(2)}) collective-permute-start(bf16[256,256]{1,0:T(8,128)(2,1)} %pad_maximum_fusion), channel_id=1, source_target_pairs={{0,515},{1,0},{2,1},{3,2},{4,3},{5,512},{6,513},{7,514},{512,519},... | collective-permute-start | bytes 393224 | tf_op jit(solution)/shard_map/ppermute | solution.py:321
  65.1 3.0 %collective-permute-start.22 = (bf16[2048,640]{1,0:T(8,128)(2,1)S(1)}, bf16[2048,640]{1,0:T(8,128)(2,1)S(1)}, u32[]{:S(2)}, u32[]{:S(2)}) collective-permute-start(bf16[2048,640]{1,0:T(8,128)(2,1)S(1)} %bundle.1.refs_15_.refs_9_), channel_id=1, source_target_pairs={{0,512},{512,0},{1,513},{513,1},{2,514},{514,2},{3,515},{515,3},{4... | collective-permute-start | bytes 7864328 | tf_op jit(solution)/shard_map/ppermute | solution.py:331
  69.0 6.1 %collective-permute-start.8 = (bf16[320,512]{1,0:T(8,128)(2,1)S(1)}, bf16[320,512]{1,0:T(8,128)(2,1)S(1)}, u32[]{:S(2)}, u32[]{:S(2)}) collective-permute-start(bf16[320,512]{1,0:T(8,128)(2,1)S(1)} %get-tuple-element.111.refs_1_), channel_id=1, source_target_pairs={{0,1},{512,519},{1,2},{513,512},{2,3},{514,513},{3,4},{515,514},{4... | collective-permute-start | bytes 983048 | tf_op jit(solution)/shard_map/ppermute | solution.py:348
  77.0 3.0 %collective-permute-start.16 = (bf16[320,512]{1,0:T(8,128)(2,1)S(1)}, bf16[320,512]{1,0:T(8,128)(2,1)S(1)}, u32[]{:S(2)}, u32[]{:S(2)}) collective-permute-start(bf16[320,512]{1,0:T(8,128)(2,1)S(1)} %get-tuple-element.111.refs_1_), channel_id=1, source_target_pairs={{0,7},{512,513},{1,0},{513,514},{2,1},{514,515},{3,2},{515,516},{4... | collective-permute-start | bytes 983048 | tf_op jit(solution)/shard_map/ppermute | solution.py:351
  80.0 2.8 %collective-permute-start.19 = (bf16[320,512]{1,0:T(8,128)(2,1)S(1)}, bf16[320,512]{1,0:T(8,128)(2,1)S(1)}, u32[]{:S(2)}, u32[]{:S(2)}) collective-permute-start(bf16[320,512]{1,0:T(8,128)(2,1)S(1)} %get-tuple-element.119.refs_8_.refs_9_), channel_id=1, source_target_pairs={{0,1},{512,519},{1,2},{513,512},{2,3},{514,513},{3,4},{515,514},{4... | collective-permute-start | bytes 983048 | tf_op jit(solution)/shard_map/ppermute | solution.py:348
  82.9 3.9 %collective-permute-start.9 = (bf16[320,512]{1,0:T(8,128)(2,1)S(1)}, bf16[320,512]{1,0:T(8,128)(2,1)S(1)}, u32[]{:S(2)}, u32[]{:S(2)}) collective-permute-start(bf16[320,512]{1,0:T(8,128)(2,1)S(1)} %collective-permute-done.8.refs_2_), channel_id=1, source_target_pairs={{0,1},{512,519},{1,2},{513,512},{2,3},{514,513},{3,4},{515,514},{4... | collective-permute-start | bytes 983048 | tf_op jit(solution)/shard_map/ppermute | solution.py:348
  86.8 3.1 %collective-permute-start.13 = (bf16[320,512]{1,0:T(8,128)(2,1)S(1)}, bf16[320,512]{1,0:T(8,128)(2,1)S(1)}, u32[]{:S(2)}, u32[]{:S(2)}) collective-permute-start(bf16[320,512]{1,0:T(8,128)(2,1)S(1)} %collective-permute-done.12.refs_14_.refs_16_), channel_id=1, source_target_pairs={{0,7},{512,513},{1,0},{513,514},{2,1},{514,515},{3,2},{515,516},{4... | collective-permute-start | bytes 983048 | tf_op jit(solution)/shard_map/ppermute | solution.py:351
  90.4 2.6 %collective-permute-start.17 = (bf16[320,512]{1,0:T(8,128)(2,1)S(1)}, bf16[320,512]{1,0:T(8,128)(2,1)S(1)}, u32[]{:S(2)}, u32[]{:S(2)}) collective-permute-start(bf16[320,512]{1,0:T(8,128)(2,1)S(1)} %collective-permute-done.16.refs_7_.refs_8_), channel_id=1, source_target_pairs={{0,7},{512,513},{1,0},{513,514},{2,1},{514,515},{3,2},{515,516},{4... | collective-permute-start | bytes 983048 | tf_op jit(solution)/shard_map/ppermute | solution.py:351
  93.0 3.3 %collective-permute-start.20 = (bf16[320,512]{1,0:T(8,128)(2,1)S(1)}, bf16[320,512]{1,0:T(8,128)(2,1)S(1)}, u32[]{:S(2)}, u32[]{:S(2)}) collective-permute-start(bf16[320,512]{1,0:T(8,128)(2,1)S(1)} %collective-permute-done.19.refs_9_.refs_10_), channel_id=1, source_target_pairs={{0,1},{512,519},{1,2},{513,512},{2,3},{514,513},{3,4},{515,514},{4... | collective-permute-start | bytes 983048 | tf_op jit(solution)/shard_map/ppermute | solution.py:348
  98.0 4.4 %collective-permute-start.10 = (bf16[320,512]{1,0:T(8,128)(2,1)S(1)}, bf16[320,512]{1,0:T(8,128)(2,1)S(1)}, u32[]{:S(2)}, u32[]{:S(2)}) collective-permute-start(bf16[320,512]{1,0:T(8,128)(2,1)S(1)} %collective-permute-done.9.refs_3_), channel_id=1, source_target_pairs={{0,1},{512,519},{1,2},{513,512},{2,3},{514,513},{3,4},{515,514},{4... | collective-permute-start | bytes 983048 | tf_op jit(solution)/shard_map/ppermute | solution.py:348
  102.4 2.7 %collective-permute-start.14 = (bf16[320,512]{1,0:T(8,128)(2,1)S(1)}, bf16[320,512]{1,0:T(8,128)(2,1)S(1)}, u32[]{:S(2)}, u32[]{:S(2)}) collective-permute-start(bf16[320,512]{1,0:T(8,128)(2,1)S(1)} %collective-permute-done.13.refs_13_.refs_15_), channel_id=1, source_target_pairs={{0,7},{512,513},{1,0},{513,514},{2,1},{514,515},{3,2},{515,516},{4... | collective-permute-start | bytes 983048 | tf_op jit(solution)/shard_map/ppermute | solution.py:351
  105.1 2.7 %collective-permute-start.18 = (bf16[320,512]{1,0:T(8,128)(2,1)S(1)}, bf16[320,512]{1,0:T(8,128)(2,1)S(1)}, u32[]{:S(2)}, u32[]{:S(2)}) collective-permute-start(bf16[320,512]{1,0:T(8,128)(2,1)S(1)} %collective-permute-done.17.refs_6_.refs_7_), channel_id=1, source_target_pairs={{0,7},{512,513},{1,0},{513,514},{2,1},{514,515},{3,2},{515,516},{4... | collective-permute-start | bytes 983048 | tf_op jit(solution)/shard_map/ppermute | solution.py:351
  107.9 3.1 %collective-permute-start.21 = (bf16[320,512]{1,0:T(8,128)(2,1)S(1)}, bf16[320,512]{1,0:T(8,128)(2,1)S(1)}, u32[]{:S(2)}, u32[]{:S(2)}) collective-permute-start(bf16[320,512]{1,0:T(8,128)(2,1)S(1)} %collective-permute-done.20.refs_10_.refs_11_), channel_id=1, source_target_pairs={{0,1},{512,519},{1,2},{513,512},{2,3},{514,513},{3,4},{515,514},{4... | collective-permute-start | bytes 983048 | tf_op jit(solution)/shard_map/ppermute | solution.py:348
  112.1 4.4 %collective-permute-start.11 = (bf16[320,512]{1,0:T(8,128)(2,1)S(1)}, bf16[320,512]{1,0:T(8,128)(2,1)S(1)}, u32[]{:S(2)}, u32[]{:S(2)}) collective-permute-start(bf16[320,512]{1,0:T(8,128)(2,1)S(1)} %collective-permute-done.10.refs_4_), channel_id=1, source_target_pairs={{0,1},{512,519},{1,2},{513,512},{2,3},{514,513},{3,4},{515,514},{4... | collective-permute-start | bytes 983048 | tf_op jit(solution)/shard_map/ppermute | solution.py:348
  116.5 2.7 %collective-permute-start.15 = (bf16[320,512]{1,0:T(8,128)(2,1)S(1)}, bf16[320,512]{1,0:T(8,128)(2,1)S(1)}, u32[]{:S(2)}, u32[]{:S(2)}) collective-permute-start(bf16[320,512]{1,0:T(8,128)(2,1)S(1)} %collective-permute-done.14.refs_12_.refs_14_), channel_id=1, source_target_pairs={{0,7},{512,513},{1,0},{513,514},{2,1},{514,515},{3,2},{515,516},{4... | collective-permute-start | bytes 983048 | tf_op jit(solution)/shard_map/ppermute | solution.py:351
  121.8 4.0 %collective-permute-done.11.x_ref.refs_5_ = bf16[320,512]{1,0:T(8,128)(2,1)S(1)} collective-permute-done((bf16[320,512]{1,0:T(8,128)(2,1)S(1)}, bf16[320,512]{1,0:T(8,128)(2,1)S(1)}, u32[]{:S(2)}, u32[]{:S(2)}) %collective-permute-start.11) | collective-permute-done | bytes 327712 | tf_op jit(solution)/shard_map/ppermute | solution.py:348
  127.1 3.5 %collective-permute-start.23 = (bf16[320,256]{1,0:T(8,128)(2,1)S(1)}, bf16[320,256]{1,0:T(8,128)(2,1)S(1)}, u32[]{:S(2)}, u32[]{:S(2)}) collective-permute-start(bf16[320,256]{1,0:T(8,128)(2,1)S(1)} %get-tuple-element.127.refs_1_.refs_17_), channel_id=1, source_target_pairs={{0,1},{1,2},{2,3},{3,4},{4,5},{5,6},{6,7},{7,0},{8,9},{9,10},{10,1... | collective-permute-start | bytes 491528 | tf_op jit(solution)/shard_map/ppermute | solution.py:348
  130.6 3.5 %collective-permute-start.27 = (bf16[320,256]{1,0:T(8,128)(2,1)S(1)}, bf16[320,256]{1,0:T(8,128)(2,1)S(1)}, u32[]{:S(2)}, u32[]{:S(2)}) collective-permute-start(bf16[320,256]{1,0:T(8,128)(2,1)S(1)} %get-tuple-element.127.refs_1_.refs_17_), channel_id=1, source_target_pairs={{0,7},{1,0},{2,1},{3,2},{4,3},{5,4},{6,5},{7,6},{8,15},{9,8},{10,9... | collective-permute-start | bytes 491528 | tf_op jit(solution)/shard_map/ppermute | solution.py:351
  137.9 4.7 %collective-permute-start.28 = (bf16[320,256]{1,0:T(8,128)(2,1)S(1)}, bf16[320,256]{1,0:T(8,128)(2,1)S(1)}, u32[]{:S(2)}, u32[]{:S(2)}) collective-permute-start(bf16[320,256]{1,0:T(8,128)(2,1)S(1)} %collective-permute-done.27.refs_8_), channel_id=1, source_target_pairs={{0,7},{1,0},{2,1},{3,2},{4,3},{5,4},{6,5},{7,6},{8,15},{9,8},{10,9... | collective-permute-start | bytes 491528 | tf_op jit(solution)/shard_map/ppermute | solution.py:351
  145.9 5.1 %collective-permute-start.29 = (bf16[320,256]{1,0:T(8,128)(2,1)S(1)}, bf16[320,256]{1,0:T(8,128)(2,1)S(1)}, u32[]{:S(2)}, u32[]{:S(2)}) collective-permute-start(bf16[320,256]{1,0:T(8,128)(2,1)S(1)} %collective-permute-done.28.refs_7_), channel_id=1, source_target_pairs={{0,7},{1,0},{2,1},{3,2},{4,3},{5,4},{6,5},{7,6},{8,15},{9,8},{10,9... | collective-permute-start | bytes 491528 | tf_op jit(solution)/shard_map/ppermute | solution.py:351
  154.3 6.5 %collective-permute-done.26.refs_5_ = bf16[320,256]{1,0:T(8,128)(2,1)S(1)} collective-permute-done((bf16[320,256]{1,0:T(8,128)(2,1)S(1)}, bf16[320,256]{1,0:T(8,128)(2,1)S(1)}, u32[]{:S(2)}, u32[]{:S(2)}) %collective-permute-start.26) | collective-permute-done | bytes 163872 | tf_op jit(solution)/shard_map/ppermute | solution.py:348
  163.2 15.1 %all-to-all-start.1 = ((bf16[64,24,128]{2,1,0:T(8,128)(2,1)}), bf16[64,24,128]{2,1,0:T(8,128)(2,1)S(1)}, u32[]{:S(2)}, u32[]{:S(2)}) async-start(bf16[64,24,128]{2,1,0:T(8,128)(2,1)} %bitcast.10), calls=%async_computation.1 | async-start | bytes 786432 | tf_op jit(solution)/shard_map/all_to_all | solution.py:399
  179.0 5.8 %grads.2 = (bf16[1,2048,128]{2,1,0:T(8,128)(2,1)}, bf16[1,2048,128]{2,1,0:T(8,128)(2,1)}, bf16[1,2048,128]{2,1,0:T(8,128)(2,1)}) custom-call(s32[3]{0:T(128)} %copy-done.26, bf16[320,512]{1,0:T(8,128)(2,1)} %copy-done, bf16[320,512]{1,0:T(8,128)(2,1)} %copy-done.2, bf16[320,512]{1,0:T(8,128)(2,1)} %copy-done.6, bf16[320,512]{1,0:T(8,128)(2,1)} %copy-done.10, ...), custom_call_target="tpu_custom_call" | custom-call | flops 503316480 | bytes 1048576 | tf_op jit(solution)/shard_map/grads/pallas_call | solution.py:26
  193.9 6.1 %grads.3 = (bf16[1,2048,128]{2,1,0:T(8,128)(2,1)}, bf16[1,2048,128]{2,1,0:T(8,128)(2,1)}, bf16[1,2048,128]{2,1,0:T(8,128)(2,1)}) custom-call(s32[3]{0:T(128)} %copy-done.27, bf16[320,512]{1,0:T(8,128)(2,1)} %copy-done, bf16[320,512]{1,0:T(8,128)(2,1)} %copy-done.2, bf16[320,512]{1,0:T(8,128)(2,1)} %copy-done.6, bf16[320,512]{1,0:T(8,128)(2,1)} %copy-done.10, ...), custom_call_target="tpu_custom_call" | custom-call | flops 503316480 | bytes 1048576 | tf_op jit(solution)/shard_map/grads/pallas_call | solution.py:26
  200.8 2.7 %combine.1 = bf16[32,512]{1,0:T(8,128)(2,1)} custom-call(s32[3]{0:T(128)} %copy-done.21, bf16[1536,128]{1,0:T(8,128)(2,1)} %bitcast.19, bf16[320,32]{1,0:T(8,128)(2,1)} %get-tuple-element.136.refs_2_), custom_call_target="tpu_custom_call" | custom-call | bytes 1048576 | tf_op jit(solution)/shard_map/combine/pallas_call | solution.py:26
  (119 shorter events, 42.9 us)
Async XLA Ops:
  3.1 61.1 %all-to-all-start = ((bf16[64,40,128]{2,1,0:T(8,128)(2,1)}), bf16[64,40,128]{2,1,0:T(8,128)(2,1)S(1)}, u32[]{:S(2)}, u32[]{:S(2)}) async-start(bf16[64,40,128]{2,1,0:T(8,128)(2,1)} %bitcast.20), calls=%async_computation | async-start | bytes 1310720 | tf_op jit(solution)/shard_map/all_to_all | solution.py:305
  26.0 21.1 %collective-permute-start.7 = (bf16[256,256]{1,0:T(8,128)(2,1)S(1)}, bf16[256,256]{1,0:T(8,128)(2,1)S(1)}, u32[]{:S(2)}, u32[]{:S(2)}) collective-permute-start(bf16[256,256]{1,0:T(8,128)(2,1)S(1)} %pad_maximum_fusion.7), channel_id=1, source_target_pairs={{0,0},{1,1},{2,2},{3,3},{4,512},{5,513},{6,514},{7,515},{512,4},{5... | collective-permute-start | bytes 393224 | tf_op jit(solution)/shard_map/ppermute | solution.py:321
  26.7 25.2 %collective-permute-start.6 = (bf16[256,256]{1,0:T(8,128)(2,1)S(1)}, bf16[256,256]{1,0:T(8,128)(2,1)S(1)}, u32[]{:S(2)}, u32[]{:S(2)}) collective-permute-start(bf16[256,256]{1,0:T(8,128)(2,1)S(1)} %pad_maximum_fusion.6), channel_id=1, source_target_pairs={{0,1},{1,2},{2,3},{3,512},{4,513},{5,514},{6,515},{7,0},{512,5},{5... | collective-permute-start | bytes 393224 | tf_op jit(solution)/shard_map/ppermute | solution.py:321
  30.2 24.7 %collective-permute-start.5 = (bf16[256,256]{1,0:T(8,128)(2,1)S(1)}, bf16[256,256]{1,0:T(8,128)(2,1)S(1)}, u32[]{:S(2)}, u32[]{:S(2)}) collective-permute-start(bf16[256,256]{1,0:T(8,128)(2,1)S(1)} %pad_maximum_fusion.5), channel_id=1, source_target_pairs={{0,2},{1,3},{2,512},{3,513},{4,514},{5,515},{6,0},{7,1},{512,6},{5... | collective-permute-start | bytes 393224 | tf_op jit(solution)/shard_map/ppermute | solution.py:321
  34.7 25.3 %collective-permute-start.4 = (bf16[256,256]{1,0:T(8,128)(2,1)S(1)}, bf16[256,256]{1,0:T(8,128)(2,1)S(1)}, u32[]{:S(2)}, u32[]{:S(2)}) collective-permute-start(bf16[256,256]{1,0:T(8,128)(2,1)S(1)} %pad_maximum_fusion.4), channel_id=1, source_target_pairs={{0,3},{1,512},{2,513},{3,514},{4,515},{5,0},{6,1},{7,2},{512,7},{5... | collective-permute-start | bytes 393224 | tf_op jit(solution)/shard_map/ppermute | solution.py:321
  43.1 16.9 %collective-permute-start.3 = (bf16[256,256]{1,0:T(8,128)(2,1)S(1)}, bf16[256,256]{1,0:T(8,128)(2,1)S(1)}, u32[]{:S(2)}, u32[]{:S(2)}) collective-permute-start(bf16[256,256]{1,0:T(8,128)(2,1)S(1)} %pad_maximum_fusion.3), channel_id=1, source_target_pairs={{0,512},{1,513},{2,514},{3,515},{4,0},{5,1},{6,2},{7,3},{512,516},... | collective-permute-start | bytes 393224 | tf_op jit(solution)/shard_map/ppermute | solution.py:321
  47.1 13.0 %collective-permute-start.2 = (bf16[256,256]{1,0:T(8,128)(2,1)}, bf16[256,256]{1,0:T(8,128)(2,1)S(1)}, u32[]{:S(2)}, u32[]{:S(2)}) collective-permute-start(bf16[256,256]{1,0:T(8,128)(2,1)} %pad_maximum_fusion.2), channel_id=1, source_target_pairs={{0,513},{1,514},{2,515},{3,0},{4,1},{5,2},{6,3},{7,512},{512,517},... | collective-permute-start | bytes 393224 | tf_op jit(solution)/shard_map/ppermute | solution.py:321
  51.9 10.1 %collective-permute-start.1 = (bf16[256,256]{1,0:T(8,128)(2,1)}, bf16[256,256]{1,0:T(8,128)(2,1)S(1)}, u32[]{:S(2)}, u32[]{:S(2)}) collective-permute-start(bf16[256,256]{1,0:T(8,128)(2,1)} %pad_maximum_fusion.1), channel_id=1, source_target_pairs={{0,514},{1,515},{2,0},{3,1},{4,2},{5,3},{6,512},{7,513},{512,518},... | collective-permute-start | bytes 393224 | tf_op jit(solution)/shard_map/ppermute | solution.py:321
  54.9 9.3 %collective-permute-start = (bf16[256,256]{1,0:T(8,128)(2,1)}, bf16[256,256]{1,0:T(8,128)(2,1)S(1)}, u32[]{:S(2)}, u32[]{:S(2)}) collective-permute-start(bf16[256,256]{1,0:T(8,128)(2,1)} %pad_maximum_fusion), channel_id=1, source_target_pairs={{0,515},{1,0},{2,1},{3,2},{4,3},{5,512},{6,513},{7,514},{512,519},... | collective-permute-start | bytes 393224 | tf_op jit(solution)/shard_map/ppermute | solution.py:321
  65.1 54.3 %collective-permute-start.22 = (bf16[2048,640]{1,0:T(8,128)(2,1)S(1)}, bf16[2048,640]{1,0:T(8,128)(2,1)S(1)}, u32[]{:S(2)}, u32[]{:S(2)}) collective-permute-start(bf16[2048,640]{1,0:T(8,128)(2,1)S(1)} %bundle.1.refs_15_.refs_9_), channel_id=1, source_target_pairs={{0,512},{512,0},{1,513},{513,1},{2,514},{514,2},{3,515},{515,3},{4... | collective-permute-start | bytes 7864328 | tf_op jit(solution)/shard_map/ppermute | solution.py:331
  69.0 13.9 %collective-permute-start.8 = (bf16[320,512]{1,0:T(8,128)(2,1)S(1)}, bf16[320,512]{1,0:T(8,128)(2,1)S(1)}, u32[]{:S(2)}, u32[]{:S(2)}) collective-permute-start(bf16[320,512]{1,0:T(8,128)(2,1)S(1)} %get-tuple-element.111.refs_1_), channel_id=1, source_target_pairs={{0,1},{512,519},{1,2},{513,512},{2,3},{514,513},{3,4},{515,514},{4... | collective-permute-start | bytes 983048 | tf_op jit(solution)/shard_map/ppermute | solution.py:348
  75.1 11.7 %collective-permute-start.12 = (bf16[320,512]{1,0:T(8,128)(2,1)S(1)}, bf16[320,512]{1,0:T(8,128)(2,1)S(1)}, u32[]{:S(2)}, u32[]{:S(2)}) collective-permute-start(bf16[320,512]{1,0:T(8,128)(2,1)S(1)} %get-tuple-element.119.refs_8_.refs_9_), channel_id=1, source_target_pairs={{0,7},{512,513},{1,0},{513,514},{2,1},{514,515},{3,2},{515,516},{4... | collective-permute-start | bytes 983048 | tf_op jit(solution)/shard_map/ppermute | solution.py:351
  77.0 13.4 %collective-permute-start.16 = (bf16[320,512]{1,0:T(8,128)(2,1)S(1)}, bf16[320,512]{1,0:T(8,128)(2,1)S(1)}, u32[]{:S(2)}, u32[]{:S(2)}) collective-permute-start(bf16[320,512]{1,0:T(8,128)(2,1)S(1)} %get-tuple-element.111.refs_1_), channel_id=1, source_target_pairs={{0,7},{512,513},{1,0},{513,514},{2,1},{514,515},{3,2},{515,516},{4... | collective-permute-start | bytes 983048 | tf_op jit(solution)/shard_map/ppermute | solution.py:351
  80.0 13.0 %collective-permute-start.19 = (bf16[320,512]{1,0:T(8,128)(2,1)S(1)}, bf16[320,512]{1,0:T(8,128)(2,1)S(1)}, u32[]{:S(2)}, u32[]{:S(2)}) collective-permute-start(bf16[320,512]{1,0:T(8,128)(2,1)S(1)} %get-tuple-element.119.refs_8_.refs_9_), channel_id=1, source_target_pairs={{0,1},{512,519},{1,2},{513,512},{2,3},{514,513},{3,4},{515,514},{4... | collective-permute-start | bytes 983048 | tf_op jit(solution)/shard_map/ppermute | solution.py:348
  82.9 15.1 %collective-permute-start.9 = (bf16[320,512]{1,0:T(8,128)(2,1)S(1)}, bf16[320,512]{1,0:T(8,128)(2,1)S(1)}, u32[]{:S(2)}, u32[]{:S(2)}) collective-permute-start(bf16[320,512]{1,0:T(8,128)(2,1)S(1)} %collective-permute-done.8.refs_2_), channel_id=1, source_target_pairs={{0,1},{512,519},{1,2},{513,512},{2,3},{514,513},{3,4},{515,514},{4... | collective-permute-start | bytes 983048 | tf_op jit(solution)/shard_map/ppermute | solution.py:348
  86.8 15.6 %collective-permute-start.13 = (bf16[320,512]{1,0:T(8,128)(2,1)S(1)}, bf16[320,512]{1,0:T(8,128)(2,1)S(1)}, u32[]{:S(2)}, u32[]{:S(2)}) collective-permute-start(bf16[320,512]{1,0:T(8,128)(2,1)S(1)} %collective-permute-done.12.refs_14_.refs_16_), channel_id=1, source_target_pairs={{0,7},{512,513},{1,0},{513,514},{2,1},{514,515},{3,2},{515,516},{4... | collective-permute-start | bytes 983048 | tf_op jit(solution)/shard_map/ppermute | solution.py:351
  90.4 14.7 %collective-permute-start.17 = (bf16[320,512]{1,0:T(8,128)(2,1)S(1)}, bf16[320,512]{1,0:T(8,128)(2,1)S(1)}, u32[]{:S(2)}, u32[]{:S(2)}) collective-permute-start(bf16[320,512]{1,0:T(8,128)(2,1)S(1)} %collective-permute-done.16.refs_7_.refs_8_), channel_id=1, source_target_pairs={{0,7},{512,513},{1,0},{513,514},{2,1},{514,515},{3,2},{515,516},{4... | collective-permute-start | bytes 983048 | tf_op jit(solution)/shard_map/ppermute | solution.py:351
  93.0 14.8 %collective-permute-start.20 = (bf16[320,512]{1,0:T(8,128)(2,1)S(1)}, bf16[320,512]{1,0:T(8,128)(2,1)S(1)}, u32[]{:S(2)}, u32[]{:S(2)}) collective-permute-start(bf16[320,512]{1,0:T(8,128)(2,1)S(1)} %collective-permute-done.19.refs_9_.refs_10_), channel_id=1, source_target_pairs={{0,1},{512,519},{1,2},{513,512},{2,3},{514,513},{3,4},{515,514},{4... | collective-permute-start | bytes 983048 | tf_op jit(solution)/shard_map/ppermute | solution.py:348
  98.0 14.0 %collective-permute-start.10 = (bf16[320,512]{1,0:T(8,128)(2,1)S(1)}, bf16[320,512]{1,0:T(8,128)(2,1)S(1)}, u32[]{:S(2)}, u32[]{:S(2)}) collective-permute-start(bf16[320,512]{1,0:T(8,128)(2,1)S(1)} %collective-permute-done.9.refs_3_), channel_id=1, source_target_pairs={{0,1},{512,519},{1,2},{513,512},{2,3},{514,513},{3,4},{515,514},{4... | collective-permute-start | bytes 983048 | tf_op jit(solution)/shard_map/ppermute | solution.py:348
  102.4 14.0 %collective-permute-start.14 = (bf16[320,512]{1,0:T(8,128)(2,1)S(1)}, bf16[320,512]{1,0:T(8,128)(2,1)S(1)}, u32[]{:S(2)}, u32[]{:S(2)}) collective-permute-start(bf16[320,512]{1,0:T(8,128)(2,1)S(1)} %collective-permute-done.13.refs_13_.refs_15_), channel_id=1, source_target_pairs={{0,7},{512,513},{1,0},{513,514},{2,1},{514,515},{3,2},{515,516},{4... | collective-permute-start | bytes 983048 | tf_op jit(solution)/shard_map/ppermute | solution.py:351
  105.1 14.0 %collective-permute-start.18 = (bf16[320,512]{1,0:T(8,128)(2,1)S(1)}, bf16[320,512]{1,0:T(8,128)(2,1)S(1)}, u32[]{:S(2)}, u32[]{:S(2)}) collective-permute-start(bf16[320,512]{1,0:T(8,128)(2,1)S(1)} %collective-permute-done.17.refs_6_.refs_7_), channel_id=1, source_target_pairs={{0,7},{512,513},{1,0},{513,514},{2,1},{514,515},{3,2},{515,516},{4... | collective-permute-start | bytes 983048 | tf_op jit(solution)/shard_map/ppermute | solution.py:351
  107.9 11.5 %collective-permute-start.21 = (bf16[320,512]{1,0:T(8,128)(2,1)S(1)}, bf16[320,512]{1,0:T(8,128)(2,1)S(1)}, u32[]{:S(2)}, u32[]{:S(2)}) collective-permute-start(bf16[320,512]{1,0:T(8,128)(2,1)S(1)} %collective-permute-done.20.refs_10_.refs_11_), channel_id=1, source_target_pairs={{0,1},{512,519},{1,2},{513,512},{2,3},{514,513},{3,4},{515,514},{4... | collective-permute-start | bytes 983048 | tf_op jit(solution)/shard_map/ppermute | solution.py:348
  112.1 13.7 %collective-permute-start.11 = (bf16[320,512]{1,0:T(8,128)(2,1)S(1)}, bf16[320,512]{1,0:T(8,128)(2,1)S(1)}, u32[]{:S(2)}, u32[]{:S(2)}) collective-permute-start(bf16[320,512]{1,0:T(8,128)(2,1)S(1)} %collective-permute-done.10.refs_4_), channel_id=1, source_target_pairs={{0,1},{512,519},{1,2},{513,512},{2,3},{514,513},{3,4},{515,514},{4... | collective-permute-start | bytes 983048 | tf_op jit(solution)/shard_map/ppermute | solution.py:348
  116.5 9.7 %collective-permute-start.15 = (bf16[320,512]{1,0:T(8,128)(2,1)S(1)}, bf16[320,512]{1,0:T(8,128)(2,1)S(1)}, u32[]{:S(2)}, u32[]{:S(2)}) collective-permute-start(bf16[320,512]{1,0:T(8,128)(2,1)S(1)} %collective-permute-done.14.refs_12_.refs_14_), channel_id=1, source_target_pairs={{0,7},{512,513},{1,0},{513,514},{2,1},{514,515},{3,2},{515,516},{4... | collective-permute-start | bytes 983048 | tf_op jit(solution)/shard_map/ppermute | solution.py:351
  127.1 8.4 %collective-permute-start.23 = (bf16[320,256]{1,0:T(8,128)(2,1)S(1)}, bf16[320,256]{1,0:T(8,128)(2,1)S(1)}, u32[]{:S(2)}, u32[]{:S(2)}) collective-permute-start(bf16[320,256]{1,0:T(8,128)(2,1)S(1)} %get-tuple-element.127.refs_1_.refs_17_), channel_id=1, source_target_pairs={{0,1},{1,2},{2,3},{3,4},{4,5},{5,6},{6,7},{7,0},{8,9},{9,10},{10,1... | collective-permute-start | bytes 491528 | tf_op jit(solution)/shard_map/ppermute | solution.py:348
  130.6 7.3 %collective-permute-start.27 = (bf16[320,256]{1,0:T(8,128)(2,1)S(1)}, bf16[320,256]{1,0:T(8,128)(2,1)S(1)}, u32[]{:S(2)}, u32[]{:S(2)}) collective-permute-start(bf16[320,256]{1,0:T(8,128)(2,1)S(1)} %get-tuple-element.127.refs_1_.refs_17_), channel_id=1, source_target_pairs={{0,7},{1,0},{2,1},{3,2},{4,3},{5,4},{6,5},{7,6},{8,15},{9,8},{10,9... | collective-permute-start | bytes 491528 | tf_op jit(solution)/shard_map/ppermute | solution.py:351
  135.5 8.4 %collective-permute-start.24 = (bf16[320,256]{1,0:T(8,128)(2,1)S(1)}, bf16[320,256]{1,0:T(8,128)(2,1)S(1)}, u32[]{:S(2)}, u32[]{:S(2)}) collective-permute-start(bf16[320,256]{1,0:T(8,128)(2,1)S(1)} %collective-permute-done.23.refs_2_), channel_id=1, source_target_pairs={{0,1},{1,2},{2,3},{3,4},{4,5},{5,6},{6,7},{7,0},{8,9},{9,10},{10,1... | collective-permute-start | bytes 491528 | tf_op jit(solution)/shard_map/ppermute | solution.py:348
  137.9 8.0 %collective-permute-start.28 = (bf16[320,256]{1,0:T(8,128)(2,1)S(1)}, bf16[320,256]{1,0:T(8,128)(2,1)S(1)}, u32[]{:S(2)}, u32[]{:S(2)}) collective-permute-start(bf16[320,256]{1,0:T(8,128)(2,1)S(1)} %collective-permute-done.27.refs_8_), channel_id=1, source_target_pairs={{0,7},{1,0},{2,1},{3,2},{4,3},{5,4},{6,5},{7,6},{8,15},{9,8},{10,9... | collective-permute-start | bytes 491528 | tf_op jit(solution)/shard_map/ppermute | solution.py:351
  144.0 8.4 %collective-permute-start.25 = (bf16[320,256]{1,0:T(8,128)(2,1)S(1)}, bf16[320,256]{1,0:T(8,128)(2,1)S(1)}, u32[]{:S(2)}, u32[]{:S(2)}) collective-permute-start(bf16[320,256]{1,0:T(8,128)(2,1)S(1)} %collective-permute-done.24.refs_3_), channel_id=1, source_target_pairs={{0,1},{1,2},{2,3},{3,4},{4,5},{5,6},{6,7},{7,0},{8,9},{9,10},{10,1... | collective-permute-start | bytes 491528 | tf_op jit(solution)/shard_map/ppermute | solution.py:348
  145.9 8.4 %collective-permute-start.29 = (bf16[320,256]{1,0:T(8,128)(2,1)S(1)}, bf16[320,256]{1,0:T(8,128)(2,1)S(1)}, u32[]{:S(2)}, u32[]{:S(2)}) collective-permute-start(bf16[320,256]{1,0:T(8,128)(2,1)S(1)} %collective-permute-done.28.refs_7_), channel_id=1, source_target_pairs={{0,7},{1,0},{2,1},{3,2},{4,3},{5,4},{6,5},{7,6},{8,15},{9,8},{10,9... | collective-permute-start | bytes 491528 | tf_op jit(solution)/shard_map/ppermute | solution.py:351
  152.4 8.4 %collective-permute-start.26 = (bf16[320,256]{1,0:T(8,128)(2,1)S(1)}, bf16[320,256]{1,0:T(8,128)(2,1)S(1)}, u32[]{:S(2)}, u32[]{:S(2)}) collective-permute-start(bf16[320,256]{1,0:T(8,128)(2,1)S(1)} %collective-permute-done.25.refs_4_), channel_id=1, source_target_pairs={{0,1},{1,2},{2,3},{3,4},{4,5},{5,6},{6,7},{7,0},{8,9},{9,10},{10,1... | collective-permute-start | bytes 491528 | tf_op jit(solution)/shard_map/ppermute | solution.py:348
  163.2 36.8 %all-to-all-start.1 = ((bf16[64,24,128]{2,1,0:T(8,128)(2,1)}), bf16[64,24,128]{2,1,0:T(8,128)(2,1)S(1)}, u32[]{:S(2)}, u32[]{:S(2)}) async-start(bf16[64,24,128]{2,1,0:T(8,128)(2,1)} %bitcast.10), calls=%async_computation.1 | async-start | bytes 786432 | tf_op jit(solution)/shard_map/all_to_all | solution.py:399
  (31 other events, 722.1 us)
